TPU v7x, 32 devices: a whole 2x2x4 slice. The times are simulated.
32 devices in a mesh: wave: 4 (over y, core), tm: 8 (over z, x).
Axes of the slice: x: 2, y: 2, z: 4, core: 2. Of those that a mesh axis runs over, the one named last changes fastest.
Arguments:
- field: float32 [4, 128, 2, 2, 8192], P(None, 'wave', None, None, 'tm'), may hold values from -3 to 3
- lit_count: int32 [4], replicated, may hold values from 32 to 128
- route_fibre: int32 [4, 64], replicated, may hold values from 0 to 3, as said below
- route_slot: int32 [4, 64], replicated, may hold values from 0 to 63, as said below
- dispersion: float32 [2, 4], replicated, may hold values from 20 to 42
- nonlinearity: float32 [2, 4], replicated, may hold values from 0.25 to 2.5
Outputs:
- received: float32 [4, 128, 2, 2, 8192], P(None, 'wave', None, None, 'tm')
Inputs may be any that keep to these rules, and one draw needn't show every extreme that they name: `route_fibre`: together with route_slot it names every block of every fibre exactly once. `route_slot`: blocks 16 g .. 16 g + 15 of all fibres form channel group g. Of the 64 blocks of one group, at most 32 land in any one group, and every draw has pairs of groups with exactly 32.
All inputs are finite; a program needn't handle non-finite values.
Results may differ from a plain program's by a relative error of at most 0.0003.
Values sent between devices are 32-bit elements; how exact they have to be, the bound alone decides.
No kernel may reach another device: no remote copies, remote signals or barrier semaphores. Data moves between devices by JAX's collectives and lax.ppermute only.
A program may use at most 64 MiB of HBM per device.

v0:
```python
import math

import jax
import jax.numpy as jnp
from jax import lax
from jax.sharding import PartitionSpec as P

CH = 128
BLK = 2
FA = 16
FB = 128
HALF = 2
MARGIN = 512
VALID = 1024


def padded(block, sides, width):
    for axis, dim in sides:
        count = lax.axis_size(axis)
        forward = [(i, i + 1) for i in range(count - 1)]
        forward.append((count - 1, 0))
        backward = [(target, source) for source, target in forward]
        low = lax.ppermute(
            lax.slice_in_dim(block, block.shape[dim] - width, None, axis=dim), axis, forward
        )
        high = lax.ppermute(lax.slice_in_dim(block, 0, width, axis=dim), axis, backward)
        block = jnp.concatenate([low, block, high], axis=dim)
    return block


def trig_table(rows, columns, period):
    first = lax.broadcasted_iota(jnp.int32, (rows, columns), 0)
    second = lax.broadcasted_iota(jnp.int32, (rows, columns), 1)
    angle = (first * second % period).astype(jnp.float32) * (2.0 * math.pi / period)
    return (jnp.cos(angle), jnp.sin(angle))


def filter_tables(spread, channel):
    period = FA * FB
    row_index = lax.broadcasted_iota(jnp.int32, (FA, FB), 0)
    col_index = lax.broadcasted_iota(jnp.int32, (FA, FB), 1)
    freq_index = row_index + FA * col_index
    signed = jnp.where(freq_index < period // 2, freq_index, freq_index - period).astype(
        jnp.float32
    )
    omega = signed * (2.0 * math.pi / period)
    offsets = math.pi / 2.0 * (2.0 * channel.astype(jnp.float32) + 1.0 - CH) / CH
    theta = spread[:, None, None, None] * (
        omega[None, None] ** 2 + 2.0 * omega[None, None] * offsets[None, :, None, None]
    )
    return (jnp.cos(theta)[:, :, None, None], jnp.sin(theta)[:, :, None, None])


def row_product(values, table):
    return jnp.einsum("fcpsjab,rksa->fcprjkb", values, table, precision=lax.Precision.HIGHEST)


def column_product(values, table):
    return jnp.einsum("fcpsjkb,sbrm->fcprjkm", values, table, precision=lax.Precision.HIGHEST)


def disperse(extended, filters):
    fibres, channels = (extended.shape[0], extended.shape[1])
    pieces_count = extended.shape[-1] // VALID
    pieces = extended.reshape(fibres, channels, 2, 2, pieces_count, VALID)
    blocks = jnp.concatenate([pieces[..., :-1, :], pieces[..., 1:, :]], axis=-1)
    blocks = blocks.reshape(fibres, channels, 2, 2, pieces_count - 1, FA, FB)
    cos_first, sin_first = trig_table(FA, FA, FA)
    cos_second, sin_second = trig_table(FB, FB, FB)
    cos_twist, sin_twist = trig_table(FA, FB, FA * FB)
    row_forward = jnp.stack(
        [jnp.stack([cos_first, sin_first], axis=1), jnp.stack([-sin_first, cos_first], axis=1)],
        axis=0,
    )
    col_forward = jnp.stack(
        [jnp.stack([cos_second, -sin_second], axis=1), jnp.stack([sin_second, cos_second], axis=1)],
        axis=0,
    )
    col_inverse = jnp.stack(
        [jnp.stack([cos_second, sin_second], axis=1), jnp.stack([-sin_second, cos_second], axis=1)],
        axis=0,
    )
    scale = 1.0 / (FA * FB)
    keep_cos = cos_first[FA // 4 : 3 * FA // 4] * scale
    keep_sin = sin_first[FA // 4 : 3 * FA // 4] * scale
    row_keep = jnp.stack(
        [jnp.stack([keep_cos, -keep_sin], axis=1), jnp.stack([keep_sin, keep_cos], axis=1)], axis=0
    )
    first = row_product(blocks, row_forward)
    first_real = first[:, :, :, 0]
    first_imag = first[:, :, :, 1]
    twisted = jnp.stack(
        [
            first_real * cos_twist + first_imag * sin_twist,
            first_imag * cos_twist - first_real * sin_twist,
        ],
        axis=3,
    )
    spectrum = column_product(twisted, col_forward)
    spec_real = spectrum[:, :, :, 0]
    spec_imag = spectrum[:, :, :, 1]
    filt_cos, filt_sin = filters
    shaped = jnp.stack(
        [spec_real * filt_cos - spec_imag * filt_sin, spec_real * filt_sin + spec_imag * filt_cos],
        axis=3,
    )
    back = column_product(shaped, col_inverse)
    back_real = back[:, :, :, 0]
    back_imag = back[:, :, :, 1]
    untwisted = jnp.stack(
        [
            back_real * cos_twist - back_imag * sin_twist,
            back_real * sin_twist + back_imag * cos_twist,
        ],
        axis=3,
    )
    result = row_product(untwisted, row_keep)
    length = (pieces_count - 1) * VALID
    return result.reshape(fibres, channels, 2, 2, length)


def nonlinear(waveform, strength):
    power = jnp.sum(waveform * waveform, axis=(2, 3))
    partial_total = jnp.sum(power, axis=1)
    fibre_total = lax.psum(partial_total, "wave")
    phase = strength[:, None, None] * (2.0 * fibre_total[:, None, :] - power) / CH
    cosine = jnp.cos(phase)[:, :, None, :]
    sine = jnp.sin(phase)[:, :, None, :]
    real_part = waveform[:, :, :, 0]
    imag_part = waveform[:, :, :, 1]
    return jnp.stack(
        [real_part * cosine - imag_part * sine, real_part * sine + imag_part * cosine], axis=3
    )


def switch_exchange(waveform, route_fibre, route_slot):
    groups = lax.axis_size("wave")
    my_group = lax.axis_index("wave")
    fibres, channels, samples = (waveform.shape[0], waveform.shape[1], waveform.shape[-1])
    group_blocks = channels // BLK
    sends = fibres * group_blocks
    capacity = 2 * sends // groups
    slot_all = (
        route_slot.reshape(fibres, groups, group_blocks).transpose(1, 0, 2).reshape(groups, sends)
    )
    fibre_all = (
        route_fibre.reshape(fibres, groups, group_blocks).transpose(1, 0, 2).reshape(groups, sends)
    )
    target_all = slot_all // group_blocks
    landing_all = fibre_all * group_blocks + slot_all % group_blocks
    position = jnp.arange(sends)
    earlier = (target_all[:, :, None] == target_all[:, None, :]) & (
        position[None, None, :] < position[None, :, None]
    )
    arrival_all = jnp.sum(earlier.astype(jnp.int32), axis=2)
    my_target = lax.dynamic_index_in_dim(target_all, my_group, 0, keepdims=False)
    my_arrival = lax.dynamic_index_in_dim(arrival_all, my_group, 0, keepdims=False)
    slot_index = my_target * capacity + my_arrival
    slot_range = jnp.arange(groups * capacity)
    matches = slot_index[None, :] == slot_range[:, None]
    source_item = jnp.sum(jnp.where(matches, position[None, :], 0), axis=1)
    occupied = jnp.any(matches, axis=1)
    items = waveform.reshape(sends, BLK, 2, 2, samples)
    outgoing = (
        jnp.take(items, source_item, axis=0)
        * occupied.astype(jnp.float32)[:, None, None, None, None]
    )
    outgoing = outgoing.reshape(groups, capacity, BLK, 2, 2, samples)
    incoming = lax.all_to_all(outgoing, "wave", split_axis=0, concat_axis=0, tiled=True)
    mine = target_all == my_group
    receive_slot = jnp.arange(groups)[:, None] * capacity + arrival_all
    hits = mine[:, :, None] & (landing_all[:, :, None] == position[None, None, :])
    take_from = jnp.sum(jnp.where(hits, receive_slot[:, :, None], 0), axis=(0, 1))
    placed = jnp.take(incoming.reshape(groups * capacity, BLK, 2, 2, samples), take_from, axis=0)
    return placed.reshape(fibres, channels, 2, 2, samples)


def local(field, lit_count, route_fibre, route_slot, dispersion, nonlinearity):
    channels = field.shape[1]
    my_group = lax.axis_index("wave")
    channel = my_group * channels + jnp.arange(channels)
    lit_mask = channel[None, :] < lit_count[:, None]
    waveform = jnp.where(lit_mask[:, :, None, None, None], field, jnp.zeros_like(field))
    for span_index in range(2):
        if span_index == 1:
            waveform = switch_exchange(waveform, route_fibre, route_slot)
        filters = filter_tables(dispersion[span_index], channel)
        for step_index in range(HALF):
            extended = padded(waveform, (("tm", 4),), MARGIN)
            waveform = nonlinear(disperse(extended, filters), nonlinearity[span_index])
    return waveform


def solution(mesh):
    return jax.shard_map(
        local,
        mesh=mesh,
        in_specs=(P(None, "wave", None, None, "tm"), P(), P(), P(), P(), P()),
        out_specs=P(None, "wave", None, None, "tm"),
        check_vma=False,
    )
```

profile of v0, /device:TPU:0, one launch (start us, length us, event | category | flops | bytes accessed | tf_op | source)
XLA Modules:
  0.0 613.0 jit_solution(11748254482175511469)
XLA Ops:
  13.4 8.8 %multiply_cosine_fusion = (f32[4,32,16,128]{3,1,2,0:T(8,128)S(1)}, f32[4,32,16,128]{3,1,2,0:T(8,128)}, f32[4,32,16,128]{3,1,2,0:T(8,128)}, f32[4,32,16,128]{3,1,2,0:T(8,128)}) fusion(f32[4]{0:T(128)S(1)} %get-tuple-element.94, f32[32,16,128]{2,0,1:T(8,128)S(1)} %multiply_add_fusion.16, f32[4]{0:T(128)S(1)} %get-tuple-element.95), kind=kLoop, calls=%fused_computation.115 | loop fusion | flops 524288 | bytes 4456480 | tf_op jit(solution)/shard_map/cos | solution.py:51
  22.2 31.4 %collective-permute-done = f32[4,32,2,2,512]{4,3,2,1,0:T(2,128)} collective-permute-done((f32[4,32,2,2,512]{4,3,2,1,0:T(2,128)}, f32[4,32,2,2,512]{4,3,2,1,0:T(2,128)}, u32[]{:S(2)}, u32[]{:S(2)}) %collective-permute-start) | collective-permute-done | bytes 1048608 | tf_op jit(solution)/shard_map/ppermute | solution.py:23
  55.9 5.4 pad_maximum_fusion
  61.2 7.9 %reshape.807 = f32[4,32,2,2,2,1024]{5,4,3,2,1,0:T(2,128)} reshape(f32[4,32,2,2,2048]{4,3,2,1,0:T(2,128)} %pad_maximum_fusion) | data formatting | bytes 8388608 | tf_op jit(solution)/shard_map/reshape | solution.py:65
  69.2 7.9 %fusion.148 = (f32[4,32,2,2,1,1024]{5,4,3,2,1,0:T(1,128)S(1)}, f32[4,32,2,2,1,1024]{5,4,3,2,1,0:T(1,128)S(1)}) fusion(f32[4,32,2,2,2,1024]{5,4,3,2,1,0:T(2,128)} %reshape.807), kind=kLoop, calls=%fused_computation.280 | loop fusion | bytes 8388608 | tf_op jit(solution)/shard_map/slice | solution.py:66
  79.2 4.6 pad_maximum_fusion.1
  83.8 6.5 %reshape.850 = f32[4,32,2,2,16,128,1]{5,4,3,2,1,0,6:T(8,128)} reshape(f32[4,32,2,2,1,2048]{5,3,2,1,0,4:T(2,128)} %pad_maximum_fusion.1) | data formatting | bytes 8388608 | tf_op jit(solution)/shard_map/reshape.3
  90.3 5.6 convolution_bitcast_fusion.2
  97.4 6.5 %fusion.35 = f32[4,32,2,2,1,16,128]{6,1,5,2,0,3,4:T(8,128)S(1)} fusion(f32[4,32,2,2,16,128]{5,4,2,1,0,3:T(8,128)S(1)} %maximum_bitcast_fusion, f32[1,128,2,128]{3,1,0,2:T(8,128)S(1)} %get-tuple-element.80, f32[1,128,2,128]{3,1,0,2:T(8,128)S(1)} %get-tuple-element.83), kind=kOutput, calls=%fused_computation.58 | convolution fusion | flops 3221291008 | bytes 8650752 | tf_op jit(solution)/shard_map/fcpsjkb,sbrm->fcprjkm/dot_general | solution.py:59
  105.8 6.7 %fusion.38 = f32[4,32,2,2,1,16,128]{6,5,2,1,0,3,4:T(8,128)S(1)} fusion(f32[4,32,2,2,16,128,1]{5,1,4,2,0,3,6:T(8,128)S(1)} %maximum_bitcast_fusion.1, f32[1,128,2,128]{3,1,2,0:T(8,128)S(1)} %copy-done.9, f32[1,128,2,128]{3,1,2,0:T(8,128)S(1)} %copy-done.5), kind=kOutput, calls=%fused_computation.59 | convolution fusion | flops 3221291008 | bytes 8650752 | tf_op jit(solution)/shard_map/fcpsjkb,sbrm->fcprjkm/dot_general | solution.py:59
  113.5 4.4 multiply_reduce_fusion.7
  119.8 10.1 %psum.28 = f32[4,1024]{1,0:T(4,128)S(1)} all-reduce(f32[4,1024]{1,0:T(4,128)S(1)} %bitcast.348), channel_id=1, replica_groups=mesh['wave'=4,'tm'=8] {'wave'}, use_global_device_ids=true, to_apply=%region_4.5 | all-reduce | flops 4096 | bytes 32768 | tf_op jit(solution)/shard_map/psum | solution.py:125
  141.4 4.4 collective-permute-start.3
  146.5 39.7 %collective-permute-done.2 = f32[4,32,2,2,512]{4,2,1,0,3:T(2,128)} collective-permute-done((f32[4,32,2,2,512]{4,2,1,0,3:T(2,128)}, f32[4,32,2,2,512]{4,2,1,0,3:T(2,128)}, u32[]{:S(2)}, u32[]{:S(2)}) %collective-permute-start.2) | collective-permute-done | bytes 1048608 | tf_op jit(solution)/shard_map/ppermute | solution.py:23
  189.1 5.7 pad_maximum_fusion.2
  194.8 7.9 %reshape.813 = f32[4,32,2,2,2,1024]{5,4,2,1,0,3:T(2,128)} reshape(f32[4,32,2,2,2048]{4,2,1,0,3:T(2,128)} %pad_maximum_fusion.2) | data formatting | bytes 8388608 | tf_op jit(solution)/shard_map/reshape | solution.py:65
  202.7 7.8 %fusion.147 = (f32[4,32,2,2,1,1024]{5,4,2,1,0,3:T(1,128)S(1)}, f32[4,32,2,2,1,1024]{5,4,2,1,0,3:T(1,128)S(1)}) fusion(f32[4,32,2,2,2,1024]{5,4,2,1,0,3:T(2,128)} %reshape.813), kind=kLoop, calls=%fused_computation.279 | loop fusion | bytes 8388608 | tf_op jit(solution)/shard_map/slice | solution.py:66
  213.8 4.6 pad_maximum_fusion.3
  218.4 6.5 %reshape.861 = f32[4,32,2,2,16,128,1]{5,4,3,2,1,0,6:T(8,128)} reshape(f32[4,32,2,2,1,2048]{5,3,2,1,0,4:T(2,128)} %pad_maximum_fusion.3) | data formatting | bytes 8388608 | tf_op jit(solution)/shard_map/reshape.42
  224.9 5.8 convolution_bitcast_fusion.1
  232.1 6.5 %fusion.41 = f32[4,32,2,2,1,16,128]{6,1,5,2,0,3,4:T(8,128)S(1)} fusion(f32[4,32,2,2,16,128]{5,4,2,1,0,3:T(8,128)S(1)} %maximum_bitcast_fusion.3, f32[1,128,2,128]{3,1,0,2:T(8,128)S(1)} %get-tuple-element.80, f32[1,128,2,128]{3,1,0,2:T(8,128)S(1)} %get-tuple-element.83), kind=kOutput, calls=%fused_computation.60 | convolution fusion | flops 3221291008 | bytes 8650752 | tf_op jit(solution)/shard_map/fcpsjkb,sbrm->fcprjkm/dot_general | solution.py:59
  240.5 6.4 %fusion.44 = f32[4,32,2,2,1,16,128]{6,5,2,1,0,3,4:T(8,128)S(1)} fusion(f32[4,32,2,2,16,128,1]{5,1,4,2,0,3,6:T(8,128)S(1)} %maximum_bitcast_fusion.4, f32[1,128,2,128]{3,1,2,0:T(8,128)S(1)} %copy-done.10, f32[1,128,2,128]{3,1,2,0:T(8,128)S(1)} %copy-done.6), kind=kOutput, calls=%fused_computation.61 | convolution fusion | flops 3221291008 | bytes 8650752 | tf_op jit(solution)/shard_map/fcpsjkb,sbrm->fcprjkm/dot_general | solution.py:59
  252.9 10.1 %psum.29 = f32[4,1024]{1,0:T(4,128)S(1)} all-reduce(f32[4,1024]{1,0:T(4,128)S(1)} %bitcast.349), channel_id=1, replica_groups=mesh['wave'=4,'tm'=8] {'wave'}, use_global_device_ids=true, to_apply=%region_7.8 | all-reduce | flops 4096 | bytes 32768 | tf_op jit(solution)/shard_map/psum | solution.py:125
  272.1 8.6 %gather_fusion = f32[128,2,2,2,1024]{4,2,1,3,0:T(2,128)} fusion(f32[64,2,2,2,1024]{4,2,1,0,3:T(2,128)S(1)} %pad_maximum_fusion.8, s32[1024]{0:T(1024)S(1)} %pad_clamp_fusion.1), kind=kCustom, calls=%fused_computation | custom fusion | bytes 8389120 | tf_op jit(solution)/shard_map/jit(_take)/gather | solution.py:165
  280.7 6.3 %copy.122 = f32[128,2,2,2,1024]{4,3,2,1,0:T(2,128)S(1)} copy(f32[128,2,2,2,1024]{4,2,1,3,0:T(2,128)} %gather_fusion) | data formatting | bytes 8388608 | tf_op jit(solution)/shard_map/jit(_take)/gather | solution.py:165
  287.0 5.9 select_multiply_fusion
  292.9 5.4 all-to-all-start
  299.0 47.4 %all-to-all-done = f32[4,32,2,2,2,1024]{5,4,3,2,1,0:T(2,128)} async-done(((f32[4,32,2,2,2,1024]{5,4,3,2,1,0:T(2,128)}), f32[4,32,2,2,2,1024]{5,4,3,2,1,0:T(2,128)}, u32[]{:S(2)}, u32[]{:S(2)}) %all-to-all-start) | async-done | bytes 4194336 | tf_op jit(solution)/shard_map/all_to_all | solution.py:169
  346.5 5.0 gather_fusion.1
  353.4 4.7 collective-permute-start.5
  358.1 40.2 %collective-permute-done.4 = f32[4,32,2,2,512]{4,3,2,1,0:T(2,128)S(1)} collective-permute-done((f32[4,32,2,2,512]{4,3,2,1,0:T(2,128)S(1)}, f32[4,32,2,2,512]{4,3,2,1,0:T(2,128)S(1)}, u32[]{:S(2)}, u32[]{:S(2)}) %collective-permute-start.4) | collective-permute-done | bytes 1048608 | tf_op jit(solution)/shard_map/ppermute | solution.py:23
  406.1 7.9 %reshape.890 = f32[4,32,2,2,2,1024]{5,4,3,2,1,0:T(2,128)} reshape(f32[4,32,2,2,2048]{4,3,2,1,0:T(2,128)} %pad_maximum_fusion.4) | data formatting | bytes 8388608 | tf_op jit(solution)/shard_map/reshape | solution.py:65
  414.1 9.2 %fusion.146 = (f32[4,32,2,2,1,1024]{5,4,3,2,1,0:T(1,128)S(1)}, f32[4,32,2,2,1,1024]{5,4,3,2,1,0:T(1,128)}) fusion(f32[4,32,2,2,2,1024]{5,4,3,2,1,0:T(2,128)} %reshape.890), kind=kLoop, calls=%fused_computation.278 | loop fusion | bytes 8388608 | tf_op jit(solution)/shard_map/slice | solution.py:66
  423.3 10.0 %pad_maximum_fusion.5 = f32[4,32,2,2,1,2048]{5,4,3,2,1,0:T(1,128)} fusion(f32[4,32,2,2,1,1024]{5,4,3,2,1,0:T(1,128)} %get-tuple-element.42, f32[4,32,2,2,1,1024]{5,4,3,2,1,0:T(1,128)S(1)} %get-tuple-element.41), kind=kLoop, calls=%fused_computation.13 | loop fusion | flops 1048576 | bytes 8388608 | tf_op jit(solution)/shard_map/concatenate | solution.py:66
  433.3 6.2 %copy.198 = f32[4,32,2,2,1,2048]{5,4,1,3,2,0:T(1,128)S(1)} copy(f32[4,32,2,2,1,2048]{5,4,3,2,1,0:T(1,128)} %pad_maximum_fusion.5) | data formatting | bytes 8388608 | tf_op jit(solution)/shard_map/concatenate | solution.py:66
  444.7 6.5 %fusion.50 = f32[4,32,2,2,1,16,128]{6,1,5,2,0,3,4:T(8,128)S(1)} fusion(f32[4,32,2,2,16,128]{5,4,2,1,0,3:T(8,128)S(1)} %maximum_bitcast_fusion.6, f32[1,128,2,128]{3,1,0,2:T(8,128)S(1)} %get-tuple-element.80, f32[1,128,2,128]{3,1,0,2:T(8,128)S(1)} %get-tuple-element.83), kind=kOutput, calls=%fused_computation.63 | convolution fusion | flops 3221291008 | bytes 8650752 | tf_op jit(solution)/shard_map/fcpsjkb,sbrm->fcprjkm/dot_general | solution.py:59
  453.3 6.2 %fusion.53 = f32[4,32,2,2,1,16,128]{6,5,2,1,0,3,4:T(8,128)S(1)} fusion(f32[4,32,2,2,16,128,1]{5,1,4,2,0,3,6:T(8,128)S(1)} %maximum_bitcast_fusion.7, f32[1,128,2,128]{3,1,2,0:T(8,128)S(1)} %copy-done.11, f32[1,128,2,128]{3,1,2,0:T(8,128)S(1)} %copy-done.7), kind=kOutput, calls=%fused_computation.64 | convolution fusion | flops 3221291008 | bytes 8650752 | tf_op jit(solution)/shard_map/fcpsjkb,sbrm->fcprjkm/dot_general | solution.py:59
  464.2 10.3 %psum.30 = f32[4,1024]{1,0:T(4,128)S(1)} all-reduce(f32[4,1024]{1,0:T(4,128)S(1)} %bitcast.350), channel_id=1, replica_groups=mesh['wave'=4,'tm'=8] {'wave'}, use_global_device_ids=true, to_apply=%region_11.12 | all-reduce | flops 4096 | bytes 32768 | tf_op jit(solution)/shard_map/psum | solution.py:125
  483.3 4.7 collective-permute-start.7
  488.0 39.0 %collective-permute-done.6 = f32[4,32,2,2,512]{4,2,1,0,3:T(2,128)S(1)} collective-permute-done((f32[4,32,2,2,512]{4,2,1,0,3:T(2,128)S(1)}, f32[4,32,2,2,512]{4,2,1,0,3:T(2,128)S(1)}, u32[]{:S(2)}, u32[]{:S(2)}) %collective-permute-start.6) | collective-permute-done | bytes 1048608 | tf_op jit(solution)/shard_map/ppermute | solution.py:23
  534.7 8.2 %reshape.826 = f32[4,32,2,2,2,1024]{5,4,2,1,0,3:T(2,128)} reshape(f32[4,32,2,2,2048]{4,2,1,0,3:T(2,128)} %pad_maximum_fusion.6) | data formatting | bytes 8388608 | tf_op jit(solution)/shard_map/reshape | solution.py:65
  542.8 7.8 %fusion.145 = (f32[4,32,2,2,1,1024]{5,4,2,1,0,3:T(1,128)S(1)}, f32[4,32,2,2,1,1024]{5,4,2,1,0,3:T(1,128)S(1)}) fusion(f32[4,32,2,2,2,1024]{5,4,2,1,0,3:T(2,128)} %reshape.826), kind=kLoop, calls=%fused_computation.277 | loop fusion | bytes 8388608 | tf_op jit(solution)/shard_map/slice | solution.py:66
  553.9 4.6 pad_maximum_fusion.7
  558.5 6.5 %reshape.879 = f32[4,32,2,2,16,128,1]{5,4,3,2,1,0,6:T(8,128)} reshape(f32[4,32,2,2,1,2048]{5,3,2,1,0,4:T(2,128)} %pad_maximum_fusion.7) | data formatting | bytes 8388608 | tf_op jit(solution)/shard_map/reshape.62
  565.0 5.6 convolution_bitcast_fusion
  572.0 6.6 %fusion.56 = f32[4,32,2,2,1,16,128]{6,1,5,2,0,3,4:T(8,128)S(1)} fusion(f32[4,32,2,2,16,128]{5,4,2,1,0,3:T(8,128)S(1)} %maximum_bitcast_fusion.9, f32[1,128,2,128]{3,1,0,2:T(8,128)S(1)} %get-tuple-element.80, f32[1,128,2,128]{3,1,0,2:T(8,128)S(1)} %get-tuple-element.83), kind=kOutput, calls=%fused_computation.65 | convolution fusion | flops 3221291008 | bytes 8650752 | tf_op jit(solution)/shard_map/fcpsjkb,sbrm->fcprjkm/dot_general | solution.py:59
  580.4 6.5 %fusion.59 = f32[4,32,2,2,1,16,128]{6,5,2,1,0,3,4:T(8,128)S(1)} fusion(f32[4,32,2,2,16,128,1]{5,1,4,2,0,3,6:T(8,128)S(1)} %maximum_bitcast_fusion.10, f32[1,128,2,128]{3,1,2,0:T(8,128)S(1)} %copy-done.12, f32[1,128,2,128]{3,1,2,0:T(8,128)S(1)} %copy-done.8), kind=kOutput, calls=%fused_computation.66 | convolution fusion | flops 3221291008 | bytes 8650752 | tf_op jit(solution)/shard_map/fcpsjkb,sbrm->fcprjkm/dot_general | solution.py:59
  590.2 10.6 %psum.31 = f32[4,1024]{1,0:T(4,128)S(1)} all-reduce(f32[4,1024]{1,0:T(4,128)S(1)} %bitcast.351), channel_id=1, replica_groups=mesh['wave'=4,'tm'=8] {'wave'}, use_global_device_ids=true, to_apply=%region_14.15 | all-reduce | flops 4096 | bytes 32768 | tf_op jit(solution)/shard_map/psum | solution.py:125
  (154 shorter events, 120.4 us)
Async XLA Ops:
  3.3 9.0 %copy-start.15 = (f32[2,4]{1,0:T(2,128)S(1)}, f32[2,4]{1,0:T(2,128)}, u32[]{:S(2)}) copy-start(f32[2,4]{1,0:T(2,128)} %param.10) | copy-start | bytes 100
  3.3 9.0 %copy-start.16 = (f32[2,4]{1,0:T(2,128)S(1)}, f32[2,4]{1,0:T(2,128)}, u32[]{:S(2)}) copy-start(f32[2,4]{1,0:T(2,128)} %param.11) | copy-start | bytes 100
  3.3 9.8 %copy-start.13 = (s32[4,64]{1,0:T(4,128)S(1)}, s32[4,64]{1,0:T(4,128)}, u32[]{:S(2)}) copy-start(s32[4,64]{1,0:T(4,128)} %param.9) | copy-start | bytes 3076
  5.5 48.1 %collective-permute-start = (f32[4,32,2,2,512]{4,3,2,1,0:T(2,128)}, f32[4,32,2,2,512]{4,3,2,1,0:T(2,128)}, u32[]{:S(2)}, u32[]{:S(2)}) collective-permute-start(f32[4,32,2,2,512]{4,3,2,1,0:T(2,128)} %get-tuple-element.63), channel_id=1, source_target_pairs={{0,1},{1,2},{2,3},{3,4},{4,5},{5,6},{6,7},{7,0},{8,9},{9,10},{10,1... | collective-permute-start | bytes 3145736 | tf_op jit(solution)/shard_map/ppermute | solution.py:23
  8.5 47.4 %collective-permute-start.1 = (f32[4,32,2,2,512]{4,3,2,1,0:T(2,128)}, f32[4,32,2,2,512]{4,3,2,1,0:T(2,128)}, u32[]{:S(2)}, u32[]{:S(2)}) collective-permute-start(f32[4,32,2,2,512]{4,3,2,1,0:T(2,128)} %get-tuple-element.64), channel_id=1, source_target_pairs={{1,0},{2,1},{3,2},{4,3},{5,4},{6,5},{7,6},{0,7},{9,8},{10,9},{11,1... | collective-permute-start | bytes 3145736 | tf_op jit(solution)/shard_map/ppermute | solution.py:26
  97.4 6.6 %copy-start.1 = (f32[4,32,16,128]{3,1,2,0:T(8,128)S(1)}, f32[4,32,16,128]{3,1,2,0:T(8,128)}, u32[]{:S(2)}) copy-start(f32[4,32,16,128]{3,1,2,0:T(8,128)} %get-tuple-element.77) | copy-start | bytes 3145732
  97.4 6.6 %copy-start.2 = (f32[4,32,16,128]{3,1,2,0:T(8,128)S(1)}, f32[4,32,16,128]{3,1,2,0:T(8,128)}, u32[]{:S(2)}) copy-start(f32[4,32,16,128]{3,1,2,0:T(8,128)} %get-tuple-element.78) | copy-start | bytes 3145732
  104.8 0.9 copy-start.5
  104.9 1.0 copy-start.9
  139.1 2.0 copy-start.3
  139.1 2.0 copy-start.4
  141.1 45.1 %collective-permute-start.2 = (f32[4,32,2,2,512]{4,2,1,0,3:T(2,128)}, f32[4,32,2,2,512]{4,2,1,0,3:T(2,128)}, u32[]{:S(2)}, u32[]{:S(2)}) collective-permute-start(f32[4,32,2,2,512]{4,2,1,0,3:T(2,128)} %get-tuple-element.61), channel_id=1, source_target_pairs={{0,1},{1,2},{2,3},{3,4},{4,5},{5,6},{6,7},{7,0},{8,9},{9,10},{10,1... | collective-permute-start | bytes 3145736 | tf_op jit(solution)/shard_map/ppermute | solution.py:23
  141.4 47.7 %collective-permute-start.3 = (f32[4,32,2,2,512]{4,2,1,0,3:T(2,128)}, f32[4,32,2,2,512]{4,2,1,0,3:T(2,128)}, u32[]{:S(2)}, u32[]{:S(2)}) collective-permute-start(f32[4,32,2,2,512]{4,2,1,0,3:T(2,128)} %get-tuple-element.62), channel_id=1, source_target_pairs={{1,0},{2,1},{3,2},{4,3},{5,4},{6,5},{7,6},{0,7},{9,8},{10,9},{11,1... | collective-permute-start | bytes 3145736 | tf_op jit(solution)/shard_map/ppermute | solution.py:26
  239.5 0.9 copy-start.6
  239.6 1.0 copy-start.10
  292.9 5.4 copy-start.14
  292.9 53.6 %all-to-all-start = ((f32[4,32,2,2,2,1024]{5,4,3,2,1,0:T(2,128)}), f32[4,32,2,2,2,1024]{5,4,3,2,1,0:T(2,128)}, u32[]{:S(2)}, u32[]{:S(2)}) async-start(f32[4,32,2,2,2,1024]{5,4,3,2,1,0:T(2,128)} %select_multiply_fusion), calls=%async_computation | async-start | bytes 8388608 | tf_op jit(solution)/shard_map/all_to_all | solution.py:169
  353.3 45.0 %collective-permute-start.4 = (f32[4,32,2,2,512]{4,3,2,1,0:T(2,128)S(1)}, f32[4,32,2,2,512]{4,3,2,1,0:T(2,128)S(1)}, u32[]{:S(2)}, u32[]{:S(2)}) collective-permute-start(f32[4,32,2,2,512]{4,3,2,1,0:T(2,128)S(1)} %get-tuple-element.59), channel_id=1, source_target_pairs={{0,1},{1,2},{2,3},{3,4},{4,5},{5,6},{6,7},{7,0},{8,9},{9,10},{10,1... | collective-permute-start | bytes 3145736 | tf_op jit(solution)/shard_map/ppermute | solution.py:23
  353.4 49.1 %collective-permute-start.5 = (f32[4,32,2,2,512]{4,3,2,1,0:T(2,128)S(1)}, f32[4,32,2,2,512]{4,3,2,1,0:T(2,128)S(1)}, u32[]{:S(2)}, u32[]{:S(2)}) collective-permute-start(f32[4,32,2,2,512]{4,3,2,1,0:T(2,128)S(1)} %get-tuple-element.60), channel_id=1, source_target_pairs={{1,0},{2,1},{3,2},{4,3},{5,4},{6,5},{7,6},{0,7},{9,8},{10,9},{11,1... | collective-permute-start | bytes 3145736 | tf_op jit(solution)/shard_map/ppermute | solution.py:26
  444.7 6.6 %copy-start = (f32[4,32,16,128]{3,1,2,0:T(8,128)S(1)}, f32[4,32,16,128]{3,1,2,0:T(8,128)}, u32[]{:S(2)}) copy-start(f32[4,32,16,128]{3,1,2,0:T(8,128)} %get-tuple-element.74) | copy-start | bytes 3145732
  452.3 0.9 copy-start.7
  452.3 1.0 copy-start.11
  483.2 43.8 %collective-permute-start.6 = (f32[4,32,2,2,512]{4,2,1,0,3:T(2,128)S(1)}, f32[4,32,2,2,512]{4,2,1,0,3:T(2,128)S(1)}, u32[]{:S(2)}, u32[]{:S(2)}) collective-permute-start(f32[4,32,2,2,512]{4,2,1,0,3:T(2,128)S(1)} %get-tuple-element.57), channel_id=1, source_target_pairs={{0,1},{1,2},{2,3},{3,4},{4,5},{5,6},{6,7},{7,0},{8,9},{9,10},{10,1... | collective-permute-start | bytes 3145736 | tf_op jit(solution)/shard_map/ppermute | solution.py:23
  483.3 47.7 %collective-permute-start.7 = (f32[4,32,2,2,512]{4,2,1,0,3:T(2,128)S(1)}, f32[4,32,2,2,512]{4,2,1,0,3:T(2,128)S(1)}, u32[]{:S(2)}, u32[]{:S(2)}) collective-permute-start(f32[4,32,2,2,512]{4,2,1,0,3:T(2,128)S(1)} %get-tuple-element.58), channel_id=1, source_target_pairs={{1,0},{2,1},{3,2},{4,3},{5,4},{6,5},{7,6},{0,7},{9,8},{10,9},{11,1... | collective-permute-start | bytes 3145736 | tf_op jit(solution)/shard_map/ppermute | solution.py:26
  579.4 0.9 copy-start.8
  579.5 1.0 copy-start.12
where the time goes:
time: 619 us; the launch traced here: 613 us
  waiting for transfers between devices  211 us (34%)
  local copies, waits for them, and re-layouts  142 us (23%)
  other arithmetic  106 us (17%)
  matrix products  86 us (14%)
  blocking collectives  41.2 us (7%)
  starting transfers between devices  25.6 us (4%)
    ppermute x4, waiting for transfers between devices, padded(): lax.ppermute(lax.slice_in_dim(block, block.shape[dim] - width, None, axis...  150 us
    dot_general x8, matrix products, column_product(): jnp.einsum('fcpsjkb,sbrm->fcprjkm', values, table, precision=lax.Precisio...  52 us
    all_to_all x1, waiting for transfers between devices, switch_exchange(): lax.all_to_all(outgoing, 'wave', split_axis=0, concat_axis=0, tiled=True)  47.4 us
    psum x4, blocking collectives, nonlinear(): fibre_total = lax.psum(partial_total, 'wave')  41.2 us
    dot_general x8, matrix products, row_product(): jnp.einsum('fcpsjab,rksa->fcprjkb', values, table, precision=lax.Precisio...  34 us
    slice x4, local copies, waits for them, and re-layouts, disperse(): blocks = jnp.concatenate([pieces[..., :-1, :], pieces[..., 1:, :]], axis=-1)  32.8 us
    reshape x4, local copies, waits for them, and re-layouts, disperse(): pieces = extended.reshape(fibres, channels, 2, 2, pieces_count, VALID)  32 us
    concatenate x4, other arithmetic, disperse(): blocks = jnp.concatenate([pieces[..., :-1, :], pieces[..., 1:, :]], axis=-1)  23.8 us
  transfers between devices with their start and end apart: 9, of which 9 were waited for; matrix products, arithmetic and copies ran while one was open for 2% of the time, Pallas kernels for 0%

commit v1 on v0

v1 whole, which is shorter than its diff:
```python
import functools
import math

import jax
import jax.numpy as jnp
import numpy as np
from jax import lax
from jax.experimental import pallas as pl
from jax.experimental.pallas import tpu as pltpu
from jax.sharding import PartitionSpec as P

BLK = 2
FA = 16
FB = 128
NFFT = FA * FB
HALF = 2
MARGIN = 512
VALID = 1024
LEAD = MARGIN // FB
STEP = VALID // FB
SUB = 8
VMEM_BYTES = 40 * 1024 * 1024


def split_bf16(values):
    high = values.astype(jnp.bfloat16)
    low = (values - high.astype(np.float64)).astype(jnp.bfloat16)
    return high, low


def matrix_tables():
    index = np.arange(FB)
    angle = 2.0 * np.pi * (np.outer(index, index) % FB) / FB
    cos, sin = np.cos(angle), np.sin(angle)
    forward = np.block([[cos, -sin], [sin, cos]])
    inverse = np.block([[cos, sin], [-sin, cos]])
    tables = []
    for matrix in (forward, inverse):
        high, low = split_bf16(matrix)
        tables.append(np.concatenate([high, low, high], axis=0))
    return tables


def twist_table():
    angle = 2.0 * np.pi * np.outer(np.arange(FA), np.arange(FB)) / NFFT
    table = np.stack([np.cos(angle), np.sin(angle)]).astype(np.float32)
    return np.ascontiguousarray(np.broadcast_to(table[:, :, None, :], (2, FA, SUB, FB)))


def filter_tables(spread, channel, channels_total):
    index = np.arange(FA)[:, None] + FA * np.arange(FB)[None, :]
    signed = np.where(index < NFFT // 2, index, index - NFFT).astype(np.float32)
    omega = jnp.asarray(signed) * (2.0 * math.pi / NFFT)
    offsets = (math.pi / 2.0) * (2.0 * channel.astype(jnp.float32) + 1.0 - channels_total)
    offsets = offsets / channels_total
    theta = spread[None, :, None] * (
        omega[:, None, :] ** 2 + 2.0 * omega[:, None, :] * offsets[None, :, None]
    )
    scale = 1.0 / NFFT
    return jnp.cos(theta) * scale, jnp.sin(theta) * scale


def cadd(a, b):
    return (a[0] + b[0], a[1] + b[1])


def csub(a, b):
    return (a[0] - b[0], a[1] - b[1])


def cturn(a, sign):
    return (-a[1], a[0]) if sign > 0 else (a[1], -a[0])


def croot(a, m, sign):
    m %= FA
    if m == 0:
        return a
    if m == 4:
        return cturn(a, sign)
    if m in (2, 6):
        h = np.float32(math.sqrt(0.5))
        c = h if m == 2 else -h
        s = h * sign
        if m == 2:
            if sign > 0:
                return ((a[0] - a[1]) * h, (a[0] + a[1]) * h)
            return ((a[0] + a[1]) * h, (a[1] - a[0]) * h)
        if sign > 0:
            return ((a[0] + a[1]) * (-h), (a[0] - a[1]) * h)
        return ((a[1] - a[0]) * h, (a[0] + a[1]) * (-h))
    c = np.float32(math.cos(2.0 * math.pi * m / FA))
    s = np.float32(sign * math.sin(2.0 * math.pi * m / FA))
    return (a[0] * c - a[1] * s, a[0] * s + a[1] * c)


def dft4(z, sign, keep=(0, 1, 2, 3)):
    even, odd = cadd(z[0], z[2]), cadd(z[1], z[3])
    out = {}
    if 0 in keep:
        out[0] = cadd(even, odd)
    if 2 in keep:
        out[2] = csub(even, odd)
    if 1 in keep or 3 in keep:
        base, turn = csub(z[0], z[2]), cturn(csub(z[1], z[3]), sign)
        if 1 in keep:
            out[1] = cadd(base, turn)
        if 3 in keep:
            out[3] = csub(base, turn)
    return out


def dft16(z, sign, keep=(0, 1, 2, 3)):
    inner = [dft4([z[4 * n1 + n2] for n1 in range(4)], sign) for n2 in range(4)]
    out = {}
    for k1 in range(4):
        column = [croot(inner[n2][k1], n2 * k1, sign) for n2 in range(4)]
        for k2, value in dft4(column, sign, keep).items():
            out[k1 + 4 * k2] = value
    return out


def sincos(x):
    n = jnp.round(x * np.float32(2.0 / math.pi))
    r = x - n * np.float32(1.5703125)
    r = r - n * np.float32(4.837512969970703125e-4)
    r = r - n * np.float32(7.54978995489188216e-8)
    q = n.astype(jnp.int32)
    r2 = r * r
    s = np.float32(-1.9515295891e-4) * r2 + np.float32(8.3321608736e-3)
    s = s * r2 + np.float32(-1.6666654611e-1)
    s = s * r2 * r + r
    c = np.float32(2.443315711809948e-5) * r2 + np.float32(-1.388731625493765e-3)
    c = c * r2 + np.float32(4.166664568298827e-2)
    c = c * r2 * r2 - np.float32(0.5) * r2 + np.float32(1.0)
    odd = (q & 1) == 1
    sine = jnp.where(odd, c, s)
    cosine = jnp.where(odd, s, c)
    sine = jnp.where((q & 2) == 2, -sine, sine)
    cosine = jnp.where(((q + 1) & 2) == 2, -cosine, cosine)
    return sine, cosine


def rotate_chunk(x_ref, q_ref, sel_ref, strength, tt, channels_total, fibres, slots, write):
    real, imag = x_ref[tt, 0], x_ref[tt, 1]
    power = real * real + imag * imag
    power = power[:slots] + power[slots:]
    if fibres == 1:
        total = q_ref[0, pl.ds(tt, 1), :]
    else:
        total = sel_ref[0] * q_ref[0, pl.ds(tt, 1), :]
        for f in range(1, fibres):
            total = total + sel_ref[f] * q_ref[f, pl.ds(tt, 1), :]
    phase = strength * (2.0 * total - power) * np.float32(1.0 / channels_total)
    sine, cosine = sincos(phase)
    sine = jnp.concatenate([sine, sine], axis=0)
    cosine = jnp.concatenate([cosine, cosine], axis=0)
    write(real * cosine - imag * sine, real * sine + imag * cosine)


def final_kernel(x_ref, q_ref, sel_ref, strength_ref, o_ref, *, channels_total, fibres, slots):
    def body(tt, carry):
        def write(real, imag):
            o_ref[tt, 0] = real
            o_ref[tt, 1] = imag

        rotate_chunk(
            x_ref, q_ref, sel_ref, strength_ref[...], tt, channels_total, fibres, slots, write
        )
        return carry

    lax.fori_loop(0, x_ref.shape[0], body, 0)


def split_store(a_ref, base, column, value):
    high = value.astype(jnp.bfloat16)
    low = (value - high.astype(jnp.float32)).astype(jnp.bfloat16)
    rows = value.shape[0]
    a_ref[base : base + rows, column : column + FB] = high
    a_ref[base : base + rows, 2 * FB + column : 3 * FB + column] = high
    a_ref[base : base + rows, 4 * FB + column : 5 * FB + column] = low


def step_kernel(
    *refs, rotate, channels_total, fibres_in, fibres_out, slots
):
    if rotate:
        (x_ref, q_ref, selin_ref, strength_ref, selout_ref, fc_ref, fs_ref, tw_ref, wf_ref, wi_ref,
         u_ref, p_ref, xs_ref, a_ref, z_ref) = refs
    else:
        (x_ref, selout_ref, fc_ref, fs_ref, tw_ref, wf_ref, wi_ref,
         u_ref, p_ref, a_ref, z_ref) = refs
        xs_ref = x_ref
    chunks = x_ref.shape[0]
    groups = 2 * slots // SUB
    half = groups // 2

    if rotate:

        def turn(tt, carry):
            def write(real, imag):
                xs_ref[tt, 0] = real
                xs_ref[tt, 1] = imag

            rotate_chunk(
                x_ref, q_ref, selin_ref, strength_ref[...], tt, channels_total, fibres_in, slots,
                write,
            )
            return carry

        lax.fori_loop(0, chunks, turn, 0)

    def block(j, carry):
        places = []
        for a in range(FA):
            at = j * STEP + (a - LEAD)
            at = jnp.where(at < 0, at + chunks, at)
            places.append(jnp.where(at >= chunks, at - chunks, at))
        for g in range(groups):
            rows = slice(g * SUB, (g + 1) * SUB)
            z = [(xs_ref[at, 0, rows, :], xs_ref[at, 1, rows, :]) for at in places]
            y = dft16(z, -1)
            for i in range(FA // 2):
                pair = []
                for k in (2 * i, 2 * i + 1):
                    real, imag = y[k]
                    if k:
                        c, s = tw_ref[0, k], tw_ref[1, k]
                        real, imag = real * c + imag * s, imag * c - real * s
                    pair.append((real, imag))
                base = (g * FA + 2 * i) * SUB
                for part in range(2):
                    value = jnp.concatenate([pair[0][part], pair[1][part]], axis=0)
                    split_store(a_ref, base, part * FB, value)
        z_ref[...] = jnp.dot(a_ref[...], wf_ref[...], preferred_element_type=jnp.float32)
        for g in range(groups):
            rows = slice((g % half) * SUB, (g % half + 1) * SUB)
            for i in range(FA // 2):
                pair = []
                for k in (2 * i, 2 * i + 1):
                    at = (g * FA + k) * SUB
                    real, imag = z_ref[at : at + SUB, :FB], z_ref[at : at + SUB, FB:]
                    c, s = fc_ref[k, rows, :], fs_ref[k, rows, :]
                    pair.append((real * c - imag * s, real * s + imag * c))
                base = (g * FA + 2 * i) * SUB
                for part in range(2):
                    value = jnp.concatenate([pair[0][part], pair[1][part]], axis=0)
                    split_store(a_ref, base, part * FB, value)
        z_ref[...] = jnp.dot(a_ref[...], wi_ref[...], preferred_element_type=jnp.float32)
        for g in range(groups):
            rows = slice(g * SUB, (g + 1) * SUB)
            z = []
            for k in range(FA):
                at = (g * FA + k) * SUB
                real, imag = z_ref[at : at + SUB, :FB], z_ref[at : at + SUB, FB:]
                if k:
                    c, s = tw_ref[0, k], tw_ref[1, k]
                    real, imag = real * c - imag * s, real * s + imag * c
                z.append((real, imag))
            y = dft16(z, 1, keep=(1, 2))
            for k in range(STEP):
                u_ref[j * STEP + k, 0, rows, :] = y[LEAD + k][0]
                u_ref[j * STEP + k, 1, rows, :] = y[LEAD + k][1]
        for k in range(STEP):
            tt = j * STEP + k
            real, imag = u_ref[tt, 0], u_ref[tt, 1]
            power = real * real + imag * imag
            power = power[:slots] + power[slots:]
            for f in range(fibres_out):
                mine = power if fibres_out == 1 else power * selout_ref[f]
                p_ref[f, pl.ds(tt, 1), :] = jnp.sum(mine, axis=0, keepdims=True)
        return carry

    lax.fori_loop(0, chunks // STEP, block, 0)


def pack_kernel(lit_ref, x_ref, o_ref, *, units, slots):
    rows = 2 * slots
    span = 2 * STEP
    for g in range(o_ref.shape[0]):
        if units < slots:
            o_ref[g] = jnp.zeros(o_ref.shape[1:], jnp.float32)
        for u in range(units):
            lit = lit_ref[g * units + u] > 0
            for p in range(2):
                at = ((g * units + u) * 2 + p) * span
                value = jnp.where(lit, x_ref[at : at + span, :], 0.0)
                o_ref[g, pl.ds(p * slots + u, span, stride=rows), :] = value


def send_kernel(item_ref, x_ref, o_ref, *, units, slots):
    rows = 2 * slots
    span = 2 * STEP

    def body(n, carry):
        for c in range(BLK):
            channel = item_ref[n] * BLK + c
            g = channel // units
            u = channel - g * units
            for p in range(2):
                at = (c * 2 + p) * span
                o_ref[n, at : at + span, :] = x_ref[g, pl.ds(p * slots + u, span, stride=rows), :]
        return carry

    lax.fori_loop(0, o_ref.shape[0], body, 0)


def place_kernel(from_ref, x_ref, o_ref):
    def body(n, carry):
        o_ref[n] = x_ref[from_ref[n]]
        return carry

    lax.fori_loop(0, o_ref.shape[0], body, 0)


def params():
    return pltpu.CompilerParams(vmem_limit_bytes=VMEM_BYTES)


def in_vmem():
    return pl.BlockSpec(memory_space=pltpu.VMEM)


def in_smem():
    return pl.BlockSpec(memory_space=pltpu.SMEM)


def summed(values, rounds):
    for axis, bit in rounds:
        pairs = [(i, i ^ bit) for i in range(lax.axis_size(axis))]
        values = values + lax.ppermute(values, axis, pairs)
    return values


def route_tables(route_fibre, route_slot, groups, my_group, capacity):
    fibres = route_slot.shape[0]
    group_blocks = route_slot.shape[1] // groups
    sends = fibres * group_blocks

    def by_group(table):
        return table.reshape(fibres, groups, group_blocks).transpose(1, 0, 2).reshape(groups, sends)

    slot_all, fibre_all = by_group(route_slot), by_group(route_fibre)
    target_all = slot_all // group_blocks
    landing_all = fibre_all * group_blocks + slot_all % group_blocks
    position = jnp.arange(sends)
    earlier = (target_all[:, :, None] == target_all[:, None, :]) & (
        position[None, None, :] < position[None, :, None]
    )
    arrival_all = jnp.sum(earlier.astype(jnp.int32), axis=2)
    my_target = lax.dynamic_index_in_dim(target_all, my_group, 0, keepdims=False)
    my_arrival = lax.dynamic_index_in_dim(arrival_all, my_group, 0, keepdims=False)
    slot_index = my_target * capacity + my_arrival
    matches = slot_index[None, :] == jnp.arange(groups * capacity)[:, None]
    source_item = jnp.sum(jnp.where(matches, position[None, :], 0), axis=1)
    mine = target_all == my_group
    receive_slot = jnp.arange(groups)[:, None] * capacity + arrival_all
    hits = mine[:, :, None] & (landing_all[:, :, None] == position[None, None, :])
    take_from = jnp.sum(jnp.where(hits, receive_slot[:, :, None], 0), axis=(0, 1))
    return source_item.astype(jnp.int32), take_from.astype(jnp.int32)


def local(field, lit_count, route_fibre, route_slot, dispersion, nonlinearity):
    fibres, channels, samples = field.shape[0], field.shape[1], field.shape[-1]
    groups, times = lax.axis_size("wave"), lax.axis_size("tm")
    my_group, my_time = lax.axis_index("wave"), lax.axis_index("tm")
    channels_total = groups * channels
    units = fibres * channels // times
    slots = -(-units // SUB) * SUB
    rows = 2 * slots
    near = samples // FB
    chunks = times * near
    same_fibre = channels % units == 0
    group_blocks = channels // BLK
    sends = fibres * group_blocks
    capacity = 2 * sends // groups

    unit = my_time * units + jnp.minimum(jnp.arange(slots), units - 1)
    in_fibre = unit // channels
    in_channel = my_group * channels + unit % channels
    in_block = in_channel // BLK
    out_fibre = route_fibre[in_fibre, in_block]
    out_channel = route_slot[in_fibre, in_block] * BLK + in_channel % BLK
    real_slot = jnp.arange(slots) < units

    def wide(values):
        return jnp.broadcast_to(values.astype(jnp.float32)[..., None], values.shape + (FB,))

    def selection(fibre):
        chosen = (fibre[None, :] == jnp.arange(fibres)[:, None]) & real_slot[None, :]
        return wide(chosen)

    spans = []
    for span, (fibre, channel) in enumerate(((in_fibre, in_channel), (out_fibre, out_channel))):
        spread, strength = dispersion[span][fibre], nonlinearity[span][fibre]
        fc, fs = filter_tables(spread, channel, channels_total)
        spans.append((fc, fs, wide(strength), selection(fibre)))
    source_item, take_from = route_tables(route_fibre, route_slot, groups, my_group, capacity)

    wave_rounds = [("wave", 1 << b) for b in range(groups.bit_length() - 1)]
    time_rounds = [("tm", 1 << b) for b in range(times.bit_length() - 1)]
    shared = channels // units if same_fibre else 0
    fibre_rounds = [("tm", 1 << b) for b in range(shared.bit_length() - 1)]

    lit_mask = (my_group * channels + jnp.arange(channels))[None, :] < lit_count[:, None]
    lit = lit_mask.reshape(-1).astype(jnp.int32)

    def natural_rows(values):
        split = values.reshape(fibres, channels, 2, 2, near, FB)
        return split.transpose(0, 1, 2, 4, 3, 5).reshape(-1, FB)

    packed = pl.pallas_call(
        functools.partial(pack_kernel, units=units, slots=slots),
        out_shape=jax.ShapeDtypeStruct((times, 2 * near * rows, FB), jnp.float32),
        in_specs=[in_smem(), in_vmem()],
        out_specs=in_vmem(),
        compiler_params=params(),
        name="pack",
    )(lit, natural_rows(field))
    wave_form = lax.all_to_all(packed, "tm", split_axis=0, concat_axis=0, tiled=True)
    wave_form = wave_form.reshape(chunks, 2, rows, FB)

    twist = jnp.asarray(twist_table())
    forward, inverse = (jnp.asarray(table) for table in matrix_tables())
    total, q_fibres, q_spec = None, 0, None
    for step in range(2 * HALF):
        span = step // HALF
        fc, fs, strength, select = spans[span]
        fibres_out = 1 if (span == 0 and same_fibre) else fibres
        rotate = step > 0
        operands = [wave_form]
        if rotate:
            operands += [total, spans[(step - 1) // HALF][3], spans[(step - 1) // HALF][2]]
        operands += [select, fc, fs, twist, forward, inverse]
        scratch = [
            pltpu.VMEM((FA * rows, 6 * FB), jnp.bfloat16),
            pltpu.VMEM((FA * rows, 2 * FB), jnp.float32),
        ]
        if rotate:
            scratch = [pltpu.VMEM(wave_form.shape, jnp.float32)] + scratch
        wave_form, partial = pl.pallas_call(
            functools.partial(
                step_kernel, rotate=rotate, channels_total=channels_total, fibres_in=q_fibres,
                fibres_out=fibres_out, slots=slots,
            ),
            out_shape=(
                jax.ShapeDtypeStruct(wave_form.shape, jnp.float32),
                jax.ShapeDtypeStruct((fibres_out, chunks, FB), jnp.float32),
            ),
            in_specs=[in_vmem()] * len(operands),
            out_specs=(in_vmem(), in_vmem()),
            scratch_shapes=scratch,
            compiler_params=params(),
            name="step",
        )(*operands)
        rounds = fibre_rounds if fibres_out == 1 else time_rounds
        total, q_fibres = summed(partial, wave_rounds + rounds), fibres_out

    _, _, strength, select = spans[1]
    finished = pl.pallas_call(
        functools.partial(
            final_kernel, channels_total=channels_total, fibres=q_fibres, slots=slots
        ),
        out_shape=jax.ShapeDtypeStruct(wave_form.shape, jnp.float32),
        in_specs=[in_vmem()] * 4,
        out_specs=in_vmem(),
        compiler_params=params(),
        name="final",
    )(wave_form, total, select, strength)

    finished = finished.reshape(times, 2 * near * rows, FB)
    gathered = lax.all_to_all(finished, "tm", split_axis=0, concat_axis=0, tiled=True)
    outgoing = pl.pallas_call(
        functools.partial(send_kernel, units=units, slots=slots),
        out_shape=jax.ShapeDtypeStruct((groups * capacity, BLK * 4 * near, FB), jnp.float32),
        in_specs=[in_smem(), in_vmem()],
        out_specs=in_vmem(),
        compiler_params=params(),
        name="send",
    )(source_item, gathered)
    incoming = lax.all_to_all(outgoing, "wave", split_axis=0, concat_axis=0, tiled=True)
    placed = pl.pallas_call(
        place_kernel,
        out_shape=jax.ShapeDtypeStruct((sends, BLK * 4 * near, FB), jnp.float32),
        in_specs=[in_smem(), in_vmem()],
        out_specs=in_vmem(),
        compiler_params=params(),
        name="place",
    )(take_from, incoming)
    result = placed.reshape(fibres, channels, 2, near, 2, FB).transpose(0, 1, 2, 4, 3, 5)
    return result.reshape(fibres, channels, 2, 2, samples)


def solution(mesh):
    return jax.shard_map(
        local,
        mesh=mesh,
        in_specs=(P(None, "wave", None, None, "tm"), P(), P(), P(), P(), P()),
        out_specs=P(None, "wave", None, None, "tm"),
        check_vma=False,
    )
```

time: 619 us -> 295 us (0.48)
  local copies, waits for them, and re-layouts: 142 us -> 17.6 us
  other arithmetic: 106 us -> 4.86 us
  matrix products: 86 us -> 0 us
  Pallas kernels: 0 us -> 58.1 us
  blocking collectives: 41.2 us -> 0 us
  waiting for transfers between devices: 211 us -> 183 us
    ppermute x8 -> x16, waiting for transfers between devices: 164 us -> 49.2 us  [summed(): values = values + lax.ppermute(values, axis, pairs)]
    all_to_all x1 -> x3, waiting for transfers between devices: 47.4 us -> 134 us  [the longest x1 47.8 us: local(): lax.all_to_all(outgoing, 'wave', split_axis=0, concat_axis=0, tiled=True)]
    dot_general x16 -> x0, matrix products: 86 us -> none  [the longest x8 52 us: column_product(): jnp.einsum('fcpsjkb,sbrm->fcprjkm', values, table, precision=lax.Precisio...]
    pallas_call x0 -> x8, Pallas kernels: none -> 58.1 us  [the longest x4 44.5 us: local(): pl.pallas_call(functools.partial(step_kernel, rotate=rotate, channels_tot...]
    reshape x11 -> x3, local copies, waits for them, and re-layouts: 42.8 us -> 0.17 us  [by_group(): table.reshape(fibres, groups, group_blocks).transpose(1, 0, 2)]
    concatenate x8 -> x1, other arithmetic: 42.2 us -> 0.03 us  [local(): out_fibre = route_fibre[in_fibre, in_block]]
    psum x4 -> x0, blocking collectives: 41.2 us -> none  [nonlinear(): fibre_total = lax.psum(partial_total, 'wave')]
    slice x7 -> x0, local copies, waits for them, and re-layouts: 38.1 us -> none  [the longest x4 32.8 us: disperse(): blocks = jnp.concatenate([pieces[..., :-1, :], pieces[..., 1:, :]], axis=-1)]
  transfers between devices with their start and end apart: 9 -> 19, of which waited for: 9 -> 19; matrix products, arithmetic and copies ran while one was open for 2% -> 3% of each run, Pallas kernels for 0% -> 0%
where the time goes in v1:
time: 295 us; the launch traced here: 294 us
  waiting for transfers between devices  183 us (62%)
  Pallas kernels  58.1 us (20%)
  starting transfers between devices  30.2 us (10%)
  local copies, waits for them, and re-layouts  17.6 us (6%)
  other arithmetic  4.86 us (2%)
    ppermute x16, waiting for transfers between devices, summed(): values = values + lax.ppermute(values, axis, pairs)  49.2 us
    all_to_all x1, waiting for transfers between devices, local(): lax.all_to_all(outgoing, 'wave', split_axis=0, concat_axis=0, tiled=True)  47.8 us
    pallas_call x4, Pallas kernels, local(): pl.pallas_call(functools.partial(step_kernel, rotate=rotate, channels_tot...  44.5 us
    all_to_all x1, waiting for transfers between devices, local(): lax.all_to_all(finished, 'tm', split_axis=0, concat_axis=0, tiled=True)  44.4 us
    all_to_all x1, waiting for transfers between devices, local(): lax.all_to_all(packed, 'tm', split_axis=0, concat_axis=0, tiled=True)  41.9 us
    ppermute x16, starting transfers between devices, summed(): values = values + lax.ppermute(values, axis, pairs)  14.3 us
    unnamed x36, local copies, waits for them, and re-layouts  9.96 us
    all_to_all x1, starting transfers between devices, local(): lax.all_to_all(packed, 'tm', split_axis=0, concat_axis=0, tiled=True)  7.38 us
  transfers between devices with their start and end apart: 19, of which 19 were waited for; matrix products, arithmetic and copies ran while one was open for 3% of the time, Pallas kernels for 0%

profile of v1, /device:TPU:0, one launch (start us, length us, event | category | flops | bytes accessed | tf_op | source)
XLA Modules:
  0.0 294.3 jit_solution(6214878539702557912)
XLA Ops:
  0.8 1.6 copy-done.5
  2.4 2.3 pack.1
  4.7 1.3 copy-done.1
  6.0 7.4 %all-to-all-start = ((f32[8,512,128]{2,1,0:T(8,128)}), f32[8,512,128]{2,1,0:T(8,128)S(1)}, u32[]{:S(2)}, u32[]{:S(2)}) async-start(f32[8,512,128]{2,1,0:T(8,128)} %copy-done.1), calls=%async_computation | async-start | bytes 4194304 | tf_op jit(solution)/shard_map/all_to_all | solution.py:420
  15.0 1.2 gather_fusion.3
  16.1 1.2 gather_fusion
  18.0 1.7 sine_multiply_fusion
  19.8 41.9 %all-to-all-done = f32[8,512,128]{2,1,0:T(8,128)S(1)} async-done(((f32[8,512,128]{2,1,0:T(8,128)}), f32[8,512,128]{2,1,0:T(8,128)S(1)}, u32[]{:S(2)}, u32[]{:S(2)}) %all-to-all-start) | async-done | bytes 2097184 | tf_op jit(solution)/shard_map/all_to_all | solution.py:420
  62.4 9.4 %step.4 = (f32[64,2,32,128]{3,2,1,0:T(8,128)S(1)}, f32[1,64,128]{2,1,0:T(8,128)S(1)}) custom-call(f32[64,2,32,128]{3,2,1,0:T(8,128)S(1)} %bitcast.36, f32[4,16,128]{2,1,0:T(8,128)S(1)} %broadcast_in_dim.28.refs_1_.refs_2_.refs_4_, f32[16,16,128]{2,1,0:T(8,128)S(1)} %get-tuple-element.27.refs_2_.refs_5_, ...), custom_call_target="tpu_custom_call" | custom-call | tf_op jit(solution)/shard_map/step/pallas_call | solution.py:441
  71.9 1.3 copy-done.6
  73.2 1.2 collective-permute-done
  74.4 1.5 collective-permute-start.1
  75.9 2.4 collective-permute-done.1
  78.3 1.5 collective-permute-start.2
  80.5 0.9 gather_fusion.1
  82.3 1.6 copy-done.7
  84.7 11.5 %step.5 = (f32[64,2,32,128]{3,2,1,0:T(8,128)S(1)}, f32[1,64,128]{2,1,0:T(8,128)S(1)}) custom-call(f32[64,2,32,128]{3,2,1,0:T(8,128)S(1)} %copy-done.7, f32[1,64,128]{2,1,0:T(8,128)S(1)} %add.310.refs_1_, f32[4,16,128]{2,1,0:T(8,128)S(1)} %copy-done.10, f32[16,128]{1,0:T(8,128)S(1)} %broadcast_in_dim.29.refs_3_, f32[4,16,128]{2,1,0:T(8,128)S(1)} %copy-done.10, ...), custom_call_target="tpu_custom_call" | custom-call | tf_op jit(solution)/shard_map/step/pallas_call | solution.py:441
  96.2 1.2 collective-permute-done.3
  97.4 1.5 collective-permute-start.4
  98.9 2.4 collective-permute-done.4
  101.3 1.5 collective-permute-start.5
  102.8 2.5 collective-permute-done.5
  105.3 11.7 %step.6 = (f32[64,2,32,128]{3,2,1,0:T(8,128)S(1)}, f32[4,64,128]{2,1,0:T(8,128)S(1)}) custom-call(f32[64,2,32,128]{3,2,1,0:T(8,128)S(1)} %get-tuple-element.15.refs_0_, f32[1,64,128]{2,1,0:T(8,128)S(1)} %add.313.refs_1_, f32[4,16,128]{2,1,0:T(8,128)S(1)} %copy-done.10, f32[16,128]{1,0:T(8,128)S(1)} %broadcast_in_dim.29.refs_3_, ...), custom_call_target="tpu_custom_call" | custom-call | tf_op jit(solution)/shard_map/step/pallas_call | solution.py:441
  117.1 1.3 collective-permute-done.6
  118.5 1.6 collective-permute-start.7
  120.1 4.0 %collective-permute-done.7 = f32[4,64,128]{2,1,0:T(8,128)S(1)} collective-permute-done((f32[4,64,128]{2,1,0:T(8,128)S(1)}, f32[4,64,128]{2,1,0:T(8,128)S(1)}, u32[]{:S(2)}, u32[]{:S(2)}) %collective-permute-start.7) | collective-permute-done | bytes 131104 | tf_op jit(solution)/shard_map/ppermute | solution.py:331
  124.1 1.5 collective-permute-start.8
  125.7 3.5 %collective-permute-done.8 = f32[4,64,128]{2,1,0:T(8,128)S(1)} collective-permute-done((f32[4,64,128]{2,1,0:T(8,128)S(1)}, f32[4,64,128]{2,1,0:T(8,128)S(1)}, u32[]{:S(2)}, u32[]{:S(2)}) %collective-permute-start.8) | collective-permute-done | bytes 131104 | tf_op jit(solution)/shard_map/ppermute | solution.py:331
  129.3 5.0 %collective-permute-done.9 = f32[4,64,128]{2,1,0:T(8,128)S(1)} collective-permute-done((f32[4,64,128]{2,1,0:T(8,128)S(1)}, f32[4,64,128]{2,1,0:T(8,128)S(1)}, u32[]{:S(2)}, u32[]{:S(2)}) %collective-permute-start.9) | collective-permute-done | bytes 131104 | tf_op jit(solution)/shard_map/ppermute | solution.py:331
  135.9 5.2 %collective-permute-done.10 = f32[4,64,128]{2,1,0:T(8,128)} collective-permute-done((f32[4,64,128]{2,1,0:T(8,128)S(1)}, f32[4,64,128]{2,1,0:T(8,128)}, u32[]{:S(2)}, u32[]{:S(2)}) %collective-permute-start.10) | collective-permute-done | bytes 131104 | tf_op jit(solution)/shard_map/ppermute | solution.py:331
  141.1 0.9 add.327.refs_1_
  142.1 11.9 %step.7 = (f32[64,2,32,128]{3,2,1,0:T(8,128)S(1)}, f32[4,64,128]{2,1,0:T(8,128)S(1)}) custom-call(f32[64,2,32,128]{3,2,1,0:T(8,128)S(1)} %get-tuple-element.17.refs_0_, f32[4,64,128]{2,1,0:T(8,128)S(1)} %add.327.refs_1_, f32[4,16,128]{2,1,0:T(8,128)S(1)} %broadcast_in_dim.30.refs_4_.refs_2_.sel_ref, f32[16,128]{1,0:T(8,128)S(1)} %broadcast_in_dim.31.refs_3_.strength_ref, ...), custom_call_target="tpu_custom_call" | custom-call | tf_op jit(solution)/shard_map/step/pallas_call | solution.py:441
  154.1 1.3 collective-permute-done.11
  155.5 1.6 collective-permute-start.12
  157.1 4.0 %collective-permute-done.12 = f32[4,64,128]{2,1,0:T(8,128)S(1)} collective-permute-done((f32[4,64,128]{2,1,0:T(8,128)S(1)}, f32[4,64,128]{2,1,0:T(8,128)S(1)}, u32[]{:S(2)}, u32[]{:S(2)}) %collective-permute-start.12) | collective-permute-done | bytes 131104 | tf_op jit(solution)/shard_map/ppermute | solution.py:331
  161.1 1.5 collective-permute-start.13
  162.7 3.5 %collective-permute-done.13 = f32[4,64,128]{2,1,0:T(8,128)S(1)} collective-permute-done((f32[4,64,128]{2,1,0:T(8,128)S(1)}, f32[4,64,128]{2,1,0:T(8,128)S(1)}, u32[]{:S(2)}, u32[]{:S(2)}) %collective-permute-start.13) | collective-permute-done | bytes 131104 | tf_op jit(solution)/shard_map/ppermute | solution.py:331
  166.3 5.0 %collective-permute-done.14 = f32[4,64,128]{2,1,0:T(8,128)S(1)} collective-permute-done((f32[4,64,128]{2,1,0:T(8,128)S(1)}, f32[4,64,128]{2,1,0:T(8,128)S(1)}, u32[]{:S(2)}, u32[]{:S(2)}) %collective-permute-start.14) | collective-permute-done | bytes 131104 | tf_op jit(solution)/shard_map/ppermute | solution.py:331
  172.1 5.9 %collective-permute-done.15 = f32[4,64,128]{2,1,0:T(8,128)S(1)} collective-permute-done((f32[4,64,128]{2,1,0:T(8,128)S(1)}, f32[4,64,128]{2,1,0:T(8,128)S(1)}, u32[]{:S(2)}, u32[]{:S(2)}) %collective-permute-start.15) | collective-permute-done | bytes 131104 | tf_op jit(solution)/shard_map/ppermute | solution.py:331
  178.0 2.3 final.1
  180.3 1.3 copy-done.2
  181.6 3.6 %all-to-all-start.1 = ((f32[8,512,128]{2,1,0:T(8,128)}), f32[8,512,128]{2,1,0:T(8,128)S(1)}, u32[]{:S(2)}, u32[]{:S(2)}) async-start(f32[8,512,128]{2,1,0:T(8,128)} %bitcast.37), calls=%async_computation.1 | async-start | bytes 4194304 | tf_op jit(solution)/shard_map/all_to_all | solution.py:472
  185.8 44.4 %all-to-all-done.1.x_ref = f32[8,512,128]{2,1,0:T(8,128)S(1)} async-done(((f32[8,512,128]{2,1,0:T(8,128)}), f32[8,512,128]{2,1,0:T(8,128)S(1)}, u32[]{:S(2)}, u32[]{:S(2)}) %all-to-all-start.1) | async-done | bytes 2097184 | tf_op jit(solution)/shard_map/all_to_all | solution.py:472
  230.2 5.1 %send.1 = f32[128,64,128]{2,1,0:T(8,128)S(1)} custom-call(s32[128]{0:T(128)S(1)} %select_reduce_fusion.1.item_ref, f32[8,512,128]{2,1,0:T(8,128)S(1)} %all-to-all-done.1.x_ref), custom_call_target="tpu_custom_call" | custom-call | tf_op jit(solution)/shard_map/send/pallas_call | solution.py:473
  235.3 2.0 copy-done
  237.3 4.9 %all-to-all-start.2 = ((f32[128,64,128]{2,1,0:T(8,128)}), f32[128,64,128]{2,1,0:T(8,128)}, u32[]{:S(2)}, u32[]{:S(2)}) async-start(f32[128,64,128]{2,1,0:T(8,128)} %copy-done), calls=%async_computation.2 | async-start | bytes 8388608 | tf_op jit(solution)/shard_map/all_to_all | solution.py:481
  242.6 47.8 %all-to-all-done.2.x_ref = f32[128,64,128]{2,1,0:T(8,128)} async-done(((f32[128,64,128]{2,1,0:T(8,128)}), f32[128,64,128]{2,1,0:T(8,128)}, u32[]{:S(2)}, u32[]{:S(2)}) %all-to-all-start.2) | async-done | bytes 4194336 | tf_op jit(solution)/shard_map/all_to_all | solution.py:481
  290.4 4.0 %place.1 = f32[64,64,128]{2,1,0:T(8,128)} custom-call(s32[64]{0:T(128)S(1)} %select_reduce_fusion.from_ref, f32[128,64,128]{2,1,0:T(8,128)} %all-to-all-done.2.x_ref), custom_call_target="tpu_custom_call" | custom-call | tf_op jit(solution)/shard_map/place/pallas_call | solution.py:482
  (89 shorter events, 10.2 us)
Async XLA Ops:
  0.8 1.6 copy-start.5
  4.7 1.3 copy-start.1
  6.0 7.5 %copy-start.12 = (s32[4,64]{1,0:T(4,128)S(1)}, s32[4,64]{1,0:T(4,128)}, u32[]{:S(2)}) copy-start(s32[4,64]{1,0:T(4,128)} %param.13) | copy-start | bytes 3076
  6.0 8.2 %copy-start.11 = (s32[4,64]{1,0:T(4,128)S(1)}, s32[4,64]{1,0:T(4,128)}, u32[]{:S(2)}) copy-start(s32[4,64]{1,0:T(4,128)} %param.14) | copy-start | bytes 3076
  6.0 8.9 %copy-start.17 = (f32[2,4]{1,0:T(2,128)S(1)}, f32[2,4]{1,0:T(2,128)}, u32[]{:S(2)}) copy-start(f32[2,4]{1,0:T(2,128)} %param.15) | copy-start | bytes 100
  6.0 55.6 %all-to-all-start = ((f32[8,512,128]{2,1,0:T(8,128)}), f32[8,512,128]{2,1,0:T(8,128)S(1)}, u32[]{:S(2)}, u32[]{:S(2)}) async-start(f32[8,512,128]{2,1,0:T(8,128)} %copy-done.1), calls=%async_computation | async-start | bytes 4194304 | tf_op jit(solution)/shard_map/all_to_all | solution.py:420
  13.4 4.6 %copy-start.13 = (f32[16,128]{1,0:T(8,128)S(1)}, f32[16,128]{1,0:T(8,128)}, u32[]{:S(2)}) copy-start(f32[16,128]{1,0:T(8,128)} %constant.136) | copy-start | bytes 24580
  13.4 49.0 %copy-start.3 = (bf16[768,256]{1,0:T(8,128)(2,1)S(1)}, bf16[768,256]{1,0:T(8,128)(2,1)}, u32[]{:S(2)}) copy-start(bf16[768,256]{1,0:T(8,128)(2,1)} %constant.132.clone.refs_6_.refs_9_) | copy-start | bytes 1179652
  13.4 49.0 %copy-start.4 = (bf16[768,256]{1,0:T(8,128)(2,1)S(1)}, bf16[768,256]{1,0:T(8,128)(2,1)}, u32[]{:S(2)}) copy-start(bf16[768,256]{1,0:T(8,128)(2,1)} %constant.131.clone.refs_5_.refs_8_) | copy-start | bytes 1179652
  13.4 49.0 %copy-start.8 = (f32[2,16,8,128]{3,2,1,0:T(8,128)S(1)}, f32[2,16,8,128]{3,2,1,0:T(8,128)}, u32[]{:S(2)}) copy-start(f32[2,16,8,128]{3,2,1,0:T(8,128)} %constant.130.clone.refs_4_.refs_7_) | copy-start | bytes 393220
  14.9 3.1 %copy-start.15 = (s32[1024]{0:T(1024)}, s32[1024]{0:T(1024)S(1)}, u32[]{:S(2)}) copy-start(s32[1024]{0:T(1024)S(1)} %pad_clamp_fusion) | copy-start | bytes 12292
  16.1 1.9 copy-start.16
  62.4 9.5 %copy-start.9 = (f32[4,16,128]{2,1,0:T(8,128)}, f32[4,16,128]{2,1,0:T(8,128)S(1)}, u32[]{:S(2)}) copy-start(f32[4,16,128]{2,1,0:T(8,128)S(1)} %broadcast_in_dim.28.refs_1_.refs_2_.refs_4_) | copy-start | bytes 98308
  71.8 1.3 copy-start.6
  73.2 1.2 collective-permute-start
  74.4 3.9 %collective-permute-start.1 = (f32[1,64,128]{2,1,0:T(8,128)S(1)}, f32[1,64,128]{2,1,0:T(8,128)S(1)}, u32[]{:S(2)}, u32[]{:S(2)}) collective-permute-start(f32[1,64,128]{2,1,0:T(8,128)S(1)} %add.308), channel_id=1, source_target_pairs={{0,16},{8,24},{16,0},{24,8},{1,17},{9,25},{17,1},{25,9},{2,18},{10... | collective-permute-start | bytes 98312 | tf_op jit(solution)/shard_map/ppermute | solution.py:331
  78.3 3.9 %collective-permute-start.2 = (f32[1,64,128]{2,1,0:T(8,128)S(1)}, f32[1,64,128]{2,1,0:T(8,128)S(1)}, u32[]{:S(2)}, u32[]{:S(2)}) collective-permute-start(f32[1,64,128]{2,1,0:T(8,128)S(1)} %add.309), channel_id=1, source_target_pairs={{0,1},{1,0},{2,3},{3,2},{4,5},{5,4},{6,7},{7,6},{8,9},{9,8},{10,11... | collective-permute-start | bytes 98312 | tf_op jit(solution)/shard_map/ppermute | solution.py:331
  80.5 24.7 %copy-start.14 = (f32[4,16]{1,0:T(4,128)S(1)}, f32[4,16]{1,0:T(4,128)}, u32[]{:S(2)}) copy-start(f32[4,16]{1,0:T(4,128)} %get-tuple-element.33) | copy-start | bytes 772
  82.3 1.6 copy-start.7
  83.9 0.8 copy-start.10
  96.1 1.3 collective-permute-start.3
  97.4 3.9 %collective-permute-start.4 = (f32[1,64,128]{2,1,0:T(8,128)S(1)}, f32[1,64,128]{2,1,0:T(8,128)S(1)}, u32[]{:S(2)}, u32[]{:S(2)}) collective-permute-start(f32[1,64,128]{2,1,0:T(8,128)S(1)} %add.311), channel_id=1, source_target_pairs={{0,16},{8,24},{16,0},{24,8},{1,17},{9,25},{17,1},{25,9},{2,18},{10... | collective-permute-start | bytes 98312 | tf_op jit(solution)/shard_map/ppermute | solution.py:331
  101.3 3.9 %collective-permute-start.5 = (f32[1,64,128]{2,1,0:T(8,128)S(1)}, f32[1,64,128]{2,1,0:T(8,128)S(1)}, u32[]{:S(2)}, u32[]{:S(2)}) collective-permute-start(f32[1,64,128]{2,1,0:T(8,128)S(1)} %add.312), channel_id=1, source_target_pairs={{0,1},{1,0},{2,3},{3,2},{4,5},{5,4},{6,7},{7,6},{8,9},{9,8},{10,11... | collective-permute-start | bytes 98312 | tf_op jit(solution)/shard_map/ppermute | solution.py:331
  117.1 1.4 collective-permute-start.6
  118.5 5.6 %collective-permute-start.7 = (f32[4,64,128]{2,1,0:T(8,128)S(1)}, f32[4,64,128]{2,1,0:T(8,128)S(1)}, u32[]{:S(2)}, u32[]{:S(2)}) collective-permute-start(f32[4,64,128]{2,1,0:T(8,128)S(1)} %add.323), channel_id=1, source_target_pairs={{0,16},{8,24},{16,0},{24,8},{1,17},{9,25},{17,1},{25,9},{2,18},{10... | collective-permute-start | bytes 393224 | tf_op jit(solution)/shard_map/ppermute | solution.py:331
  124.1 5.0 %collective-permute-start.8 = (f32[4,64,128]{2,1,0:T(8,128)S(1)}, f32[4,64,128]{2,1,0:T(8,128)S(1)}, u32[]{:S(2)}, u32[]{:S(2)}) collective-permute-start(f32[4,64,128]{2,1,0:T(8,128)S(1)} %add.324), channel_id=1, source_target_pairs={{0,1},{1,0},{2,3},{3,2},{4,5},{5,4},{6,7},{7,6},{8,9},{9,8},{10,11... | collective-permute-start | bytes 393224 | tf_op jit(solution)/shard_map/ppermute | solution.py:331
  129.2 5.0 %collective-permute-start.9 = (f32[4,64,128]{2,1,0:T(8,128)S(1)}, f32[4,64,128]{2,1,0:T(8,128)S(1)}, u32[]{:S(2)}, u32[]{:S(2)}) collective-permute-start(f32[4,64,128]{2,1,0:T(8,128)S(1)} %add.325), channel_id=1, source_target_pairs={{0,2},{1,3},{2,0},{3,1},{4,6},{5,7},{6,4},{7,5},{8,10},{9,11},{10,... | collective-permute-start | bytes 393224 | tf_op jit(solution)/shard_map/ppermute | solution.py:331
  134.2 6.9 %collective-permute-start.10 = (f32[4,64,128]{2,1,0:T(8,128)S(1)}, f32[4,64,128]{2,1,0:T(8,128)}, u32[]{:S(2)}, u32[]{:S(2)}) collective-permute-start(f32[4,64,128]{2,1,0:T(8,128)S(1)} %add.326), channel_id=1, source_target_pairs={{0,4},{1,5},{2,6},{3,7},{4,0},{5,1},{6,2},{7,3},{8,12},{9,13},{10,... | collective-permute-start | bytes 393224 | tf_op jit(solution)/shard_map/ppermute | solution.py:331
  154.1 1.4 collective-permute-start.11
  155.5 5.6 %collective-permute-start.12 = (f32[4,64,128]{2,1,0:T(8,128)S(1)}, f32[4,64,128]{2,1,0:T(8,128)S(1)}, u32[]{:S(2)}, u32[]{:S(2)}) collective-permute-start(f32[4,64,128]{2,1,0:T(8,128)S(1)} %add.328), channel_id=1, source_target_pairs={{0,16},{8,24},{16,0},{24,8},{1,17},{9,25},{17,1},{25,9},{2,18},{10... | collective-permute-start | bytes 393224 | tf_op jit(solution)/shard_map/ppermute | solution.py:331
  161.1 5.0 %collective-permute-start.13 = (f32[4,64,128]{2,1,0:T(8,128)S(1)}, f32[4,64,128]{2,1,0:T(8,128)S(1)}, u32[]{:S(2)}, u32[]{:S(2)}) collective-permute-start(f32[4,64,128]{2,1,0:T(8,128)S(1)} %add.329), channel_id=1, source_target_pairs={{0,1},{1,0},{2,3},{3,2},{4,5},{5,4},{6,7},{7,6},{8,9},{9,8},{10,11... | collective-permute-start | bytes 393224 | tf_op jit(solution)/shard_map/ppermute | solution.py:331
  166.2 5.0 %collective-permute-start.14 = (f32[4,64,128]{2,1,0:T(8,128)S(1)}, f32[4,64,128]{2,1,0:T(8,128)S(1)}, u32[]{:S(2)}, u32[]{:S(2)}) collective-permute-start(f32[4,64,128]{2,1,0:T(8,128)S(1)} %add.330), channel_id=1, source_target_pairs={{0,2},{1,3},{2,0},{3,1},{4,6},{5,7},{6,4},{7,5},{8,10},{9,11},{10,... | collective-permute-start | bytes 393224 | tf_op jit(solution)/shard_map/ppermute | solution.py:331
  171.2 6.8 %collective-permute-start.15 = (f32[4,64,128]{2,1,0:T(8,128)S(1)}, f32[4,64,128]{2,1,0:T(8,128)S(1)}, u32[]{:S(2)}, u32[]{:S(2)}) collective-permute-start(f32[4,64,128]{2,1,0:T(8,128)S(1)} %add.331), channel_id=1, source_target_pairs={{0,4},{1,5},{2,6},{3,7},{4,0},{5,1},{6,2},{7,3},{8,12},{9,13},{10,... | collective-permute-start | bytes 393224 | tf_op jit(solution)/shard_map/ppermute | solution.py:331
  180.3 1.3 copy-start.2
  181.6 48.6 %all-to-all-start.1 = ((f32[8,512,128]{2,1,0:T(8,128)}), f32[8,512,128]{2,1,0:T(8,128)S(1)}, u32[]{:S(2)}, u32[]{:S(2)}) async-start(f32[8,512,128]{2,1,0:T(8,128)} %bitcast.37), calls=%async_computation.1 | async-start | bytes 4194304 | tf_op jit(solution)/shard_map/all_to_all | solution.py:472
  235.3 2.0 copy-start
  237.3 53.1 %all-to-all-start.2 = ((f32[128,64,128]{2,1,0:T(8,128)}), f32[128,64,128]{2,1,0:T(8,128)}, u32[]{:S(2)}, u32[]{:S(2)}) async-start(f32[128,64,128]{2,1,0:T(8,128)} %copy-done), calls=%async_computation.2 | async-start | bytes 8388608 | tf_op jit(solution)/shard_map/all_to_all | solution.py:481

commit v2 on v1

--- a/solution.py
+++ b/solution.py
@@ -158,20 +158,6 @@
     write(real * cosine - imag * sine, real * sine + imag * cosine)
 
 
-def final_kernel(x_ref, q_ref, sel_ref, strength_ref, o_ref, *, channels_total, fibres, slots):
-    def body(tt, carry):
-        def write(real, imag):
-            o_ref[tt, 0] = real
-            o_ref[tt, 1] = imag
-
-        rotate_chunk(
-            x_ref, q_ref, sel_ref, strength_ref[...], tt, channels_total, fibres, slots, write
-        )
-        return carry
-
-    lax.fori_loop(0, x_ref.shape[0], body, 0)
-
-
 def split_store(a_ref, base, column, value):
     high = value.astype(jnp.bfloat16)
     low = (value - high.astype(jnp.float32)).astype(jnp.bfloat16)
@@ -182,25 +168,32 @@
 
 
 def step_kernel(
-    *refs, rotate, channels_total, fibres_in, fibres_out, slots
+    *refs, rotate, hold, channels_total, fibres_in, fibres_out, slots
 ):
+    refs = list(refs)
+    x_ref = refs.pop(0)
     if rotate:
-        (x_ref, q_ref, selin_ref, strength_ref, selout_ref, fc_ref, fs_ref, tw_ref, wf_ref, wi_ref,
-         u_ref, p_ref, xs_ref, a_ref, z_ref) = refs
-    else:
-        (x_ref, selout_ref, fc_ref, fs_ref, tw_ref, wf_ref, wi_ref,
-         u_ref, p_ref, a_ref, z_ref) = refs
-        xs_ref = x_ref
+        q_ref, selin_ref, strength_ref = refs[:3]
+        refs = refs[3:]
+    selout_ref, fc_ref, fs_ref, tw_ref, wf_ref, wi_ref, u_ref, p_ref = refs[:8]
+    refs = refs[8:]
+    rest_ref = refs.pop(0) if hold else None
+    xs_ref = refs.pop(0) if rotate else x_ref
+    a_ref, z_ref = refs
     chunks = x_ref.shape[0]
-    groups = 2 * slots // SUB
-    half = groups // 2
+    held = xs_ref.shape[2]
+    groups = held // SUB
+    half = slots // SUB
 
     if rotate:
 
         def turn(tt, carry):
             def write(real, imag):
-                xs_ref[tt, 0] = real
-                xs_ref[tt, 1] = imag
+                xs_ref[tt, 0] = real[:held]
+                xs_ref[tt, 1] = imag[:held]
+                if hold:
+                    rest_ref[tt, 0] = real[held:]
+                    rest_ref[tt, 1] = imag[held:]
 
             rotate_chunk(
                 x_ref, q_ref, selin_ref, strength_ref[...], tt, channels_total, fibres_in, slots,
@@ -265,7 +258,8 @@
             tt = j * STEP + k
             real, imag = u_ref[tt, 0], u_ref[tt, 1]
             power = real * real + imag * imag
-            power = power[:slots] + power[slots:]
+            if held > slots:
+                power = power[:slots] + power[slots:]
             for f in range(fibres_out):
                 mine = power if fibres_out == 1 else power * selout_ref[f]
                 p_ref[f, pl.ds(tt, 1), :] = jnp.sum(mine, axis=0, keepdims=True)
@@ -288,29 +282,70 @@
                 o_ref[g, pl.ds(p * slots + u, span, stride=rows), :] = value
 
 
-def send_kernel(item_ref, x_ref, o_ref, *, units, slots):
-    rows = 2 * slots
-    span = 2 * STEP
-
-    def body(n, carry):
-        for c in range(BLK):
-            channel = item_ref[n] * BLK + c
-            g = channel // units
-            u = channel - g * units
-            for p in range(2):
-                at = (c * 2 + p) * span
-                o_ref[n, at : at + span, :] = x_ref[g, pl.ds(p * slots + u, span, stride=rows), :]
-        return carry
-
-    lax.fori_loop(0, o_ref.shape[0], body, 0)
-
-
-def place_kernel(from_ref, x_ref, o_ref):
-    def body(n, carry):
-        o_ref[n] = x_ref[from_ref[n]]
-        return carry
-
-    lax.fori_loop(0, o_ref.shape[0], body, 0)
+def send_kernel(item_ref, count_ref, x_ref, *o_refs, units, slots):
+    capacity, near = o_refs[0].shape[0], o_refs[0].shape[1] // (2 * BLK)
+    for s, o_ref in enumerate(o_refs):
+
+        def body(n, carry, s=s, o_ref=o_ref):
+            for c in range(BLK):
+                channel = item_ref[s * capacity + n] * BLK + c
+                g = channel // units
+                u = channel - g * units
+                for part in range(2):
+                    at = (c * 2 + part) * near
+                    o_ref[n, at : at + near, :] = x_ref[
+                        g, pl.ds(part * slots + u, near, stride=2 * slots), :
+                    ]
+            return carry
+
+        lax.fori_loop(0, count_ref[s], body, 0)
+
+
+def place_kernel(from_ref, strength_ref, q_ref, *refs, channels_total, sources):
+    in_refs, (o_ref, held_ref, sems) = refs[: 2 * sources], refs[2 * sources :]
+    capacity, near = in_refs[0].shape[0], in_refs[0].shape[1] // (2 * BLK)
+    copies = []
+    for p in range(2):
+        for s in range(sources):
+            copies.append(
+                pltpu.make_async_copy(
+                    in_refs[p * sources + s],
+                    held_ref.at[p, pl.ds(s * capacity, capacity)],
+                    sems.at[p, s],
+                )
+            )
+    for copy in copies:
+        copy.start()
+    for copy in copies:
+        copy.wait()
+    fibres = q_ref.shape[0]
+    group_blocks = o_ref.shape[0] // fibres
+    for f in range(fibres):
+        total = 2.0 * q_ref[f]
+        strength = strength_ref[f]
+
+        def body(b, carry, f=f, total=total, strength=strength):
+            n = f * group_blocks + b
+            source = from_ref[n]
+            for c in range(BLK):
+                parts = []
+                power = None
+                for p in range(2):
+                    at = c * 2 * near
+                    real = held_ref[p, source, at : at + near, :]
+                    imag = held_ref[p, source, at + near : at + 2 * near, :]
+                    parts.append((real, imag))
+                    mine = real * real + imag * imag
+                    power = mine if power is None else power + mine
+                phase = strength * (total - power) * np.float32(1.0 / channels_total)
+                sine, cosine = sincos(phase)
+                for p, (real, imag) in enumerate(parts):
+                    at = (c * 2 + p) * 2 * near
+                    o_ref[n, pl.ds(at, near, stride=2), :] = real * cosine - imag * sine
+                    o_ref[n, pl.ds(at + 1, near, stride=2), :] = real * sine + imag * cosine
+            return carry
+
+        lax.fori_loop(0, group_blocks, body, 0)
 
 
 def params():
@@ -350,14 +385,29 @@
     arrival_all = jnp.sum(earlier.astype(jnp.int32), axis=2)
     my_target = lax.dynamic_index_in_dim(target_all, my_group, 0, keepdims=False)
     my_arrival = lax.dynamic_index_in_dim(arrival_all, my_group, 0, keepdims=False)
-    slot_index = my_target * capacity + my_arrival
+    partner = my_target ^ my_group
+    slot_index = partner * capacity + my_arrival
     matches = slot_index[None, :] == jnp.arange(groups * capacity)[:, None]
     source_item = jnp.sum(jnp.where(matches, position[None, :], 0), axis=1)
+    counts = jnp.sum((partner[None, :] == jnp.arange(groups)[:, None]).astype(jnp.int32), axis=1)
     mine = target_all == my_group
-    receive_slot = jnp.arange(groups)[:, None] * capacity + arrival_all
+    receive_slot = (jnp.arange(groups) ^ my_group)[:, None] * capacity + arrival_all
     hits = mine[:, :, None] & (landing_all[:, :, None] == position[None, None, :])
     take_from = jnp.sum(jnp.where(hits, receive_slot[:, :, None], 0), axis=(0, 1))
-    return source_item.astype(jnp.int32), take_from.astype(jnp.int32)
+    return source_item.astype(jnp.int32), counts, take_from.astype(jnp.int32)
+
+
+def local_total(values, times, my_time, wave_rounds):
+    bit = times // 2
+    while bit:
+        halves = values.reshape(values.shape[0], 2, -1, FB)
+        high = (my_time // bit) % 2
+        keep = lax.dynamic_index_in_dim(halves, high, 1, keepdims=False)
+        give = lax.dynamic_index_in_dim(halves, 1 - high, 1, keepdims=False)
+        pairs = [(i, i ^ bit) for i in range(times)]
+        values = keep + lax.ppermute(give, "tm", pairs)
+        bit //= 2
+    return summed(values, wave_rounds)
 
 
 def local(field, lit_count, route_fibre, route_slot, dispersion, nonlinearity):
@@ -395,7 +445,7 @@
         spread, strength = dispersion[span][fibre], nonlinearity[span][fibre]
         fc, fs = filter_tables(spread, channel, channels_total)
         spans.append((fc, fs, wide(strength), selection(fibre)))
-    source_item, take_from = route_tables(route_fibre, route_slot, groups, my_group, capacity)
+    source_item, counts, take_from = route_tables(route_fibre, route_slot, groups, my_group, capacity)
 
     wave_rounds = [("wave", 1 << b) for b in range(groups.bit_length() - 1)]
     time_rounds = [("tm", 1 << b) for b in range(times.bit_length() - 1)]
@@ -422,71 +472,83 @@
 
     twist = jnp.asarray(twist_table())
     forward, inverse = (jnp.asarray(table) for table in matrix_tables())
-    total, q_fibres, q_spec = None, 0, None
-    for step in range(2 * HALF):
-        span = step // HALF
-        fc, fs, strength, select = spans[span]
-        fibres_out = 1 if (span == 0 and same_fibre) else fibres
-        rotate = step > 0
-        operands = [wave_form]
+    def dispersed(x, step, total, q_fibres, fibres_out, hold):
+        fc, fs, _, select = spans[step // HALF]
+        rotate = total is not None
+        operands = [x]
         if rotate:
             operands += [total, spans[(step - 1) // HALF][3], spans[(step - 1) // HALF][2]]
         operands += [select, fc, fs, twist, forward, inverse]
-        scratch = [
-            pltpu.VMEM((FA * rows, 6 * FB), jnp.bfloat16),
-            pltpu.VMEM((FA * rows, 2 * FB), jnp.float32),
+        held = slots if hold else x.shape[2]
+        part = jax.ShapeDtypeStruct((chunks, 2, held, FB), jnp.float32)
+        outs = [part, jax.ShapeDtypeStruct((fibres_out, chunks, FB), jnp.float32)]
+        outs += [part] if hold else []
+        scratch = [pltpu.VMEM(part.shape, jnp.float32)] if rotate else []
+        scratch += [
+            pltpu.VMEM((FA * held, 6 * FB), jnp.bfloat16),
+            pltpu.VMEM((FA * held, 2 * FB), jnp.float32),
         ]
-        if rotate:
-            scratch = [pltpu.VMEM(wave_form.shape, jnp.float32)] + scratch
-        wave_form, partial = pl.pallas_call(
+        return pl.pallas_call(
             functools.partial(
-                step_kernel, rotate=rotate, channels_total=channels_total, fibres_in=q_fibres,
-                fibres_out=fibres_out, slots=slots,
+                step_kernel, rotate=rotate, hold=hold, channels_total=channels_total,
+                fibres_in=q_fibres, fibres_out=fibres_out, slots=slots,
             ),
-            out_shape=(
-                jax.ShapeDtypeStruct(wave_form.shape, jnp.float32),
-                jax.ShapeDtypeStruct((fibres_out, chunks, FB), jnp.float32),
-            ),
+            out_shape=tuple(outs),
             in_specs=[in_vmem()] * len(operands),
-            out_specs=(in_vmem(), in_vmem()),
+            out_specs=tuple([in_vmem()] * len(outs)),
             scratch_shapes=scratch,
             compiler_params=params(),
             name="step",
         )(*operands)
+
+    total, q_fibres = None, 0
+    for step in range(2 * HALF - 1):
+        fibres_out = 1 if (step < HALF and same_fibre) else fibres
+        wave_form, partial = dispersed(wave_form, step, total, q_fibres, fibres_out, False)
         rounds = fibre_rounds if fibres_out == 1 else time_rounds
         total, q_fibres = summed(partial, wave_rounds + rounds), fibres_out
 
-    _, _, strength, select = spans[1]
-    finished = pl.pallas_call(
-        functools.partial(
-            final_kernel, channels_total=channels_total, fibres=q_fibres, slots=slots
-        ),
-        out_shape=jax.ShapeDtypeStruct(wave_form.shape, jnp.float32),
-        in_specs=[in_vmem()] * 4,
+    last = 2 * HALF - 1
+
+    def to_times(values):
+        values = values.reshape(times, 2 * near * slots, FB)
+        return lax.all_to_all(values, "tm", split_axis=0, concat_axis=0, tiled=True)
+
+    def to_groups(values):
+        block = jax.ShapeDtypeStruct((capacity, BLK * 2 * near, FB), jnp.float32)
+        outgoing = pl.pallas_call(
+            functools.partial(send_kernel, units=units, slots=slots),
+            out_shape=(block,) * groups,
+            in_specs=[in_smem(), in_smem(), in_vmem()],
+            out_specs=(in_vmem(),) * groups,
+            compiler_params=params(),
+            name="send",
+        )(source_item, counts, values)
+        moved = [outgoing[0]]
+        for s in range(1, groups):
+            moved.append(lax.ppermute(outgoing[s], "wave", [(i, i ^ s) for i in range(groups)]))
+        return moved
+
+    first, partial, rest = dispersed(wave_form, last, total, q_fibres, fibres, True)
+    first = to_times(first)
+    second, more = dispersed(rest, last, None, 0, fibres, False)
+    second = to_times(second)
+    own_total = local_total(partial + more, times, my_time, wave_rounds)
+    blocks = to_groups(first) + to_groups(second)
+    strength = jnp.broadcast_to(nonlinearity[1][:, None, None], (fibres, near, FB))
+    placed = pl.pallas_call(
+        functools.partial(place_kernel, channels_total=channels_total, sources=groups),
+        out_shape=jax.ShapeDtypeStruct((sends, BLK * 4 * near, FB), jnp.float32),
+        in_specs=[in_smem(), in_vmem(), in_vmem()]
+        + [pl.BlockSpec(memory_space=pl.ANY)] * (2 * groups),
         out_specs=in_vmem(),
-        compiler_params=params(),
-        name="final",
-    )(wave_form, total, select, strength)
-
-    finished = finished.reshape(times, 2 * near * rows, FB)
-    gathered = lax.all_to_all(finished, "tm", split_axis=0, concat_axis=0, tiled=True)
-    outgoing = pl.pallas_call(
-        functools.partial(send_kernel, units=units, slots=slots),
-        out_shape=jax.ShapeDtypeStruct((groups * capacity, BLK * 4 * near, FB), jnp.float32),
-        in_specs=[in_smem(), in_vmem()],
-        out_specs=in_vmem(),
-        compiler_params=params(),
-        name="send",
-    )(source_item, gathered)
-    incoming = lax.all_to_all(outgoing, "wave", split_axis=0, concat_axis=0, tiled=True)
-    placed = pl.pallas_call(
-        place_kernel,
-        out_shape=jax.ShapeDtypeStruct((sends, BLK * 4 * near, FB), jnp.float32),
-        in_specs=[in_smem(), in_vmem()],
-        out_specs=in_vmem(),
+        scratch_shapes=[
+            pltpu.VMEM((2, groups * capacity, BLK * 2 * near, FB), jnp.float32),
+            pltpu.SemaphoreType.DMA((2, groups)),
+        ],
         compiler_params=params(),
         name="place",
-    )(take_from, incoming)
+    )(take_from, strength, own_total, *blocks)
     result = placed.reshape(fibres, channels, 2, near, 2, FB).transpose(0, 1, 2, 4, 3, 5)
     return result.reshape(fibres, channels, 2, 2, samples)
 

time: 295 us -> 279 us (0.946)
  waiting for transfers between devices: 183 us -> 160 us
  Pallas kernels: 58.1 us -> 62.6 us
  starting transfers between devices: 30.2 us -> 34 us
    all_to_all x2, waiting for transfers between devices: 92.1 us -> 22.2 us  [to_times(): return lax.all_to_all(values, 'tm', split_axis=0, concat_axis=0, tiled=True)]
    ppermute x0 -> x9, waiting for transfers between devices: none -> 64.9 us  [the longest x6 38.3 us: to_groups(): lax.ppermute(outgoing[s], 'wave', [(i, i ^ s) for i in range(groups)])]
    ppermute x16 -> x13, waiting for transfers between devices: 49.2 us -> 30.8 us  [summed(): values = values + lax.ppermute(values, axis, pairs)]
    ppermute x0 -> x9, starting transfers between devices: none -> 7.73 us  [the longest x3 4.23 us: local_total(): values = keep + lax.ppermute(give, 'tm', pairs)]
    pallas_call x7 -> x8, Pallas kernels: 55.8 us -> 60.4 us  [the longest x5 48.5 us: dispersed(): pl.pallas_call(functools.partial(step_kernel, rotate=rotate, hold=hold, c...]
    ppermute x16 -> x13, starting transfers between devices: 14.3 us -> 11.7 us  [summed(): values = values + lax.ppermute(values, axis, pairs)]
  transfers between devices with their start and end apart: 19 -> 25, of which waited for: 19 -> 20; matrix products, arithmetic and copies ran while one was open for 3% -> 3% of each run, Pallas kernels for 0% -> 0%
where the time goes in v2:
time: 279 us; the launch traced here: 278 us
  waiting for transfers between devices  160 us (57%)
  Pallas kernels  62.6 us (22%)
  starting transfers between devices  34 us (12%)
  local copies, waits for them, and re-layouts  16.2 us (6%)
  other arithmetic  4.39 us (2%)
    pallas_call x5, Pallas kernels, dispersed(): pl.pallas_call(functools.partial(step_kernel, rotate=rotate, hold=hold, c...  48.5 us
    all_to_all x1, waiting for transfers between devices, local(): lax.all_to_all(packed, 'tm', split_axis=0, concat_axis=0, tiled=True)  42.4 us
    ppermute x6, waiting for transfers between devices, to_groups(): lax.ppermute(outgoing[s], 'wave', [(i, i ^ s) for i in range(groups)])  38.3 us
    ppermute x13, waiting for transfers between devices, summed(): values = values + lax.ppermute(values, axis, pairs)  30.8 us
    ppermute x3, waiting for transfers between devices, local_total(): values = keep + lax.ppermute(give, 'tm', pairs)  26.6 us
    all_to_all x2, waiting for transfers between devices, to_times(): return lax.all_to_all(values, 'tm', split_axis=0, concat_axis=0, tiled=True)  22.2 us
    ppermute x13, starting transfers between devices, summed(): values = values + lax.ppermute(values, axis, pairs)  11.7 us
    unnamed x36, local copies, waits for them, and re-layouts  9.27 us
  transfers between devices with their start and end apart: 25, of which 20 were waited for; matrix products, arithmetic and copies ran while one was open for 3% of the time, Pallas kernels for 0%

profile of v2, /device:TPU:0, one launch (start us, length us, event | category | flops | bytes accessed | tf_op | source)
XLA Modules:
  0.0 278.0 jit_solution(11833626831041683861)
XLA Ops:
  0.8 1.6 copy-done.4
  2.4 2.3 pack.1
  4.7 1.3 copy-done.2
  6.0 7.4 %all-to-all-start = ((f32[8,512,128]{2,1,0:T(8,128)}), f32[8,512,128]{2,1,0:T(8,128)S(1)}, u32[]{:S(2)}, u32[]{:S(2)}) async-start(f32[8,512,128]{2,1,0:T(8,128)} %copy-done.2), calls=%async_computation | async-start | bytes 4194304 | tf_op jit(solution)/shard_map/all_to_all | solution.py:470
  14.9 1.2 gather_fusion.3
  16.2 1.2 gather_fusion
  17.5 1.7 sine_multiply_fusion
  19.2 42.4 %all-to-all-done = f32[8,512,128]{2,1,0:T(8,128)S(1)} async-done(((f32[8,512,128]{2,1,0:T(8,128)}), f32[8,512,128]{2,1,0:T(8,128)S(1)}, u32[]{:S(2)}, u32[]{:S(2)}) %all-to-all-start) | async-done | bytes 2097184 | tf_op jit(solution)/shard_map/all_to_all | solution.py:470
  61.7 9.3 %step.5 = (f32[64,2,32,128]{3,2,1,0:T(8,128)S(1)}, f32[1,64,128]{2,1,0:T(8,128)S(1)}) custom-call(f32[64,2,32,128]{3,2,1,0:T(8,128)S(1)} %bitcast.57, f32[4,16,128]{2,1,0:T(8,128)S(1)} %broadcast_in_dim.32.refs_1_.refs_2_.refs_4_, f32[16,16,128]{2,1,0:T(8,128)S(1)} %get-tuple-element.49.refs_2_.refs_5_, ...), custom_call_target="tpu_custom_call" | custom-call | tf_op jit(solution)/shard_map/step/pallas_call | solution.py:491
  71.1 1.3 copy-done.5
  72.4 1.2 collective-permute-done
  73.6 1.5 collective-permute-start.1
  75.1 2.4 collective-permute-done.1
  77.5 1.5 collective-permute-start.2
  81.5 1.6 copy-done.6
  83.8 11.3 %step.6 = (f32[64,2,32,128]{3,2,1,0:T(8,128)S(1)}, f32[1,64,128]{2,1,0:T(8,128)S(1)}) custom-call(f32[64,2,32,128]{3,2,1,0:T(8,128)S(1)} %copy-done.6, f32[1,64,128]{2,1,0:T(8,128)S(1)} %add.348.refs_1_, f32[4,16,128]{2,1,0:T(8,128)S(1)} %copy-done.8, f32[16,128]{1,0:T(8,128)S(1)} %broadcast_in_dim.33.refs_3_, f32[4,16,128]{2,1,0:T(8,128)S(1)} %copy-done.8, ...), custom_call_target="tpu_custom_call" | custom-call | tf_op jit(solution)/shard_map/step/pallas_call | solution.py:491
  95.3 1.2 collective-permute-done.3
  96.5 1.5 collective-permute-start.4
  98.0 2.4 collective-permute-done.4
  100.4 1.5 collective-permute-start.5
  101.8 2.5 collective-permute-done.5
  104.4 11.6 %step.7 = (f32[64,2,32,128]{3,2,1,0:T(8,128)S(1)}, f32[4,64,128]{2,1,0:T(8,128)S(1)}) custom-call(f32[64,2,32,128]{3,2,1,0:T(8,128)S(1)} %get-tuple-element.26.refs_0_, f32[1,64,128]{2,1,0:T(8,128)S(1)} %add.351.refs_1_, f32[4,16,128]{2,1,0:T(8,128)S(1)} %copy-done.8, f32[16,128]{1,0:T(8,128)S(1)} %broadcast_in_dim.33.refs_3_, ...), custom_call_target="tpu_custom_call" | custom-call | tf_op jit(solution)/shard_map/step/pallas_call | solution.py:491
  116.0 1.3 collective-permute-done.6
  117.4 1.6 collective-permute-start.7
  119.0 4.0 %collective-permute-done.7 = f32[4,64,128]{2,1,0:T(8,128)S(1)} collective-permute-done((f32[4,64,128]{2,1,0:T(8,128)S(1)}, f32[4,64,128]{2,1,0:T(8,128)S(1)}, u32[]{:S(2)}, u32[]{:S(2)}) %collective-permute-start.7) | collective-permute-done | bytes 131104 | tf_op jit(solution)/shard_map/ppermute | solution.py:366
  123.0 1.5 collective-permute-start.8
  124.6 3.5 %collective-permute-done.8 = f32[4,64,128]{2,1,0:T(8,128)S(1)} collective-permute-done((f32[4,64,128]{2,1,0:T(8,128)S(1)}, f32[4,64,128]{2,1,0:T(8,128)S(1)}, u32[]{:S(2)}, u32[]{:S(2)}) %collective-permute-start.8) | collective-permute-done | bytes 131104 | tf_op jit(solution)/shard_map/ppermute | solution.py:366
  128.2 5.0 %collective-permute-done.9 = f32[4,64,128]{2,1,0:T(8,128)S(1)} collective-permute-done((f32[4,64,128]{2,1,0:T(8,128)S(1)}, f32[4,64,128]{2,1,0:T(8,128)S(1)}, u32[]{:S(2)}, u32[]{:S(2)}) %collective-permute-start.9) | collective-permute-done | bytes 131104 | tf_op jit(solution)/shard_map/ppermute | solution.py:366
  134.8 5.2 %collective-permute-done.10 = f32[4,64,128]{2,1,0:T(8,128)} collective-permute-done((f32[4,64,128]{2,1,0:T(8,128)S(1)}, f32[4,64,128]{2,1,0:T(8,128)}, u32[]{:S(2)}, u32[]{:S(2)}) %collective-permute-start.10) | collective-permute-done | bytes 131104 | tf_op jit(solution)/shard_map/ppermute | solution.py:366
  141.0 9.3 %step.8 = (f32[64,2,16,128]{3,2,1,0:T(8,128)}, f32[4,64,128]{2,1,0:T(8,128)S(1)}, f32[64,2,16,128]{3,2,1,0:T(8,128)S(1)}) custom-call(f32[64,2,32,128]{3,2,1,0:T(8,128)S(1)} %get-tuple-element.28.refs_0_, f32[4,64,128]{2,1,0:T(8,128)S(1)} %add.365.refs_1_, f32[4,16,128]{2,1,0:T(8,128)S(1)} %broadcast_in_dim.34.refs_4_.refs_2_.refs_1_, ...), custom_call_target="tpu_custom_call" | custom-call | tf_op jit(solution)/shard_map/step/pallas_call | solution.py:491
  150.3 7.0 %step.9 = (f32[64,2,16,128]{3,2,1,0:T(8,128)}, f32[4,64,128]{2,1,0:T(8,128)S(1)}) custom-call(f32[64,2,16,128]{3,2,1,0:T(8,128)S(1)} %get-tuple-element.31.refs_0_, f32[4,16,128]{2,1,0:T(8,128)S(1)} %broadcast_in_dim.34.refs_4_.refs_2_.refs_1_, f32[16,16,128]{2,1,0:T(8,128)S(1)} %get-tuple-element.46.refs_5_.refs_2_, ...), custom_call_target="tpu_custom_call" | custom-call | tf_op jit(solution)/shard_map/step/pallas_call | solution.py:491
  157.3 3.6 %all-to-all-start.2 = ((f32[8,256,128]{2,1,0:T(8,128)}), f32[8,256,128]{2,1,0:T(8,128)S(1)}, u32[]{:S(2)}, u32[]{:S(2)}) async-start(f32[8,256,128]{2,1,0:T(8,128)} %bitcast.26), calls=%async_computation.2 | async-start | bytes 2097152 | tf_op jit(solution)/shard_map/all_to_all | solution.py:515
  161.1 22.2 %all-to-all-done.2.x_ref = f32[8,256,128]{2,1,0:T(8,128)S(1)} async-done(((f32[8,256,128]{2,1,0:T(8,128)}), f32[8,256,128]{2,1,0:T(8,128)S(1)}, u32[]{:S(2)}, u32[]{:S(2)}) %all-to-all-start.2) | async-done | bytes 1048608 | tf_op jit(solution)/shard_map/all_to_all | solution.py:515
  183.4 3.6 %all-to-all-start.1 = ((f32[8,256,128]{2,1,0:T(8,128)}), f32[8,256,128]{2,1,0:T(8,128)S(1)}, u32[]{:S(2)}, u32[]{:S(2)}) async-start(f32[8,256,128]{2,1,0:T(8,128)} %bitcast.25), calls=%async_computation.1 | async-start | bytes 2097152 | tf_op jit(solution)/shard_map/all_to_all | solution.py:515
  187.2 2.9 %collective-permute-start.11 = (f32[4,32,128]{2,1,0:T(8,128)S(1)}, f32[4,32,128]{2,1,0:T(8,128)S(1)}, u32[]{:S(2)}, u32[]{:S(2)}) collective-permute-start(f32[4,32,128]{2,1,0:T(8,128)S(1)} %dynamic-slice_bitcast_fusion), channel_id=1, source_target_pairs={{0,4},{1,5},{2,6},{3,7},{4,0},{5,1},{6,2},{7,3},{8,12},{9,13},{10,... | collective-permute-start | bytes 196616 | tf_op jit(solution)/shard_map/ppermute | solution.py:408
  190.2 24.0 %collective-permute-done.11 = f32[4,32,128]{2,1,0:T(8,128)S(1)} collective-permute-done((f32[4,32,128]{2,1,0:T(8,128)S(1)}, f32[4,32,128]{2,1,0:T(8,128)S(1)}, u32[]{:S(2)}, u32[]{:S(2)}) %collective-permute-start.11) | collective-permute-done | bytes 65568 | tf_op jit(solution)/shard_map/ppermute | solution.py:408
  214.5 3.1 %send.3 = (f32[32,32,128]{2,1,0:T(8,128)S(1)}, f32[32,32,128]{2,1,0:T(8,128)}, f32[32,32,128]{2,1,0:T(8,128)S(1)}, f32[32,32,128]{2,1,0:T(8,128)S(1)}) custom-call(s32[128]{0:T(128)S(1)} %select_reduce_fusion.1.item_ref, s32[4]{0:T(128)S(1)} %convert_reduce_fusion.1.count_ref, f32[8,256,128]{2,1,0:T(8,128)S(1)} %all-to-all-done.2.x_ref), custom_call_target="tpu_custom_call" | custom-call | tf_op jit(solution)/shard_map/send/pallas_call | solution.py:519
  218.5 1.3 collective-permute-start.13
  219.7 2.5 collective-permute-done.13
  222.3 1.2 collective-permute-done.14
  223.5 1.6 collective-permute-start.15
  226.2 3.4 %send.2 = (f32[32,32,128]{2,1,0:T(8,128)S(1)}, f32[32,32,128]{2,1,0:T(8,128)}, f32[32,32,128]{2,1,0:T(8,128)}, f32[32,32,128]{2,1,0:T(8,128)}) custom-call(s32[128]{0:T(128)S(1)} %select_reduce_fusion.1.item_ref, s32[4]{0:T(128)S(1)} %convert_reduce_fusion.1.count_ref, f32[8,256,128]{2,1,0:T(8,128)S(1)} %all-to-all-done.1.x_ref), custom_call_target="tpu_custom_call" | custom-call | tf_op jit(solution)/shard_map/send/pallas_call | solution.py:519
  233.2 6.8 %collective-permute-done.20.refs_6_ = f32[32,32,128]{2,1,0:T(8,128)S(1)} collective-permute-done((f32[32,32,128]{2,1,0:T(8,128)}, f32[32,32,128]{2,1,0:T(8,128)S(1)}, u32[]{:S(2)}, u32[]{:S(2)}) %collective-permute-start.20) | collective-permute-done | bytes 524320 | tf_op jit(solution)/shard_map/ppermute | solution.py:529
  240.0 9.3 %collective-permute-done.21.refs_7_ = f32[32,32,128]{2,1,0:T(8,128)S(1)} collective-permute-done((f32[32,32,128]{2,1,0:T(8,128)}, f32[32,32,128]{2,1,0:T(8,128)S(1)}, u32[]{:S(2)}, u32[]{:S(2)}) %collective-permute-start.21) | collective-permute-done | bytes 524320 | tf_op jit(solution)/shard_map/ppermute | solution.py:529
  249.4 13.1 %collective-permute-done.17.refs_2_ = f32[32,32,128]{2,1,0:T(8,128)S(1)} collective-permute-done((f32[32,32,128]{2,1,0:T(8,128)}, f32[32,32,128]{2,1,0:T(8,128)S(1)}, u32[]{:S(2)}, u32[]{:S(2)}) %collective-permute-start.17) | collective-permute-done | bytes 524320 | tf_op jit(solution)/shard_map/ppermute | solution.py:529
  262.5 9.1 %collective-permute-done.18.refs_3_ = f32[32,32,128]{2,1,0:T(8,128)} collective-permute-done((f32[32,32,128]{2,1,0:T(8,128)}, f32[32,32,128]{2,1,0:T(8,128)}, u32[]{:S(2)}, u32[]{:S(2)}) %collective-permute-start.18) | collective-permute-done | bytes 524320 | tf_op jit(solution)/shard_map/ppermute | solution.py:529
  271.6 1.0 copy-done.10
  272.7 5.4 %place.1 = f32[64,64,128]{2,1,0:T(8,128)} custom-call(s32[64]{0:T(128)S(1)} %select_reduce_fusion.from_ref, f32[4,8,128]{2,1,0:T(8,128)S(1)} %broadcast_in_dim.31.strength_ref, f32[4,8,128]{2,1,0:T(8,128)S(1)} %add.380.q_ref, f32[32,32,128]{2,1,0:T(8,128)S(1)} %copy-done.10, f32[32,32,128]{2,1,0:T(8,128)S(1)} %collective-permute-done.16.refs_1_, ...), custom_call_target="tpu_custom_call" | custom-call | tf_op jit(solution)/shard_map/place/pallas_call | solution.py:539
  (108 shorter events, 15.2 us)
Async XLA Ops:
  0.8 1.6 copy-start.4
  4.7 1.3 copy-start.2
  6.0 7.5 %copy-start.14 = (s32[4,64]{1,0:T(4,128)S(1)}, s32[4,64]{1,0:T(4,128)}, u32[]{:S(2)}) copy-start(s32[4,64]{1,0:T(4,128)} %param.13) | copy-start | bytes 3076
  6.0 8.2 %copy-start.13 = (s32[4,64]{1,0:T(4,128)S(1)}, s32[4,64]{1,0:T(4,128)}, u32[]{:S(2)}) copy-start(s32[4,64]{1,0:T(4,128)} %param.14) | copy-start | bytes 3076
  6.0 8.9 %copy-start.17 = (f32[2,4]{1,0:T(2,128)S(1)}, f32[2,4]{1,0:T(2,128)}, u32[]{:S(2)}) copy-start(f32[2,4]{1,0:T(2,128)} %param.15) | copy-start | bytes 100
  6.0 55.6 %all-to-all-start = ((f32[8,512,128]{2,1,0:T(8,128)}), f32[8,512,128]{2,1,0:T(8,128)S(1)}, u32[]{:S(2)}, u32[]{:S(2)}) async-start(f32[8,512,128]{2,1,0:T(8,128)} %copy-done.2), calls=%async_computation | async-start | bytes 4194304 | tf_op jit(solution)/shard_map/all_to_all | solution.py:470
  13.4 48.3 %copy-start = (bf16[768,256]{1,0:T(8,128)(2,1)S(1)}, bf16[768,256]{1,0:T(8,128)(2,1)}, u32[]{:S(2)}) copy-start(bf16[768,256]{1,0:T(8,128)(2,1)} %constant.195.clone.refs_6_.refs_9_) | copy-start | bytes 1179652
  13.4 48.3 %copy-start.1 = (bf16[768,256]{1,0:T(8,128)(2,1)S(1)}, bf16[768,256]{1,0:T(8,128)(2,1)}, u32[]{:S(2)}) copy-start(bf16[768,256]{1,0:T(8,128)(2,1)} %constant.194.clone.refs_5_.refs_8_) | copy-start | bytes 1179652
  13.4 48.3 %copy-start.3 = (f32[2,16,8,128]{3,2,1,0:T(8,128)S(1)}, f32[2,16,8,128]{3,2,1,0:T(8,128)}, u32[]{:S(2)}) copy-start(f32[2,16,8,128]{3,2,1,0:T(8,128)} %constant.193.clone.refs_4_.refs_7_) | copy-start | bytes 393220
  14.9 2.5 copy-start.15
  16.2 1.3 copy-start.16
  61.7 9.3 %copy-start.7 = (f32[4,16,128]{2,1,0:T(8,128)}, f32[4,16,128]{2,1,0:T(8,128)S(1)}, u32[]{:S(2)}) copy-start(f32[4,16,128]{2,1,0:T(8,128)S(1)} %broadcast_in_dim.32.refs_1_.refs_2_.refs_4_) | copy-start | bytes 98308
  71.0 1.3 copy-start.5
  72.4 1.2 collective-permute-start
  73.6 3.9 %collective-permute-start.1 = (f32[1,64,128]{2,1,0:T(8,128)S(1)}, f32[1,64,128]{2,1,0:T(8,128)S(1)}, u32[]{:S(2)}, u32[]{:S(2)}) collective-permute-start(f32[1,64,128]{2,1,0:T(8,128)S(1)} %add.346), channel_id=1, source_target_pairs={{0,16},{8,24},{16,0},{24,8},{1,17},{9,25},{17,1},{25,9},{2,18},{10... | collective-permute-start | bytes 98312 | tf_op jit(solution)/shard_map/ppermute | solution.py:366
  77.5 3.9 %collective-permute-start.2 = (f32[1,64,128]{2,1,0:T(8,128)S(1)}, f32[1,64,128]{2,1,0:T(8,128)S(1)}, u32[]{:S(2)}, u32[]{:S(2)}) collective-permute-start(f32[1,64,128]{2,1,0:T(8,128)S(1)} %add.347), channel_id=1, source_target_pairs={{0,1},{1,0},{2,3},{3,2},{4,5},{5,4},{6,7},{7,6},{8,9},{9,8},{10,11... | collective-permute-start | bytes 98312 | tf_op jit(solution)/shard_map/ppermute | solution.py:366
  81.5 1.6 copy-start.6
  83.1 0.8 copy-start.8
  95.2 1.3 collective-permute-start.3
  96.5 3.9 %collective-permute-start.4 = (f32[1,64,128]{2,1,0:T(8,128)S(1)}, f32[1,64,128]{2,1,0:T(8,128)S(1)}, u32[]{:S(2)}, u32[]{:S(2)}) collective-permute-start(f32[1,64,128]{2,1,0:T(8,128)S(1)} %add.349), channel_id=1, source_target_pairs={{0,16},{8,24},{16,0},{24,8},{1,17},{9,25},{17,1},{25,9},{2,18},{10... | collective-permute-start | bytes 98312 | tf_op jit(solution)/shard_map/ppermute | solution.py:366
  100.4 3.9 %collective-permute-start.5 = (f32[1,64,128]{2,1,0:T(8,128)S(1)}, f32[1,64,128]{2,1,0:T(8,128)S(1)}, u32[]{:S(2)}, u32[]{:S(2)}) collective-permute-start(f32[1,64,128]{2,1,0:T(8,128)S(1)} %add.350), channel_id=1, source_target_pairs={{0,1},{1,0},{2,3},{3,2},{4,5},{5,4},{6,7},{7,6},{8,9},{9,8},{10,11... | collective-permute-start | bytes 98312 | tf_op jit(solution)/shard_map/ppermute | solution.py:366
  116.0 1.4 collective-permute-start.6
  117.4 5.6 %collective-permute-start.7 = (f32[4,64,128]{2,1,0:T(8,128)S(1)}, f32[4,64,128]{2,1,0:T(8,128)S(1)}, u32[]{:S(2)}, u32[]{:S(2)}) collective-permute-start(f32[4,64,128]{2,1,0:T(8,128)S(1)} %add.361), channel_id=1, source_target_pairs={{0,16},{8,24},{16,0},{24,8},{1,17},{9,25},{17,1},{25,9},{2,18},{10... | collective-permute-start | bytes 393224 | tf_op jit(solution)/shard_map/ppermute | solution.py:366
  123.0 5.0 %collective-permute-start.8 = (f32[4,64,128]{2,1,0:T(8,128)S(1)}, f32[4,64,128]{2,1,0:T(8,128)S(1)}, u32[]{:S(2)}, u32[]{:S(2)}) collective-permute-start(f32[4,64,128]{2,1,0:T(8,128)S(1)} %add.362), channel_id=1, source_target_pairs={{0,1},{1,0},{2,3},{3,2},{4,5},{5,4},{6,7},{7,6},{8,9},{9,8},{10,11... | collective-permute-start | bytes 393224 | tf_op jit(solution)/shard_map/ppermute | solution.py:366
  128.1 5.0 %collective-permute-start.9 = (f32[4,64,128]{2,1,0:T(8,128)S(1)}, f32[4,64,128]{2,1,0:T(8,128)S(1)}, u32[]{:S(2)}, u32[]{:S(2)}) collective-permute-start(f32[4,64,128]{2,1,0:T(8,128)S(1)} %add.363), channel_id=1, source_target_pairs={{0,2},{1,3},{2,0},{3,1},{4,6},{5,7},{6,4},{7,5},{8,10},{9,11},{10,... | collective-permute-start | bytes 393224 | tf_op jit(solution)/shard_map/ppermute | solution.py:366
  133.1 6.9 %collective-permute-start.10 = (f32[4,64,128]{2,1,0:T(8,128)S(1)}, f32[4,64,128]{2,1,0:T(8,128)}, u32[]{:S(2)}, u32[]{:S(2)}) collective-permute-start(f32[4,64,128]{2,1,0:T(8,128)S(1)} %add.364), channel_id=1, source_target_pairs={{0,4},{1,5},{2,6},{3,7},{4,0},{5,1},{6,2},{7,3},{8,12},{9,13},{10,... | collective-permute-start | bytes 393224 | tf_op jit(solution)/shard_map/ppermute | solution.py:366
  157.3 26.0 %all-to-all-start.2 = ((f32[8,256,128]{2,1,0:T(8,128)}), f32[8,256,128]{2,1,0:T(8,128)S(1)}, u32[]{:S(2)}, u32[]{:S(2)}) async-start(f32[8,256,128]{2,1,0:T(8,128)} %bitcast.26), calls=%async_computation.2 | async-start | bytes 2097152 | tf_op jit(solution)/shard_map/all_to_all | solution.py:515
  183.4 42.9 %all-to-all-start.1 = ((f32[8,256,128]{2,1,0:T(8,128)}), f32[8,256,128]{2,1,0:T(8,128)S(1)}, u32[]{:S(2)}, u32[]{:S(2)}) async-start(f32[8,256,128]{2,1,0:T(8,128)} %bitcast.25), calls=%async_computation.1 | async-start | bytes 2097152 | tf_op jit(solution)/shard_map/all_to_all | solution.py:515
  187.2 27.0 %collective-permute-start.11 = (f32[4,32,128]{2,1,0:T(8,128)S(1)}, f32[4,32,128]{2,1,0:T(8,128)S(1)}, u32[]{:S(2)}, u32[]{:S(2)}) collective-permute-start(f32[4,32,128]{2,1,0:T(8,128)S(1)} %dynamic-slice_bitcast_fusion), channel_id=1, source_target_pairs={{0,4},{1,5},{2,6},{3,7},{4,0},{5,1},{6,2},{7,3},{8,12},{9,13},{10,... | collective-permute-start | bytes 196616 | tf_op jit(solution)/shard_map/ppermute | solution.py:408
  214.3 4.1 %collective-permute-start.12 = (f32[4,16,128]{2,1,0:T(8,128)S(1)}, f32[4,16,128]{2,1,0:T(8,128)S(1)}, u32[]{:S(2)}, u32[]{:S(2)}) collective-permute-start(f32[4,16,128]{2,1,0:T(8,128)S(1)} %dynamic-slice_bitcast_fusion.1), channel_id=1, source_target_pairs={{0,2},{1,3},{2,0},{3,1},{4,6},{5,7},{6,4},{7,5},{8,10},{9,11},{10,... | collective-permute-start | bytes 98312 | tf_op jit(solution)/shard_map/ppermute | solution.py:408
  217.6 0.8 copy-start.12
  218.4 7.1 %copy-start.11 = (f32[32,32,128]{2,1,0:T(8,128)}, f32[32,32,128]{2,1,0:T(8,128)S(1)}, u32[]{:S(2)}) copy-start(f32[32,32,128]{2,1,0:T(8,128)S(1)} %get-tuple-element.42) | copy-start | bytes 1572868
  218.4 13.5 %collective-permute-start.19 = (f32[32,32,128]{2,1,0:T(8,128)}, f32[32,32,128]{2,1,0:T(8,128)S(1)}, u32[]{:S(2)}, u32[]{:S(2)}) collective-permute-start(f32[32,32,128]{2,1,0:T(8,128)} %get-tuple-element.40), channel_id=1, source_target_pairs={{0,8},{8,0},{16,24},{24,16},{1,9},{9,1},{17,25},{25,17},{2,10},{10... | collective-permute-start | bytes 1572872 | tf_op jit(solution)/shard_map/ppermute | solution.py:529
  218.5 3.8 %collective-permute-start.13 = (f32[4,8,128]{2,1,0:T(8,128)S(1)}, f32[4,8,128]{2,1,0:T(8,128)S(1)}, u32[]{:S(2)}, u32[]{:S(2)}) collective-permute-start(f32[4,8,128]{2,1,0:T(8,128)S(1)} %dynamic-slice_bitcast_fusion.2), channel_id=1, source_target_pairs={{0,1},{1,0},{2,3},{3,2},{4,5},{5,4},{6,7},{7,6},{8,9},{9,8},{10,11... | collective-permute-start | bytes 49160 | tf_op jit(solution)/shard_map/ppermute | solution.py:408
  222.3 1.2 collective-permute-start.14
  223.5 8.0 %collective-permute-start.15 = (f32[4,8,128]{2,1,0:T(8,128)S(1)}, f32[4,8,128]{2,1,0:T(8,128)S(1)}, u32[]{:S(2)}, u32[]{:S(2)}) collective-permute-start(f32[4,8,128]{2,1,0:T(8,128)S(1)} %add.379), channel_id=1, source_target_pairs={{0,16},{8,24},{16,0},{24,8},{1,17},{9,25},{17,1},{25,9},{2,18},{10... | collective-permute-start | bytes 49160 | tf_op jit(solution)/shard_map/ppermute | solution.py:366
  225.0 15.0 %collective-permute-start.20 = (f32[32,32,128]{2,1,0:T(8,128)}, f32[32,32,128]{2,1,0:T(8,128)S(1)}, u32[]{:S(2)}, u32[]{:S(2)}) collective-permute-start(f32[32,32,128]{2,1,0:T(8,128)} %copy-done.12), channel_id=1, source_target_pairs={{0,16},{8,24},{16,0},{24,8},{1,17},{9,25},{17,1},{25,9},{2,18},{10... | collective-permute-start | bytes 1572872 | tf_op jit(solution)/shard_map/ppermute | solution.py:529
  225.5 23.9 %collective-permute-start.21 = (f32[32,32,128]{2,1,0:T(8,128)}, f32[32,32,128]{2,1,0:T(8,128)S(1)}, u32[]{:S(2)}, u32[]{:S(2)}) collective-permute-start(f32[32,32,128]{2,1,0:T(8,128)} %copy-done.11), channel_id=1, source_target_pairs={{0,24},{8,16},{16,8},{24,0},{1,25},{9,17},{17,9},{25,1},{2,26},{10... | collective-permute-start | bytes 1572872 | tf_op jit(solution)/shard_map/ppermute | solution.py:529
  229.7 0.8 copy-start.9
  230.5 18.9 %collective-permute-start.16 = (f32[32,32,128]{2,1,0:T(8,128)}, f32[32,32,128]{2,1,0:T(8,128)S(1)}, u32[]{:S(2)}, u32[]{:S(2)}) collective-permute-start(f32[32,32,128]{2,1,0:T(8,128)} %get-tuple-element.35), channel_id=1, source_target_pairs={{0,8},{8,0},{16,24},{24,16},{1,9},{9,1},{17,25},{25,17},{2,10},{10... | collective-permute-start | bytes 1572872 | tf_op jit(solution)/shard_map/ppermute | solution.py:529
  231.4 31.1 %collective-permute-start.17 = (f32[32,32,128]{2,1,0:T(8,128)}, f32[32,32,128]{2,1,0:T(8,128)S(1)}, u32[]{:S(2)}, u32[]{:S(2)}) collective-permute-start(f32[32,32,128]{2,1,0:T(8,128)} %get-tuple-element.36), channel_id=1, source_target_pairs={{0,16},{8,24},{16,0},{24,8},{1,17},{9,25},{17,1},{25,9},{2,18},{10... | collective-permute-start | bytes 1572872 | tf_op jit(solution)/shard_map/ppermute | solution.py:529
  231.9 39.7 %collective-permute-start.18 = (f32[32,32,128]{2,1,0:T(8,128)}, f32[32,32,128]{2,1,0:T(8,128)}, u32[]{:S(2)}, u32[]{:S(2)}) collective-permute-start(f32[32,32,128]{2,1,0:T(8,128)} %get-tuple-element.37), channel_id=1, source_target_pairs={{0,24},{8,16},{16,8},{24,0},{1,25},{9,17},{17,9},{25,1},{2,26},{10... | collective-permute-start | bytes 1572872 | tf_op jit(solution)/shard_map/ppermute | solution.py:529
  271.6 1.0 copy-start.10

commit v3 on v2

--- a/solution.py
+++ b/solution.py
@@ -168,32 +168,29 @@
 
 
 def step_kernel(
-    *refs, rotate, hold, channels_total, fibres_in, fibres_out, slots
+    *refs, rotate, apart, channels_total, fibres_in, fibres_out, slots
 ):
     refs = list(refs)
     x_ref = refs.pop(0)
     if rotate:
         q_ref, selin_ref, strength_ref = refs[:3]
         refs = refs[3:]
-    selout_ref, fc_ref, fs_ref, tw_ref, wf_ref, wi_ref, u_ref, p_ref = refs[:8]
-    refs = refs[8:]
-    rest_ref = refs.pop(0) if hold else None
+    selout_ref, fc_ref, fs_ref, tw_ref, wf_ref, wi_ref, u_ref = refs[:7]
+    refs = refs[7:]
+    u_refs = [u_ref, refs.pop(0)] if apart else [u_ref]
+    p_ref = refs.pop(0)
     xs_ref = refs.pop(0) if rotate else x_ref
     a_ref, z_ref = refs
     chunks = x_ref.shape[0]
-    held = xs_ref.shape[2]
-    groups = held // SUB
-    half = slots // SUB
+    groups = 2 * slots // SUB
+    half = groups // 2
 
     if rotate:
 
         def turn(tt, carry):
             def write(real, imag):
-                xs_ref[tt, 0] = real[:held]
-                xs_ref[tt, 1] = imag[:held]
-                if hold:
-                    rest_ref[tt, 0] = real[held:]
-                    rest_ref[tt, 1] = imag[held:]
+                xs_ref[tt, 0] = real
+                xs_ref[tt, 1] = imag
 
             rotate_chunk(
                 x_ref, q_ref, selin_ref, strength_ref[...], tt, channels_total, fibres_in, slots,
@@ -241,7 +238,9 @@
                     split_store(a_ref, base, part * FB, value)
         z_ref[...] = jnp.dot(a_ref[...], wi_ref[...], preferred_element_type=jnp.float32)
         for g in range(groups):
-            rows = slice(g * SUB, (g + 1) * SUB)
+            to_ref = u_refs[g // half] if apart else u_ref
+            place = g % half if apart else g
+            rows = slice(place * SUB, (place + 1) * SUB)
             z = []
             for k in range(FA):
                 at = (g * FA + k) * SUB
@@ -252,14 +251,19 @@
                 z.append((real, imag))
             y = dft16(z, 1, keep=(1, 2))
             for k in range(STEP):
-                u_ref[j * STEP + k, 0, rows, :] = y[LEAD + k][0]
-                u_ref[j * STEP + k, 1, rows, :] = y[LEAD + k][1]
+                to_ref[j * STEP + k, 0, rows, :] = y[LEAD + k][0]
+                to_ref[j * STEP + k, 1, rows, :] = y[LEAD + k][1]
         for k in range(STEP):
             tt = j * STEP + k
-            real, imag = u_ref[tt, 0], u_ref[tt, 1]
-            power = real * real + imag * imag
-            if held > slots:
-                power = power[:slots] + power[slots:]
+            power = None
+            for p in range(2):
+                if apart:
+                    real, imag = u_refs[p][tt, 0], u_refs[p][tt, 1]
+                else:
+                    rows = slice(p * slots, (p + 1) * slots)
+                    real, imag = u_ref[tt, 0, rows, :], u_ref[tt, 1, rows, :]
+                mine = real * real + imag * imag
+                power = mine if power is None else power + mine
             for f in range(fibres_out):
                 mine = power if fibres_out == 1 else power * selout_ref[f]
                 p_ref[f, pl.ds(tt, 1), :] = jnp.sum(mine, axis=0, keepdims=True)
@@ -352,6 +356,10 @@
     return pltpu.CompilerParams(vmem_limit_bytes=VMEM_BYTES)
 
 
+def cost(flops, moved):
+    return pl.CostEstimate(flops=int(flops), bytes_accessed=int(moved), transcendentals=0)
+
+
 def in_vmem():
     return pl.BlockSpec(memory_space=pltpu.VMEM)
 
@@ -397,17 +405,16 @@
     return source_item.astype(jnp.int32), counts, take_from.astype(jnp.int32)
 
 
-def local_total(values, times, my_time, wave_rounds):
-    bit = times // 2
-    while bit:
-        halves = values.reshape(values.shape[0], 2, -1, FB)
-        high = (my_time // bit) % 2
-        keep = lax.dynamic_index_in_dim(halves, high, 1, keepdims=False)
-        give = lax.dynamic_index_in_dim(halves, 1 - high, 1, keepdims=False)
-        pairs = [(i, i ^ bit) for i in range(times)]
-        values = keep + lax.ppermute(give, "tm", pairs)
-        bit //= 2
-    return summed(values, wave_rounds)
+def time_halves(values, bits):
+    times = lax.axis_size("tm")
+    count = times.bit_length() - 1
+    for b in bits:
+        side = (lax.axis_index("tm") >> b) & 1
+        dim = count - b
+        keep = lax.dynamic_index_in_dim(values, side, dim)
+        give = lax.dynamic_index_in_dim(values, 1 - side, dim)
+        values = keep + lax.ppermute(give, "tm", [(i, i ^ (1 << b)) for i in range(times)])
+    return values
 
 
 def local(field, lit_count, route_fibre, route_slot, dispersion, nonlinearity):
@@ -472,25 +479,24 @@
 
     twist = jnp.asarray(twist_table())
     forward, inverse = (jnp.asarray(table) for table in matrix_tables())
-    def dispersed(x, step, total, q_fibres, fibres_out, hold):
+    def dispersed(x, step, total, q_fibres, fibres_out, part):
         fc, fs, _, select = spans[step // HALF]
         rotate = total is not None
         operands = [x]
         if rotate:
             operands += [total, spans[(step - 1) // HALF][3], spans[(step - 1) // HALF][2]]
         operands += [select, fc, fs, twist, forward, inverse]
-        held = slots if hold else x.shape[2]
-        part = jax.ShapeDtypeStruct((chunks, 2, held, FB), jnp.float32)
-        outs = [part, jax.ShapeDtypeStruct((fibres_out, chunks, FB), jnp.float32)]
-        outs += [part] if hold else []
-        scratch = [pltpu.VMEM(part.shape, jnp.float32)] if rotate else []
+        shape = (chunks, 2, slots if part else rows, FB)
+        outs = [jax.ShapeDtypeStruct(shape, jnp.float32)] * (2 if part else 1)
+        outs += [jax.ShapeDtypeStruct((fibres_out, chunks, FB), jnp.float32)]
+        scratch = [pltpu.VMEM(x.shape, jnp.float32)] if rotate else []
         scratch += [
-            pltpu.VMEM((FA * held, 6 * FB), jnp.bfloat16),
-            pltpu.VMEM((FA * held, 2 * FB), jnp.float32),
+            pltpu.VMEM((FA * rows, 6 * FB), jnp.bfloat16),
+            pltpu.VMEM((FA * rows, 2 * FB), jnp.float32),
         ]
         return pl.pallas_call(
             functools.partial(
-                step_kernel, rotate=rotate, hold=hold, channels_total=channels_total,
+                step_kernel, rotate=rotate, apart=part, channels_total=channels_total,
                 fibres_in=q_fibres, fibres_out=fibres_out, slots=slots,
             ),
             out_shape=tuple(outs),
@@ -498,6 +504,7 @@
             out_specs=tuple([in_vmem()] * len(outs)),
             scratch_shapes=scratch,
             compiler_params=params(),
+            cost_estimate=cost(chunks * rows * FB * 6400, 4 * x.size * 4),
             name="step",
         )(*operands)
 
@@ -514,27 +521,34 @@
         values = values.reshape(times, 2 * near * slots, FB)
         return lax.all_to_all(values, "tm", split_axis=0, concat_axis=0, tiled=True)
 
-    def to_groups(values):
+    def prepared(values):
         block = jax.ShapeDtypeStruct((capacity, BLK * 2 * near, FB), jnp.float32)
-        outgoing = pl.pallas_call(
+        return pl.pallas_call(
             functools.partial(send_kernel, units=units, slots=slots),
             out_shape=(block,) * groups,
             in_specs=[in_smem(), in_smem(), in_vmem()],
             out_specs=(in_vmem(),) * groups,
             compiler_params=params(),
+            cost_estimate=cost(0, 4 * 4 * values.size),
             name="send",
         )(source_item, counts, values)
+
+    def to_groups(outgoing):
         moved = [outgoing[0]]
         for s in range(1, groups):
             moved.append(lax.ppermute(outgoing[s], "wave", [(i, i ^ s) for i in range(groups)]))
         return moved
 
-    first, partial, rest = dispersed(wave_form, last, total, q_fibres, fibres, True)
-    first = to_times(first)
-    second, more = dispersed(rest, last, None, 0, fibres, False)
-    second = to_times(second)
-    own_total = local_total(partial + more, times, my_time, wave_rounds)
-    blocks = to_groups(first) + to_groups(second)
+    first, second, partial = dispersed(wave_form, last, total, q_fibres, fibres, True)
+    bits = list(range(times.bit_length() - 1))
+    partial = summed(partial, wave_rounds).reshape([fibres] + [2] * len(bits) + [near, FB])
+    first, partial = lax.optimization_barrier((to_times(first), partial))
+    first = prepared(first)
+    first, second = lax.optimization_barrier((first, second))
+    partial = time_halves(partial, bits[:1] + bits[2:])
+    second, partial, *first = lax.optimization_barrier((to_times(second), partial, *to_groups(first)))
+    blocks = first + to_groups(prepared(second))
+    own_total = time_halves(partial, bits[1:2]).reshape(fibres, near, FB)
     strength = jnp.broadcast_to(nonlinearity[1][:, None, None], (fibres, near, FB))
     placed = pl.pallas_call(
         functools.partial(place_kernel, channels_total=channels_total, sources=groups),
@@ -547,6 +561,7 @@
             pltpu.SemaphoreType.DMA((2, groups)),
         ],
         compiler_params=params(),
+        cost_estimate=cost(0, 4 * 4 * field.size),
         name="place",
     )(take_from, strength, own_total, *blocks)
     result = placed.reshape(fibres, channels, 2, near, 2, FB).transpose(0, 1, 2, 4, 3, 5)

time: 279 us -> 255 us (0.914)
  waiting for transfers between devices: 160 us -> 136 us
  starting transfers between devices: 34 us -> 37.1 us
    ppermute x6, waiting for transfers between devices: 38.3 us -> 21 us  [to_groups(): lax.ppermute(outgoing[s], 'wave', [(i, i ^ s) for i in range(groups)])]
    all_to_all x2, waiting for transfers between devices: 22.2 us -> 15.1 us  [to_times(): return lax.all_to_all(values, 'tm', split_axis=0, concat_axis=0, tiled=True)]
    ppermute x3, waiting for transfers between devices: 26.6 us -> 20.4 us  [time_halves(): lax.ppermute(give, 'tm', [(i, i ^ 1 << b) for i in range(times)])]
    ppermute x13, waiting for transfers between devices: 30.8 us -> 35.4 us  [summed(): values = values + lax.ppermute(values, axis, pairs)]
    pallas_call x7 -> x6, Pallas kernels: 55 us -> 51.9 us  [the longest x4 45.2 us: dispersed(): pl.pallas_call(functools.partial(step_kernel, rotate=rotate, apart=part,...]
    unnamed x36 -> x38, local copies, waits for them, and re-layouts: 9.27 us -> 11.9 us
  transfers between devices with their start and end apart: 25 -> 25, of which waited for: 20 -> 21; matrix products, arithmetic and copies ran while one was open for 3% -> 2% of each run, Pallas kernels for 0% -> 0%
where the time goes in v3:
time: 255 us; the launch traced here: 254 us
  waiting for transfers between devices  136 us (53%)
  Pallas kernels  61.1 us (24%)
  starting transfers between devices  37.1 us (15%)
  local copies, waits for them, and re-layouts  16.7 us (7%)
  other arithmetic  2.74 us (1%)
    pallas_call x4, Pallas kernels, dispersed(): pl.pallas_call(functools.partial(step_kernel, rotate=rotate, apart=part,...  45.2 us
    all_to_all x1, waiting for transfers between devices, local(): lax.all_to_all(packed, 'tm', split_axis=0, concat_axis=0, tiled=True)  44.3 us
    ppermute x13, waiting for transfers between devices, summed(): values = values + lax.ppermute(values, axis, pairs)  35.4 us
    ppermute x6, waiting for transfers between devices, to_groups(): lax.ppermute(outgoing[s], 'wave', [(i, i ^ s) for i in range(groups)])  21 us
    ppermute x3, waiting for transfers between devices, time_halves(): lax.ppermute(give, 'tm', [(i, i ^ 1 << b) for i in range(times)])  20.4 us
    all_to_all x2, waiting for transfers between devices, to_times(): return lax.all_to_all(values, 'tm', split_axis=0, concat_axis=0, tiled=True)  15.1 us
    unnamed x38, local copies, waits for them, and re-layouts  11.9 us
    ppermute x13, starting transfers between devices, summed(): values = values + lax.ppermute(values, axis, pairs)  11.8 us
  transfers between devices with their start and end apart: 25, of which 21 were waited for; matrix products, arithmetic and copies ran while one was open for 2% of the time, Pallas kernels for 0%

profile of v3, /device:TPU:0, one launch (start us, length us, event | category | flops | bytes accessed | tf_op | source)
XLA Modules:
  0.0 254.2 jit_solution(1799774765113407023)
XLA Ops:
  0.8 1.6 copy-done
  2.4 3.6 %pack.1 = f32[8,512,128]{2,1,0:T(8,128)} custom-call(s32[128]{0:T(128)S(1)} %reshape.486.lit_ref, f32[4096,128]{1,0:T(8,128)S(1)} %bitcast.42), custom_call_target="tpu_custom_call" | custom-call | tf_op jit(solution)/shard_map/pack/pallas_call | solution.py:469
  6.0 7.4 %all-to-all-start = ((f32[8,512,128]{2,1,0:T(8,128)}), f32[8,512,128]{2,1,0:T(8,128)S(1)}, u32[]{:S(2)}, u32[]{:S(2)}) async-start(f32[8,512,128]{2,1,0:T(8,128)} %pack.1), calls=%async_computation | async-start | bytes 4194304 | tf_op jit(solution)/shard_map/all_to_all | solution.py:477
  17.4 44.3 %all-to-all-done = f32[8,512,128]{2,1,0:T(8,128)S(1)} async-done(((f32[8,512,128]{2,1,0:T(8,128)}), f32[8,512,128]{2,1,0:T(8,128)S(1)}, u32[]{:S(2)}, u32[]{:S(2)}) %all-to-all-start) | async-done | bytes 2097184 | tf_op jit(solution)/shard_map/all_to_all | solution.py:477
  62.6 9.3 %step.4 = (f32[64,2,32,128]{3,2,1,0:T(8,128)S(1)}, f32[1,64,128]{2,1,0:T(8,128)S(1)}) custom-call(f32[64,2,32,128]{3,2,1,0:T(8,128)S(1)} %bitcast.43, f32[4,16,128]{2,1,0:T(8,128)S(1)} %broadcast_in_dim.34.refs_1_.refs_2_.refs_4_, f32[16,16,128]{2,1,0:T(8,128)S(1)} %get-tuple-element.71.refs_2_.refs_5_, ...), custom_call_target="tpu_custom_call" | custom-call | flops 1677721600 | bytes 8388608 | tf_op jit(solution)/shard_map/step/pallas_call | solution.py:497
  71.9 1.3 copy-done.11
  73.2 1.2 collective-permute-done
  74.4 1.5 collective-permute-start.1
  76.0 2.4 collective-permute-done.1
  78.4 1.5 collective-permute-start.2
  80.5 1.8 collective-permute-done.2
  83.3 1.6 copy-done.12
  84.9 11.3 %step.5 = (f32[64,2,32,128]{3,2,1,0:T(8,128)S(1)}, f32[1,64,128]{2,1,0:T(8,128)S(1)}) custom-call(f32[64,2,32,128]{3,2,1,0:T(8,128)S(1)} %copy-done.12, f32[1,64,128]{2,1,0:T(8,128)S(1)} %add.334.refs_1_, f32[4,16,128]{2,1,0:T(8,128)S(1)} %broadcast_in_dim.34.refs_1_.refs_2_.refs_4_, f32[16,128]{1,0:T(8,128)S(1)} %broadcast_in_dim.35.refs_3_, ...), custom_call_target="tpu_custom_call" | custom-call | flops 1677721600 | bytes 8388608 | tf_op jit(solution)/shard_map/step/pallas_call | solution.py:497
  96.3 1.2 collective-permute-done.3
  97.5 1.5 collective-permute-start.4
  99.0 2.4 collective-permute-done.4
  101.4 1.5 collective-permute-start.5
  102.9 2.5 collective-permute-done.5
  105.4 11.6 %step.6 = (f32[64,2,32,128]{3,2,1,0:T(8,128)S(1)}, f32[4,64,128]{2,1,0:T(8,128)S(1)}) custom-call(f32[64,2,32,128]{3,2,1,0:T(8,128)S(1)} %get-tuple-element.37.refs_0_, f32[1,64,128]{2,1,0:T(8,128)S(1)} %add.337.refs_1_, f32[4,16,128]{2,1,0:T(8,128)S(1)} %broadcast_in_dim.34.refs_1_.refs_2_.refs_4_, f32[16,128]{1,0:T(8,128)S(1)} %broadcast_in_dim.35.refs_3_, ...), custom_call_target="tpu_custom_call" | custom-call | flops 1677721600 | bytes 8388608 | tf_op jit(solution)/shard_map/step/pallas_call | solution.py:497
  117.0 1.3 copy-done.9
  118.3 1.3 collective-permute-done.6
  119.7 1.6 collective-permute-start.7
  121.3 4.0 %collective-permute-done.7 = f32[4,64,128]{2,1,0:T(8,128)S(1)} collective-permute-done((f32[4,64,128]{2,1,0:T(8,128)S(1)}, f32[4,64,128]{2,1,0:T(8,128)S(1)}, u32[]{:S(2)}, u32[]{:S(2)}) %collective-permute-start.7) | collective-permute-done | bytes 131104 | tf_op jit(solution)/shard_map/ppermute | solution.py:374
  125.3 1.5 collective-permute-start.8
  126.9 3.5 %collective-permute-done.8 = f32[4,64,128]{2,1,0:T(8,128)S(1)} collective-permute-done((f32[4,64,128]{2,1,0:T(8,128)S(1)}, f32[4,64,128]{2,1,0:T(8,128)S(1)}, u32[]{:S(2)}, u32[]{:S(2)}) %collective-permute-start.8) | collective-permute-done | bytes 131104 | tf_op jit(solution)/shard_map/ppermute | solution.py:374
  130.5 5.0 %collective-permute-done.9 = f32[4,64,128]{2,1,0:T(8,128)S(1)} collective-permute-done((f32[4,64,128]{2,1,0:T(8,128)S(1)}, f32[4,64,128]{2,1,0:T(8,128)S(1)}, u32[]{:S(2)}, u32[]{:S(2)}) %collective-permute-start.9) | collective-permute-done | bytes 131104 | tf_op jit(solution)/shard_map/ppermute | solution.py:374
  137.0 5.2 %collective-permute-done.10 = f32[4,64,128]{2,1,0:T(8,128)S(1)} collective-permute-done((f32[4,64,128]{2,1,0:T(8,128)S(1)}, f32[4,64,128]{2,1,0:T(8,128)S(1)}, u32[]{:S(2)}, u32[]{:S(2)}) %collective-permute-start.10) | collective-permute-done | bytes 131104 | tf_op jit(solution)/shard_map/ppermute | solution.py:374
  142.3 1.6 copy-done.10
  143.9 13.0 %step.7 = (f32[64,2,16,128]{3,2,1,0:T(8,128)}, f32[64,2,16,128]{3,2,1,0:T(8,128)}, f32[4,64,128]{2,1,0:T(8,128)S(1)}) custom-call(f32[64,2,32,128]{3,2,1,0:T(8,128)S(1)} %copy-done.10, f32[4,64,128]{2,1,0:T(8,128)S(1)} %add.351.refs_1_, f32[4,16,128]{2,1,0:T(8,128)S(1)} %broadcast_in_dim.36.refs_4_.refs_2_, f32[16,128]{1,0:T(8,128)S(1)} %broadcast_in_dim.37.refs_3_, ...), custom_call_target="tpu_custom_call" | custom-call | flops 1677721600 | bytes 8388608 | tf_op jit(solution)/shard_map/step/pallas_call | solution.py:497
  156.9 3.6 %all-to-all-start.1 = ((f32[8,256,128]{2,1,0:T(8,128)}), f32[8,256,128]{2,1,0:T(8,128)S(1)}, u32[]{:S(2)}, u32[]{:S(2)}) async-start(f32[8,256,128]{2,1,0:T(8,128)} %bitcast.16), calls=%async_computation.1 | async-start | bytes 2097152 | tf_op jit(solution)/shard_map/all_to_all | solution.py:522
  162.2 1.6 collective-permute-start.12
  164.0 3.8 %collective-permute-done.12 = f32[4,64,128]{2,1,0:T(8,128)S(1)} collective-permute-done((f32[4,64,128]{2,1,0:T(8,128)S(1)}, f32[4,64,128]{2,1,0:T(8,128)S(1)}, u32[]{:S(2)}, u32[]{:S(2)}) %collective-permute-start.12) | collective-permute-done | bytes 131104 | tf_op jit(solution)/shard_map/ppermute | solution.py:374
  167.8 15.1 %all-to-all-done.1.x_ref = f32[8,256,128]{2,1,0:T(8,128)S(1)} async-done(((f32[8,256,128]{2,1,0:T(8,128)}), f32[8,256,128]{2,1,0:T(8,128)S(1)}, u32[]{:S(2)}, u32[]{:S(2)}) %all-to-all-start.1) | async-done | bytes 1048608 | tf_op jit(solution)/shard_map/all_to_all | solution.py:522
  183.0 3.3 %send.2 = (f32[32,32,128]{2,1,0:T(8,128)S(1)}, f32[32,32,128]{2,1,0:T(8,128)}, f32[32,32,128]{2,1,0:T(8,128)}, f32[32,32,128]{2,1,0:T(8,128)S(1)}) custom-call(s32[128]{0:T(128)S(1)} %select_reduce_fusion.1.item_ref, s32[4]{0:T(128)S(1)} %convert_reduce_fusion.1.count_ref, f32[8,256,128]{2,1,0:T(8,128)S(1)} %all-to-all-done.1.x_ref), custom_call_target="tpu_custom_call" | custom-call | bytes 4194304 | tf_op jit(solution)/shard_map/send/pallas_call | solution.py:526
  187.0 3.6 %all-to-all-start.2 = ((f32[8,256,128]{2,1,0:T(8,128)}), f32[8,256,128]{2,1,0:T(8,128)S(1)}, u32[]{:S(2)}, u32[]{:S(2)}) async-start(f32[8,256,128]{2,1,0:T(8,128)} %bitcast.18), calls=%async_computation.2 | async-start | bytes 2097152 | tf_op jit(solution)/shard_map/all_to_all | solution.py:522
  190.6 2.0 collective-permute-start.13
  192.6 1.5 collective-permute-start.16
  194.5 4.8 %collective-permute-done.13 = f32[4,2,2,1,8,128]{5,4,0,3,2,1:T(8,128)S(1)} collective-permute-done((f32[4,2,2,1,8,128]{5,4,0,3,2,1:T(8,128)S(1)}, f32[4,2,2,1,8,128]{5,4,0,3,2,1:T(8,128)S(1)}, u32[]{:S(2)}, u32[]{:S(2)}) %collective-permute-start.13) | collective-permute-done | bytes 65568 | tf_op jit(solution)/shard_map/ppermute | solution.py:416
  199.3 3.6 %collective-permute-start.14 = (f32[4,1,2,1,8,128]{5,4,0,3,2,1:T(8,128)S(1)}, f32[4,1,2,1,8,128]{5,4,0,3,2,1:T(8,128)S(1)}, u32[]{:S(2)}, u32[]{:S(2)}) collective-permute-start(f32[4,1,2,1,8,128]{5,4,0,3,2,1:T(8,128)S(1)} %constant_dynamic-slice_fusion), channel_id=1, source_target_pairs={{0,4},{1,5},{2,6},{3,7},{4,0},{5,1},{6,2},{7,3},{8,12},{9,13},{10,... | collective-permute-start | bytes 98312 | tf_op jit(solution)/shard_map/ppermute | solution.py:416
  203.0 13.6 %collective-permute-done.14 = f32[4,1,2,1,8,128]{5,4,0,3,2,1:T(8,128)S(1)} collective-permute-done((f32[4,1,2,1,8,128]{5,4,0,3,2,1:T(8,128)S(1)}, f32[4,1,2,1,8,128]{5,4,0,3,2,1:T(8,128)S(1)}, u32[]{:S(2)}, u32[]{:S(2)}) %collective-permute-start.14) | collective-permute-done | bytes 32800 | tf_op jit(solution)/shard_map/ppermute | solution.py:416
  216.6 1.4 collective-permute-done.17.refs_3_
  218.0 3.5 %send.3 = (f32[32,32,128]{2,1,0:T(8,128)S(1)}, f32[32,32,128]{2,1,0:T(8,128)}, f32[32,32,128]{2,1,0:T(8,128)}, f32[32,32,128]{2,1,0:T(8,128)}) custom-call(s32[128]{0:T(128)S(1)} %select_reduce_fusion.1.item_ref, s32[4]{0:T(128)S(1)} %convert_reduce_fusion.1.count_ref, f32[8,256,128]{2,1,0:T(8,128)S(1)} %all-to-all-done.2.x_ref), custom_call_target="tpu_custom_call" | custom-call | bytes 4194304 | tf_op jit(solution)/shard_map/send/pallas_call | solution.py:526
  222.5 1.5 collective-permute-start.20
  224.2 1.5 collective-permute-start.18
  225.9 2.1 collective-permute-done.18
  228.0 9.5 %collective-permute-done.20.refs_6_ = f32[32,32,128]{2,1,0:T(8,128)S(1)} collective-permute-done((f32[32,32,128]{2,1,0:T(8,128)}, f32[32,32,128]{2,1,0:T(8,128)S(1)}, u32[]{:S(2)}, u32[]{:S(2)}) %collective-permute-start.20) | collective-permute-done | bytes 524320 | tf_op jit(solution)/shard_map/ppermute | solution.py:539
  237.4 10.1 %collective-permute-done.21.refs_7_ = f32[32,32,128]{2,1,0:T(8,128)} collective-permute-done((f32[32,32,128]{2,1,0:T(8,128)}, f32[32,32,128]{2,1,0:T(8,128)}, u32[]{:S(2)}, u32[]{:S(2)}) %collective-permute-start.21) | collective-permute-done | bytes 524320 | tf_op jit(solution)/shard_map/ppermute | solution.py:539
  248.7 5.5 %place.1 = f32[64,64,128]{2,1,0:T(8,128)} custom-call(s32[64]{0:T(128)S(1)} %select_reduce_fusion.from_ref, f32[4,8,128]{2,1,0:T(8,128)S(1)} %broadcast_in_dim.31.strength_ref, f32[4,8,128]{2,1,0:T(8,128)S(1)} %add_bitcast_fusion.q_ref, f32[32,32,128]{2,1,0:T(8,128)S(1)} %get-tuple-element.56.refs_0_, f32[32,32,128]{2,1,0:T(8,128)S(1)} %collective-permute-done.15.refs_1_, ...), custom_call_target="tpu_custom_call" | custom-call | bytes 8388608 | tf_op jit(solution)/shard_map/place/pallas_call | solution.py:553
  (108 shorter events, 15.0 us)
Async XLA Ops:
  0.8 1.6 copy-start
  6.0 7.5 %copy-start.14 = (s32[4,64]{1,0:T(4,128)S(1)}, s32[4,64]{1,0:T(4,128)}, u32[]{:S(2)}) copy-start(s32[4,64]{1,0:T(4,128)} %param.13) | copy-start | bytes 3076
  6.0 8.2 %copy-start.13 = (s32[4,64]{1,0:T(4,128)S(1)}, s32[4,64]{1,0:T(4,128)}, u32[]{:S(2)}) copy-start(s32[4,64]{1,0:T(4,128)} %param.14) | copy-start | bytes 3076
  6.0 8.9 %copy-start.17 = (f32[2,4]{1,0:T(2,128)S(1)}, f32[2,4]{1,0:T(2,128)}, u32[]{:S(2)}) copy-start(f32[2,4]{1,0:T(2,128)} %param.15) | copy-start | bytes 100
  6.0 55.6 %all-to-all-start = ((f32[8,512,128]{2,1,0:T(8,128)}), f32[8,512,128]{2,1,0:T(8,128)S(1)}, u32[]{:S(2)}, u32[]{:S(2)}) async-start(f32[8,512,128]{2,1,0:T(8,128)} %pack.1), calls=%async_computation | async-start | bytes 4194304 | tf_op jit(solution)/shard_map/all_to_all | solution.py:477
  13.4 2.9 %copy-start.15 = (f32[16,128]{1,0:T(8,128)S(1)}, f32[16,128]{1,0:T(8,128)}, u32[]{:S(2)}) copy-start(f32[16,128]{1,0:T(8,128)} %constant.159) | copy-start | bytes 24580
  13.4 2.9 %copy-start.16 = (f32[16,128]{1,0:T(8,128)S(1)}, f32[16,128]{1,0:T(8,128)}, u32[]{:S(2)}) copy-start(f32[16,128]{1,0:T(8,128)} %constant.158) | copy-start | bytes 24580
  13.4 48.3 %copy-start.4 = (bf16[768,256]{1,0:T(8,128)(2,1)S(1)}, bf16[768,256]{1,0:T(8,128)(2,1)}, u32[]{:S(2)}) copy-start(bf16[768,256]{1,0:T(8,128)(2,1)} %constant.155.clone.refs_6_.refs_9_) | copy-start | bytes 1179652
  13.4 48.3 %copy-start.5 = (bf16[768,256]{1,0:T(8,128)(2,1)S(1)}, bf16[768,256]{1,0:T(8,128)(2,1)}, u32[]{:S(2)}) copy-start(bf16[768,256]{1,0:T(8,128)(2,1)} %constant.154.clone.refs_5_.refs_8_) | copy-start | bytes 1179652
  61.7 0.9 copy-start.6
  62.6 17.2 %copy-start.18 = (f32[2,4]{1,0:T(2,128)S(1)}, f32[2,4]{1,0:T(2,128)}, u32[]{:S(2)}) copy-start(f32[2,4]{1,0:T(2,128)} %param.16) | copy-start | bytes 100
  71.9 1.3 copy-start.11
  73.2 1.2 collective-permute-start
  74.4 3.9 %collective-permute-start.1 = (f32[1,64,128]{2,1,0:T(8,128)S(1)}, f32[1,64,128]{2,1,0:T(8,128)S(1)}, u32[]{:S(2)}, u32[]{:S(2)}) collective-permute-start(f32[1,64,128]{2,1,0:T(8,128)S(1)} %add.332), channel_id=1, source_target_pairs={{0,16},{8,24},{16,0},{24,8},{1,17},{9,25},{17,1},{25,9},{2,18},{10... | collective-permute-start | bytes 98312 | tf_op jit(solution)/shard_map/ppermute | solution.py:374
  78.4 3.9 %collective-permute-start.2 = (f32[1,64,128]{2,1,0:T(8,128)S(1)}, f32[1,64,128]{2,1,0:T(8,128)S(1)}, u32[]{:S(2)}, u32[]{:S(2)}) collective-permute-start(f32[1,64,128]{2,1,0:T(8,128)S(1)} %add.333), channel_id=1, source_target_pairs={{0,1},{1,0},{2,3},{3,2},{4,5},{5,4},{6,7},{7,6},{8,9},{9,8},{10,11... | collective-permute-start | bytes 98312 | tf_op jit(solution)/shard_map/ppermute | solution.py:374
  82.4 0.9 copy-start.7
  83.3 1.6 copy-start.12
  96.2 1.3 collective-permute-start.3
  97.5 3.9 %collective-permute-start.4 = (f32[1,64,128]{2,1,0:T(8,128)S(1)}, f32[1,64,128]{2,1,0:T(8,128)S(1)}, u32[]{:S(2)}, u32[]{:S(2)}) collective-permute-start(f32[1,64,128]{2,1,0:T(8,128)S(1)} %add.335), channel_id=1, source_target_pairs={{0,16},{8,24},{16,0},{24,8},{1,17},{9,25},{17,1},{25,9},{2,18},{10... | collective-permute-start | bytes 98312 | tf_op jit(solution)/shard_map/ppermute | solution.py:374
  101.4 3.9 %collective-permute-start.5 = (f32[1,64,128]{2,1,0:T(8,128)S(1)}, f32[1,64,128]{2,1,0:T(8,128)S(1)}, u32[]{:S(2)}, u32[]{:S(2)}) collective-permute-start(f32[1,64,128]{2,1,0:T(8,128)S(1)} %add.336), channel_id=1, source_target_pairs={{0,1},{1,0},{2,3},{3,2},{4,5},{5,4},{6,7},{7,6},{8,9},{9,8},{10,11... | collective-permute-start | bytes 98312 | tf_op jit(solution)/shard_map/ppermute | solution.py:374
  117.0 1.3 copy-start.9
  118.3 24.0 %copy-start.8 = (f32[2,16,8,128]{3,2,1,0:T(8,128)S(1)}, f32[2,16,8,128]{3,2,1,0:T(8,128)}, u32[]{:S(2)}) copy-start(f32[2,16,8,128]{3,2,1,0:T(8,128)} %constant.153.clone.refs_4_.refs_7_) | copy-start | bytes 393220
  118.3 1.3 collective-permute-start.6
  119.7 5.6 %collective-permute-start.7 = (f32[4,64,128]{2,1,0:T(8,128)S(1)}, f32[4,64,128]{2,1,0:T(8,128)S(1)}, u32[]{:S(2)}, u32[]{:S(2)}) collective-permute-start(f32[4,64,128]{2,1,0:T(8,128)S(1)} %add.347), channel_id=1, source_target_pairs={{0,16},{8,24},{16,0},{24,8},{1,17},{9,25},{17,1},{25,9},{2,18},{10... | collective-permute-start | bytes 393224 | tf_op jit(solution)/shard_map/ppermute | solution.py:374
  125.3 5.0 %collective-permute-start.8 = (f32[4,64,128]{2,1,0:T(8,128)S(1)}, f32[4,64,128]{2,1,0:T(8,128)S(1)}, u32[]{:S(2)}, u32[]{:S(2)}) collective-permute-start(f32[4,64,128]{2,1,0:T(8,128)S(1)} %add.348), channel_id=1, source_target_pairs={{0,1},{1,0},{2,3},{3,2},{4,5},{5,4},{6,7},{7,6},{8,9},{9,8},{10,11... | collective-permute-start | bytes 393224 | tf_op jit(solution)/shard_map/ppermute | solution.py:374
  130.4 5.0 %collective-permute-start.9 = (f32[4,64,128]{2,1,0:T(8,128)S(1)}, f32[4,64,128]{2,1,0:T(8,128)S(1)}, u32[]{:S(2)}, u32[]{:S(2)}) collective-permute-start(f32[4,64,128]{2,1,0:T(8,128)S(1)} %add.349), channel_id=1, source_target_pairs={{0,2},{1,3},{2,0},{3,1},{4,6},{5,7},{6,4},{7,5},{8,10},{9,11},{10,... | collective-permute-start | bytes 393224 | tf_op jit(solution)/shard_map/ppermute | solution.py:374
  135.4 6.8 %collective-permute-start.10 = (f32[4,64,128]{2,1,0:T(8,128)S(1)}, f32[4,64,128]{2,1,0:T(8,128)S(1)}, u32[]{:S(2)}, u32[]{:S(2)}) collective-permute-start(f32[4,64,128]{2,1,0:T(8,128)S(1)} %add.350), channel_id=1, source_target_pairs={{0,4},{1,5},{2,6},{3,7},{4,0},{5,1},{6,2},{7,3},{8,12},{9,13},{10,... | collective-permute-start | bytes 393224 | tf_op jit(solution)/shard_map/ppermute | solution.py:374
  142.3 1.6 copy-start.10
  156.9 26.0 %all-to-all-start.1 = ((f32[8,256,128]{2,1,0:T(8,128)}), f32[8,256,128]{2,1,0:T(8,128)S(1)}, u32[]{:S(2)}, u32[]{:S(2)}) async-start(f32[8,256,128]{2,1,0:T(8,128)} %bitcast.16), calls=%async_computation.1 | async-start | bytes 2097152 | tf_op jit(solution)/shard_map/all_to_all | solution.py:522
  160.8 1.4 collective-permute-start.11
  162.2 5.6 %collective-permute-start.12 = (f32[4,64,128]{2,1,0:T(8,128)S(1)}, f32[4,64,128]{2,1,0:T(8,128)S(1)}, u32[]{:S(2)}, u32[]{:S(2)}) collective-permute-start(f32[4,64,128]{2,1,0:T(8,128)S(1)} %add.352), channel_id=1, source_target_pairs={{0,16},{8,24},{16,0},{24,8},{1,17},{9,25},{17,1},{25,9},{2,18},{10... | collective-permute-start | bytes 393224 | tf_op jit(solution)/shard_map/ppermute | solution.py:374
  186.2 0.8 copy-start.3
  187.0 31.0 %all-to-all-start.2 = ((f32[8,256,128]{2,1,0:T(8,128)}), f32[8,256,128]{2,1,0:T(8,128)S(1)}, u32[]{:S(2)}, u32[]{:S(2)}) async-start(f32[8,256,128]{2,1,0:T(8,128)} %bitcast.18), calls=%async_computation.2 | async-start | bytes 2097152 | tf_op jit(solution)/shard_map/all_to_all | solution.py:522
  190.6 8.6 %collective-permute-start.13 = (f32[4,2,2,1,8,128]{5,4,0,3,2,1:T(8,128)S(1)}, f32[4,2,2,1,8,128]{5,4,0,3,2,1:T(8,128)S(1)}, u32[]{:S(2)}, u32[]{:S(2)}) collective-permute-start(f32[4,2,2,1,8,128]{5,4,0,3,2,1:T(8,128)S(1)} %constant_dynamic-slice_fusion.1), channel_id=1, source_target_pairs={{0,1},{1,0},{2,3},{3,2},{4,5},{5,4},{6,7},{7,6},{8,9},{9,8},{10,11... | collective-permute-start | bytes 196616 | tf_op jit(solution)/shard_map/ppermute | solution.py:416
  192.6 24.0 %collective-permute-start.15 = (f32[32,32,128]{2,1,0:T(8,128)}, f32[32,32,128]{2,1,0:T(8,128)S(1)}, u32[]{:S(2)}, u32[]{:S(2)}) collective-permute-start(f32[32,32,128]{2,1,0:T(8,128)} %get-tuple-element.52), channel_id=1, source_target_pairs={{0,8},{8,0},{16,24},{24,16},{1,9},{9,1},{17,25},{25,17},{2,10},{10... | collective-permute-start | bytes 1572872 | tf_op jit(solution)/shard_map/ppermute | solution.py:539
  192.6 24.0 %collective-permute-start.16 = (f32[32,32,128]{2,1,0:T(8,128)}, f32[32,32,128]{2,1,0:T(8,128)S(1)}, u32[]{:S(2)}, u32[]{:S(2)}) collective-permute-start(f32[32,32,128]{2,1,0:T(8,128)} %get-tuple-element.53), channel_id=1, source_target_pairs={{0,16},{8,24},{16,0},{24,8},{1,17},{9,25},{17,1},{25,9},{2,18},{10... | collective-permute-start | bytes 1572872 | tf_op jit(solution)/shard_map/ppermute | solution.py:539
  194.1 23.9 %collective-permute-start.17 = (f32[32,32,128]{2,1,0:T(8,128)}, f32[32,32,128]{2,1,0:T(8,128)S(1)}, u32[]{:S(2)}, u32[]{:S(2)}) collective-permute-start(f32[32,32,128]{2,1,0:T(8,128)} %copy-done.3), channel_id=1, source_target_pairs={{0,24},{8,16},{16,8},{24,0},{1,25},{9,17},{17,9},{25,1},{2,26},{10... | collective-permute-start | bytes 1572872 | tf_op jit(solution)/shard_map/ppermute | solution.py:539
  199.3 17.3 %collective-permute-start.14 = (f32[4,1,2,1,8,128]{5,4,0,3,2,1:T(8,128)S(1)}, f32[4,1,2,1,8,128]{5,4,0,3,2,1:T(8,128)S(1)}, u32[]{:S(2)}, u32[]{:S(2)}) collective-permute-start(f32[4,1,2,1,8,128]{5,4,0,3,2,1:T(8,128)S(1)} %constant_dynamic-slice_fusion), channel_id=1, source_target_pairs={{0,4},{1,5},{2,6},{3,7},{4,0},{5,1},{6,2},{7,3},{8,12},{9,13},{10,... | collective-permute-start | bytes 98312 | tf_op jit(solution)/shard_map/ppermute | solution.py:416
  221.5 0.8 copy-start.1
  222.3 5.7 %collective-permute-start.19 = (f32[32,32,128]{2,1,0:T(8,128)}, f32[32,32,128]{2,1,0:T(8,128)S(1)}, u32[]{:S(2)}, u32[]{:S(2)}) collective-permute-start(f32[32,32,128]{2,1,0:T(8,128)} %get-tuple-element.62), channel_id=1, source_target_pairs={{0,8},{8,0},{16,24},{24,16},{1,9},{9,1},{17,25},{25,17},{2,10},{10... | collective-permute-start | bytes 1572872 | tf_op jit(solution)/shard_map/ppermute | solution.py:539
  222.5 15.0 %collective-permute-start.20 = (f32[32,32,128]{2,1,0:T(8,128)}, f32[32,32,128]{2,1,0:T(8,128)S(1)}, u32[]{:S(2)}, u32[]{:S(2)}) collective-permute-start(f32[32,32,128]{2,1,0:T(8,128)} %get-tuple-element.63), channel_id=1, source_target_pairs={{0,16},{8,24},{16,0},{24,8},{1,17},{9,25},{17,1},{25,9},{2,18},{10... | collective-permute-start | bytes 1572872 | tf_op jit(solution)/shard_map/ppermute | solution.py:539
  224.0 23.5 %collective-permute-start.21 = (f32[32,32,128]{2,1,0:T(8,128)}, f32[32,32,128]{2,1,0:T(8,128)}, u32[]{:S(2)}, u32[]{:S(2)}) collective-permute-start(f32[32,32,128]{2,1,0:T(8,128)} %get-tuple-element.64), channel_id=1, source_target_pairs={{0,24},{8,16},{16,8},{24,0},{1,25},{9,17},{17,9},{25,1},{2,26},{10... | collective-permute-start | bytes 1572872 | tf_op jit(solution)/shard_map/ppermute | solution.py:539
  224.2 3.8 %collective-permute-start.18 = (f32[4,1,1,1,8,128]{5,4,0,3,2,1:T(8,128)S(1)}, f32[4,1,1,1,8,128]{5,4,0,3,2,1:T(8,128)S(1)}, u32[]{:S(2)}, u32[]{:S(2)}) collective-permute-start(f32[4,1,1,1,8,128]{5,4,0,3,2,1:T(8,128)S(1)} %constant_dynamic-slice_fusion.4), channel_id=1, source_target_pairs={{0,2},{1,3},{2,0},{3,1},{4,6},{5,7},{6,4},{7,5},{8,10},{9,11},{10,... | collective-permute-start | bytes 49160 | tf_op jit(solution)/shard_map/ppermute | solution.py:416
  247.6 1.0 copy-start.2

commit v4 on v3

--- a/solution.py
+++ b/solution.py
@@ -19,6 +19,8 @@
 LEAD = MARGIN // FB
 STEP = VALID // FB
 SUB = 8
+UNROLL = 4
+LAG = 1
 VMEM_BYTES = 40 * 1024 * 1024
 
 
@@ -37,7 +39,7 @@
     tables = []
     for matrix in (forward, inverse):
         high, low = split_bf16(matrix)
-        tables.append(np.concatenate([high, low, high], axis=0))
+        tables.append(np.concatenate([high, low], axis=0))
     return tables
 
 
@@ -163,8 +165,7 @@
     low = (value - high.astype(jnp.float32)).astype(jnp.bfloat16)
     rows = value.shape[0]
     a_ref[base : base + rows, column : column + FB] = high
-    a_ref[base : base + rows, 2 * FB + column : 3 * FB + column] = high
-    a_ref[base : base + rows, 4 * FB + column : 5 * FB + column] = low
+    a_ref[base : base + rows, 2 * FB + column : 3 * FB + column] = low
 
 
 def step_kernel(
@@ -180,7 +181,7 @@
     u_refs = [u_ref, refs.pop(0)] if apart else [u_ref]
     p_ref = refs.pop(0)
     xs_ref = refs.pop(0) if rotate else x_ref
-    a_ref, z_ref = refs
+    lanes = refs
     chunks = x_ref.shape[0]
     groups = 2 * slots // SUB
     half = groups // 2
@@ -198,61 +199,57 @@
             )
             return carry
 
-        lax.fori_loop(0, chunks, turn, 0)
-
-    def block(j, carry):
+        lax.fori_loop(0, chunks, turn, 0, unroll=STEP)
+
+    def gather(j, a_ref, g):
         places = []
         for a in range(FA):
             at = j * STEP + (a - LEAD)
             at = jnp.where(at < 0, at + chunks, at)
             places.append(jnp.where(at >= chunks, at - chunks, at))
-        for g in range(groups):
-            rows = slice(g * SUB, (g + 1) * SUB)
-            z = [(xs_ref[at, 0, rows, :], xs_ref[at, 1, rows, :]) for at in places]
-            y = dft16(z, -1)
-            for i in range(FA // 2):
-                pair = []
-                for k in (2 * i, 2 * i + 1):
-                    real, imag = y[k]
-                    if k:
-                        c, s = tw_ref[0, k], tw_ref[1, k]
-                        real, imag = real * c + imag * s, imag * c - real * s
-                    pair.append((real, imag))
-                base = (g * FA + 2 * i) * SUB
-                for part in range(2):
-                    value = jnp.concatenate([pair[0][part], pair[1][part]], axis=0)
-                    split_store(a_ref, base, part * FB, value)
-        z_ref[...] = jnp.dot(a_ref[...], wf_ref[...], preferred_element_type=jnp.float32)
-        for g in range(groups):
-            rows = slice((g % half) * SUB, (g % half + 1) * SUB)
-            for i in range(FA // 2):
-                pair = []
-                for k in (2 * i, 2 * i + 1):
-                    at = (g * FA + k) * SUB
-                    real, imag = z_ref[at : at + SUB, :FB], z_ref[at : at + SUB, FB:]
-                    c, s = fc_ref[k, rows, :], fs_ref[k, rows, :]
-                    pair.append((real * c - imag * s, real * s + imag * c))
-                base = (g * FA + 2 * i) * SUB
-                for part in range(2):
-                    value = jnp.concatenate([pair[0][part], pair[1][part]], axis=0)
-                    split_store(a_ref, base, part * FB, value)
-        z_ref[...] = jnp.dot(a_ref[...], wi_ref[...], preferred_element_type=jnp.float32)
-        for g in range(groups):
-            to_ref = u_refs[g // half] if apart else u_ref
-            place = g % half if apart else g
-            rows = slice(place * SUB, (place + 1) * SUB)
-            z = []
-            for k in range(FA):
+        rows = slice(g * SUB, (g + 1) * SUB)
+        z = [(xs_ref[at, 0, rows, :], xs_ref[at, 1, rows, :]) for at in places]
+        y = dft16(z, -1)
+        for i in range(FA // 2):
+            pair = []
+            for k in (2 * i, 2 * i + 1):
+                real, imag = y[k]
+                if k:
+                    c, s = tw_ref[0, k], tw_ref[1, k]
+                    real, imag = real * c + imag * s, imag * c - real * s
+                pair.append((real, imag))
+            store_pair(a_ref, (g * FA + 2 * i) * SUB, pair)
+
+    def shape(a_ref, z_ref, g):
+        rows = slice((g % half) * SUB, (g % half + 1) * SUB)
+        for i in range(FA // 2):
+            pair = []
+            for k in (2 * i, 2 * i + 1):
                 at = (g * FA + k) * SUB
                 real, imag = z_ref[at : at + SUB, :FB], z_ref[at : at + SUB, FB:]
-                if k:
-                    c, s = tw_ref[0, k], tw_ref[1, k]
-                    real, imag = real * c - imag * s, real * s + imag * c
-                z.append((real, imag))
-            y = dft16(z, 1, keep=(1, 2))
-            for k in range(STEP):
-                to_ref[j * STEP + k, 0, rows, :] = y[LEAD + k][0]
-                to_ref[j * STEP + k, 1, rows, :] = y[LEAD + k][1]
+                c, s = fc_ref[k, rows, :], fs_ref[k, rows, :]
+                pair.append((real * c - imag * s, real * s + imag * c))
+            store_pair(a_ref, (g * FA + 2 * i) * SUB, pair)
+
+    def spread(j, z_ref, g):
+        to_ref = u_refs[g // half] if apart else u_ref
+        place = g % half if apart else g
+        rows = slice(place * SUB, (place + 1) * SUB)
+        z = []
+        for k in range(FA):
+            at = (g * FA + k) * SUB
+            real, imag = z_ref[at : at + SUB, :FB], z_ref[at : at + SUB, FB:]
+            if k:
+                c, s = tw_ref[0, k], tw_ref[1, k]
+                real, imag = real * c - imag * s, real * s + imag * c
+            z.append((real, imag))
+        y = dft16(z, 1, keep=(1, 2))
+        for k in range(STEP):
+            real, imag = y[LEAD + k]
+            to_ref[j * STEP + k, 0, rows, :] = real
+            to_ref[j * STEP + k, 1, rows, :] = imag
+
+    def add_up(j):
         for k in range(STEP):
             tt = j * STEP + k
             power = None
@@ -267,9 +264,66 @@
             for f in range(fibres_out):
                 mine = power if fibres_out == 1 else power * selout_ref[f]
                 p_ref[f, pl.ds(tt, 1), :] = jnp.sum(mine, axis=0, keepdims=True)
+
+    count = len(lanes) // 4
+    size = FA * SUB
+
+    def blocks(n, carry):
+        stage = [lanes[4 * i : 4 * i + 4] for i in range(count)]
+
+        def times(a_ref, w_ref, z_ref, g):
+            at = slice(g * size, (g + 1) * size)
+            z_ref[at, :] = product(a_ref[at, :], w_ref)
+
+        units = [(i, g) for i in range(count) for g in range(groups)]
+
+        def unit(turn, stages_back):
+            at = turn - stages_back * LAG
+            return units[at] if 0 <= at < len(units) else None
+
+        for turn in range(len(units) + 4 * LAG):
+            if now := unit(turn, 4):
+                i, g = now
+                spread(n * count + i, stage[i][3], g)
+                if g == groups - 1:
+                    add_up(n * count + i)
+            if now := unit(turn, 3):
+                i, g = now
+                times(stage[i][2], wi_ref, stage[i][3], g)
+            if now := unit(turn, 2):
+                i, g = now
+                shape(stage[i][2], stage[i][1], g)
+            if now := unit(turn, 1):
+                i, g = now
+                times(stage[i][0], wf_ref, stage[i][1], g)
+            if now := unit(turn, 0):
+                i, g = now
+                gather(n * count + i, stage[i][0], g)
         return carry
 
-    lax.fori_loop(0, chunks // STEP, block, 0)
+    lax.fori_loop(0, chunks // STEP // count, blocks, 0)
+
+
+def product(operand, w_ref):
+    width = 2 * FB
+    high, low = operand[:, :width], operand[:, width:]
+    matrix_high, matrix_low = w_ref[:width, :], w_ref[width:, :]
+    return (
+        jnp.dot(high, matrix_high, preferred_element_type=jnp.float32)
+        + jnp.dot(high, matrix_low, preferred_element_type=jnp.float32)
+        + jnp.dot(low, matrix_high, preferred_element_type=jnp.float32)
+    )
+
+
+def store_pair(a_ref, base, pair):
+    for part in range(2):
+        split_store(a_ref, base, part * FB, jnp.concatenate([pair[0][part], pair[1][part]], axis=0))
+
+
+def step_scratch(rows, count):
+    operand = pltpu.VMEM((FA * rows, 4 * FB), jnp.bfloat16)
+    product = pltpu.VMEM((FA * rows, 2 * FB), jnp.float32)
+    return [operand, product, operand, product] * count
 
 
 def pack_kernel(lit_ref, x_ref, o_ref, *, units, slots):
@@ -349,7 +403,7 @@
                     o_ref[n, pl.ds(at + 1, near, stride=2), :] = real * sine + imag * cosine
             return carry
 
-        lax.fori_loop(0, group_blocks, body, 0)
+        lax.fori_loop(0, group_blocks, body, 0, unroll=4)
 
 
 def params():
@@ -490,10 +544,7 @@
         outs = [jax.ShapeDtypeStruct(shape, jnp.float32)] * (2 if part else 1)
         outs += [jax.ShapeDtypeStruct((fibres_out, chunks, FB), jnp.float32)]
         scratch = [pltpu.VMEM(x.shape, jnp.float32)] if rotate else []
-        scratch += [
-            pltpu.VMEM((FA * rows, 6 * FB), jnp.bfloat16),
-            pltpu.VMEM((FA * rows, 2 * FB), jnp.float32),
-        ]
+        scratch += step_scratch(rows, math.gcd(UNROLL, chunks // STEP))
         return pl.pallas_call(
             functools.partial(
                 step_kernel, rotate=rotate, apart=part, channels_total=channels_total,

time: 255 us -> 231 us (0.906)
  Pallas kernels: 61.1 us -> 42 us
  local copies, waits for them, and re-layouts: 16.7 us -> 12 us
    pallas_call x4, Pallas kernels: 45.2 us -> 27.2 us  [dispersed(): pl.pallas_call(functools.partial(step_kernel, rotate=rotate, apart=part,...]
    unnamed x38 -> x30, local copies, waits for them, and re-layouts: 11.9 us -> 7.18 us
  transfers between devices with their start and end apart: 25 -> 25, of which waited for: 21 -> 21; matrix products, arithmetic and copies ran while one was open for 2% -> 3% of each run, Pallas kernels for 0% -> 0%
where the time goes in v4:
time: 231 us
  waiting for transfers between devices  136 us (59%)
  Pallas kernels  42 us (18%)
  starting transfers between devices  37.2 us (16%)
  local copies, waits for them, and re-layouts  12 us (5%)
  other arithmetic  2.76 us (1%)
    all_to_all x1, waiting for transfers between devices, local(): lax.all_to_all(packed, 'tm', split_axis=0, concat_axis=0, tiled=True)  44.2 us
    ppermute x13, waiting for transfers between devices, summed(): values = values + lax.ppermute(values, axis, pairs)  35.4 us
    pallas_call x4, Pallas kernels, dispersed(): pl.pallas_call(functools.partial(step_kernel, rotate=rotate, apart=part,...  27.2 us
    ppermute x6, waiting for transfers between devices, to_groups(): lax.ppermute(outgoing[s], 'wave', [(i, i ^ s) for i in range(groups)])  21 us
    ppermute x3, waiting for transfers between devices, time_halves(): lax.ppermute(give, 'tm', [(i, i ^ 1 << b) for i in range(times)])  20.4 us
    all_to_all x2, waiting for transfers between devices, to_times(): return lax.all_to_all(values, 'tm', split_axis=0, concat_axis=0, tiled=True)  15.1 us
    ppermute x13, starting transfers between devices, summed(): values = values + lax.ppermute(values, axis, pairs)  11.8 us
    all_to_all x1, starting transfers between devices, local(): lax.all_to_all(packed, 'tm', split_axis=0, concat_axis=0, tiled=True)  7.38 us
  transfers between devices with their start and end apart: 25, of which 21 were waited for; matrix products, arithmetic and copies ran while one was open for 3% of the time, Pallas kernels for 0%

profile of v4, /device:TPU:0, one launch (start us, length us, event | category | flops | bytes accessed | tf_op | source)
XLA Modules:
  0.0 230.6 jit_solution(14050879894119063405)
XLA Ops:
  0.8 1.6 copy-done
  2.4 3.6 %pack.1 = f32[8,512,128]{2,1,0:T(8,128)} custom-call(s32[128]{0:T(128)S(1)} %reshape.486.lit_ref, f32[4096,128]{1,0:T(8,128)S(1)} %bitcast.42), custom_call_target="tpu_custom_call" | custom-call | tf_op jit(solution)/shard_map/pack/pallas_call | solution.py:523
  6.0 7.4 %all-to-all-start = ((f32[8,512,128]{2,1,0:T(8,128)}), f32[8,512,128]{2,1,0:T(8,128)S(1)}, u32[]{:S(2)}, u32[]{:S(2)}) async-start(f32[8,512,128]{2,1,0:T(8,128)} %pack.1), calls=%async_computation | async-start | bytes 4194304 | tf_op jit(solution)/shard_map/all_to_all | solution.py:531
  17.4 44.2 %all-to-all-done = f32[8,512,128]{2,1,0:T(8,128)S(1)} async-done(((f32[8,512,128]{2,1,0:T(8,128)}), f32[8,512,128]{2,1,0:T(8,128)S(1)}, u32[]{:S(2)}, u32[]{:S(2)}) %all-to-all-start) | async-done | bytes 2097184 | tf_op jit(solution)/shard_map/all_to_all | solution.py:531
  61.8 5.5 %step.4 = (f32[64,2,32,128]{3,2,1,0:T(8,128)S(1)}, f32[1,64,128]{2,1,0:T(8,128)S(1)}) custom-call(f32[64,2,32,128]{3,2,1,0:T(8,128)S(1)} %bitcast.43, f32[4,16,128]{2,1,0:T(8,128)S(1)} %broadcast_in_dim.34.refs_1_.refs_2_.refs_4_, f32[16,16,128]{2,1,0:T(8,128)S(1)} %get-tuple-element.71.refs_2_.refs_5_, ...), custom_call_target="tpu_custom_call" | custom-call | flops 1677721600 | bytes 8388608 | tf_op jit(solution)/shard_map/step/pallas_call | solution.py:548
  67.2 1.3 copy-done.7
  68.6 1.2 collective-permute-done
  69.8 1.5 collective-permute-start.1
  71.3 2.4 %collective-permute-done.1 = f32[1,64,128]{2,1,0:T(8,128)S(1)} collective-permute-done((f32[1,64,128]{2,1,0:T(8,128)S(1)}, f32[1,64,128]{2,1,0:T(8,128)S(1)}, u32[]{:S(2)}, u32[]{:S(2)}) %collective-permute-start.1) | collective-permute-done | bytes 32800 | tf_op jit(solution)/shard_map/ppermute | solution.py:428
  73.7 1.5 collective-permute-start.2
  75.8 1.8 collective-permute-done.2
  77.7 1.6 copy-done.8
  79.3 6.6 %step.5 = (f32[64,2,32,128]{3,2,1,0:T(8,128)S(1)}, f32[1,64,128]{2,1,0:T(8,128)S(1)}) custom-call(f32[64,2,32,128]{3,2,1,0:T(8,128)S(1)} %copy-done.8, f32[1,64,128]{2,1,0:T(8,128)S(1)} %add.334.refs_1_, f32[4,16,128]{2,1,0:T(8,128)S(1)} %broadcast_in_dim.34.refs_1_.refs_2_.refs_4_, f32[16,128]{1,0:T(8,128)S(1)} %broadcast_in_dim.35.refs_3_, ...), custom_call_target="tpu_custom_call" | custom-call | flops 1677721600 | bytes 8388608 | tf_op jit(solution)/shard_map/step/pallas_call | solution.py:548
  86.0 1.2 collective-permute-done.3
  87.2 1.5 collective-permute-start.4
  88.7 2.4 %collective-permute-done.4 = f32[1,64,128]{2,1,0:T(8,128)S(1)} collective-permute-done((f32[1,64,128]{2,1,0:T(8,128)S(1)}, f32[1,64,128]{2,1,0:T(8,128)S(1)}, u32[]{:S(2)}, u32[]{:S(2)}) %collective-permute-start.4) | collective-permute-done | bytes 32800 | tf_op jit(solution)/shard_map/ppermute | solution.py:428
  91.1 1.5 collective-permute-start.5
  92.6 2.5 %collective-permute-done.5 = f32[1,64,128]{2,1,0:T(8,128)S(1)} collective-permute-done((f32[1,64,128]{2,1,0:T(8,128)S(1)}, f32[1,64,128]{2,1,0:T(8,128)S(1)}, u32[]{:S(2)}, u32[]{:S(2)}) %collective-permute-start.5) | collective-permute-done | bytes 32800 | tf_op jit(solution)/shard_map/ppermute | solution.py:428
  95.1 6.8 %step.6 = (f32[64,2,32,128]{3,2,1,0:T(8,128)S(1)}, f32[4,64,128]{2,1,0:T(8,128)S(1)}) custom-call(f32[64,2,32,128]{3,2,1,0:T(8,128)S(1)} %get-tuple-element.37.refs_0_, f32[1,64,128]{2,1,0:T(8,128)S(1)} %add.337.refs_1_, f32[4,16,128]{2,1,0:T(8,128)S(1)} %broadcast_in_dim.34.refs_1_.refs_2_.refs_4_, f32[16,128]{1,0:T(8,128)S(1)} %broadcast_in_dim.35.refs_3_, ...), custom_call_target="tpu_custom_call" | custom-call | flops 1677721600 | bytes 8388608 | tf_op jit(solution)/shard_map/step/pallas_call | solution.py:548
  102.0 1.3 collective-permute-done.6
  103.4 1.6 collective-permute-start.7
  105.0 4.0 %collective-permute-done.7 = f32[4,64,128]{2,1,0:T(8,128)S(1)} collective-permute-done((f32[4,64,128]{2,1,0:T(8,128)S(1)}, f32[4,64,128]{2,1,0:T(8,128)S(1)}, u32[]{:S(2)}, u32[]{:S(2)}) %collective-permute-start.7) | collective-permute-done | bytes 131104 | tf_op jit(solution)/shard_map/ppermute | solution.py:428
  109.0 1.5 collective-permute-start.8
  110.5 3.5 %collective-permute-done.8 = f32[4,64,128]{2,1,0:T(8,128)S(1)} collective-permute-done((f32[4,64,128]{2,1,0:T(8,128)S(1)}, f32[4,64,128]{2,1,0:T(8,128)S(1)}, u32[]{:S(2)}, u32[]{:S(2)}) %collective-permute-start.8) | collective-permute-done | bytes 131104 | tf_op jit(solution)/shard_map/ppermute | solution.py:428
  114.1 5.0 %collective-permute-done.9 = f32[4,64,128]{2,1,0:T(8,128)S(1)} collective-permute-done((f32[4,64,128]{2,1,0:T(8,128)S(1)}, f32[4,64,128]{2,1,0:T(8,128)S(1)}, u32[]{:S(2)}, u32[]{:S(2)}) %collective-permute-start.9) | collective-permute-done | bytes 131104 | tf_op jit(solution)/shard_map/ppermute | solution.py:428
  120.7 5.2 %collective-permute-done.10 = f32[4,64,128]{2,1,0:T(8,128)S(1)} collective-permute-done((f32[4,64,128]{2,1,0:T(8,128)S(1)}, f32[4,64,128]{2,1,0:T(8,128)S(1)}, u32[]{:S(2)}, u32[]{:S(2)}) %collective-permute-start.10) | collective-permute-done | bytes 131104 | tf_op jit(solution)/shard_map/ppermute | solution.py:428
  126.0 8.3 %step.7 = (f32[64,2,16,128]{3,2,1,0:T(8,128)}, f32[64,2,16,128]{3,2,1,0:T(8,128)}, f32[4,64,128]{2,1,0:T(8,128)S(1)}) custom-call(f32[64,2,32,128]{3,2,1,0:T(8,128)S(1)} %get-tuple-element.39.refs_0_, f32[4,64,128]{2,1,0:T(8,128)S(1)} %add.351.refs_1_, f32[4,16,128]{2,1,0:T(8,128)S(1)} %broadcast_in_dim.36.refs_4_.refs_2_, ...), custom_call_target="tpu_custom_call" | custom-call | flops 1677721600 | bytes 8388608 | tf_op jit(solution)/shard_map/step/pallas_call | solution.py:548
  134.2 3.6 %all-to-all-start.1 = ((f32[8,256,128]{2,1,0:T(8,128)}), f32[8,256,128]{2,1,0:T(8,128)S(1)}, u32[]{:S(2)}, u32[]{:S(2)}) async-start(f32[8,256,128]{2,1,0:T(8,128)} %bitcast.16), calls=%async_computation.1 | async-start | bytes 2097152 | tf_op jit(solution)/shard_map/all_to_all | solution.py:573
  138.4 1.1 collective-permute-done.11
  139.5 1.6 collective-permute-start.12
  141.3 3.8 %collective-permute-done.12 = f32[4,64,128]{2,1,0:T(8,128)S(1)} collective-permute-done((f32[4,64,128]{2,1,0:T(8,128)S(1)}, f32[4,64,128]{2,1,0:T(8,128)S(1)}, u32[]{:S(2)}, u32[]{:S(2)}) %collective-permute-start.12) | collective-permute-done | bytes 131104 | tf_op jit(solution)/shard_map/ppermute | solution.py:428
  145.2 15.1 %all-to-all-done.1.x_ref = f32[8,256,128]{2,1,0:T(8,128)S(1)} async-done(((f32[8,256,128]{2,1,0:T(8,128)}), f32[8,256,128]{2,1,0:T(8,128)S(1)}, u32[]{:S(2)}, u32[]{:S(2)}) %all-to-all-start.1) | async-done | bytes 1048608 | tf_op jit(solution)/shard_map/all_to_all | solution.py:573
  160.3 3.2 %send.2 = (f32[32,32,128]{2,1,0:T(8,128)S(1)}, f32[32,32,128]{2,1,0:T(8,128)}, f32[32,32,128]{2,1,0:T(8,128)}, f32[32,32,128]{2,1,0:T(8,128)S(1)}) custom-call(s32[128]{0:T(128)S(1)} %select_reduce_fusion.1.item_ref, s32[4]{0:T(128)S(1)} %convert_reduce_fusion.1.count_ref, f32[8,256,128]{2,1,0:T(8,128)S(1)} %all-to-all-done.1.x_ref), custom_call_target="tpu_custom_call" | custom-call | bytes 4194304 | tf_op jit(solution)/shard_map/send/pallas_call | solution.py:577
  164.3 3.6 %all-to-all-start.2 = ((f32[8,256,128]{2,1,0:T(8,128)}), f32[8,256,128]{2,1,0:T(8,128)S(1)}, u32[]{:S(2)}, u32[]{:S(2)}) async-start(f32[8,256,128]{2,1,0:T(8,128)} %bitcast.18), calls=%async_computation.2 | async-start | bytes 2097152 | tf_op jit(solution)/shard_map/all_to_all | solution.py:573
  167.9 2.0 collective-permute-start.13
  169.9 1.5 collective-permute-start.16
  171.8 4.8 %collective-permute-done.13 = f32[4,2,2,1,8,128]{5,4,0,3,2,1:T(8,128)S(1)} collective-permute-done((f32[4,2,2,1,8,128]{5,4,0,3,2,1:T(8,128)S(1)}, f32[4,2,2,1,8,128]{5,4,0,3,2,1:T(8,128)S(1)}, u32[]{:S(2)}, u32[]{:S(2)}) %collective-permute-start.13) | collective-permute-done | bytes 65568 | tf_op jit(solution)/shard_map/ppermute | solution.py:470
  176.5 3.6 %collective-permute-start.14 = (f32[4,1,2,1,8,128]{5,4,0,3,2,1:T(8,128)S(1)}, f32[4,1,2,1,8,128]{5,4,0,3,2,1:T(8,128)S(1)}, u32[]{:S(2)}, u32[]{:S(2)}) collective-permute-start(f32[4,1,2,1,8,128]{5,4,0,3,2,1:T(8,128)S(1)} %constant_dynamic-slice_fusion), channel_id=1, source_target_pairs={{0,4},{1,5},{2,6},{3,7},{4,0},{5,1},{6,2},{7,3},{8,12},{9,13},{10,... | collective-permute-start | bytes 98312 | tf_op jit(solution)/shard_map/ppermute | solution.py:470
  180.3 13.6 %collective-permute-done.14 = f32[4,1,2,1,8,128]{5,4,0,3,2,1:T(8,128)S(1)} collective-permute-done((f32[4,1,2,1,8,128]{5,4,0,3,2,1:T(8,128)S(1)}, f32[4,1,2,1,8,128]{5,4,0,3,2,1:T(8,128)S(1)}, u32[]{:S(2)}, u32[]{:S(2)}) %collective-permute-start.14) | collective-permute-done | bytes 32800 | tf_op jit(solution)/shard_map/ppermute | solution.py:470
  193.9 1.4 collective-permute-done.17.refs_3_
  195.3 3.5 %send.3 = (f32[32,32,128]{2,1,0:T(8,128)S(1)}, f32[32,32,128]{2,1,0:T(8,128)}, f32[32,32,128]{2,1,0:T(8,128)}, f32[32,32,128]{2,1,0:T(8,128)}) custom-call(s32[128]{0:T(128)S(1)} %select_reduce_fusion.1.item_ref, s32[4]{0:T(128)S(1)} %convert_reduce_fusion.1.count_ref, f32[8,256,128]{2,1,0:T(8,128)S(1)} %all-to-all-done.2.x_ref), custom_call_target="tpu_custom_call" | custom-call | bytes 4194304 | tf_op jit(solution)/shard_map/send/pallas_call | solution.py:577
  199.8 1.5 collective-permute-start.20
  201.5 1.5 collective-permute-start.18
  203.2 2.1 collective-permute-done.18
  205.3 9.5 %collective-permute-done.20.refs_6_ = f32[32,32,128]{2,1,0:T(8,128)S(1)} collective-permute-done((f32[32,32,128]{2,1,0:T(8,128)}, f32[32,32,128]{2,1,0:T(8,128)S(1)}, u32[]{:S(2)}, u32[]{:S(2)}) %collective-permute-start.20) | collective-permute-done | bytes 524320 | tf_op jit(solution)/shard_map/ppermute | solution.py:590
  214.7 10.1 %collective-permute-done.21.refs_7_ = f32[32,32,128]{2,1,0:T(8,128)} collective-permute-done((f32[32,32,128]{2,1,0:T(8,128)}, f32[32,32,128]{2,1,0:T(8,128)}, u32[]{:S(2)}, u32[]{:S(2)}) %collective-permute-start.21) | collective-permute-done | bytes 524320 | tf_op jit(solution)/shard_map/ppermute | solution.py:590
  224.9 1.0 copy-done.2
  225.9 4.5 %place.1 = f32[64,64,128]{2,1,0:T(8,128)} custom-call(s32[64]{0:T(128)S(1)} %select_reduce_fusion.from_ref, f32[4,8,128]{2,1,0:T(8,128)S(1)} %broadcast_in_dim.31.strength_ref, f32[4,8,128]{2,1,0:T(8,128)S(1)} %add_bitcast_fusion.q_ref, f32[32,32,128]{2,1,0:T(8,128)S(1)} %get-tuple-element.56.refs_0_, f32[32,32,128]{2,1,0:T(8,128)S(1)} %collective-permute-done.15.refs_1_, ...), custom_call_target="tpu_custom_call" | custom-call | bytes 8388608 | tf_op jit(solution)/shard_map/place/pallas_call | solution.py:604
  (100 shorter events, 11.1 us)
Async XLA Ops:
  0.8 1.6 copy-start
  6.0 7.5 %copy-start.10 = (s32[4,64]{1,0:T(4,128)S(1)}, s32[4,64]{1,0:T(4,128)}, u32[]{:S(2)}) copy-start(s32[4,64]{1,0:T(4,128)} %param.13) | copy-start | bytes 3076
  6.0 8.2 %copy-start.9 = (s32[4,64]{1,0:T(4,128)S(1)}, s32[4,64]{1,0:T(4,128)}, u32[]{:S(2)}) copy-start(s32[4,64]{1,0:T(4,128)} %param.14) | copy-start | bytes 3076
  6.0 8.9 %copy-start.13 = (f32[2,4]{1,0:T(2,128)S(1)}, f32[2,4]{1,0:T(2,128)}, u32[]{:S(2)}) copy-start(f32[2,4]{1,0:T(2,128)} %param.15) | copy-start | bytes 100
  6.0 55.6 %all-to-all-start = ((f32[8,512,128]{2,1,0:T(8,128)}), f32[8,512,128]{2,1,0:T(8,128)S(1)}, u32[]{:S(2)}, u32[]{:S(2)}) async-start(f32[8,512,128]{2,1,0:T(8,128)} %pack.1), calls=%async_computation | async-start | bytes 4194304 | tf_op jit(solution)/shard_map/all_to_all | solution.py:531
  13.4 2.9 %copy-start.11 = (f32[16,128]{1,0:T(8,128)S(1)}, f32[16,128]{1,0:T(8,128)}, u32[]{:S(2)}) copy-start(f32[16,128]{1,0:T(8,128)} %constant.159) | copy-start | bytes 24580
  13.4 3.0 %copy-start.12 = (f32[16,128]{1,0:T(8,128)S(1)}, f32[16,128]{1,0:T(8,128)}, u32[]{:S(2)}) copy-start(f32[16,128]{1,0:T(8,128)} %constant.158) | copy-start | bytes 24580
  13.4 48.3 %copy-start.4 = (bf16[512,256]{1,0:T(8,128)(2,1)S(1)}, bf16[512,256]{1,0:T(8,128)(2,1)}, u32[]{:S(2)}) copy-start(bf16[512,256]{1,0:T(8,128)(2,1)} %constant.155.clone.refs_6_.refs_9_) | copy-start | bytes 786436
  13.4 48.3 %copy-start.5 = (bf16[512,256]{1,0:T(8,128)(2,1)S(1)}, bf16[512,256]{1,0:T(8,128)(2,1)}, u32[]{:S(2)}) copy-start(bf16[512,256]{1,0:T(8,128)(2,1)} %constant.154.clone.refs_5_.refs_8_) | copy-start | bytes 786436
  13.5 48.3 %copy-start.6 = (f32[2,16,8,128]{3,2,1,0:T(8,128)S(1)}, f32[2,16,8,128]{3,2,1,0:T(8,128)}, u32[]{:S(2)}) copy-start(f32[2,16,8,128]{3,2,1,0:T(8,128)} %constant.153.clone.refs_4_.refs_7_) | copy-start | bytes 393220
  61.7 13.4 %copy-start.14 = (f32[2,4]{1,0:T(2,128)S(1)}, f32[2,4]{1,0:T(2,128)}, u32[]{:S(2)}) copy-start(f32[2,4]{1,0:T(2,128)} %param.16) | copy-start | bytes 100
  67.2 1.3 copy-start.7
  68.6 1.2 collective-permute-start
  69.8 3.9 %collective-permute-start.1 = (f32[1,64,128]{2,1,0:T(8,128)S(1)}, f32[1,64,128]{2,1,0:T(8,128)S(1)}, u32[]{:S(2)}, u32[]{:S(2)}) collective-permute-start(f32[1,64,128]{2,1,0:T(8,128)S(1)} %add.332), channel_id=1, source_target_pairs={{0,16},{8,24},{16,0},{24,8},{1,17},{9,25},{17,1},{25,9},{2,18},{10... | collective-permute-start | bytes 98312 | tf_op jit(solution)/shard_map/ppermute | solution.py:428
  73.7 3.9 %collective-permute-start.2 = (f32[1,64,128]{2,1,0:T(8,128)S(1)}, f32[1,64,128]{2,1,0:T(8,128)S(1)}, u32[]{:S(2)}, u32[]{:S(2)}) collective-permute-start(f32[1,64,128]{2,1,0:T(8,128)S(1)} %add.333), channel_id=1, source_target_pairs={{0,1},{1,0},{2,3},{3,2},{4,5},{5,4},{6,7},{7,6},{8,9},{9,8},{10,11... | collective-permute-start | bytes 98312 | tf_op jit(solution)/shard_map/ppermute | solution.py:428
  77.7 1.6 copy-start.8
  85.9 1.3 collective-permute-start.3
  87.2 3.9 %collective-permute-start.4 = (f32[1,64,128]{2,1,0:T(8,128)S(1)}, f32[1,64,128]{2,1,0:T(8,128)S(1)}, u32[]{:S(2)}, u32[]{:S(2)}) collective-permute-start(f32[1,64,128]{2,1,0:T(8,128)S(1)} %add.335), channel_id=1, source_target_pairs={{0,16},{8,24},{16,0},{24,8},{1,17},{9,25},{17,1},{25,9},{2,18},{10... | collective-permute-start | bytes 98312 | tf_op jit(solution)/shard_map/ppermute | solution.py:428
  91.1 3.9 %collective-permute-start.5 = (f32[1,64,128]{2,1,0:T(8,128)S(1)}, f32[1,64,128]{2,1,0:T(8,128)S(1)}, u32[]{:S(2)}, u32[]{:S(2)}) collective-permute-start(f32[1,64,128]{2,1,0:T(8,128)S(1)} %add.336), channel_id=1, source_target_pairs={{0,1},{1,0},{2,3},{3,2},{4,5},{5,4},{6,7},{7,6},{8,9},{9,8},{10,11... | collective-permute-start | bytes 98312 | tf_op jit(solution)/shard_map/ppermute | solution.py:428
  101.9 1.4 collective-permute-start.6
  103.4 5.6 %collective-permute-start.7 = (f32[4,64,128]{2,1,0:T(8,128)S(1)}, f32[4,64,128]{2,1,0:T(8,128)S(1)}, u32[]{:S(2)}, u32[]{:S(2)}) collective-permute-start(f32[4,64,128]{2,1,0:T(8,128)S(1)} %add.347), channel_id=1, source_target_pairs={{0,16},{8,24},{16,0},{24,8},{1,17},{9,25},{17,1},{25,9},{2,18},{10... | collective-permute-start | bytes 393224 | tf_op jit(solution)/shard_map/ppermute | solution.py:428
  109.0 5.0 %collective-permute-start.8 = (f32[4,64,128]{2,1,0:T(8,128)S(1)}, f32[4,64,128]{2,1,0:T(8,128)S(1)}, u32[]{:S(2)}, u32[]{:S(2)}) collective-permute-start(f32[4,64,128]{2,1,0:T(8,128)S(1)} %add.348), channel_id=1, source_target_pairs={{0,1},{1,0},{2,3},{3,2},{4,5},{5,4},{6,7},{7,6},{8,9},{9,8},{10,11... | collective-permute-start | bytes 393224 | tf_op jit(solution)/shard_map/ppermute | solution.py:428
  114.1 5.0 %collective-permute-start.9 = (f32[4,64,128]{2,1,0:T(8,128)S(1)}, f32[4,64,128]{2,1,0:T(8,128)S(1)}, u32[]{:S(2)}, u32[]{:S(2)}) collective-permute-start(f32[4,64,128]{2,1,0:T(8,128)S(1)} %add.349), channel_id=1, source_target_pairs={{0,2},{1,3},{2,0},{3,1},{4,6},{5,7},{6,4},{7,5},{8,10},{9,11},{10,... | collective-permute-start | bytes 393224 | tf_op jit(solution)/shard_map/ppermute | solution.py:428
  119.1 6.8 %collective-permute-start.10 = (f32[4,64,128]{2,1,0:T(8,128)S(1)}, f32[4,64,128]{2,1,0:T(8,128)S(1)}, u32[]{:S(2)}, u32[]{:S(2)}) collective-permute-start(f32[4,64,128]{2,1,0:T(8,128)S(1)} %add.350), channel_id=1, source_target_pairs={{0,4},{1,5},{2,6},{3,7},{4,0},{5,1},{6,2},{7,3},{8,12},{9,13},{10,... | collective-permute-start | bytes 393224 | tf_op jit(solution)/shard_map/ppermute | solution.py:428
  134.2 26.0 %all-to-all-start.1 = ((f32[8,256,128]{2,1,0:T(8,128)}), f32[8,256,128]{2,1,0:T(8,128)S(1)}, u32[]{:S(2)}, u32[]{:S(2)}) async-start(f32[8,256,128]{2,1,0:T(8,128)} %bitcast.16), calls=%async_computation.1 | async-start | bytes 2097152 | tf_op jit(solution)/shard_map/all_to_all | solution.py:573
  138.1 1.4 collective-permute-start.11
  139.5 5.6 %collective-permute-start.12 = (f32[4,64,128]{2,1,0:T(8,128)S(1)}, f32[4,64,128]{2,1,0:T(8,128)S(1)}, u32[]{:S(2)}, u32[]{:S(2)}) collective-permute-start(f32[4,64,128]{2,1,0:T(8,128)S(1)} %add.352), channel_id=1, source_target_pairs={{0,16},{8,24},{16,0},{24,8},{1,17},{9,25},{17,1},{25,9},{2,18},{10... | collective-permute-start | bytes 393224 | tf_op jit(solution)/shard_map/ppermute | solution.py:428
  163.5 0.8 copy-start.3
  164.3 31.0 %all-to-all-start.2 = ((f32[8,256,128]{2,1,0:T(8,128)}), f32[8,256,128]{2,1,0:T(8,128)S(1)}, u32[]{:S(2)}, u32[]{:S(2)}) async-start(f32[8,256,128]{2,1,0:T(8,128)} %bitcast.18), calls=%async_computation.2 | async-start | bytes 2097152 | tf_op jit(solution)/shard_map/all_to_all | solution.py:573
  167.9 8.6 %collective-permute-start.13 = (f32[4,2,2,1,8,128]{5,4,0,3,2,1:T(8,128)S(1)}, f32[4,2,2,1,8,128]{5,4,0,3,2,1:T(8,128)S(1)}, u32[]{:S(2)}, u32[]{:S(2)}) collective-permute-start(f32[4,2,2,1,8,128]{5,4,0,3,2,1:T(8,128)S(1)} %constant_dynamic-slice_fusion.1), channel_id=1, source_target_pairs={{0,1},{1,0},{2,3},{3,2},{4,5},{5,4},{6,7},{7,6},{8,9},{9,8},{10,11... | collective-permute-start | bytes 196616 | tf_op jit(solution)/shard_map/ppermute | solution.py:470
  169.9 24.0 %collective-permute-start.15 = (f32[32,32,128]{2,1,0:T(8,128)}, f32[32,32,128]{2,1,0:T(8,128)S(1)}, u32[]{:S(2)}, u32[]{:S(2)}) collective-permute-start(f32[32,32,128]{2,1,0:T(8,128)} %get-tuple-element.52), channel_id=1, source_target_pairs={{0,8},{8,0},{16,24},{24,16},{1,9},{9,1},{17,25},{25,17},{2,10},{10... | collective-permute-start | bytes 1572872 | tf_op jit(solution)/shard_map/ppermute | solution.py:590
  169.9 24.0 %collective-permute-start.16 = (f32[32,32,128]{2,1,0:T(8,128)}, f32[32,32,128]{2,1,0:T(8,128)S(1)}, u32[]{:S(2)}, u32[]{:S(2)}) collective-permute-start(f32[32,32,128]{2,1,0:T(8,128)} %get-tuple-element.53), channel_id=1, source_target_pairs={{0,16},{8,24},{16,0},{24,8},{1,17},{9,25},{17,1},{25,9},{2,18},{10... | collective-permute-start | bytes 1572872 | tf_op jit(solution)/shard_map/ppermute | solution.py:590
  171.4 23.9 %collective-permute-start.17 = (f32[32,32,128]{2,1,0:T(8,128)}, f32[32,32,128]{2,1,0:T(8,128)S(1)}, u32[]{:S(2)}, u32[]{:S(2)}) collective-permute-start(f32[32,32,128]{2,1,0:T(8,128)} %copy-done.3), channel_id=1, source_target_pairs={{0,24},{8,16},{16,8},{24,0},{1,25},{9,17},{17,9},{25,1},{2,26},{10... | collective-permute-start | bytes 1572872 | tf_op jit(solution)/shard_map/ppermute | solution.py:590
  176.5 17.3 %collective-permute-start.14 = (f32[4,1,2,1,8,128]{5,4,0,3,2,1:T(8,128)S(1)}, f32[4,1,2,1,8,128]{5,4,0,3,2,1:T(8,128)S(1)}, u32[]{:S(2)}, u32[]{:S(2)}) collective-permute-start(f32[4,1,2,1,8,128]{5,4,0,3,2,1:T(8,128)S(1)} %constant_dynamic-slice_fusion), channel_id=1, source_target_pairs={{0,4},{1,5},{2,6},{3,7},{4,0},{5,1},{6,2},{7,3},{8,12},{9,13},{10,... | collective-permute-start | bytes 98312 | tf_op jit(solution)/shard_map/ppermute | solution.py:470
  198.8 0.8 copy-start.1
  199.6 5.7 %collective-permute-start.19 = (f32[32,32,128]{2,1,0:T(8,128)}, f32[32,32,128]{2,1,0:T(8,128)S(1)}, u32[]{:S(2)}, u32[]{:S(2)}) collective-permute-start(f32[32,32,128]{2,1,0:T(8,128)} %get-tuple-element.62), channel_id=1, source_target_pairs={{0,8},{8,0},{16,24},{24,16},{1,9},{9,1},{17,25},{25,17},{2,10},{10... | collective-permute-start | bytes 1572872 | tf_op jit(solution)/shard_map/ppermute | solution.py:590
  199.8 15.0 %collective-permute-start.20 = (f32[32,32,128]{2,1,0:T(8,128)}, f32[32,32,128]{2,1,0:T(8,128)S(1)}, u32[]{:S(2)}, u32[]{:S(2)}) collective-permute-start(f32[32,32,128]{2,1,0:T(8,128)} %get-tuple-element.63), channel_id=1, source_target_pairs={{0,16},{8,24},{16,0},{24,8},{1,17},{9,25},{17,1},{25,9},{2,18},{10... | collective-permute-start | bytes 1572872 | tf_op jit(solution)/shard_map/ppermute | solution.py:590
  201.3 23.5 %collective-permute-start.21 = (f32[32,32,128]{2,1,0:T(8,128)}, f32[32,32,128]{2,1,0:T(8,128)}, u32[]{:S(2)}, u32[]{:S(2)}) collective-permute-start(f32[32,32,128]{2,1,0:T(8,128)} %get-tuple-element.64), channel_id=1, source_target_pairs={{0,24},{8,16},{16,8},{24,0},{1,25},{9,17},{17,9},{25,1},{2,26},{10... | collective-permute-start | bytes 1572872 | tf_op jit(solution)/shard_map/ppermute | solution.py:590
  201.5 3.8 %collective-permute-start.18 = (f32[4,1,1,1,8,128]{5,4,0,3,2,1:T(8,128)S(1)}, f32[4,1,1,1,8,128]{5,4,0,3,2,1:T(8,128)S(1)}, u32[]{:S(2)}, u32[]{:S(2)}) collective-permute-start(f32[4,1,1,1,8,128]{5,4,0,3,2,1:T(8,128)S(1)} %constant_dynamic-slice_fusion.4), channel_id=1, source_target_pairs={{0,2},{1,3},{2,0},{3,1},{4,6},{5,7},{6,4},{7,5},{8,10},{9,11},{10,... | collective-permute-start | bytes 49160 | tf_op jit(solution)/shard_map/ppermute | solution.py:470
  224.9 1.0 copy-start.2

commit v5 on v4

--- a/solution.py
+++ b/solution.py
@@ -21,7 +21,7 @@
 SUB = 8
 UNROLL = 4
 LAG = 1
-VMEM_BYTES = 40 * 1024 * 1024
+SPARE = 6 * 1024 * 1024
 
 
 def split_bf16(values):
@@ -169,29 +169,37 @@
 
 
 def step_kernel(
-    *refs, rotate, apart, channels_total, fibres_in, fibres_out, slots
+    *refs, rotate, hold, fetch, leave, channels_total, fibres_in, fibres_out, slots
 ):
     refs = list(refs)
     x_ref = refs.pop(0)
     if rotate:
         q_ref, selin_ref, strength_ref = refs[:3]
         refs = refs[3:]
-    selout_ref, fc_ref, fs_ref, tw_ref, wf_ref, wi_ref, u_ref = refs[:7]
+    selout_ref, fc_ref, fs_ref, tw_ref, wf_ref, wi_ref, u_out = refs[:7]
     refs = refs[7:]
-    u_refs = [u_ref, refs.pop(0)] if apart else [u_ref]
     p_ref = refs.pop(0)
+    rest_ref = refs.pop(0) if hold else None
     xs_ref = refs.pop(0) if rotate else x_ref
+    u_ref, out_sems = (refs.pop(0), refs.pop(0)) if leave else (u_out, None)
+    from_ref, in_sems = x_ref, None
+    if fetch:
+        x_ref, in_sems = refs.pop(0), refs.pop(0)
     lanes = refs
     chunks = x_ref.shape[0]
-    groups = 2 * slots // SUB
-    half = groups // 2
+    held = u_ref.shape[2]
+    groups = held // SUB
+    half = slots // SUB
 
     if rotate:
 
         def turn(tt, carry):
             def write(real, imag):
-                xs_ref[tt, 0] = real
-                xs_ref[tt, 1] = imag
+                xs_ref[tt, 0] = real[:held]
+                xs_ref[tt, 1] = imag[:held]
+                if hold:
+                    rest_ref[tt, 0] = real[held:]
+                    rest_ref[tt, 1] = imag[held:]
 
             rotate_chunk(
                 x_ref, q_ref, selin_ref, strength_ref[...], tt, channels_total, fibres_in, slots,
@@ -199,7 +207,21 @@
             )
             return carry
 
-        lax.fori_loop(0, chunks, turn, 0, unroll=STEP)
+        if fetch:
+            copies = []
+            pieces = in_sems.shape[0]
+            length = chunks // pieces
+            for i in range(pieces):
+                at = pl.ds(i * length, length)
+                copies.append(
+                    pltpu.make_async_copy(from_ref.at[at], x_ref.at[at], in_sems.at[i])
+                )
+                copies[-1].start()
+            for i, copy in enumerate(copies):
+                copy.wait()
+                lax.fori_loop(i * length, (i + 1) * length, turn, 0, unroll=STEP)
+        else:
+            lax.fori_loop(0, chunks, turn, 0, unroll=STEP)
 
     def gather(j, a_ref, g):
         places = []
@@ -232,9 +254,7 @@
             store_pair(a_ref, (g * FA + 2 * i) * SUB, pair)
 
     def spread(j, z_ref, g):
-        to_ref = u_refs[g // half] if apart else u_ref
-        place = g % half if apart else g
-        rows = slice(place * SUB, (place + 1) * SUB)
+        rows = slice(g * SUB, (g + 1) * SUB)
         z = []
         for k in range(FA):
             at = (g * FA + k) * SUB
@@ -246,19 +266,16 @@
         y = dft16(z, 1, keep=(1, 2))
         for k in range(STEP):
             real, imag = y[LEAD + k]
-            to_ref[j * STEP + k, 0, rows, :] = real
-            to_ref[j * STEP + k, 1, rows, :] = imag
+            u_ref[j * STEP + k, 0, rows, :] = real
+            u_ref[j * STEP + k, 1, rows, :] = imag
 
     def add_up(j):
         for k in range(STEP):
             tt = j * STEP + k
             power = None
-            for p in range(2):
-                if apart:
-                    real, imag = u_refs[p][tt, 0], u_refs[p][tt, 1]
-                else:
-                    rows = slice(p * slots, (p + 1) * slots)
-                    real, imag = u_ref[tt, 0, rows, :], u_ref[tt, 1, rows, :]
+            for p in range(held // slots):
+                rows = slice(p * slots, (p + 1) * slots)
+                real, imag = u_ref[tt, 0, rows, :], u_ref[tt, 1, rows, :]
                 mine = real * real + imag * imag
                 power = mine if power is None else power + mine
             for f in range(fibres_out):
@@ -301,7 +318,23 @@
                 gather(n * count + i, stage[i][0], g)
         return carry
 
-    lax.fori_loop(0, chunks // STEP // count, blocks, 0)
+    turns = chunks // STEP // count
+
+    def leaving(n):
+        at = pl.ds(n * count * STEP, count * STEP)
+        return pltpu.make_async_copy(u_ref.at[at], u_out.at[at], out_sems.at[n])
+
+    def blocks_out(n, carry):
+        blocks(n, carry)
+        leaving(n).start()
+        return carry
+
+    if leave:
+        lax.fori_loop(0, turns, blocks_out, 0)
+        for n in range(turns):
+            leaving(n).wait()
+    else:
+        lax.fori_loop(0, turns, blocks, 0)
 
 
 def product(operand, w_ref):
@@ -328,35 +361,47 @@
 
 def pack_kernel(lit_ref, x_ref, o_ref, *, units, slots):
     rows = 2 * slots
-    span = 2 * STEP
+    span = o_ref.shape[1] // rows
+    first = pl.program_id(0) * o_ref.shape[0] * units
     for g in range(o_ref.shape[0]):
         if units < slots:
             o_ref[g] = jnp.zeros(o_ref.shape[1:], jnp.float32)
         for u in range(units):
-            lit = lit_ref[g * units + u] > 0
+            channel = g * units + u
+            lit = lit_ref[first + channel] > 0
             for p in range(2):
-                at = ((g * units + u) * 2 + p) * span
+                at = (channel * 2 + p) * span
                 value = jnp.where(lit, x_ref[at : at + span, :], 0.0)
                 o_ref[g, pl.ds(p * slots + u, span, stride=rows), :] = value
 
 
-def send_kernel(item_ref, count_ref, x_ref, *o_refs, units, slots):
-    capacity, near = o_refs[0].shape[0], o_refs[0].shape[1] // (2 * BLK)
-    for s, o_ref in enumerate(o_refs):
-
-        def body(n, carry, s=s, o_ref=o_ref):
-            for c in range(BLK):
-                channel = item_ref[s * capacity + n] * BLK + c
-                g = channel // units
-                u = channel - g * units
-                for part in range(2):
-                    at = (c * 2 + part) * near
-                    o_ref[n, at : at + near, :] = x_ref[
-                        g, pl.ds(part * slots + u, near, stride=2 * slots), :
-                    ]
+def send_kernel(item_ref, count_ref, x_ref, *refs, units, slots):
+    *out_refs, held_ref, sems = refs
+    capacity, near = held_ref.shape[1], held_ref.shape[2] // (2 * BLK)
+    several = math.gcd(capacity, 4)
+    copies = []
+    for s, out_ref in enumerate(out_refs):
+        o_ref = held_ref.at[s]
+
+        def body(m, carry, s=s, o_ref=o_ref):
+            for k in range(several):
+                n = m * several + k
+                for c in range(BLK):
+                    channel = item_ref[s * capacity + n] * BLK + c
+                    g = channel // units
+                    u = channel - g * units
+                    for part in range(2):
+                        at = (c * 2 + part) * near
+                        o_ref[n, at : at + near, :] = x_ref[
+                            g, pl.ds(part * slots + u, near, stride=2 * slots), :
+                        ]
             return carry
 
-        lax.fori_loop(0, count_ref[s], body, 0)
+        lax.fori_loop(0, (count_ref[s] + several - 1) // several, body, 0)
+        copies.append(pltpu.make_async_copy(o_ref, out_ref, sems.at[s]))
+        copies[-1].start()
+    for copy in copies:
+        copy.wait()
 
 
 def place_kernel(from_ref, strength_ref, q_ref, *refs, channels_total, sources):
@@ -406,8 +451,10 @@
         lax.fori_loop(0, group_blocks, body, 0, unroll=4)
 
 
-def params():
-    return pltpu.CompilerParams(vmem_limit_bytes=VMEM_BYTES)
+def params(*shapes):
+    return pltpu.CompilerParams(
+        vmem_limit_bytes=SPARE + sum(4 * math.prod(shape) for shape in shapes)
+    )
 
 
 def cost(flops, moved):
@@ -423,9 +470,17 @@
 
 
 def summed(values, rounds):
-    for axis, bit in rounds:
-        pairs = [(i, i ^ bit) for i in range(lax.axis_size(axis))]
-        values = values + lax.ppermute(values, axis, pairs)
+    size = lax.axis_size("wave") * lax.axis_size("tm")
+    for bits in rounds:
+        masks = [0]
+        for bit in bits:
+            masks += [mask | bit for mask in masks]
+        others = [
+            lax.ppermute(values, ("wave", "tm"), [(i, i ^ mask) for i in range(size)])
+            for mask in masks[1:]
+        ]
+        for other in others:
+            values = values + other
     return values
 
 
@@ -459,16 +514,22 @@
     return source_item.astype(jnp.int32), counts, take_from.astype(jnp.int32)
 
 
-def time_halves(values, bits):
+def time_parts(values, bits):
     times = lax.axis_size("tm")
     count = times.bit_length() - 1
+    masks = [0]
     for b in bits:
-        side = (lax.axis_index("tm") >> b) & 1
-        dim = count - b
-        keep = lax.dynamic_index_in_dim(values, side, dim)
-        give = lax.dynamic_index_in_dim(values, 1 - side, dim)
-        values = keep + lax.ppermute(give, "tm", [(i, i ^ (1 << b)) for i in range(times)])
-    return values
+        masks += [mask | (1 << b) for mask in masks]
+    kept = None
+    for mask in masks:
+        part = values
+        for b in bits:
+            side = ((lax.axis_index("tm") ^ mask) >> b) & 1
+            part = lax.dynamic_index_in_dim(part, side, count - b)
+        if mask:
+            part = lax.ppermute(part, "tm", [(i, i ^ mask) for i in range(times)])
+        kept = part if kept is None else kept + part
+    return kept
 
 
 def local(field, lit_count, route_fibre, route_slot, dispersion, nonlinearity):
@@ -508,10 +569,14 @@
         spans.append((fc, fs, wide(strength), selection(fibre)))
     source_item, counts, take_from = route_tables(route_fibre, route_slot, groups, my_group, capacity)
 
-    wave_rounds = [("wave", 1 << b) for b in range(groups.bit_length() - 1)]
-    time_rounds = [("tm", 1 << b) for b in range(times.bit_length() - 1)]
+    wave_bits = [times << b for b in range(groups.bit_length() - 1)]
+    time_bits = [1 << b for b in range(times.bit_length() - 1)]
+    wave_rounds = [(bit,) for bit in wave_bits]
+    all_rounds = wave_rounds + [(bit,) for bit in time_bits]
     shared = channels // units if same_fibre else 0
-    fibre_rounds = [("tm", 1 << b) for b in range(shared.bit_length() - 1)]
+    fibre_bits = wave_bits + time_bits[: max(shared.bit_length() - 1, 0)]
+    fibre_rounds = [tuple(fibre_bits[:1])]
+    fibre_rounds += [tuple(fibre_bits[i : i + 2]) for i in range(1, len(fibre_bits), 2)]
 
     lit_mask = (my_group * channels + jnp.arange(channels))[None, :] < lit_count[:, None]
     lit = lit_mask.reshape(-1).astype(jnp.int32)
@@ -520,42 +585,64 @@
         split = values.reshape(fibres, channels, 2, 2, near, FB)
         return split.transpose(0, 1, 2, 4, 3, 5).reshape(-1, FB)
 
+    strips = math.gcd(times, 4)
+    block = (times // strips, 2 * near * rows, FB)
+    natural = pltpu.with_memory_space_constraint(natural_rows(field), pltpu.HBM)
     packed = pl.pallas_call(
         functools.partial(pack_kernel, units=units, slots=slots),
-        out_shape=jax.ShapeDtypeStruct((times, 2 * near * rows, FB), jnp.float32),
-        in_specs=[in_smem(), in_vmem()],
-        out_specs=in_vmem(),
-        compiler_params=params(),
+        out_shape=pltpu.HBM((times,) + block[1:], jnp.float32),
+        grid=(strips,),
+        in_specs=[in_smem(), pl.BlockSpec((natural.shape[0] // strips, FB), lambda i: (i, 0))],
+        out_specs=pl.BlockSpec(block, lambda i: (i, 0, 0)),
+        compiler_params=params(field.shape, block, block),
         name="pack",
-    )(lit, natural_rows(field))
+    )(lit, natural)
     wave_form = lax.all_to_all(packed, "tm", split_axis=0, concat_axis=0, tiled=True)
     wave_form = wave_form.reshape(chunks, 2, rows, FB)
 
     twist = jnp.asarray(twist_table())
     forward, inverse = (jnp.asarray(table) for table in matrix_tables())
-    def dispersed(x, step, total, q_fibres, fibres_out, part):
+    def dispersed(x, step, total, q_fibres, fibres_out, hold):
         fc, fs, _, select = spans[step // HALF]
         rotate = total is not None
         operands = [x]
         if rotate:
             operands += [total, spans[(step - 1) // HALF][3], spans[(step - 1) // HALF][2]]
         operands += [select, fc, fs, twist, forward, inverse]
-        shape = (chunks, 2, slots if part else rows, FB)
-        outs = [jax.ShapeDtypeStruct(shape, jnp.float32)] * (2 if part else 1)
-        outs += [jax.ShapeDtypeStruct((fibres_out, chunks, FB), jnp.float32)]
-        scratch = [pltpu.VMEM(x.shape, jnp.float32)] if rotate else []
-        scratch += step_scratch(rows, math.gcd(UNROLL, chunks // STEP))
+        held = slots if hold else x.shape[2]
+        shape = (chunks, 2, held, FB)
+        leave, fetch = not rotate or hold, step == 1
+        wave = (pltpu.HBM if leave else jax.ShapeDtypeStruct)(shape, jnp.float32)
+        outs = [wave, jax.ShapeDtypeStruct((fibres_out, chunks, FB), jnp.float32)]
+        outs += [pltpu.HBM(shape, jnp.float32)] if hold else []
+        specs_in = [in_vmem()] * len(operands)
+        specs_out = [in_vmem()] * len(outs)
+        unroll = math.gcd(UNROLL, chunks // STEP)
+        scratch = [pltpu.VMEM(shape, jnp.float32)] if rotate else []
+        if leave:
+            specs_out[0] = pl.BlockSpec(memory_space=pltpu.HBM)
+            turns = chunks // STEP // unroll
+            scratch += [pltpu.VMEM(shape, jnp.float32), pltpu.SemaphoreType.DMA((turns,))]
+        if fetch:
+            specs_in[0] = pl.BlockSpec(memory_space=pltpu.HBM)
+            operands[0] = pltpu.with_memory_space_constraint(x, pltpu.HBM)
+            scratch += [
+                pltpu.VMEM(x.shape, jnp.float32),
+                pltpu.SemaphoreType.DMA((math.gcd(4, chunks // STEP),)),
+            ]
+        scratch += step_scratch(held, unroll)
         return pl.pallas_call(
             functools.partial(
-                step_kernel, rotate=rotate, apart=part, channels_total=channels_total,
-                fibres_in=q_fibres, fibres_out=fibres_out, slots=slots,
+                step_kernel, rotate=rotate, hold=hold, fetch=fetch, leave=leave,
+                channels_total=channels_total, fibres_in=q_fibres, fibres_out=fibres_out,
+                slots=slots,
             ),
             out_shape=tuple(outs),
-            in_specs=[in_vmem()] * len(operands),
-            out_specs=tuple([in_vmem()] * len(outs)),
+            in_specs=specs_in,
+            out_specs=tuple(specs_out),
             scratch_shapes=scratch,
-            compiler_params=params(),
-            cost_estimate=cost(chunks * rows * FB * 6400, 4 * x.size * 4),
+            compiler_params=params(*[x.shape] * 5, *[ref.shape for ref in scratch]),
+            cost_estimate=cost(chunks * held * FB * 6400, 4 * x.size * 4),
             name="step",
         )(*operands)
 
@@ -563,8 +650,8 @@
     for step in range(2 * HALF - 1):
         fibres_out = 1 if (step < HALF and same_fibre) else fibres
         wave_form, partial = dispersed(wave_form, step, total, q_fibres, fibres_out, False)
-        rounds = fibre_rounds if fibres_out == 1 else time_rounds
-        total, q_fibres = summed(partial, wave_rounds + rounds), fibres_out
+        rounds = fibre_rounds if fibres_out == 1 else all_rounds
+        total, q_fibres = summed(partial, rounds), fibres_out
 
     last = 2 * HALF - 1
 
@@ -573,33 +660,41 @@
         return lax.all_to_all(values, "tm", split_axis=0, concat_axis=0, tiled=True)
 
     def prepared(values):
-        block = jax.ShapeDtypeStruct((capacity, BLK * 2 * near, FB), jnp.float32)
+        block = pltpu.HBM((capacity, BLK * 2 * near, FB), jnp.float32)
         return pl.pallas_call(
             functools.partial(send_kernel, units=units, slots=slots),
             out_shape=(block,) * groups,
             in_specs=[in_smem(), in_smem(), in_vmem()],
-            out_specs=(in_vmem(),) * groups,
-            compiler_params=params(),
+            out_specs=(pl.BlockSpec(memory_space=pltpu.HBM),) * groups,
+            scratch_shapes=[
+                pltpu.VMEM((groups,) + block.shape, jnp.float32),
+                pltpu.SemaphoreType.DMA((groups,)),
+            ],
+            compiler_params=params(values.shape, (groups,) + block.shape),
             cost_estimate=cost(0, 4 * 4 * values.size),
             name="send",
         )(source_item, counts, values)
 
     def to_groups(outgoing):
-        moved = [outgoing[0]]
+        moved = [pltpu.with_memory_space_constraint(outgoing[0], pltpu.HBM)]
         for s in range(1, groups):
             moved.append(lax.ppermute(outgoing[s], "wave", [(i, i ^ s) for i in range(groups)]))
         return moved
 
-    first, second, partial = dispersed(wave_form, last, total, q_fibres, fibres, True)
+    first, partial, rest = dispersed(wave_form, last, total, q_fibres, fibres, True)
+    second, more = dispersed(rest, last, None, 0, fibres, False)
     bits = list(range(times.bit_length() - 1))
-    partial = summed(partial, wave_rounds).reshape([fibres] + [2] * len(bits) + [near, FB])
+    partial = summed(partial + more, wave_rounds)
+    partial = partial.reshape([fibres] + [2] * len(bits) + [near, FB])
+    partial = time_parts(partial, bits[:1])
     first, partial = lax.optimization_barrier((to_times(first), partial))
     first = prepared(first)
     first, second = lax.optimization_barrier((first, second))
-    partial = time_halves(partial, bits[:1] + bits[2:])
-    second, partial, *first = lax.optimization_barrier((to_times(second), partial, *to_groups(first)))
+    second, *first = lax.optimization_barrier((to_times(second), *to_groups(first)))
     blocks = first + to_groups(prepared(second))
-    own_total = time_halves(partial, bits[1:2]).reshape(fibres, near, FB)
+    for i in range(1, len(bits), 2):
+        partial = time_parts(partial, bits[i : i + 2])
+    own_total = partial.reshape(fibres, near, FB)
     strength = jnp.broadcast_to(nonlinearity[1][:, None, None], (fibres, near, FB))
     placed = pl.pallas_call(
         functools.partial(place_kernel, channels_total=channels_total, sources=groups),
@@ -611,7 +706,7 @@
             pltpu.VMEM((2, groups * capacity, BLK * 2 * near, FB), jnp.float32),
             pltpu.SemaphoreType.DMA((2, groups)),
         ],
-        compiler_params=params(),
+        compiler_params=params(field.shape, (2, groups * capacity, BLK * 2 * near, FB)),
         cost_estimate=cost(0, 4 * 4 * field.size),
         name="place",
     )(take_from, strength, own_total, *blocks)

time: 231 us -> 219 us (0.948)
  waiting for transfers between devices: 136 us -> 125 us
  local copies, waits for them, and re-layouts: 12 us -> 4.89 us
  Pallas kernels: 42 us -> 45.7 us
    ppermute x16 -> x19, waiting for transfers between devices: 55.8 us -> 38.2 us  [the longest x15 31.6 us: summed(): lax.ppermute(values, ('wave', 'tm'), [(i, i ^ mask) for i in range(size)])]
    ppermute x6, waiting for transfers between devices: 21 us -> 36.1 us  [to_groups(): lax.ppermute(outgoing[s], 'wave', [(i, i ^ s) for i in range(groups)])]
    all_to_all x2, waiting for transfers between devices: 15.1 us -> 6.8 us  [to_times(): return lax.all_to_all(values, 'tm', split_axis=0, concat_axis=0, tiled=True)]
    unnamed x30 -> x21, local copies, waits for them, and re-layouts: 7.18 us -> 0.06 us
    pallas_call x4 -> x5, Pallas kernels: 27.2 us -> 31.2 us  [dispersed(): pl.pallas_call(functools.partial(step_kernel, rotate=rotate, hold=hold, f...]
    ppermute x16 -> x19, starting transfers between devices: 18.8 us -> 20.7 us  [the longest x15 12.9 us: summed(): lax.ppermute(values, ('wave', 'tm'), [(i, i ^ mask) for i in range(size)])]
  transfers between devices with their start and end apart: 25 -> 28, of which waited for: 21 -> 24; matrix products, arithmetic and copies ran while one was open for 3% -> 3% of each run, Pallas kernels for 0% -> 2%
where the time goes in v5:
time: 219 us; the launch traced here: 218 us
  waiting for transfers between devices  125 us (57%)
  Pallas kernels  45.7 us (21%)
  starting transfers between devices  39.3 us (18%)
  local copies, waits for them, and re-layouts  4.89 us (2%)
  other arithmetic  2.78 us (1%)
    all_to_all x1, waiting for transfers between devices, local(): lax.all_to_all(packed, 'tm', split_axis=0, concat_axis=0, tiled=True)  44.2 us
    ppermute x6, waiting for transfers between devices, to_groups(): lax.ppermute(outgoing[s], 'wave', [(i, i ^ s) for i in range(groups)])  36.1 us
    ppermute x15, waiting for transfers between devices, summed(): lax.ppermute(values, ('wave', 'tm'), [(i, i ^ mask) for i in range(size)])  31.6 us
    pallas_call x5, Pallas kernels, dispersed(): pl.pallas_call(functools.partial(step_kernel, rotate=rotate, hold=hold, f...  31.2 us
    ppermute x15, starting transfers between devices, summed(): lax.ppermute(values, ('wave', 'tm'), [(i, i ^ mask) for i in range(size)])  12.9 us
    ppermute x4, starting transfers between devices, time_parts(): part = lax.ppermute(part, 'tm', [(i, i ^ mask) for i in range(times)])  7.75 us
    all_to_all x1, starting transfers between devices, local(): lax.all_to_all(packed, 'tm', split_axis=0, concat_axis=0, tiled=True)  7.4 us
    all_to_all x2, starting transfers between devices, to_times(): return lax.all_to_all(values, 'tm', split_axis=0, concat_axis=0, tiled=True)  7.35 us
  transfers between devices with their start and end apart: 28, of which 24 were waited for; matrix products, arithmetic and copies ran while one was open for 3% of the time, Pallas kernels for 2%

profile of v5, /device:TPU:0, one launch (start us, length us, event | category | flops | bytes accessed | tf_op | source)
XLA Modules:
  0.0 218.5 jit_solution(471435568516971184)
XLA Ops:
  0.0 0.7 compare_convert_fusion
  0.8 4.6 %pack.1 = f32[8,512,128]{2,1,0:T(8,128)} custom-call(s32[128]{0:T(128)S(1)} %reshape.486.lit_ref, f32[4096,128]{1,0:T(8,128)} %bitcast.43), custom_call_target="tpu_custom_call" | custom-call | tf_op jit(solution)/shard_map/pack/pallas_call | solution.py:591
  5.4 7.4 %all-to-all-start = ((f32[8,512,128]{2,1,0:T(8,128)}), f32[8,512,128]{2,1,0:T(8,128)S(1)}, u32[]{:S(2)}, u32[]{:S(2)}) async-start(f32[8,512,128]{2,1,0:T(8,128)} %pack.1), calls=%async_computation | async-start | bytes 4194304 | tf_op jit(solution)/shard_map/all_to_all | solution.py:600
  12.9 0.7 gather_fusion.2
  13.6 0.7 gather_fusion.4
  15.8 1.0 sine_multiply_fusion
  16.8 44.2 %all-to-all-done = f32[8,512,128]{2,1,0:T(8,128)S(1)} async-done(((f32[8,512,128]{2,1,0:T(8,128)}), f32[8,512,128]{2,1,0:T(8,128)S(1)}, u32[]{:S(2)}, u32[]{:S(2)}) %all-to-all-start) | async-done | bytes 2097184 | tf_op jit(solution)/shard_map/all_to_all | solution.py:600
  61.2 6.5 %step.5 = (f32[64,2,32,128]{3,2,1,0:T(8,128)}, f32[1,64,128]{2,1,0:T(8,128)S(1)}) custom-call(f32[64,2,32,128]{3,2,1,0:T(8,128)S(1)} %bitcast.42, f32[4,16,128]{2,1,0:T(8,128)S(1)} %broadcast_in_dim.32.refs_1_.refs_2_.refs_4_, f32[16,16,128]{2,1,0:T(8,128)S(1)} %get-tuple-element.78.refs_2_.refs_5_, f32[16,16,128]{2,1,0:T(8,128)S(1)} %get-tuple-element.79.refs_3_.refs_6_, ...), custom_call_target="tpu_custom_call" | custom-call | flops 1677721600 | bytes 8388608 | tf_op jit(solution)/shard_map/step/pallas_call | solution.py:634
  67.7 1.2 collective-permute-done
  68.9 2.4 %collective-permute-start.3 = (f32[1,64,128]{2,1,0:T(8,128)S(1)}, f32[1,64,128]{2,1,0:T(8,128)S(1)}, u32[]{:S(2)}, u32[]{:S(2)}) collective-permute-start(f32[1,64,128]{2,1,0:T(8,128)S(1)} %add.375), channel_id=1, source_target_pairs={{0,17},{1,16},{2,19},{3,18},{4,21},{5,20},{6,23},{7,22},{8,25},{9,... | collective-permute-start | bytes 98312 | tf_op jit(solution)/shard_map/ppermute | solution.py:479
  73.7 1.5 collective-permute-done.2
  75.9 7.7 %step.6 = (f32[64,2,32,128]{3,2,1,0:T(8,128)S(1)}, f32[1,64,128]{2,1,0:T(8,128)S(1)}) custom-call(f32[64,2,32,128]{3,2,1,0:T(8,128)} %get-tuple-element.36.refs_0_, f32[1,64,128]{2,1,0:T(8,128)S(1)} %add_add_fusion.1.refs_1_, f32[4,16,128]{2,1,0:T(8,128)S(1)} %broadcast_in_dim.32.refs_1_.refs_2_.refs_4_, f32[16,128]{1,0:T(8,128)S(1)} %broadcast_in_dim.33.refs_3_, ...), custom_call_target="tpu_custom_call" | custom-call | flops 1677721600 | bytes 8388608 | tf_op jit(solution)/shard_map/step/pallas_call | solution.py:634
  83.7 1.2 collective-permute-done.4
  84.9 1.4 collective-permute-start.7
  86.9 1.5 collective-permute-start.5
  88.4 1.4 collective-permute-done.7
  90.9 6.8 %step.7 = (f32[64,2,32,128]{3,2,1,0:T(8,128)S(1)}, f32[4,64,128]{2,1,0:T(8,128)S(1)}) custom-call(f32[64,2,32,128]{3,2,1,0:T(8,128)S(1)} %get-tuple-element.38.refs_0_, f32[1,64,128]{2,1,0:T(8,128)S(1)} %add_add_fusion.refs_1_, f32[4,16,128]{2,1,0:T(8,128)S(1)} %broadcast_in_dim.32.refs_1_.refs_2_.refs_4_, f32[16,128]{1,0:T(8,128)S(1)} %broadcast_in_dim.33.refs_3_, ...), custom_call_target="tpu_custom_call" | custom-call | flops 1677721600 | bytes 8388608 | tf_op jit(solution)/shard_map/step/pallas_call | solution.py:634
  97.8 1.3 collective-permute-done.8
  99.1 1.6 collective-permute-start.9
  100.7 4.0 %collective-permute-done.9 = f32[4,64,128]{2,1,0:T(8,128)S(1)} collective-permute-done((f32[4,64,128]{2,1,0:T(8,128)S(1)}, f32[4,64,128]{2,1,0:T(8,128)S(1)}, u32[]{:S(2)}, u32[]{:S(2)}) %collective-permute-start.9) | collective-permute-done | bytes 131104 | tf_op jit(solution)/shard_map/ppermute | solution.py:479
  104.8 1.5 collective-permute-start.10
  106.3 3.5 %collective-permute-done.10 = f32[4,64,128]{2,1,0:T(8,128)S(1)} collective-permute-done((f32[4,64,128]{2,1,0:T(8,128)S(1)}, f32[4,64,128]{2,1,0:T(8,128)S(1)}, u32[]{:S(2)}, u32[]{:S(2)}) %collective-permute-start.10) | collective-permute-done | bytes 131104 | tf_op jit(solution)/shard_map/ppermute | solution.py:479
  109.9 5.0 %collective-permute-done.11 = f32[4,64,128]{2,1,0:T(8,128)S(1)} collective-permute-done((f32[4,64,128]{2,1,0:T(8,128)S(1)}, f32[4,64,128]{2,1,0:T(8,128)S(1)}, u32[]{:S(2)}, u32[]{:S(2)}) %collective-permute-start.11) | collective-permute-done | bytes 131104 | tf_op jit(solution)/shard_map/ppermute | solution.py:479
  114.9 0.9 collective-permute-start.12
  116.4 5.2 %collective-permute-done.12 = f32[4,64,128]{2,1,0:T(8,128)S(1)} collective-permute-done((f32[4,64,128]{2,1,0:T(8,128)S(1)}, f32[4,64,128]{2,1,0:T(8,128)S(1)}, u32[]{:S(2)}, u32[]{:S(2)}) %collective-permute-start.12) | collective-permute-done | bytes 131104 | tf_op jit(solution)/shard_map/ppermute | solution.py:479
  121.7 6.3 %step.8 = (f32[64,2,16,128]{3,2,1,0:T(8,128)}, f32[4,64,128]{2,1,0:T(8,128)S(1)}, f32[64,2,16,128]{3,2,1,0:T(8,128)}) custom-call(f32[64,2,32,128]{3,2,1,0:T(8,128)S(1)} %get-tuple-element.40.refs_0_, f32[4,64,128]{2,1,0:T(8,128)S(1)} %add.396.refs_1_, f32[4,16,128]{2,1,0:T(8,128)S(1)} %broadcast_in_dim.34.refs_4_.refs_2_.refs_1_, ...), custom_call_target="tpu_custom_call" | custom-call | flops 838860800 | bytes 8388608 | tf_op jit(solution)/shard_map/step/pallas_call | solution.py:634
  128.1 3.8 %all-to-all-start.1 = ((f32[8,256,128]{2,1,0:T(8,128)}), f32[8,256,128]{2,1,0:T(8,128)S(1)}, u32[]{:S(2)}, u32[]{:S(2)}) async-start(f32[8,256,128]{2,1,0:T(8,128)} %bitcast.44), calls=%async_computation.1 | async-start | bytes 2097152 | tf_op jit(solution)/shard_map/all_to_all | solution.py:660
  132.1 3.9 %step.9 = (f32[64,2,16,128]{3,2,1,0:T(8,128)}, f32[4,64,128]{2,1,0:T(8,128)S(1)}) custom-call(f32[64,2,16,128]{3,2,1,0:T(8,128)S(1)} %copy-done.3, f32[4,16,128]{2,1,0:T(8,128)S(1)} %broadcast_in_dim.34.refs_4_.refs_2_.refs_1_, f32[16,16,128]{2,1,0:T(8,128)S(1)} %get-tuple-element.75.refs_5_.refs_2_, f32[16,16,128]{2,1,0:T(8,128)S(1)} %get-tuple-element.74.refs_6_.refs_3_, ...), custom_call_target="tpu_custom_call" | custom-call | flops 838860800 | bytes 4194304 | tf_op jit(solution)/shard_map/step/pallas_call | solution.py:634
  136.3 1.1 collective-permute-done.13
  137.5 1.6 collective-permute-start.14
  139.1 3.9 %collective-permute-done.14 = f32[4,64,128]{2,1,0:T(8,128)S(1)} collective-permute-done((f32[4,64,128]{2,1,0:T(8,128)S(1)}, f32[4,64,128]{2,1,0:T(8,128)S(1)}, u32[]{:S(2)}, u32[]{:S(2)}) %collective-permute-start.14) | collective-permute-done | bytes 131104 | tf_op jit(solution)/shard_map/ppermute | solution.py:479
  143.1 2.1 collective-permute-start.15
  145.3 2.1 collective-permute-done.15
  147.5 6.8 %all-to-all-done.1.x_ref = f32[8,256,128]{2,1,0:T(8,128)S(1)} async-done(((f32[8,256,128]{2,1,0:T(8,128)}), f32[8,256,128]{2,1,0:T(8,128)S(1)}, u32[]{:S(2)}, u32[]{:S(2)}) %all-to-all-start.1) | async-done | bytes 1048608 | tf_op jit(solution)/shard_map/all_to_all | solution.py:660
  154.3 2.7 %send.2 = (f32[32,32,128]{2,1,0:T(8,128)}, f32[32,32,128]{2,1,0:T(8,128)}, f32[32,32,128]{2,1,0:T(8,128)}, f32[32,32,128]{2,1,0:T(8,128)}) custom-call(s32[128]{0:T(128)S(1)} %select_reduce_fusion.1.item_ref, s32[4]{0:T(128)S(1)} %convert_reduce_fusion.1.count_ref, f32[8,256,128]{2,1,0:T(8,128)S(1)} %all-to-all-done.1.x_ref), custom_call_target="tpu_custom_call" | custom-call | bytes 4194304 | tf_op jit(solution)/shard_map/send/pallas_call | solution.py:664
  157.0 3.6 %all-to-all-start.2 = ((f32[8,256,128]{2,1,0:T(8,128)}), f32[8,256,128]{2,1,0:T(8,128)S(1)}, u32[]{:S(2)}, u32[]{:S(2)}) async-start(f32[8,256,128]{2,1,0:T(8,128)} %bitcast.19), calls=%async_computation.2 | async-start | bytes 2097152 | tf_op jit(solution)/shard_map/all_to_all | solution.py:660
  160.7 1.6 collective-permute-start.20
  162.7 1.9 collective-permute-start.16
  164.6 11.0 %collective-permute-done.20.refs_2_ = f32[32,32,128]{2,1,0:T(8,128)S(1)} collective-permute-done((f32[32,32,128]{2,1,0:T(8,128)}, f32[32,32,128]{2,1,0:T(8,128)S(1)}, u32[]{:S(2)}, u32[]{:S(2)}) %collective-permute-start.20) | collective-permute-done | bytes 524320 | tf_op jit(solution)/shard_map/ppermute | solution.py:681
  175.7 10.3 %collective-permute-done.21.refs_3_ = f32[32,32,128]{2,1,0:T(8,128)S(1)} collective-permute-done((f32[32,32,128]{2,1,0:T(8,128)}, f32[32,32,128]{2,1,0:T(8,128)S(1)}, u32[]{:S(2)}, u32[]{:S(2)}) %collective-permute-start.21) | collective-permute-done | bytes 524320 | tf_op jit(solution)/shard_map/ppermute | solution.py:681
  186.0 2.7 %send.3 = (f32[32,32,128]{2,1,0:T(8,128)}, f32[32,32,128]{2,1,0:T(8,128)}, f32[32,32,128]{2,1,0:T(8,128)}, f32[32,32,128]{2,1,0:T(8,128)}) custom-call(s32[128]{0:T(128)S(1)} %select_reduce_fusion.1.item_ref, s32[4]{0:T(128)S(1)} %convert_reduce_fusion.1.count_ref, f32[8,256,128]{2,1,0:T(8,128)S(1)} %all-to-all-done.2.x_ref), custom_call_target="tpu_custom_call" | custom-call | bytes 4194304 | tf_op jit(solution)/shard_map/send/pallas_call | solution.py:664
  189.1 1.5 collective-permute-start.23
  190.7 3.7 %collective-permute-start.18 = (f32[4,1,1,1,8,128]{5,4,0,3,2,1:T(8,128)S(1)}, f32[4,1,1,1,8,128]{5,4,0,3,2,1:T(8,128)S(1)}, u32[]{:S(2)}, u32[]{:S(2)}) collective-permute-start(f32[4,1,1,1,8,128]{5,4,0,3,2,1:T(8,128)S(1)} %get-tuple-element.72), channel_id=1, source_target_pairs={{0,6},{1,7},{2,4},{3,5},{4,2},{5,3},{6,0},{7,1},{8,14},{9,15},{10,... | collective-permute-start | bytes 49160 | tf_op jit(solution)/shard_map/ppermute | solution.py:530
  194.6 1.6 collective-permute-done.18
  196.3 2.8 %collective-permute-done.17 = f32[4,1,1,1,8,128]{5,4,0,3,2,1:T(8,128)S(1)} collective-permute-done((f32[4,1,1,1,8,128]{5,4,0,3,2,1:T(8,128)S(1)}, f32[4,1,1,1,8,128]{5,4,0,3,2,1:T(8,128)S(1)}, u32[]{:S(2)}, u32[]{:S(2)}) %collective-permute-start.17) | collective-permute-done | bytes 16416 | tf_op jit(solution)/shard_map/ppermute | solution.py:530
  199.1 4.9 %collective-permute-done.23.refs_6_ = f32[32,32,128]{2,1,0:T(8,128)S(1)} collective-permute-done((f32[32,32,128]{2,1,0:T(8,128)}, f32[32,32,128]{2,1,0:T(8,128)S(1)}, u32[]{:S(2)}, u32[]{:S(2)}) %collective-permute-start.23) | collective-permute-done | bytes 524320 | tf_op jit(solution)/shard_map/ppermute | solution.py:681
  204.0 9.8 %collective-permute-done.24.refs_7_ = f32[32,32,128]{2,1,0:T(8,128)S(1)} collective-permute-done((f32[32,32,128]{2,1,0:T(8,128)}, f32[32,32,128]{2,1,0:T(8,128)S(1)}, u32[]{:S(2)}, u32[]{:S(2)}) %collective-permute-start.24) | collective-permute-done | bytes 524320 | tf_op jit(solution)/shard_map/ppermute | solution.py:681
  213.9 4.4 %place.1 = f32[64,64,128]{2,1,0:T(8,128)} custom-call(s32[64]{0:T(128)S(1)} %select_reduce_fusion.from_ref, f32[4,8,128]{2,1,0:T(8,128)S(1)} %broadcast_in_dim.31.strength_ref, f32[4,8,128]{2,1,0:T(8,128)S(1)} %add_bitcast_fusion.q_ref, f32[32,32,128]{2,1,0:T(8,128)} %get-tuple-element.58.refs_0_, f32[32,32,128]{2,1,0:T(8,128)S(1)} %collective-permute-done.19.refs_1_, ...), custom_call_target="tpu_custom_call" | custom-call | bytes 8388608 | tf_op jit(solution)/shard_map/place/pallas_call | solution.py:699
  (95 shorter events, 9.6 us)
Async XLA Ops:
  5.4 7.5 %copy-start.5 = (s32[4,64]{1,0:T(4,128)S(1)}, s32[4,64]{1,0:T(4,128)}, u32[]{:S(2)}) copy-start(s32[4,64]{1,0:T(4,128)} %param.13) | copy-start | bytes 3076
  5.4 8.2 %copy-start.4 = (s32[4,64]{1,0:T(4,128)S(1)}, s32[4,64]{1,0:T(4,128)}, u32[]{:S(2)}) copy-start(s32[4,64]{1,0:T(4,128)} %param.14) | copy-start | bytes 3076
  5.4 8.9 %copy-start.8 = (f32[2,4]{1,0:T(2,128)S(1)}, f32[2,4]{1,0:T(2,128)}, u32[]{:S(2)}) copy-start(f32[2,4]{1,0:T(2,128)} %param.15) | copy-start | bytes 100
  5.4 55.6 %all-to-all-start = ((f32[8,512,128]{2,1,0:T(8,128)}), f32[8,512,128]{2,1,0:T(8,128)S(1)}, u32[]{:S(2)}, u32[]{:S(2)}) async-start(f32[8,512,128]{2,1,0:T(8,128)} %pack.1), calls=%async_computation | async-start | bytes 4194304 | tf_op jit(solution)/shard_map/all_to_all | solution.py:600
  12.8 2.9 %copy-start.6 = (f32[16,128]{1,0:T(8,128)S(1)}, f32[16,128]{1,0:T(8,128)}, u32[]{:S(2)}) copy-start(f32[16,128]{1,0:T(8,128)} %constant.274) | copy-start | bytes 24580
  12.8 3.0 %copy-start.7 = (f32[16,128]{1,0:T(8,128)S(1)}, f32[16,128]{1,0:T(8,128)}, u32[]{:S(2)}) copy-start(f32[16,128]{1,0:T(8,128)} %constant.273) | copy-start | bytes 24580
  12.8 48.3 %copy-start = (bf16[512,256]{1,0:T(8,128)(2,1)S(1)}, bf16[512,256]{1,0:T(8,128)(2,1)}, u32[]{:S(2)}) copy-start(bf16[512,256]{1,0:T(8,128)(2,1)} %constant.270.clone.refs_6_.refs_9_) | copy-start | bytes 786436
  12.9 48.3 %copy-start.1 = (bf16[512,256]{1,0:T(8,128)(2,1)S(1)}, bf16[512,256]{1,0:T(8,128)(2,1)}, u32[]{:S(2)}) copy-start(bf16[512,256]{1,0:T(8,128)(2,1)} %constant.269.clone.refs_5_.refs_8_) | copy-start | bytes 786436
  12.9 48.3 %copy-start.2 = (f32[2,16,8,128]{3,2,1,0:T(8,128)S(1)}, f32[2,16,8,128]{3,2,1,0:T(8,128)}, u32[]{:S(2)}) copy-start(f32[2,16,8,128]{3,2,1,0:T(8,128)} %constant.268.clone.refs_4_.refs_7_) | copy-start | bytes 393220
  61.2 11.2 %copy-start.9 = (f32[2,4]{1,0:T(2,128)S(1)}, f32[2,4]{1,0:T(2,128)}, u32[]{:S(2)}) copy-start(f32[2,4]{1,0:T(2,128)} %param.16) | copy-start | bytes 100
  67.6 1.3 collective-permute-start
  68.9 4.8 %collective-permute-start.3 = (f32[1,64,128]{2,1,0:T(8,128)S(1)}, f32[1,64,128]{2,1,0:T(8,128)S(1)}, u32[]{:S(2)}, u32[]{:S(2)}) collective-permute-start(f32[1,64,128]{2,1,0:T(8,128)S(1)} %add.375), channel_id=1, source_target_pairs={{0,17},{1,16},{2,19},{3,18},{4,21},{5,20},{6,23},{7,22},{8,25},{9,... | collective-permute-start | bytes 98312 | tf_op jit(solution)/shard_map/ppermute | solution.py:479
  71.3 3.9 %collective-permute-start.2 = (f32[1,64,128]{2,1,0:T(8,128)S(1)}, f32[1,64,128]{2,1,0:T(8,128)S(1)}, u32[]{:S(2)}, u32[]{:S(2)}) collective-permute-start(f32[1,64,128]{2,1,0:T(8,128)S(1)} %add.375), channel_id=1, source_target_pairs={{0,1},{1,0},{2,3},{3,2},{4,5},{5,4},{6,7},{7,6},{8,9},{9,8},{10,11... | collective-permute-start | bytes 98312 | tf_op jit(solution)/shard_map/ppermute | solution.py:479
  71.9 3.9 %collective-permute-start.1 = (f32[1,64,128]{2,1,0:T(8,128)S(1)}, f32[1,64,128]{2,1,0:T(8,128)S(1)}, u32[]{:S(2)}, u32[]{:S(2)}) collective-permute-start(f32[1,64,128]{2,1,0:T(8,128)S(1)} %add.375), channel_id=1, source_target_pairs={{0,16},{1,17},{2,18},{3,19},{4,20},{5,21},{6,22},{7,23},{8,24},{9,... | collective-permute-start | bytes 98312 | tf_op jit(solution)/shard_map/ppermute | solution.py:479
  83.6 1.3 collective-permute-start.4
  84.9 4.9 %collective-permute-start.7 = (f32[1,64,128]{2,1,0:T(8,128)S(1)}, f32[1,64,128]{2,1,0:T(8,128)S(1)}, u32[]{:S(2)}, u32[]{:S(2)}) collective-permute-start(f32[1,64,128]{2,1,0:T(8,128)S(1)} %add.379), channel_id=1, source_target_pairs={{0,17},{1,16},{2,19},{3,18},{4,21},{5,20},{6,23},{7,22},{8,25},{9,... | collective-permute-start | bytes 98312 | tf_op jit(solution)/shard_map/ppermute | solution.py:479
  86.3 3.9 %collective-permute-start.6 = (f32[1,64,128]{2,1,0:T(8,128)S(1)}, f32[1,64,128]{2,1,0:T(8,128)S(1)}, u32[]{:S(2)}, u32[]{:S(2)}) collective-permute-start(f32[1,64,128]{2,1,0:T(8,128)S(1)} %add.379), channel_id=1, source_target_pairs={{0,1},{1,0},{2,3},{3,2},{4,5},{5,4},{6,7},{7,6},{8,9},{9,8},{10,11... | collective-permute-start | bytes 98312 | tf_op jit(solution)/shard_map/ppermute | solution.py:479
  86.9 3.9 %collective-permute-start.5 = (f32[1,64,128]{2,1,0:T(8,128)S(1)}, f32[1,64,128]{2,1,0:T(8,128)S(1)}, u32[]{:S(2)}, u32[]{:S(2)}) collective-permute-start(f32[1,64,128]{2,1,0:T(8,128)S(1)} %add.379), channel_id=1, source_target_pairs={{0,16},{1,17},{2,18},{3,19},{4,20},{5,21},{6,22},{7,23},{8,24},{9,... | collective-permute-start | bytes 98312 | tf_op jit(solution)/shard_map/ppermute | solution.py:479
  97.7 1.4 collective-permute-start.8
  99.1 5.6 %collective-permute-start.9 = (f32[4,64,128]{2,1,0:T(8,128)S(1)}, f32[4,64,128]{2,1,0:T(8,128)S(1)}, u32[]{:S(2)}, u32[]{:S(2)}) collective-permute-start(f32[4,64,128]{2,1,0:T(8,128)S(1)} %add.392), channel_id=1, source_target_pairs={{0,16},{1,17},{2,18},{3,19},{4,20},{5,21},{6,22},{7,23},{8,24},{9,... | collective-permute-start | bytes 393224 | tf_op jit(solution)/shard_map/ppermute | solution.py:479
  104.8 5.0 %collective-permute-start.10 = (f32[4,64,128]{2,1,0:T(8,128)S(1)}, f32[4,64,128]{2,1,0:T(8,128)S(1)}, u32[]{:S(2)}, u32[]{:S(2)}) collective-permute-start(f32[4,64,128]{2,1,0:T(8,128)S(1)} %add.393), channel_id=1, source_target_pairs={{0,1},{1,0},{2,3},{3,2},{4,5},{5,4},{6,7},{7,6},{8,9},{9,8},{10,11... | collective-permute-start | bytes 393224 | tf_op jit(solution)/shard_map/ppermute | solution.py:479
  109.8 5.0 %collective-permute-start.11 = (f32[4,64,128]{2,1,0:T(8,128)S(1)}, f32[4,64,128]{2,1,0:T(8,128)S(1)}, u32[]{:S(2)}, u32[]{:S(2)}) collective-permute-start(f32[4,64,128]{2,1,0:T(8,128)S(1)} %add.394), channel_id=1, source_target_pairs={{0,2},{1,3},{2,0},{3,1},{4,6},{5,7},{6,4},{7,5},{8,10},{9,11},{10,... | collective-permute-start | bytes 393224 | tf_op jit(solution)/shard_map/ppermute | solution.py:479
  114.9 6.8 %collective-permute-start.12 = (f32[4,64,128]{2,1,0:T(8,128)S(1)}, f32[4,64,128]{2,1,0:T(8,128)S(1)}, u32[]{:S(2)}, u32[]{:S(2)}) collective-permute-start(f32[4,64,128]{2,1,0:T(8,128)S(1)} %add.395), channel_id=1, source_target_pairs={{0,4},{1,5},{2,6},{3,7},{4,0},{5,1},{6,2},{7,3},{8,12},{9,13},{10,... | collective-permute-start | bytes 393224 | tf_op jit(solution)/shard_map/ppermute | solution.py:479
  128.1 4.0 %copy-start.3 = (f32[64,2,16,128]{3,2,1,0:T(8,128)S(1)}, f32[64,2,16,128]{3,2,1,0:T(8,128)}, u32[]{:S(2)}) copy-start(f32[64,2,16,128]{3,2,1,0:T(8,128)} %get-tuple-element.44.refs_0_) | copy-start | bytes 3145732
  128.1 26.2 %all-to-all-start.1 = ((f32[8,256,128]{2,1,0:T(8,128)}), f32[8,256,128]{2,1,0:T(8,128)S(1)}, u32[]{:S(2)}, u32[]{:S(2)}) async-start(f32[8,256,128]{2,1,0:T(8,128)} %bitcast.44), calls=%async_computation.1 | async-start | bytes 2097152 | tf_op jit(solution)/shard_map/all_to_all | solution.py:660
  136.0 1.4 collective-permute-start.13
  137.5 5.6 %collective-permute-start.14 = (f32[4,64,128]{2,1,0:T(8,128)S(1)}, f32[4,64,128]{2,1,0:T(8,128)S(1)}, u32[]{:S(2)}, u32[]{:S(2)}) collective-permute-start(f32[4,64,128]{2,1,0:T(8,128)S(1)} %add.398), channel_id=1, source_target_pairs={{0,16},{1,17},{2,18},{3,19},{4,20},{5,21},{6,22},{7,23},{8,24},{9,... | collective-permute-start | bytes 393224 | tf_op jit(solution)/shard_map/ppermute | solution.py:479
  143.1 4.3 %collective-permute-start.15 = (f32[4,2,2,1,8,128]{5,4,0,3,2,1:T(8,128)S(1)}, f32[4,2,2,1,8,128]{5,4,0,3,2,1:T(8,128)S(1)}, u32[]{:S(2)}, u32[]{:S(2)}) collective-permute-start(f32[4,2,2,1,8,128]{5,4,0,3,2,1:T(8,128)S(1)} %copy.29), channel_id=1, source_target_pairs={{0,1},{1,0},{2,3},{3,2},{4,5},{5,4},{6,7},{7,6},{8,9},{9,8},{10,11... | collective-permute-start | bytes 196616 | tf_op jit(solution)/shard_map/ppermute | solution.py:530
  157.0 29.0 %all-to-all-start.2 = ((f32[8,256,128]{2,1,0:T(8,128)}), f32[8,256,128]{2,1,0:T(8,128)S(1)}, u32[]{:S(2)}, u32[]{:S(2)}) async-start(f32[8,256,128]{2,1,0:T(8,128)} %bitcast.19), calls=%async_computation.2 | async-start | bytes 2097152 | tf_op jit(solution)/shard_map/all_to_all | solution.py:660
  160.6 4.1 %collective-permute-start.19 = (f32[32,32,128]{2,1,0:T(8,128)}, f32[32,32,128]{2,1,0:T(8,128)S(1)}, u32[]{:S(2)}, u32[]{:S(2)}) collective-permute-start(f32[32,32,128]{2,1,0:T(8,128)} %get-tuple-element.55), channel_id=1, source_target_pairs={{0,8},{8,0},{16,24},{24,16},{1,9},{9,1},{17,25},{25,17},{2,10},{10... | collective-permute-start | bytes 1572872 | tf_op jit(solution)/shard_map/ppermute | solution.py:681
  160.7 15.0 %collective-permute-start.20 = (f32[32,32,128]{2,1,0:T(8,128)}, f32[32,32,128]{2,1,0:T(8,128)S(1)}, u32[]{:S(2)}, u32[]{:S(2)}) collective-permute-start(f32[32,32,128]{2,1,0:T(8,128)} %get-tuple-element.56), channel_id=1, source_target_pairs={{0,16},{8,24},{16,0},{24,8},{1,17},{9,25},{17,1},{25,9},{2,18},{10... | collective-permute-start | bytes 1572872 | tf_op jit(solution)/shard_map/ppermute | solution.py:681
  162.2 23.7 %collective-permute-start.21 = (f32[32,32,128]{2,1,0:T(8,128)}, f32[32,32,128]{2,1,0:T(8,128)S(1)}, u32[]{:S(2)}, u32[]{:S(2)}) collective-permute-start(f32[32,32,128]{2,1,0:T(8,128)} %get-tuple-element.57), channel_id=1, source_target_pairs={{0,24},{8,16},{16,8},{24,0},{1,25},{9,17},{17,9},{25,1},{2,26},{10... | collective-permute-start | bytes 1572872 | tf_op jit(solution)/shard_map/ppermute | solution.py:681
  162.7 31.7 %collective-permute-start.16 = (f32[4,1,1,1,8,128]{5,4,0,3,2,1:T(8,128)S(1)}, f32[4,1,1,1,8,128]{5,4,0,3,2,1:T(8,128)S(1)}, u32[]{:S(2)}, u32[]{:S(2)}) collective-permute-start(f32[4,1,1,1,8,128]{5,4,0,3,2,1:T(8,128)S(1)} %get-tuple-element.71), channel_id=1, source_target_pairs={{0,2},{1,3},{2,0},{3,1},{4,6},{5,7},{6,4},{7,5},{8,10},{9,11},{10,... | collective-permute-start | bytes 49160 | tf_op jit(solution)/shard_map/ppermute | solution.py:530
  188.7 10.4 %collective-permute-start.22 = (f32[32,32,128]{2,1,0:T(8,128)}, f32[32,32,128]{2,1,0:T(8,128)S(1)}, u32[]{:S(2)}, u32[]{:S(2)}) collective-permute-start(f32[32,32,128]{2,1,0:T(8,128)} %get-tuple-element.64), channel_id=1, source_target_pairs={{0,8},{8,0},{16,24},{24,16},{1,9},{9,1},{17,25},{25,17},{2,10},{10... | collective-permute-start | bytes 1572872 | tf_op jit(solution)/shard_map/ppermute | solution.py:681
  189.1 15.0 %collective-permute-start.23 = (f32[32,32,128]{2,1,0:T(8,128)}, f32[32,32,128]{2,1,0:T(8,128)S(1)}, u32[]{:S(2)}, u32[]{:S(2)}) collective-permute-start(f32[32,32,128]{2,1,0:T(8,128)} %get-tuple-element.65), channel_id=1, source_target_pairs={{0,16},{8,24},{16,0},{24,8},{1,17},{9,25},{17,1},{25,9},{2,18},{10... | collective-permute-start | bytes 1572872 | tf_op jit(solution)/shard_map/ppermute | solution.py:681
  190.6 23.3 %collective-permute-start.24 = (f32[32,32,128]{2,1,0:T(8,128)}, f32[32,32,128]{2,1,0:T(8,128)S(1)}, u32[]{:S(2)}, u32[]{:S(2)}) collective-permute-start(f32[32,32,128]{2,1,0:T(8,128)} %get-tuple-element.66), channel_id=1, source_target_pairs={{0,24},{8,16},{16,8},{24,0},{1,25},{9,17},{17,9},{25,1},{2,26},{10... | collective-permute-start | bytes 1572872 | tf_op jit(solution)/shard_map/ppermute | solution.py:681
  190.7 5.5 %collective-permute-start.18 = (f32[4,1,1,1,8,128]{5,4,0,3,2,1:T(8,128)S(1)}, f32[4,1,1,1,8,128]{5,4,0,3,2,1:T(8,128)S(1)}, u32[]{:S(2)}, u32[]{:S(2)}) collective-permute-start(f32[4,1,1,1,8,128]{5,4,0,3,2,1:T(8,128)S(1)} %get-tuple-element.72), channel_id=1, source_target_pairs={{0,6},{1,7},{2,4},{3,5},{4,2},{5,3},{6,0},{7,1},{8,14},{9,15},{10,... | collective-permute-start | bytes 49160 | tf_op jit(solution)/shard_map/ppermute | solution.py:530
  194.5 4.6 %collective-permute-start.17 = (f32[4,1,1,1,8,128]{5,4,0,3,2,1:T(8,128)S(1)}, f32[4,1,1,1,8,128]{5,4,0,3,2,1:T(8,128)S(1)}, u32[]{:S(2)}, u32[]{:S(2)}) collective-permute-start(f32[4,1,1,1,8,128]{5,4,0,3,2,1:T(8,128)S(1)} %get-tuple-element.73), channel_id=1, source_target_pairs={{0,4},{1,5},{2,6},{3,7},{4,0},{5,1},{6,2},{7,3},{8,12},{9,13},{10,... | collective-permute-start | bytes 49160 | tf_op jit(solution)/shard_map/ppermute | solution.py:530

commit v6 on v5

--- a/solution.py
+++ b/solution.py
@@ -359,20 +359,38 @@
     return [operand, product, operand, product] * count
 
 
-def pack_kernel(lit_ref, x_ref, o_ref, *, units, slots):
+def pack_kernel(count_ref, x_hbm, o_hbm, x_ref, o_ref, sems, *, units, slots, channels):
     rows = 2 * slots
     span = o_ref.shape[1] // rows
-    first = pl.program_id(0) * o_ref.shape[0] * units
-    for g in range(o_ref.shape[0]):
-        if units < slots:
-            o_ref[g] = jnp.zeros(o_ref.shape[1:], jnp.float32)
-        for u in range(units):
-            channel = g * units + u
-            lit = lit_ref[first + channel] > 0
-            for p in range(2):
-                at = (channel * 2 + p) * span
-                value = jnp.where(lit, x_ref[at : at + span, :], 0.0)
-                o_ref[g, pl.ds(p * slots + u, span, stride=rows), :] = value
+    strips = sems.shape[1]
+    length, devices = x_ref.shape[0] // strips, o_ref.shape[0] // strips
+    base = lax.axis_index("wave") * channels
+
+    def copy_in(i):
+        at = pl.ds(i * length, length)
+        return pltpu.make_async_copy(x_hbm.at[at], x_ref.at[at], sems.at[0, i])
+
+    def copy_out(i):
+        at = pl.ds(i * devices, devices)
+        return pltpu.make_async_copy(o_ref.at[at], o_hbm.at[at], sems.at[1, i])
+
+    for i in range(strips):
+        copy_in(i).start()
+    for i in range(strips):
+        copy_in(i).wait()
+        for g in range(i * devices, (i + 1) * devices):
+            if units < slots:
+                o_ref[g] = jnp.zeros(o_ref.shape[1:], jnp.float32)
+            for u in range(units):
+                unit = g * units + u
+                lit = base + unit % channels < count_ref[unit // channels]
+                for p in range(2):
+                    at = (unit * 2 + p) * span
+                    value = jnp.where(lit, x_ref[at : at + span, :], 0.0)
+                    o_ref[g, pl.ds(p * slots + u, span, stride=rows), :] = value
+        copy_out(i).start()
+    for i in range(strips):
+        copy_out(i).wait()
 
 
 def send_kernel(item_ref, count_ref, x_ref, *refs, units, slots):
@@ -405,7 +423,7 @@
 
 
 def place_kernel(from_ref, strength_ref, q_ref, *refs, channels_total, sources):
-    in_refs, (o_ref, held_ref, sems) = refs[: 2 * sources], refs[2 * sources :]
+    in_refs, (o_hbm, o_ref, held_ref, sems, out_sems) = refs[: 2 * sources], refs[2 * sources :]
     capacity, near = in_refs[0].shape[0], in_refs[0].shape[1] // (2 * BLK)
     copies = []
     for p in range(2):
@@ -421,6 +439,7 @@
         copy.start()
     for copy in copies:
         copy.wait()
+    copies = []
     fibres = q_ref.shape[0]
     group_blocks = o_ref.shape[0] // fibres
     for f in range(fibres):
@@ -449,6 +468,11 @@
             return carry
 
         lax.fori_loop(0, group_blocks, body, 0, unroll=4)
+        at = pl.ds(f * group_blocks, group_blocks)
+        copies.append(pltpu.make_async_copy(o_ref.at[at], o_hbm.at[at], out_sems.at[f]))
+        copies[-1].start()
+    for copy in copies:
+        copy.wait()
 
 
 def params(*shapes):
@@ -572,31 +596,33 @@
     wave_bits = [times << b for b in range(groups.bit_length() - 1)]
     time_bits = [1 << b for b in range(times.bit_length() - 1)]
     wave_rounds = [(bit,) for bit in wave_bits]
-    all_rounds = wave_rounds + [(bit,) for bit in time_bits]
+    all_rounds = [(bit,) for bit in wave_bits + time_bits]
     shared = channels // units if same_fibre else 0
     fibre_bits = wave_bits + time_bits[: max(shared.bit_length() - 1, 0)]
     fibre_rounds = [tuple(fibre_bits[:1])]
     fibre_rounds += [tuple(fibre_bits[i : i + 2]) for i in range(1, len(fibre_bits), 2)]
 
-    lit_mask = (my_group * channels + jnp.arange(channels))[None, :] < lit_count[:, None]
-    lit = lit_mask.reshape(-1).astype(jnp.int32)
-
     def natural_rows(values):
         split = values.reshape(fibres, channels, 2, 2, near, FB)
         return split.transpose(0, 1, 2, 4, 3, 5).reshape(-1, FB)
 
     strips = math.gcd(times, 4)
-    block = (times // strips, 2 * near * rows, FB)
+    in_hbm = pl.BlockSpec(memory_space=pltpu.HBM)
     natural = pltpu.with_memory_space_constraint(natural_rows(field), pltpu.HBM)
+    shape = (times, 2 * near * rows, FB)
     packed = pl.pallas_call(
-        functools.partial(pack_kernel, units=units, slots=slots),
-        out_shape=pltpu.HBM((times,) + block[1:], jnp.float32),
-        grid=(strips,),
-        in_specs=[in_smem(), pl.BlockSpec((natural.shape[0] // strips, FB), lambda i: (i, 0))],
-        out_specs=pl.BlockSpec(block, lambda i: (i, 0, 0)),
-        compiler_params=params(field.shape, block, block),
+        functools.partial(pack_kernel, units=units, slots=slots, channels=channels),
+        out_shape=pltpu.HBM(shape, jnp.float32),
+        in_specs=[in_smem(), in_hbm],
+        out_specs=in_hbm,
+        scratch_shapes=[
+            pltpu.VMEM(natural.shape, jnp.float32),
+            pltpu.VMEM(shape, jnp.float32),
+            pltpu.SemaphoreType.DMA((2, strips)),
+        ],
+        compiler_params=params(field.shape, shape),
         name="pack",
-    )(lit, natural)
+    )(lit_count, natural)
     wave_form = lax.all_to_all(packed, "tm", split_axis=0, concat_axis=0, tiled=True)
     wave_form = wave_form.reshape(chunks, 2, rows, FB)
 
@@ -650,8 +676,15 @@
     for step in range(2 * HALF - 1):
         fibres_out = 1 if (step < HALF and same_fibre) else fibres
         wave_form, partial = dispersed(wave_form, step, total, q_fibres, fibres_out, False)
-        rounds = fibre_rounds if fibres_out == 1 else all_rounds
-        total, q_fibres = summed(partial, rounds), fibres_out
+        if fibres_out == 1:
+            total = summed(partial, fibre_rounds)
+        else:
+            cut = fibres_out // 2
+            there, back = all_rounds, all_rounds[:1] + all_rounds[:0:-1]
+            total = jnp.concatenate(
+                [summed(partial[:cut], there), summed(partial[cut:], back)], axis=0
+            )
+        q_fibres = fibres_out
 
     last = 2 * HALF - 1
 
@@ -698,15 +731,17 @@
     strength = jnp.broadcast_to(nonlinearity[1][:, None, None], (fibres, near, FB))
     placed = pl.pallas_call(
         functools.partial(place_kernel, channels_total=channels_total, sources=groups),
-        out_shape=jax.ShapeDtypeStruct((sends, BLK * 4 * near, FB), jnp.float32),
+        out_shape=pltpu.HBM((sends, BLK * 4 * near, FB), jnp.float32),
         in_specs=[in_smem(), in_vmem(), in_vmem()]
         + [pl.BlockSpec(memory_space=pl.ANY)] * (2 * groups),
-        out_specs=in_vmem(),
+        out_specs=in_hbm,
         scratch_shapes=[
+            pltpu.VMEM((sends, BLK * 4 * near, FB), jnp.float32),
             pltpu.VMEM((2, groups * capacity, BLK * 2 * near, FB), jnp.float32),
             pltpu.SemaphoreType.DMA((2, groups)),
+            pltpu.SemaphoreType.DMA((fibres,)),
         ],
-        compiler_params=params(field.shape, (2, groups * capacity, BLK * 2 * near, FB)),
+        compiler_params=params(field.shape, field.shape, (2, groups * capacity, BLK * 2 * near, FB)),
         cost_estimate=cost(0, 4 * 4 * field.size),
         name="place",
     )(take_from, strength, own_total, *blocks)

time: 219 us -> 217 us (level)
  waiting for transfers between devices: 125 us -> 122 us
    ppermute x15 -> x20, waiting for transfers between devices: 31.6 us -> 28.6 us  [summed(): lax.ppermute(values, ('wave', 'tm'), [(i, i ^ mask) for i in range(size)])]
    ppermute x15 -> x20, starting transfers between devices: 12.9 us -> 14.6 us  [summed(): lax.ppermute(values, ('wave', 'tm'), [(i, i ^ mask) for i in range(size)])]
  transfers between devices with their start and end apart: 28 -> 33, of which waited for: 24 -> 29; matrix products, arithmetic and copies ran while one was open for 3% -> 3% of each run, Pallas kernels for 2% -> 2%
where the time goes in v6:
time: 217 us; the launch traced here: 216 us
  waiting for transfers between devices  122 us (56%)
  Pallas kernels  44.6 us (21%)
  starting transfers between devices  41 us (19%)
  local copies, waits for them, and re-layouts  5.48 us (3%)
    all_to_all x1, waiting for transfers between devices, local(): lax.all_to_all(packed, 'tm', split_axis=0, concat_axis=0, tiled=True)  44.2 us
    ppermute x6, waiting for transfers between devices, to_groups(): lax.ppermute(outgoing[s], 'wave', [(i, i ^ s) for i in range(groups)])  35.9 us
    pallas_call x5, Pallas kernels, dispersed(): pl.pallas_call(functools.partial(step_kernel, rotate=rotate, hold=hold, f...  31.2 us
    ppermute x20, waiting for transfers between devices, summed(): lax.ppermute(values, ('wave', 'tm'), [(i, i ^ mask) for i in range(size)])  28.6 us
    ppermute x20, starting transfers between devices, summed(): lax.ppermute(values, ('wave', 'tm'), [(i, i ^ mask) for i in range(size)])  14.6 us
    ppermute x4, starting transfers between devices, time_parts(): part = lax.ppermute(part, 'tm', [(i, i ^ mask) for i in range(times)])  7.74 us
    all_to_all x2, starting transfers between devices, to_times(): return lax.all_to_all(values, 'tm', split_axis=0, concat_axis=0, tiled=True)  7.44 us
    all_to_all x1, starting transfers between devices, local(): lax.all_to_all(packed, 'tm', split_axis=0, concat_axis=0, tiled=True)  7.4 us
  transfers between devices with their start and end apart: 33, of which 29 were waited for; matrix products, arithmetic and copies ran while one was open for 3% of the time, Pallas kernels for 2%

profile of v6, /device:TPU:0, one launch (start us, length us, event | category | flops | bytes accessed | tf_op | source)
XLA Modules:
  0.0 215.8 jit_solution(16105422035339348072)
XLA Ops:
  0.7 4.1 %pack.1 = f32[8,512,128]{2,1,0:T(8,128)} custom-call(s32[4]{0:T(128)S(1)} %copy-done.3, f32[4096,128]{1,0:T(8,128)} %bitcast.43), custom_call_target="tpu_custom_call" | custom-call | tf_op jit(solution)/shard_map/pack/pallas_call | solution.py:613
  4.8 7.4 %all-to-all-start = ((f32[8,512,128]{2,1,0:T(8,128)}), f32[8,512,128]{2,1,0:T(8,128)S(1)}, u32[]{:S(2)}, u32[]{:S(2)}) async-start(f32[8,512,128]{2,1,0:T(8,128)} %pack.1), calls=%async_computation | async-start | bytes 4194304 | tf_op jit(solution)/shard_map/all_to_all | solution.py:626
  15.2 1.0 sine_multiply_fusion
  16.2 44.2 %all-to-all-done = f32[8,512,128]{2,1,0:T(8,128)S(1)} async-done(((f32[8,512,128]{2,1,0:T(8,128)}), f32[8,512,128]{2,1,0:T(8,128)S(1)}, u32[]{:S(2)}, u32[]{:S(2)}) %all-to-all-start) | async-done | bytes 2097184 | tf_op jit(solution)/shard_map/all_to_all | solution.py:626
  60.5 6.5 %step.5 = (f32[64,2,32,128]{3,2,1,0:T(8,128)}, f32[1,64,128]{2,1,0:T(8,128)S(1)}) custom-call(f32[64,2,32,128]{3,2,1,0:T(8,128)S(1)} %bitcast.42, f32[4,16,128]{2,1,0:T(8,128)S(1)} %broadcast_in_dim.32.refs_1_.refs_2_.refs_4_, f32[16,16,128]{2,1,0:T(8,128)S(1)} %get-tuple-element.82.refs_2_.refs_5_, f32[16,16,128]{2,1,0:T(8,128)S(1)} %get-tuple-element.83.refs_3_.refs_6_, ...), custom_call_target="tpu_custom_call" | custom-call | flops 1677721600 | bytes 8388608 | tf_op jit(solution)/shard_map/step/pallas_call | solution.py:660
  67.1 1.2 collective-permute-done
  68.3 2.4 %collective-permute-start.3 = (f32[1,64,128]{2,1,0:T(8,128)S(1)}, f32[1,64,128]{2,1,0:T(8,128)S(1)}, u32[]{:S(2)}, u32[]{:S(2)}) collective-permute-start(f32[1,64,128]{2,1,0:T(8,128)S(1)} %add.378), channel_id=1, source_target_pairs={{0,17},{1,16},{2,19},{3,18},{4,21},{5,20},{6,23},{7,22},{8,25},{9,... | collective-permute-start | bytes 98312 | tf_op jit(solution)/shard_map/ppermute | solution.py:503
  73.1 1.5 collective-permute-done.2
  75.3 7.7 %step.6 = (f32[64,2,32,128]{3,2,1,0:T(8,128)S(1)}, f32[1,64,128]{2,1,0:T(8,128)S(1)}) custom-call(f32[64,2,32,128]{3,2,1,0:T(8,128)} %get-tuple-element.36.refs_0_, f32[1,64,128]{2,1,0:T(8,128)S(1)} %add_add_fusion.1.refs_1_, f32[4,16,128]{2,1,0:T(8,128)S(1)} %broadcast_in_dim.32.refs_1_.refs_2_.refs_4_, f32[16,128]{1,0:T(8,128)S(1)} %broadcast_in_dim.33.refs_3_, ...), custom_call_target="tpu_custom_call" | custom-call | flops 1677721600 | bytes 8388608 | tf_op jit(solution)/shard_map/step/pallas_call | solution.py:660
  83.1 1.2 collective-permute-done.4
  84.3 1.4 collective-permute-start.7
  86.3 1.5 collective-permute-start.5
  87.8 1.4 collective-permute-done.7
  90.3 7.0 %step.7 = (f32[64,2,32,128]{3,2,1,0:T(8,128)S(1)}, f32[4,64,128]{2,1,0:T(8,128)S(1)}) custom-call(f32[64,2,32,128]{3,2,1,0:T(8,128)S(1)} %get-tuple-element.38.refs_0_, f32[1,64,128]{2,1,0:T(8,128)S(1)} %add_add_fusion.refs_1_, f32[4,16,128]{2,1,0:T(8,128)S(1)} %broadcast_in_dim.32.refs_1_.refs_2_.refs_4_, f32[16,128]{1,0:T(8,128)S(1)} %broadcast_in_dim.33.refs_3_, ...), custom_call_target="tpu_custom_call" | custom-call | flops 1677721600 | bytes 8388608 | tf_op jit(solution)/shard_map/step/pallas_call | solution.py:660
  97.9 0.7 collective-permute-done.8
  98.8 1.6 collective-permute-start.9
  100.4 2.8 %collective-permute-done.9 = f32[2,64,128]{2,1,0:T(8,128)S(1)} collective-permute-done((f32[2,64,128]{2,1,0:T(8,128)S(1)}, f32[2,64,128]{2,1,0:T(8,128)S(1)}, u32[]{:S(2)}, u32[]{:S(2)}) %collective-permute-start.9) | collective-permute-done | bytes 65568 | tf_op jit(solution)/shard_map/ppermute | solution.py:503
  103.2 1.5 collective-permute-start.10
  104.8 1.6 collective-permute-done.14
  106.5 1.1 collective-permute-done.10
  107.6 1.0 collective-permute-start.11
  108.6 2.6 %collective-permute-done.15 = f32[2,64,128]{2,1,0:T(8,128)S(1)} collective-permute-done((f32[2,64,128]{2,1,0:T(8,128)S(1)}, f32[2,64,128]{2,1,0:T(8,128)S(1)}, u32[]{:S(2)}, u32[]{:S(2)}) %collective-permute-start.15) | collective-permute-done | bytes 65568 | tf_op jit(solution)/shard_map/ppermute | solution.py:503
  111.9 1.1 collective-permute-start.12
  113.0 2.5 %collective-permute-done.16 = f32[2,64,128]{2,1,0:T(8,128)S(1)} collective-permute-done((f32[2,64,128]{2,1,0:T(8,128)S(1)}, f32[2,64,128]{2,1,0:T(8,128)S(1)}, u32[]{:S(2)}, u32[]{:S(2)}) %collective-permute-start.16) | collective-permute-done | bytes 65568 | tf_op jit(solution)/shard_map/ppermute | solution.py:503
  116.8 1.1 collective-permute-done.12
  117.9 2.0 collective-permute-done.17
  120.0 6.2 %step.8 = (f32[64,2,16,128]{3,2,1,0:T(8,128)}, f32[4,64,128]{2,1,0:T(8,128)S(1)}, f32[64,2,16,128]{3,2,1,0:T(8,128)}) custom-call(f32[64,2,32,128]{3,2,1,0:T(8,128)S(1)} %get-tuple-element.40.refs_0_, f32[4,64,128]{2,1,0:T(8,128)S(1)} %pad_maximum_fusion.refs_1_, f32[4,16,128]{2,1,0:T(8,128)S(1)} %broadcast_in_dim.34.refs_4_.refs_2_.refs_1_, ...), custom_call_target="tpu_custom_call" | custom-call | flops 838860800 | bytes 8388608 | tf_op jit(solution)/shard_map/step/pallas_call | solution.py:660
  126.2 3.9 %all-to-all-start.1 = ((f32[8,256,128]{2,1,0:T(8,128)}), f32[8,256,128]{2,1,0:T(8,128)S(1)}, u32[]{:S(2)}, u32[]{:S(2)}) async-start(f32[8,256,128]{2,1,0:T(8,128)} %bitcast.44), calls=%async_computation.1 | async-start | bytes 2097152 | tf_op jit(solution)/shard_map/all_to_all | solution.py:693
  130.2 3.9 %step.9 = (f32[64,2,16,128]{3,2,1,0:T(8,128)}, f32[4,64,128]{2,1,0:T(8,128)S(1)}) custom-call(f32[64,2,16,128]{3,2,1,0:T(8,128)S(1)} %copy-done.4, f32[4,16,128]{2,1,0:T(8,128)S(1)} %broadcast_in_dim.34.refs_4_.refs_2_.refs_1_, f32[16,16,128]{2,1,0:T(8,128)S(1)} %get-tuple-element.79.refs_5_.refs_2_, f32[16,16,128]{2,1,0:T(8,128)S(1)} %get-tuple-element.78.refs_6_.refs_3_, ...), custom_call_target="tpu_custom_call" | custom-call | flops 838860800 | bytes 4194304 | tf_op jit(solution)/shard_map/step/pallas_call | solution.py:660
  134.5 1.1 collective-permute-done.18
  136.3 4.9 %collective-permute-done.19 = f32[4,64,128]{2,1,0:T(8,128)S(1)} collective-permute-done((f32[4,64,128]{2,1,0:T(8,128)S(1)}, f32[4,64,128]{2,1,0:T(8,128)S(1)}, u32[]{:S(2)}, u32[]{:S(2)}) %collective-permute-start.19) | collective-permute-done | bytes 131104 | tf_op jit(solution)/shard_map/ppermute | solution.py:503
  141.3 2.1 collective-permute-start.20
  143.5 2.1 collective-permute-done.20
  145.6 6.7 %all-to-all-done.1.x_ref = f32[8,256,128]{2,1,0:T(8,128)S(1)} async-done(((f32[8,256,128]{2,1,0:T(8,128)}), f32[8,256,128]{2,1,0:T(8,128)S(1)}, u32[]{:S(2)}, u32[]{:S(2)}) %all-to-all-start.1) | async-done | bytes 1048608 | tf_op jit(solution)/shard_map/all_to_all | solution.py:693
  152.3 2.7 %send.2 = (f32[32,32,128]{2,1,0:T(8,128)}, f32[32,32,128]{2,1,0:T(8,128)}, f32[32,32,128]{2,1,0:T(8,128)}, f32[32,32,128]{2,1,0:T(8,128)}) custom-call(s32[128]{0:T(128)S(1)} %select_reduce_fusion.1.item_ref, s32[4]{0:T(128)S(1)} %convert_reduce_fusion.1.count_ref, f32[8,256,128]{2,1,0:T(8,128)S(1)} %all-to-all-done.1.x_ref), custom_call_target="tpu_custom_call" | custom-call | bytes 4194304 | tf_op jit(solution)/shard_map/send/pallas_call | solution.py:697
  155.0 3.6 %all-to-all-start.2 = ((f32[8,256,128]{2,1,0:T(8,128)}), f32[8,256,128]{2,1,0:T(8,128)S(1)}, u32[]{:S(2)}, u32[]{:S(2)}) async-start(f32[8,256,128]{2,1,0:T(8,128)} %bitcast.19), calls=%async_computation.2 | async-start | bytes 2097152 | tf_op jit(solution)/shard_map/all_to_all | solution.py:693
  158.7 0.8 collective-permute-start.25
  159.5 1.1 collective-permute-start.26
  160.7 1.9 collective-permute-start.21
  162.6 11.0 %collective-permute-done.25.refs_2_ = f32[32,32,128]{2,1,0:T(8,128)S(1)} collective-permute-done((f32[32,32,128]{2,1,0:T(8,128)}, f32[32,32,128]{2,1,0:T(8,128)S(1)}, u32[]{:S(2)}, u32[]{:S(2)}) %collective-permute-start.25) | collective-permute-done | bytes 524320 | tf_op jit(solution)/shard_map/ppermute | solution.py:714
  173.7 10.3 %collective-permute-done.26.refs_3_ = f32[32,32,128]{2,1,0:T(8,128)S(1)} collective-permute-done((f32[32,32,128]{2,1,0:T(8,128)}, f32[32,32,128]{2,1,0:T(8,128)S(1)}, u32[]{:S(2)}, u32[]{:S(2)}) %collective-permute-start.26) | collective-permute-done | bytes 524320 | tf_op jit(solution)/shard_map/ppermute | solution.py:714
  184.0 2.7 %send.3 = (f32[32,32,128]{2,1,0:T(8,128)}, f32[32,32,128]{2,1,0:T(8,128)}, f32[32,32,128]{2,1,0:T(8,128)}, f32[32,32,128]{2,1,0:T(8,128)}) custom-call(s32[128]{0:T(128)S(1)} %select_reduce_fusion.1.item_ref, s32[4]{0:T(128)S(1)} %convert_reduce_fusion.1.count_ref, f32[8,256,128]{2,1,0:T(8,128)S(1)} %all-to-all-done.2.x_ref), custom_call_target="tpu_custom_call" | custom-call | bytes 4194304 | tf_op jit(solution)/shard_map/send/pallas_call | solution.py:697
  188.7 3.7 %collective-permute-start.23 = (f32[4,1,1,1,8,128]{5,4,0,3,2,1:T(8,128)S(1)}, f32[4,1,1,1,8,128]{5,4,0,3,2,1:T(8,128)S(1)}, u32[]{:S(2)}, u32[]{:S(2)}) collective-permute-start(f32[4,1,1,1,8,128]{5,4,0,3,2,1:T(8,128)S(1)} %get-tuple-element.76), channel_id=1, source_target_pairs={{0,6},{1,7},{2,4},{3,5},{4,2},{5,3},{6,0},{7,1},{8,14},{9,15},{10,... | collective-permute-start | bytes 49160 | tf_op jit(solution)/shard_map/ppermute | solution.py:554
  192.6 1.7 collective-permute-done.23
  194.3 2.8 %collective-permute-done.22 = f32[4,1,1,1,8,128]{5,4,0,3,2,1:T(8,128)S(1)} collective-permute-done((f32[4,1,1,1,8,128]{5,4,0,3,2,1:T(8,128)S(1)}, f32[4,1,1,1,8,128]{5,4,0,3,2,1:T(8,128)S(1)}, u32[]{:S(2)}, u32[]{:S(2)}) %collective-permute-start.22) | collective-permute-done | bytes 16416 | tf_op jit(solution)/shard_map/ppermute | solution.py:554
  197.1 5.1 %collective-permute-done.28.refs_6_ = f32[32,32,128]{2,1,0:T(8,128)S(1)} collective-permute-done((f32[32,32,128]{2,1,0:T(8,128)}, f32[32,32,128]{2,1,0:T(8,128)S(1)}, u32[]{:S(2)}, u32[]{:S(2)}) %collective-permute-start.28) | collective-permute-done | bytes 524320 | tf_op jit(solution)/shard_map/ppermute | solution.py:714
  202.2 9.5 %collective-permute-done.29.refs_7_ = f32[32,32,128]{2,1,0:T(8,128)S(1)} collective-permute-done((f32[32,32,128]{2,1,0:T(8,128)}, f32[32,32,128]{2,1,0:T(8,128)S(1)}, u32[]{:S(2)}, u32[]{:S(2)}) %collective-permute-start.29) | collective-permute-done | bytes 524320 | tf_op jit(solution)/shard_map/ppermute | solution.py:714
  211.7 3.9 %place.1 = f32[64,64,128]{2,1,0:T(8,128)} custom-call(s32[64]{0:T(128)S(1)} %select_reduce_fusion.from_ref, f32[4,8,128]{2,1,0:T(8,128)S(1)} %broadcast_in_dim.31.strength_ref, f32[4,8,128]{2,1,0:T(8,128)S(1)} %add_bitcast_fusion.q_ref, f32[32,32,128]{2,1,0:T(8,128)} %get-tuple-element.58.refs_0_, f32[32,32,128]{2,1,0:T(8,128)S(1)} %collective-permute-done.24.refs_1_, ...), custom_call_target="tpu_custom_call" | custom-call | bytes 8388608 | tf_op jit(solution)/shard_map/place/pallas_call | solution.py:732
  (110 shorter events, 15.3 us)
Async XLA Ops:
  0.0 0.7 copy-start.3
  4.8 7.5 %copy-start.6 = (s32[4,64]{1,0:T(4,128)S(1)}, s32[4,64]{1,0:T(4,128)}, u32[]{:S(2)}) copy-start(s32[4,64]{1,0:T(4,128)} %param.13) | copy-start | bytes 3076
  4.8 8.2 %copy-start.5 = (s32[4,64]{1,0:T(4,128)S(1)}, s32[4,64]{1,0:T(4,128)}, u32[]{:S(2)}) copy-start(s32[4,64]{1,0:T(4,128)} %param.14) | copy-start | bytes 3076
  4.8 8.9 %copy-start.9 = (f32[2,4]{1,0:T(2,128)S(1)}, f32[2,4]{1,0:T(2,128)}, u32[]{:S(2)}) copy-start(f32[2,4]{1,0:T(2,128)} %param.15) | copy-start | bytes 100
  4.8 55.6 %all-to-all-start = ((f32[8,512,128]{2,1,0:T(8,128)}), f32[8,512,128]{2,1,0:T(8,128)S(1)}, u32[]{:S(2)}, u32[]{:S(2)}) async-start(f32[8,512,128]{2,1,0:T(8,128)} %pack.1), calls=%async_computation | async-start | bytes 4194304 | tf_op jit(solution)/shard_map/all_to_all | solution.py:626
  12.2 3.0 %copy-start.7 = (f32[16,128]{1,0:T(8,128)S(1)}, f32[16,128]{1,0:T(8,128)}, u32[]{:S(2)}) copy-start(f32[16,128]{1,0:T(8,128)} %constant.274) | copy-start | bytes 24580
  12.2 3.0 %copy-start.8 = (f32[16,128]{1,0:T(8,128)S(1)}, f32[16,128]{1,0:T(8,128)}, u32[]{:S(2)}) copy-start(f32[16,128]{1,0:T(8,128)} %constant.273) | copy-start | bytes 24580
  12.2 48.3 %copy-start = (bf16[512,256]{1,0:T(8,128)(2,1)S(1)}, bf16[512,256]{1,0:T(8,128)(2,1)}, u32[]{:S(2)}) copy-start(bf16[512,256]{1,0:T(8,128)(2,1)} %constant.270.clone.refs_6_.refs_9_) | copy-start | bytes 786436
  12.2 48.3 %copy-start.1 = (bf16[512,256]{1,0:T(8,128)(2,1)S(1)}, bf16[512,256]{1,0:T(8,128)(2,1)}, u32[]{:S(2)}) copy-start(bf16[512,256]{1,0:T(8,128)(2,1)} %constant.269.clone.refs_5_.refs_8_) | copy-start | bytes 786436
  12.3 48.3 %copy-start.2 = (f32[2,16,8,128]{3,2,1,0:T(8,128)S(1)}, f32[2,16,8,128]{3,2,1,0:T(8,128)}, u32[]{:S(2)}) copy-start(f32[2,16,8,128]{3,2,1,0:T(8,128)} %constant.268.clone.refs_4_.refs_7_) | copy-start | bytes 393220
  60.5 11.2 %copy-start.10 = (f32[2,4]{1,0:T(2,128)S(1)}, f32[2,4]{1,0:T(2,128)}, u32[]{:S(2)}) copy-start(f32[2,4]{1,0:T(2,128)} %param.16) | copy-start | bytes 100
  67.0 1.3 collective-permute-start
  68.3 4.8 %collective-permute-start.3 = (f32[1,64,128]{2,1,0:T(8,128)S(1)}, f32[1,64,128]{2,1,0:T(8,128)S(1)}, u32[]{:S(2)}, u32[]{:S(2)}) collective-permute-start(f32[1,64,128]{2,1,0:T(8,128)S(1)} %add.378), channel_id=1, source_target_pairs={{0,17},{1,16},{2,19},{3,18},{4,21},{5,20},{6,23},{7,22},{8,25},{9,... | collective-permute-start | bytes 98312 | tf_op jit(solution)/shard_map/ppermute | solution.py:503
  70.7 3.9 %collective-permute-start.2 = (f32[1,64,128]{2,1,0:T(8,128)S(1)}, f32[1,64,128]{2,1,0:T(8,128)S(1)}, u32[]{:S(2)}, u32[]{:S(2)}) collective-permute-start(f32[1,64,128]{2,1,0:T(8,128)S(1)} %add.378), channel_id=1, source_target_pairs={{0,1},{1,0},{2,3},{3,2},{4,5},{5,4},{6,7},{7,6},{8,9},{9,8},{10,11... | collective-permute-start | bytes 98312 | tf_op jit(solution)/shard_map/ppermute | solution.py:503
  71.3 3.9 %collective-permute-start.1 = (f32[1,64,128]{2,1,0:T(8,128)S(1)}, f32[1,64,128]{2,1,0:T(8,128)S(1)}, u32[]{:S(2)}, u32[]{:S(2)}) collective-permute-start(f32[1,64,128]{2,1,0:T(8,128)S(1)} %add.378), channel_id=1, source_target_pairs={{0,16},{1,17},{2,18},{3,19},{4,20},{5,21},{6,22},{7,23},{8,24},{9,... | collective-permute-start | bytes 98312 | tf_op jit(solution)/shard_map/ppermute | solution.py:503
  83.0 1.3 collective-permute-start.4
  84.3 4.9 %collective-permute-start.7 = (f32[1,64,128]{2,1,0:T(8,128)S(1)}, f32[1,64,128]{2,1,0:T(8,128)S(1)}, u32[]{:S(2)}, u32[]{:S(2)}) collective-permute-start(f32[1,64,128]{2,1,0:T(8,128)S(1)} %add.382), channel_id=1, source_target_pairs={{0,17},{1,16},{2,19},{3,18},{4,21},{5,20},{6,23},{7,22},{8,25},{9,... | collective-permute-start | bytes 98312 | tf_op jit(solution)/shard_map/ppermute | solution.py:503
  85.7 3.9 %collective-permute-start.6 = (f32[1,64,128]{2,1,0:T(8,128)S(1)}, f32[1,64,128]{2,1,0:T(8,128)S(1)}, u32[]{:S(2)}, u32[]{:S(2)}) collective-permute-start(f32[1,64,128]{2,1,0:T(8,128)S(1)} %add.382), channel_id=1, source_target_pairs={{0,1},{1,0},{2,3},{3,2},{4,5},{5,4},{6,7},{7,6},{8,9},{9,8},{10,11... | collective-permute-start | bytes 98312 | tf_op jit(solution)/shard_map/ppermute | solution.py:503
  86.3 3.9 %collective-permute-start.5 = (f32[1,64,128]{2,1,0:T(8,128)S(1)}, f32[1,64,128]{2,1,0:T(8,128)S(1)}, u32[]{:S(2)}, u32[]{:S(2)}) collective-permute-start(f32[1,64,128]{2,1,0:T(8,128)S(1)} %add.382), channel_id=1, source_target_pairs={{0,16},{1,17},{2,18},{3,19},{4,20},{5,21},{6,22},{7,23},{8,24},{9,... | collective-permute-start | bytes 98312 | tf_op jit(solution)/shard_map/ppermute | solution.py:503
  97.3 1.3 collective-permute-start.8
  97.4 1.4 collective-permute-start.13
  98.8 4.4 %collective-permute-start.9 = (f32[2,64,128]{2,1,0:T(8,128)S(1)}, f32[2,64,128]{2,1,0:T(8,128)S(1)}, u32[]{:S(2)}, u32[]{:S(2)}) collective-permute-start(f32[2,64,128]{2,1,0:T(8,128)S(1)} %get-tuple-element.71), channel_id=1, source_target_pairs={{0,16},{1,17},{2,18},{3,19},{4,20},{5,21},{6,22},{7,23},{8,24},{9,... | collective-permute-start | bytes 196616 | tf_op jit(solution)/shard_map/ppermute | solution.py:503
  100.4 6.0 %collective-permute-start.14 = (f32[2,64,128]{2,1,0:T(8,128)S(1)}, f32[2,64,128]{2,1,0:T(8,128)S(1)}, u32[]{:S(2)}, u32[]{:S(2)}) collective-permute-start(f32[2,64,128]{2,1,0:T(8,128)S(1)} %get-tuple-element.72), channel_id=1, source_target_pairs={{0,4},{1,5},{2,6},{3,7},{4,0},{5,1},{6,2},{7,3},{8,12},{9,13},{10,... | collective-permute-start | bytes 196616 | tf_op jit(solution)/shard_map/ppermute | solution.py:503
  103.2 4.3 %collective-permute-start.10 = (f32[2,64,128]{2,1,0:T(8,128)S(1)}, f32[2,64,128]{2,1,0:T(8,128)S(1)}, u32[]{:S(2)}, u32[]{:S(2)}) collective-permute-start(f32[2,64,128]{2,1,0:T(8,128)S(1)} %add.396), channel_id=1, source_target_pairs={{0,1},{1,0},{2,3},{3,2},{4,5},{5,4},{6,7},{7,6},{8,9},{9,8},{10,11... | collective-permute-start | bytes 196616 | tf_op jit(solution)/shard_map/ppermute | solution.py:503
  106.4 4.8 %collective-permute-start.15 = (f32[2,64,128]{2,1,0:T(8,128)S(1)}, f32[2,64,128]{2,1,0:T(8,128)S(1)}, u32[]{:S(2)}, u32[]{:S(2)}) collective-permute-start(f32[2,64,128]{2,1,0:T(8,128)S(1)} %add.401), channel_id=1, source_target_pairs={{0,2},{1,3},{2,0},{3,1},{4,6},{5,7},{6,4},{7,5},{8,10},{9,11},{10,... | collective-permute-start | bytes 196616 | tf_op jit(solution)/shard_map/ppermute | solution.py:503
  107.6 4.3 %collective-permute-start.11 = (f32[2,64,128]{2,1,0:T(8,128)S(1)}, f32[2,64,128]{2,1,0:T(8,128)S(1)}, u32[]{:S(2)}, u32[]{:S(2)}) collective-permute-start(f32[2,64,128]{2,1,0:T(8,128)S(1)} %add.397), channel_id=1, source_target_pairs={{0,2},{1,3},{2,0},{3,1},{4,6},{5,7},{6,4},{7,5},{8,10},{9,11},{10,... | collective-permute-start | bytes 196616 | tf_op jit(solution)/shard_map/ppermute | solution.py:503
  111.2 4.3 %collective-permute-start.16 = (f32[2,64,128]{2,1,0:T(8,128)S(1)}, f32[2,64,128]{2,1,0:T(8,128)S(1)}, u32[]{:S(2)}, u32[]{:S(2)}) collective-permute-start(f32[2,64,128]{2,1,0:T(8,128)S(1)} %add.402), channel_id=1, source_target_pairs={{0,1},{1,0},{2,3},{3,2},{4,5},{5,4},{6,7},{7,6},{8,9},{9,8},{10,11... | collective-permute-start | bytes 196616 | tf_op jit(solution)/shard_map/ppermute | solution.py:503
  111.9 5.9 %collective-permute-start.12 = (f32[2,64,128]{2,1,0:T(8,128)S(1)}, f32[2,64,128]{2,1,0:T(8,128)S(1)}, u32[]{:S(2)}, u32[]{:S(2)}) collective-permute-start(f32[2,64,128]{2,1,0:T(8,128)S(1)} %add.398), channel_id=1, source_target_pairs={{0,4},{1,5},{2,6},{3,7},{4,0},{5,1},{6,2},{7,3},{8,12},{9,13},{10,... | collective-permute-start | bytes 196616 | tf_op jit(solution)/shard_map/ppermute | solution.py:503
  115.6 4.3 %collective-permute-start.17 = (f32[2,64,128]{2,1,0:T(8,128)S(1)}, f32[2,64,128]{2,1,0:T(8,128)S(1)}, u32[]{:S(2)}, u32[]{:S(2)}) collective-permute-start(f32[2,64,128]{2,1,0:T(8,128)S(1)} %add.403), channel_id=1, source_target_pairs={{0,16},{1,17},{2,18},{3,19},{4,20},{5,21},{6,22},{7,23},{8,24},{9,... | collective-permute-start | bytes 196616 | tf_op jit(solution)/shard_map/ppermute | solution.py:503
  126.2 4.1 %copy-start.4 = (f32[64,2,16,128]{3,2,1,0:T(8,128)S(1)}, f32[64,2,16,128]{3,2,1,0:T(8,128)}, u32[]{:S(2)}) copy-start(f32[64,2,16,128]{3,2,1,0:T(8,128)} %get-tuple-element.44.refs_0_) | copy-start | bytes 3145732
  126.2 26.1 %all-to-all-start.1 = ((f32[8,256,128]{2,1,0:T(8,128)}), f32[8,256,128]{2,1,0:T(8,128)S(1)}, u32[]{:S(2)}, u32[]{:S(2)}) async-start(f32[8,256,128]{2,1,0:T(8,128)} %bitcast.44), calls=%async_computation.1 | async-start | bytes 2097152 | tf_op jit(solution)/shard_map/all_to_all | solution.py:693
  134.1 1.4 collective-permute-start.18
  135.6 5.6 %collective-permute-start.19 = (f32[4,64,128]{2,1,0:T(8,128)S(1)}, f32[4,64,128]{2,1,0:T(8,128)S(1)}, u32[]{:S(2)}, u32[]{:S(2)}) collective-permute-start(f32[4,64,128]{2,1,0:T(8,128)S(1)} %add.406), channel_id=1, source_target_pairs={{0,16},{1,17},{2,18},{3,19},{4,20},{5,21},{6,22},{7,23},{8,24},{9,... | collective-permute-start | bytes 393224 | tf_op jit(solution)/shard_map/ppermute | solution.py:503
  141.3 4.3 %collective-permute-start.20 = (f32[4,2,2,1,8,128]{5,4,0,3,2,1:T(8,128)S(1)}, f32[4,2,2,1,8,128]{5,4,0,3,2,1:T(8,128)S(1)}, u32[]{:S(2)}, u32[]{:S(2)}) collective-permute-start(f32[4,2,2,1,8,128]{5,4,0,3,2,1:T(8,128)S(1)} %copy.29), channel_id=1, source_target_pairs={{0,1},{1,0},{2,3},{3,2},{4,5},{5,4},{6,7},{7,6},{8,9},{9,8},{10,11... | collective-permute-start | bytes 196616 | tf_op jit(solution)/shard_map/ppermute | solution.py:554
  155.0 29.0 %all-to-all-start.2 = ((f32[8,256,128]{2,1,0:T(8,128)}), f32[8,256,128]{2,1,0:T(8,128)S(1)}, u32[]{:S(2)}, u32[]{:S(2)}) async-start(f32[8,256,128]{2,1,0:T(8,128)} %bitcast.19), calls=%async_computation.2 | async-start | bytes 2097152 | tf_op jit(solution)/shard_map/all_to_all | solution.py:693
  158.6 4.1 %collective-permute-start.24 = (f32[32,32,128]{2,1,0:T(8,128)}, f32[32,32,128]{2,1,0:T(8,128)S(1)}, u32[]{:S(2)}, u32[]{:S(2)}) collective-permute-start(f32[32,32,128]{2,1,0:T(8,128)} %get-tuple-element.55), channel_id=1, source_target_pairs={{0,8},{8,0},{16,24},{24,16},{1,9},{9,1},{17,25},{25,17},{2,10},{10... | collective-permute-start | bytes 1572872 | tf_op jit(solution)/shard_map/ppermute | solution.py:714
  158.7 15.0 %collective-permute-start.25 = (f32[32,32,128]{2,1,0:T(8,128)}, f32[32,32,128]{2,1,0:T(8,128)S(1)}, u32[]{:S(2)}, u32[]{:S(2)}) collective-permute-start(f32[32,32,128]{2,1,0:T(8,128)} %get-tuple-element.56), channel_id=1, source_target_pairs={{0,16},{8,24},{16,0},{24,8},{1,17},{9,25},{17,1},{25,9},{2,18},{10... | collective-permute-start | bytes 1572872 | tf_op jit(solution)/shard_map/ppermute | solution.py:714
  159.5 24.5 %collective-permute-start.26 = (f32[32,32,128]{2,1,0:T(8,128)}, f32[32,32,128]{2,1,0:T(8,128)S(1)}, u32[]{:S(2)}, u32[]{:S(2)}) collective-permute-start(f32[32,32,128]{2,1,0:T(8,128)} %get-tuple-element.57), channel_id=1, source_target_pairs={{0,24},{8,16},{16,8},{24,0},{1,25},{9,17},{17,9},{25,1},{2,26},{10... | collective-permute-start | bytes 1572872 | tf_op jit(solution)/shard_map/ppermute | solution.py:714
  160.7 31.7 %collective-permute-start.21 = (f32[4,1,1,1,8,128]{5,4,0,3,2,1:T(8,128)S(1)}, f32[4,1,1,1,8,128]{5,4,0,3,2,1:T(8,128)S(1)}, u32[]{:S(2)}, u32[]{:S(2)}) collective-permute-start(f32[4,1,1,1,8,128]{5,4,0,3,2,1:T(8,128)S(1)} %get-tuple-element.75), channel_id=1, source_target_pairs={{0,2},{1,3},{2,0},{3,1},{4,6},{5,7},{6,4},{7,5},{8,10},{9,11},{10,... | collective-permute-start | bytes 49160 | tf_op jit(solution)/shard_map/ppermute | solution.py:554
  186.7 10.4 %collective-permute-start.27 = (f32[32,32,128]{2,1,0:T(8,128)}, f32[32,32,128]{2,1,0:T(8,128)S(1)}, u32[]{:S(2)}, u32[]{:S(2)}) collective-permute-start(f32[32,32,128]{2,1,0:T(8,128)} %get-tuple-element.64), channel_id=1, source_target_pairs={{0,8},{8,0},{16,24},{24,16},{1,9},{9,1},{17,25},{25,17},{2,10},{10... | collective-permute-start | bytes 1572872 | tf_op jit(solution)/shard_map/ppermute | solution.py:714
  187.2 15.0 %collective-permute-start.28 = (f32[32,32,128]{2,1,0:T(8,128)}, f32[32,32,128]{2,1,0:T(8,128)S(1)}, u32[]{:S(2)}, u32[]{:S(2)}) collective-permute-start(f32[32,32,128]{2,1,0:T(8,128)} %get-tuple-element.65), channel_id=1, source_target_pairs={{0,16},{8,24},{16,0},{24,8},{1,17},{9,25},{17,1},{25,9},{2,18},{10... | collective-permute-start | bytes 1572872 | tf_op jit(solution)/shard_map/ppermute | solution.py:714
  187.9 23.7 %collective-permute-start.29 = (f32[32,32,128]{2,1,0:T(8,128)}, f32[32,32,128]{2,1,0:T(8,128)S(1)}, u32[]{:S(2)}, u32[]{:S(2)}) collective-permute-start(f32[32,32,128]{2,1,0:T(8,128)} %get-tuple-element.66), channel_id=1, source_target_pairs={{0,24},{8,16},{16,8},{24,0},{1,25},{9,17},{17,9},{25,1},{2,26},{10... | collective-permute-start | bytes 1572872 | tf_op jit(solution)/shard_map/ppermute | solution.py:714
  188.7 5.6 %collective-permute-start.23 = (f32[4,1,1,1,8,128]{5,4,0,3,2,1:T(8,128)S(1)}, f32[4,1,1,1,8,128]{5,4,0,3,2,1:T(8,128)S(1)}, u32[]{:S(2)}, u32[]{:S(2)}) collective-permute-start(f32[4,1,1,1,8,128]{5,4,0,3,2,1:T(8,128)S(1)} %get-tuple-element.76), channel_id=1, source_target_pairs={{0,6},{1,7},{2,4},{3,5},{4,2},{5,3},{6,0},{7,1},{8,14},{9,15},{10,... | collective-permute-start | bytes 49160 | tf_op jit(solution)/shard_map/ppermute | solution.py:554
  192.4 4.7 %collective-permute-start.22 = (f32[4,1,1,1,8,128]{5,4,0,3,2,1:T(8,128)S(1)}, f32[4,1,1,1,8,128]{5,4,0,3,2,1:T(8,128)S(1)}, u32[]{:S(2)}, u32[]{:S(2)}) collective-permute-start(f32[4,1,1,1,8,128]{5,4,0,3,2,1:T(8,128)S(1)} %get-tuple-element.77), channel_id=1, source_target_pairs={{0,4},{1,5},{2,6},{3,7},{4,0},{5,1},{6,2},{7,3},{8,12},{9,13},{10,... | collective-permute-start | bytes 49160 | tf_op jit(solution)/shard_map/ppermute | solution.py:554

commit v7 on v6

--- a/solution.py
+++ b/solution.py
@@ -379,23 +379,29 @@
     for i in range(strips):
         copy_in(i).wait()
         for g in range(i * devices, (i + 1) * devices):
-            if units < slots:
-                o_ref[g] = jnp.zeros(o_ref.shape[1:], jnp.float32)
-            for u in range(units):
-                unit = g * units + u
-                lit = base + unit % channels < count_ref[unit // channels]
-                for p in range(2):
+            for p in range(2):
+                values = [jnp.zeros((span, FB), jnp.float32)] * slots
+                for u in range(units):
+                    unit = g * units + u
+                    lit = base + unit % channels < count_ref[unit // channels]
                     at = (unit * 2 + p) * span
-                    value = jnp.where(lit, x_ref[at : at + span, :], 0.0)
-                    o_ref[g, pl.ds(p * slots + u, span, stride=rows), :] = value
+                    values[u] = jnp.where(lit, x_ref[at : at + span, :], 0.0)
+                turned = jnp.swapaxes(jnp.stack(values), 0, 1)
+                for r in range(span):
+                    at = r * rows + p * slots
+                    o_ref[g, at : at + slots, :] = turned[r]
         copy_out(i).start()
     for i in range(strips):
         copy_out(i).wait()
 
 
 def send_kernel(item_ref, count_ref, x_ref, *refs, units, slots):
-    *out_refs, held_ref, sems = refs
+    *out_refs, held_ref, turned_ref, sems = refs
     capacity, near = held_ref.shape[1], held_ref.shape[2] // (2 * BLK)
+    for g in range(x_ref.shape[0]):
+        for part in range(2):
+            rows = [x_ref[g, (2 * k + part) * slots : (2 * k + part + 1) * slots, :] for k in range(near)]
+            turned_ref[g, :, part] = jnp.swapaxes(jnp.stack(rows), 0, 1)
     several = math.gcd(capacity, 4)
     copies = []
     for s, out_ref in enumerate(out_refs):
@@ -410,9 +416,7 @@
                     u = channel - g * units
                     for part in range(2):
                         at = (c * 2 + part) * near
-                        o_ref[n, at : at + near, :] = x_ref[
-                            g, pl.ds(part * slots + u, near, stride=2 * slots), :
-                        ]
+                        o_ref[n, at : at + near, :] = turned_ref[g, u, part]
             return carry
 
         lax.fori_loop(0, (count_ref[s] + several - 1) // several, body, 0)
@@ -680,7 +684,8 @@
             total = summed(partial, fibre_rounds)
         else:
             cut = fibres_out // 2
-            there, back = all_rounds, all_rounds[:1] + all_rounds[:0:-1]
+            there = all_rounds[:1] + all_rounds[2:] + all_rounds[1:2]
+            back = all_rounds[:1] + all_rounds[:0:-1]
             total = jnp.concatenate(
                 [summed(partial[:cut], there), summed(partial[cut:], back)], axis=0
             )
@@ -701,9 +706,10 @@
             out_specs=(pl.BlockSpec(memory_space=pltpu.HBM),) * groups,
             scratch_shapes=[
                 pltpu.VMEM((groups,) + block.shape, jnp.float32),
+                pltpu.VMEM((times, slots, 2, near, FB), jnp.float32),
                 pltpu.SemaphoreType.DMA((groups,)),
             ],
-            compiler_params=params(values.shape, (groups,) + block.shape),
+            compiler_params=params(values.shape, values.shape, (groups,) + block.shape),
             cost_estimate=cost(0, 4 * 4 * values.size),
             name="send",
         )(source_item, counts, values)

time: 217 us -> 215 us (level)
  waiting for transfers between devices: 122 us -> 119 us
  starting transfers between devices: 41 us -> 43.6 us
    ppermute x20, waiting for transfers between devices: 28.6 us -> 25.3 us  [summed(): lax.ppermute(values, ('wave', 'tm'), [(i, i ^ mask) for i in range(size)])]
    ppermute x20, starting transfers between devices: 14.6 us -> 16.9 us  [summed(): lax.ppermute(values, ('wave', 'tm'), [(i, i ^ mask) for i in range(size)])]
  transfers between devices with their start and end apart: 33 -> 33, of which waited for: 29 -> 28; matrix products, arithmetic and copies ran while one was open for 3% -> 3% of each run, Pallas kernels for 2% -> 2%
where the time goes in v7:
time: 215 us; the launch traced here: 214 us
  waiting for transfers between devices  119 us (55%)
  Pallas kernels  43.6 us (20%)
  starting transfers between devices  43.6 us (20%)
  local copies, waits for them, and re-layouts  5.48 us (3%)
    all_to_all x1, waiting for transfers between devices, local(): lax.all_to_all(packed, 'tm', split_axis=0, concat_axis=0, tiled=True)  44.2 us
    ppermute x6, waiting for transfers between devices, to_groups(): lax.ppermute(outgoing[s], 'wave', [(i, i ^ s) for i in range(groups)])  36.2 us
    pallas_call x5, Pallas kernels, dispersed(): pl.pallas_call(functools.partial(step_kernel, rotate=rotate, hold=hold, f...  31.2 us
    ppermute x20, waiting for transfers between devices, summed(): lax.ppermute(values, ('wave', 'tm'), [(i, i ^ mask) for i in range(size)])  25.3 us
    ppermute x20, starting transfers between devices, summed(): lax.ppermute(values, ('wave', 'tm'), [(i, i ^ mask) for i in range(size)])  16.9 us
    ppermute x4, starting transfers between devices, time_parts(): part = lax.ppermute(part, 'tm', [(i, i ^ mask) for i in range(times)])  7.76 us
    all_to_all x2, starting transfers between devices, to_times(): return lax.all_to_all(values, 'tm', split_axis=0, concat_axis=0, tiled=True)  7.62 us
    all_to_all x1, starting transfers between devices, local(): lax.all_to_all(packed, 'tm', split_axis=0, concat_axis=0, tiled=True)  7.4 us
  transfers between devices with their start and end apart: 33, of which 28 were waited for; matrix products, arithmetic and copies ran while one was open for 3% of the time, Pallas kernels for 2%

profile of v7, /device:TPU:0, one launch (start us, length us, event | category | flops | bytes accessed | tf_op | source)
XLA Modules:
  0.0 214.4 jit_solution(14679638780898790257)
XLA Ops:
  0.7 3.1 %pack.1 = f32[8,512,128]{2,1,0:T(8,128)} custom-call(s32[4]{0:T(128)S(1)} %copy-done.3, f32[4096,128]{1,0:T(8,128)} %bitcast.43), custom_call_target="tpu_custom_call" | custom-call | tf_op jit(solution)/shard_map/pack/pallas_call | solution.py:617
  3.8 7.4 %all-to-all-start = ((f32[8,512,128]{2,1,0:T(8,128)}), f32[8,512,128]{2,1,0:T(8,128)S(1)}, u32[]{:S(2)}, u32[]{:S(2)}) async-start(f32[8,512,128]{2,1,0:T(8,128)} %pack.1), calls=%async_computation | async-start | bytes 4194304 | tf_op jit(solution)/shard_map/all_to_all | solution.py:630
  14.1 1.0 sine_multiply_fusion
  15.2 44.2 %all-to-all-done = f32[8,512,128]{2,1,0:T(8,128)S(1)} async-done(((f32[8,512,128]{2,1,0:T(8,128)}), f32[8,512,128]{2,1,0:T(8,128)S(1)}, u32[]{:S(2)}, u32[]{:S(2)}) %all-to-all-start) | async-done | bytes 2097184 | tf_op jit(solution)/shard_map/all_to_all | solution.py:630
  59.5 6.5 %step.5 = (f32[64,2,32,128]{3,2,1,0:T(8,128)}, f32[1,64,128]{2,1,0:T(8,128)S(1)}) custom-call(f32[64,2,32,128]{3,2,1,0:T(8,128)S(1)} %bitcast.42, f32[4,16,128]{2,1,0:T(8,128)S(1)} %broadcast_in_dim.32.refs_1_.refs_2_.refs_4_, f32[16,16,128]{2,1,0:T(8,128)S(1)} %get-tuple-element.82.refs_2_.refs_5_, f32[16,16,128]{2,1,0:T(8,128)S(1)} %get-tuple-element.83.refs_3_.refs_6_, ...), custom_call_target="tpu_custom_call" | custom-call | flops 1677721600 | bytes 8388608 | tf_op jit(solution)/shard_map/step/pallas_call | solution.py:664
  66.0 1.2 collective-permute-done
  67.2 2.4 %collective-permute-start.3 = (f32[1,64,128]{2,1,0:T(8,128)S(1)}, f32[1,64,128]{2,1,0:T(8,128)S(1)}, u32[]{:S(2)}, u32[]{:S(2)}) collective-permute-start(f32[1,64,128]{2,1,0:T(8,128)S(1)} %add.378), channel_id=1, source_target_pairs={{0,17},{1,16},{2,19},{3,18},{4,21},{5,20},{6,23},{7,22},{8,25},{9,... | collective-permute-start | bytes 98312 | tf_op jit(solution)/shard_map/ppermute | solution.py:507
  72.1 1.5 collective-permute-done.2
  74.2 7.7 %step.6 = (f32[64,2,32,128]{3,2,1,0:T(8,128)S(1)}, f32[1,64,128]{2,1,0:T(8,128)S(1)}) custom-call(f32[64,2,32,128]{3,2,1,0:T(8,128)} %get-tuple-element.36.refs_0_, f32[1,64,128]{2,1,0:T(8,128)S(1)} %add_add_fusion.1.refs_1_, f32[4,16,128]{2,1,0:T(8,128)S(1)} %broadcast_in_dim.32.refs_1_.refs_2_.refs_4_, f32[16,128]{1,0:T(8,128)S(1)} %broadcast_in_dim.33.refs_3_, ...), custom_call_target="tpu_custom_call" | custom-call | flops 1677721600 | bytes 8388608 | tf_op jit(solution)/shard_map/step/pallas_call | solution.py:664
  82.1 1.2 collective-permute-done.4
  83.3 1.4 collective-permute-start.7
  85.2 1.5 collective-permute-start.5
  86.7 1.4 collective-permute-done.7
  89.2 7.0 %step.7 = (f32[64,2,32,128]{3,2,1,0:T(8,128)S(1)}, f32[4,64,128]{2,1,0:T(8,128)S(1)}) custom-call(f32[64,2,32,128]{3,2,1,0:T(8,128)S(1)} %get-tuple-element.38.refs_0_, f32[1,64,128]{2,1,0:T(8,128)S(1)} %add_add_fusion.refs_1_, f32[4,16,128]{2,1,0:T(8,128)S(1)} %broadcast_in_dim.32.refs_1_.refs_2_.refs_4_, f32[16,128]{1,0:T(8,128)S(1)} %broadcast_in_dim.33.refs_3_, ...), custom_call_target="tpu_custom_call" | custom-call | flops 1677721600 | bytes 8388608 | tf_op jit(solution)/shard_map/step/pallas_call | solution.py:664
  97.7 1.5 collective-permute-start.9
  99.3 2.9 %collective-permute-done.9 = f32[2,64,128]{2,1,0:T(8,128)S(1)} collective-permute-done((f32[2,64,128]{2,1,0:T(8,128)S(1)}, f32[2,64,128]{2,1,0:T(8,128)S(1)}, u32[]{:S(2)}, u32[]{:S(2)}) %collective-permute-start.9) | collective-permute-done | bytes 65568 | tf_op jit(solution)/shard_map/ppermute | solution.py:507
  102.3 2.2 %collective-permute-done.14 = f32[2,64,128]{2,1,0:T(8,128)S(1)} collective-permute-done((f32[2,64,128]{2,1,0:T(8,128)S(1)}, f32[2,64,128]{2,1,0:T(8,128)S(1)}, u32[]{:S(2)}, u32[]{:S(2)}) %collective-permute-start.14) | collective-permute-done | bytes 65568 | tf_op jit(solution)/shard_map/ppermute | solution.py:507
  104.6 1.9 collective-permute-done.10
  106.5 1.1 collective-permute-start.11
  107.6 1.7 collective-permute-done.15
  109.3 1.7 collective-permute-start.16
  111.0 1.0 collective-permute-done.11
  112.0 1.6 collective-permute-start.12
  113.6 1.6 collective-permute-start.17
  116.3 1.6 collective-permute-done.17
  118.1 6.2 %step.8 = (f32[64,2,16,128]{3,2,1,0:T(8,128)}, f32[4,64,128]{2,1,0:T(8,128)S(1)}, f32[64,2,16,128]{3,2,1,0:T(8,128)}) custom-call(f32[64,2,32,128]{3,2,1,0:T(8,128)S(1)} %get-tuple-element.40.refs_0_, f32[4,64,128]{2,1,0:T(8,128)S(1)} %pad_maximum_fusion.refs_1_, f32[4,16,128]{2,1,0:T(8,128)S(1)} %broadcast_in_dim.34.refs_4_.refs_2_.refs_1_, ...), custom_call_target="tpu_custom_call" | custom-call | flops 838860800 | bytes 8388608 | tf_op jit(solution)/shard_map/step/pallas_call | solution.py:664
  124.2 4.1 %all-to-all-start.1 = ((f32[8,256,128]{2,1,0:T(8,128)}), f32[8,256,128]{2,1,0:T(8,128)S(1)}, u32[]{:S(2)}, u32[]{:S(2)}) async-start(f32[8,256,128]{2,1,0:T(8,128)} %bitcast.44), calls=%async_computation.1 | async-start | bytes 2097152 | tf_op jit(solution)/shard_map/all_to_all | solution.py:698
  128.5 3.9 %step.9 = (f32[64,2,16,128]{3,2,1,0:T(8,128)}, f32[4,64,128]{2,1,0:T(8,128)S(1)}) custom-call(f32[64,2,16,128]{3,2,1,0:T(8,128)S(1)} %copy-done.4, f32[4,16,128]{2,1,0:T(8,128)S(1)} %broadcast_in_dim.34.refs_4_.refs_2_.refs_1_, f32[16,16,128]{2,1,0:T(8,128)S(1)} %get-tuple-element.79.refs_5_.refs_2_, f32[16,16,128]{2,1,0:T(8,128)S(1)} %get-tuple-element.78.refs_6_.refs_3_, ...), custom_call_target="tpu_custom_call" | custom-call | flops 838860800 | bytes 4194304 | tf_op jit(solution)/shard_map/step/pallas_call | solution.py:664
  132.7 1.1 collective-permute-done.18
  133.8 1.6 collective-permute-start.19
  135.5 3.9 %collective-permute-done.19 = f32[4,64,128]{2,1,0:T(8,128)S(1)} collective-permute-done((f32[4,64,128]{2,1,0:T(8,128)S(1)}, f32[4,64,128]{2,1,0:T(8,128)S(1)}, u32[]{:S(2)}, u32[]{:S(2)}) %collective-permute-start.19) | collective-permute-done | bytes 131104 | tf_op jit(solution)/shard_map/ppermute | solution.py:507
  139.5 2.1 collective-permute-start.20
  141.7 2.1 collective-permute-done.20
  143.8 6.7 %all-to-all-done.1.x_ref = f32[8,256,128]{2,1,0:T(8,128)S(1)} async-done(((f32[8,256,128]{2,1,0:T(8,128)}), f32[8,256,128]{2,1,0:T(8,128)S(1)}, u32[]{:S(2)}, u32[]{:S(2)}) %all-to-all-start.1) | async-done | bytes 1048608 | tf_op jit(solution)/shard_map/all_to_all | solution.py:698
  150.6 2.7 %send.2 = (f32[32,32,128]{2,1,0:T(8,128)}, f32[32,32,128]{2,1,0:T(8,128)}, f32[32,32,128]{2,1,0:T(8,128)}, f32[32,32,128]{2,1,0:T(8,128)}) custom-call(s32[128]{0:T(128)S(1)} %select_reduce_fusion.1.item_ref, s32[4]{0:T(128)S(1)} %convert_reduce_fusion.1.count_ref, f32[8,256,128]{2,1,0:T(8,128)S(1)} %all-to-all-done.1.x_ref), custom_call_target="tpu_custom_call" | custom-call | bytes 4194304 | tf_op jit(solution)/shard_map/send/pallas_call | solution.py:702
  153.3 3.6 %all-to-all-start.2 = ((f32[8,256,128]{2,1,0:T(8,128)}), f32[8,256,128]{2,1,0:T(8,128)S(1)}, u32[]{:S(2)}, u32[]{:S(2)}) async-start(f32[8,256,128]{2,1,0:T(8,128)} %bitcast.19), calls=%async_computation.2 | async-start | bytes 2097152 | tf_op jit(solution)/shard_map/all_to_all | solution.py:698
  156.9 1.6 collective-permute-start.25
  159.0 1.9 collective-permute-start.21
  160.9 11.0 %collective-permute-done.25.refs_2_ = f32[32,32,128]{2,1,0:T(8,128)S(1)} collective-permute-done((f32[32,32,128]{2,1,0:T(8,128)}, f32[32,32,128]{2,1,0:T(8,128)S(1)}, u32[]{:S(2)}, u32[]{:S(2)}) %collective-permute-start.25) | collective-permute-done | bytes 524320 | tf_op jit(solution)/shard_map/ppermute | solution.py:720
  171.9 10.3 %collective-permute-done.26.refs_3_ = f32[32,32,128]{2,1,0:T(8,128)S(1)} collective-permute-done((f32[32,32,128]{2,1,0:T(8,128)}, f32[32,32,128]{2,1,0:T(8,128)S(1)}, u32[]{:S(2)}, u32[]{:S(2)}) %collective-permute-start.26) | collective-permute-done | bytes 524320 | tf_op jit(solution)/shard_map/ppermute | solution.py:720
  182.3 2.7 %send.3 = (f32[32,32,128]{2,1,0:T(8,128)}, f32[32,32,128]{2,1,0:T(8,128)}, f32[32,32,128]{2,1,0:T(8,128)}, f32[32,32,128]{2,1,0:T(8,128)}) custom-call(s32[128]{0:T(128)S(1)} %select_reduce_fusion.1.item_ref, s32[4]{0:T(128)S(1)} %convert_reduce_fusion.1.count_ref, f32[8,256,128]{2,1,0:T(8,128)S(1)} %all-to-all-done.2.x_ref), custom_call_target="tpu_custom_call" | custom-call | bytes 4194304 | tf_op jit(solution)/shard_map/send/pallas_call | solution.py:702
  185.1 1.5 collective-permute-start.28
  187.0 3.8 %collective-permute-start.23 = (f32[4,1,1,1,8,128]{5,4,0,3,2,1:T(8,128)S(1)}, f32[4,1,1,1,8,128]{5,4,0,3,2,1:T(8,128)S(1)}, u32[]{:S(2)}, u32[]{:S(2)}) collective-permute-start(f32[4,1,1,1,8,128]{5,4,0,3,2,1:T(8,128)S(1)} %get-tuple-element.76), channel_id=1, source_target_pairs={{0,6},{1,7},{2,4},{3,5},{4,2},{5,3},{6,0},{7,1},{8,14},{9,15},{10,... | collective-permute-start | bytes 49160 | tf_op jit(solution)/shard_map/ppermute | solution.py:558
  190.9 1.6 collective-permute-done.23
  192.5 2.9 %collective-permute-done.22 = f32[4,1,1,1,8,128]{5,4,0,3,2,1:T(8,128)S(1)} collective-permute-done((f32[4,1,1,1,8,128]{5,4,0,3,2,1:T(8,128)S(1)}, f32[4,1,1,1,8,128]{5,4,0,3,2,1:T(8,128)S(1)}, u32[]{:S(2)}, u32[]{:S(2)}) %collective-permute-start.22) | collective-permute-done | bytes 16416 | tf_op jit(solution)/shard_map/ppermute | solution.py:558
  195.4 4.7 %collective-permute-done.28.refs_6_ = f32[32,32,128]{2,1,0:T(8,128)S(1)} collective-permute-done((f32[32,32,128]{2,1,0:T(8,128)}, f32[32,32,128]{2,1,0:T(8,128)S(1)}, u32[]{:S(2)}, u32[]{:S(2)}) %collective-permute-start.28) | collective-permute-done | bytes 524320 | tf_op jit(solution)/shard_map/ppermute | solution.py:720
  200.1 10.1 %collective-permute-done.29.refs_7_ = f32[32,32,128]{2,1,0:T(8,128)S(1)} collective-permute-done((f32[32,32,128]{2,1,0:T(8,128)}, f32[32,32,128]{2,1,0:T(8,128)S(1)}, u32[]{:S(2)}, u32[]{:S(2)}) %collective-permute-start.29) | collective-permute-done | bytes 524320 | tf_op jit(solution)/shard_map/ppermute | solution.py:720
  210.3 3.9 %place.1 = f32[64,64,128]{2,1,0:T(8,128)} custom-call(s32[64]{0:T(128)S(1)} %select_reduce_fusion.from_ref, f32[4,8,128]{2,1,0:T(8,128)S(1)} %broadcast_in_dim.31.strength_ref, f32[4,8,128]{2,1,0:T(8,128)S(1)} %add_bitcast_fusion.q_ref, f32[32,32,128]{2,1,0:T(8,128)} %get-tuple-element.58.refs_0_, f32[32,32,128]{2,1,0:T(8,128)S(1)} %collective-permute-done.24.refs_1_, ...), custom_call_target="tpu_custom_call" | custom-call | bytes 8388608 | tf_op jit(solution)/shard_map/place/pallas_call | solution.py:738
  (110 shorter events, 13.4 us)
Async XLA Ops:
  0.0 0.7 copy-start.3
  3.7 7.5 %copy-start.6 = (s32[4,64]{1,0:T(4,128)S(1)}, s32[4,64]{1,0:T(4,128)}, u32[]{:S(2)}) copy-start(s32[4,64]{1,0:T(4,128)} %param.13) | copy-start | bytes 3076
  3.7 8.2 %copy-start.5 = (s32[4,64]{1,0:T(4,128)S(1)}, s32[4,64]{1,0:T(4,128)}, u32[]{:S(2)}) copy-start(s32[4,64]{1,0:T(4,128)} %param.14) | copy-start | bytes 3076
  3.8 8.9 %copy-start.9 = (f32[2,4]{1,0:T(2,128)S(1)}, f32[2,4]{1,0:T(2,128)}, u32[]{:S(2)}) copy-start(f32[2,4]{1,0:T(2,128)} %param.15) | copy-start | bytes 100
  3.8 55.6 %all-to-all-start = ((f32[8,512,128]{2,1,0:T(8,128)}), f32[8,512,128]{2,1,0:T(8,128)S(1)}, u32[]{:S(2)}, u32[]{:S(2)}) async-start(f32[8,512,128]{2,1,0:T(8,128)} %pack.1), calls=%async_computation | async-start | bytes 4194304 | tf_op jit(solution)/shard_map/all_to_all | solution.py:630
  11.2 3.0 %copy-start.7 = (f32[16,128]{1,0:T(8,128)S(1)}, f32[16,128]{1,0:T(8,128)}, u32[]{:S(2)}) copy-start(f32[16,128]{1,0:T(8,128)} %constant.274) | copy-start | bytes 24580
  11.2 3.0 %copy-start.8 = (f32[16,128]{1,0:T(8,128)S(1)}, f32[16,128]{1,0:T(8,128)}, u32[]{:S(2)}) copy-start(f32[16,128]{1,0:T(8,128)} %constant.273) | copy-start | bytes 24580
  11.2 48.3 %copy-start = (bf16[512,256]{1,0:T(8,128)(2,1)S(1)}, bf16[512,256]{1,0:T(8,128)(2,1)}, u32[]{:S(2)}) copy-start(bf16[512,256]{1,0:T(8,128)(2,1)} %constant.270.clone.refs_6_.refs_9_) | copy-start | bytes 786436
  11.2 48.3 %copy-start.1 = (bf16[512,256]{1,0:T(8,128)(2,1)S(1)}, bf16[512,256]{1,0:T(8,128)(2,1)}, u32[]{:S(2)}) copy-start(bf16[512,256]{1,0:T(8,128)(2,1)} %constant.269.clone.refs_5_.refs_8_) | copy-start | bytes 786436
  11.2 48.3 %copy-start.2 = (f32[2,16,8,128]{3,2,1,0:T(8,128)S(1)}, f32[2,16,8,128]{3,2,1,0:T(8,128)}, u32[]{:S(2)}) copy-start(f32[2,16,8,128]{3,2,1,0:T(8,128)} %constant.268.clone.refs_4_.refs_7_) | copy-start | bytes 393220
  59.5 11.2 %copy-start.10 = (f32[2,4]{1,0:T(2,128)S(1)}, f32[2,4]{1,0:T(2,128)}, u32[]{:S(2)}) copy-start(f32[2,4]{1,0:T(2,128)} %param.16) | copy-start | bytes 100
  66.0 1.3 collective-permute-start
  67.2 4.8 %collective-permute-start.3 = (f32[1,64,128]{2,1,0:T(8,128)S(1)}, f32[1,64,128]{2,1,0:T(8,128)S(1)}, u32[]{:S(2)}, u32[]{:S(2)}) collective-permute-start(f32[1,64,128]{2,1,0:T(8,128)S(1)} %add.378), channel_id=1, source_target_pairs={{0,17},{1,16},{2,19},{3,18},{4,21},{5,20},{6,23},{7,22},{8,25},{9,... | collective-permute-start | bytes 98312 | tf_op jit(solution)/shard_map/ppermute | solution.py:507
  69.7 3.9 %collective-permute-start.2 = (f32[1,64,128]{2,1,0:T(8,128)S(1)}, f32[1,64,128]{2,1,0:T(8,128)S(1)}, u32[]{:S(2)}, u32[]{:S(2)}) collective-permute-start(f32[1,64,128]{2,1,0:T(8,128)S(1)} %add.378), channel_id=1, source_target_pairs={{0,1},{1,0},{2,3},{3,2},{4,5},{5,4},{6,7},{7,6},{8,9},{9,8},{10,11... | collective-permute-start | bytes 98312 | tf_op jit(solution)/shard_map/ppermute | solution.py:507
  70.2 3.9 %collective-permute-start.1 = (f32[1,64,128]{2,1,0:T(8,128)S(1)}, f32[1,64,128]{2,1,0:T(8,128)S(1)}, u32[]{:S(2)}, u32[]{:S(2)}) collective-permute-start(f32[1,64,128]{2,1,0:T(8,128)S(1)} %add.378), channel_id=1, source_target_pairs={{0,16},{1,17},{2,18},{3,19},{4,20},{5,21},{6,22},{7,23},{8,24},{9,... | collective-permute-start | bytes 98312 | tf_op jit(solution)/shard_map/ppermute | solution.py:507
  82.0 1.3 collective-permute-start.4
  83.3 4.9 %collective-permute-start.7 = (f32[1,64,128]{2,1,0:T(8,128)S(1)}, f32[1,64,128]{2,1,0:T(8,128)S(1)}, u32[]{:S(2)}, u32[]{:S(2)}) collective-permute-start(f32[1,64,128]{2,1,0:T(8,128)S(1)} %add.382), channel_id=1, source_target_pairs={{0,17},{1,16},{2,19},{3,18},{4,21},{5,20},{6,23},{7,22},{8,25},{9,... | collective-permute-start | bytes 98312 | tf_op jit(solution)/shard_map/ppermute | solution.py:507
  84.7 3.9 %collective-permute-start.6 = (f32[1,64,128]{2,1,0:T(8,128)S(1)}, f32[1,64,128]{2,1,0:T(8,128)S(1)}, u32[]{:S(2)}, u32[]{:S(2)}) collective-permute-start(f32[1,64,128]{2,1,0:T(8,128)S(1)} %add.382), channel_id=1, source_target_pairs={{0,1},{1,0},{2,3},{3,2},{4,5},{5,4},{6,7},{7,6},{8,9},{9,8},{10,11... | collective-permute-start | bytes 98312 | tf_op jit(solution)/shard_map/ppermute | solution.py:507
  85.2 3.9 %collective-permute-start.5 = (f32[1,64,128]{2,1,0:T(8,128)S(1)}, f32[1,64,128]{2,1,0:T(8,128)S(1)}, u32[]{:S(2)}, u32[]{:S(2)}) collective-permute-start(f32[1,64,128]{2,1,0:T(8,128)S(1)} %add.382), channel_id=1, source_target_pairs={{0,16},{1,17},{2,18},{3,19},{4,20},{5,21},{6,22},{7,23},{8,24},{9,... | collective-permute-start | bytes 98312 | tf_op jit(solution)/shard_map/ppermute | solution.py:507
  96.2 1.3 collective-permute-start.8
  96.3 1.4 collective-permute-start.13
  97.7 4.4 %collective-permute-start.9 = (f32[2,64,128]{2,1,0:T(8,128)S(1)}, f32[2,64,128]{2,1,0:T(8,128)S(1)}, u32[]{:S(2)}, u32[]{:S(2)}) collective-permute-start(f32[2,64,128]{2,1,0:T(8,128)S(1)} %get-tuple-element.71), channel_id=1, source_target_pairs={{0,1},{1,0},{2,3},{3,2},{4,5},{5,4},{6,7},{7,6},{8,9},{9,8},{10,11... | collective-permute-start | bytes 196616 | tf_op jit(solution)/shard_map/ppermute | solution.py:507
  99.3 5.2 %collective-permute-start.14 = (f32[2,64,128]{2,1,0:T(8,128)S(1)}, f32[2,64,128]{2,1,0:T(8,128)S(1)}, u32[]{:S(2)}, u32[]{:S(2)}) collective-permute-start(f32[2,64,128]{2,1,0:T(8,128)S(1)} %get-tuple-element.72), channel_id=1, source_target_pairs={{0,4},{1,5},{2,6},{3,7},{4,0},{5,1},{6,2},{7,3},{8,12},{9,13},{10,... | collective-permute-start | bytes 196616 | tf_op jit(solution)/shard_map/ppermute | solution.py:507
  102.2 4.3 %collective-permute-start.10 = (f32[2,64,128]{2,1,0:T(8,128)S(1)}, f32[2,64,128]{2,1,0:T(8,128)S(1)}, u32[]{:S(2)}, u32[]{:S(2)}) collective-permute-start(f32[2,64,128]{2,1,0:T(8,128)S(1)} %add.396), channel_id=1, source_target_pairs={{0,2},{1,3},{2,0},{3,1},{4,6},{5,7},{6,4},{7,5},{8,10},{9,11},{10,... | collective-permute-start | bytes 196616 | tf_op jit(solution)/shard_map/ppermute | solution.py:507
  104.5 4.8 %collective-permute-start.15 = (f32[2,64,128]{2,1,0:T(8,128)S(1)}, f32[2,64,128]{2,1,0:T(8,128)S(1)}, u32[]{:S(2)}, u32[]{:S(2)}) collective-permute-start(f32[2,64,128]{2,1,0:T(8,128)S(1)} %add.401), channel_id=1, source_target_pairs={{0,2},{1,3},{2,0},{3,1},{4,6},{5,7},{6,4},{7,5},{8,10},{9,11},{10,... | collective-permute-start | bytes 196616 | tf_op jit(solution)/shard_map/ppermute | solution.py:507
  106.5 5.4 %collective-permute-start.11 = (f32[2,64,128]{2,1,0:T(8,128)S(1)}, f32[2,64,128]{2,1,0:T(8,128)S(1)}, u32[]{:S(2)}, u32[]{:S(2)}) collective-permute-start(f32[2,64,128]{2,1,0:T(8,128)S(1)} %add.397), channel_id=1, source_target_pairs={{0,4},{1,5},{2,6},{3,7},{4,0},{5,1},{6,2},{7,3},{8,12},{9,13},{10,... | collective-permute-start | bytes 196616 | tf_op jit(solution)/shard_map/ppermute | solution.py:507
  109.3 4.3 %collective-permute-start.16 = (f32[2,64,128]{2,1,0:T(8,128)S(1)}, f32[2,64,128]{2,1,0:T(8,128)S(1)}, u32[]{:S(2)}, u32[]{:S(2)}) collective-permute-start(f32[2,64,128]{2,1,0:T(8,128)S(1)} %add.402), channel_id=1, source_target_pairs={{0,1},{1,0},{2,3},{3,2},{4,5},{5,4},{6,7},{7,6},{8,9},{9,8},{10,11... | collective-permute-start | bytes 196616 | tf_op jit(solution)/shard_map/ppermute | solution.py:507
  112.0 4.3 %collective-permute-start.12 = (f32[2,64,128]{2,1,0:T(8,128)S(1)}, f32[2,64,128]{2,1,0:T(8,128)S(1)}, u32[]{:S(2)}, u32[]{:S(2)}) collective-permute-start(f32[2,64,128]{2,1,0:T(8,128)S(1)} %add.398), channel_id=1, source_target_pairs={{0,16},{1,17},{2,18},{3,19},{4,20},{5,21},{6,22},{7,23},{8,24},{9,... | collective-permute-start | bytes 196616 | tf_op jit(solution)/shard_map/ppermute | solution.py:507
  113.6 4.3 %collective-permute-start.17 = (f32[2,64,128]{2,1,0:T(8,128)S(1)}, f32[2,64,128]{2,1,0:T(8,128)S(1)}, u32[]{:S(2)}, u32[]{:S(2)}) collective-permute-start(f32[2,64,128]{2,1,0:T(8,128)S(1)} %add.403), channel_id=1, source_target_pairs={{0,16},{1,17},{2,18},{3,19},{4,20},{5,21},{6,22},{7,23},{8,24},{9,... | collective-permute-start | bytes 196616 | tf_op jit(solution)/shard_map/ppermute | solution.py:507
  124.2 4.3 %copy-start.4 = (f32[64,2,16,128]{3,2,1,0:T(8,128)S(1)}, f32[64,2,16,128]{3,2,1,0:T(8,128)}, u32[]{:S(2)}) copy-start(f32[64,2,16,128]{3,2,1,0:T(8,128)} %get-tuple-element.44.refs_0_) | copy-start | bytes 3145732
  124.2 26.4 %all-to-all-start.1 = ((f32[8,256,128]{2,1,0:T(8,128)}), f32[8,256,128]{2,1,0:T(8,128)S(1)}, u32[]{:S(2)}, u32[]{:S(2)}) async-start(f32[8,256,128]{2,1,0:T(8,128)} %bitcast.44), calls=%async_computation.1 | async-start | bytes 2097152 | tf_op jit(solution)/shard_map/all_to_all | solution.py:698
  132.4 1.4 collective-permute-start.18
  133.8 5.6 %collective-permute-start.19 = (f32[4,64,128]{2,1,0:T(8,128)S(1)}, f32[4,64,128]{2,1,0:T(8,128)S(1)}, u32[]{:S(2)}, u32[]{:S(2)}) collective-permute-start(f32[4,64,128]{2,1,0:T(8,128)S(1)} %add.406), channel_id=1, source_target_pairs={{0,16},{1,17},{2,18},{3,19},{4,20},{5,21},{6,22},{7,23},{8,24},{9,... | collective-permute-start | bytes 393224 | tf_op jit(solution)/shard_map/ppermute | solution.py:507
  139.5 4.3 %collective-permute-start.20 = (f32[4,2,2,1,8,128]{5,4,0,3,2,1:T(8,128)S(1)}, f32[4,2,2,1,8,128]{5,4,0,3,2,1:T(8,128)S(1)}, u32[]{:S(2)}, u32[]{:S(2)}) collective-permute-start(f32[4,2,2,1,8,128]{5,4,0,3,2,1:T(8,128)S(1)} %copy.29), channel_id=1, source_target_pairs={{0,1},{1,0},{2,3},{3,2},{4,5},{5,4},{6,7},{7,6},{8,9},{9,8},{10,11... | collective-permute-start | bytes 196616 | tf_op jit(solution)/shard_map/ppermute | solution.py:558
  153.3 29.0 %all-to-all-start.2 = ((f32[8,256,128]{2,1,0:T(8,128)}), f32[8,256,128]{2,1,0:T(8,128)S(1)}, u32[]{:S(2)}, u32[]{:S(2)}) async-start(f32[8,256,128]{2,1,0:T(8,128)} %bitcast.19), calls=%async_computation.2 | async-start | bytes 2097152 | tf_op jit(solution)/shard_map/all_to_all | solution.py:698
  156.9 4.1 %collective-permute-start.24 = (f32[32,32,128]{2,1,0:T(8,128)}, f32[32,32,128]{2,1,0:T(8,128)S(1)}, u32[]{:S(2)}, u32[]{:S(2)}) collective-permute-start(f32[32,32,128]{2,1,0:T(8,128)} %get-tuple-element.55), channel_id=1, source_target_pairs={{0,8},{8,0},{16,24},{24,16},{1,9},{9,1},{17,25},{25,17},{2,10},{10... | collective-permute-start | bytes 1572872 | tf_op jit(solution)/shard_map/ppermute | solution.py:720
  156.9 15.0 %collective-permute-start.25 = (f32[32,32,128]{2,1,0:T(8,128)}, f32[32,32,128]{2,1,0:T(8,128)S(1)}, u32[]{:S(2)}, u32[]{:S(2)}) collective-permute-start(f32[32,32,128]{2,1,0:T(8,128)} %get-tuple-element.56), channel_id=1, source_target_pairs={{0,16},{8,24},{16,0},{24,8},{1,17},{9,25},{17,1},{25,9},{2,18},{10... | collective-permute-start | bytes 1572872 | tf_op jit(solution)/shard_map/ppermute | solution.py:720
  158.5 23.7 %collective-permute-start.26 = (f32[32,32,128]{2,1,0:T(8,128)}, f32[32,32,128]{2,1,0:T(8,128)S(1)}, u32[]{:S(2)}, u32[]{:S(2)}) collective-permute-start(f32[32,32,128]{2,1,0:T(8,128)} %get-tuple-element.57), channel_id=1, source_target_pairs={{0,24},{8,16},{16,8},{24,0},{1,25},{9,17},{17,9},{25,1},{2,26},{10... | collective-permute-start | bytes 1572872 | tf_op jit(solution)/shard_map/ppermute | solution.py:720
  159.0 31.7 %collective-permute-start.21 = (f32[4,1,1,1,8,128]{5,4,0,3,2,1:T(8,128)S(1)}, f32[4,1,1,1,8,128]{5,4,0,3,2,1:T(8,128)S(1)}, u32[]{:S(2)}, u32[]{:S(2)}) collective-permute-start(f32[4,1,1,1,8,128]{5,4,0,3,2,1:T(8,128)S(1)} %get-tuple-element.75), channel_id=1, source_target_pairs={{0,2},{1,3},{2,0},{3,1},{4,6},{5,7},{6,4},{7,5},{8,10},{9,11},{10,... | collective-permute-start | bytes 49160 | tf_op jit(solution)/shard_map/ppermute | solution.py:558
  185.0 10.4 %collective-permute-start.27 = (f32[32,32,128]{2,1,0:T(8,128)}, f32[32,32,128]{2,1,0:T(8,128)S(1)}, u32[]{:S(2)}, u32[]{:S(2)}) collective-permute-start(f32[32,32,128]{2,1,0:T(8,128)} %get-tuple-element.64), channel_id=1, source_target_pairs={{0,8},{8,0},{16,24},{24,16},{1,9},{9,1},{17,25},{25,17},{2,10},{10... | collective-permute-start | bytes 1572872 | tf_op jit(solution)/shard_map/ppermute | solution.py:720
  185.1 15.0 %collective-permute-start.28 = (f32[32,32,128]{2,1,0:T(8,128)}, f32[32,32,128]{2,1,0:T(8,128)S(1)}, u32[]{:S(2)}, u32[]{:S(2)}) collective-permute-start(f32[32,32,128]{2,1,0:T(8,128)} %get-tuple-element.65), channel_id=1, source_target_pairs={{0,16},{8,24},{16,0},{24,8},{1,17},{9,25},{17,1},{25,9},{2,18},{10... | collective-permute-start | bytes 1572872 | tf_op jit(solution)/shard_map/ppermute | solution.py:720
  186.7 23.6 %collective-permute-start.29 = (f32[32,32,128]{2,1,0:T(8,128)}, f32[32,32,128]{2,1,0:T(8,128)S(1)}, u32[]{:S(2)}, u32[]{:S(2)}) collective-permute-start(f32[32,32,128]{2,1,0:T(8,128)} %get-tuple-element.66), channel_id=1, source_target_pairs={{0,24},{8,16},{16,8},{24,0},{1,25},{9,17},{17,9},{25,1},{2,26},{10... | collective-permute-start | bytes 1572872 | tf_op jit(solution)/shard_map/ppermute | solution.py:720
  187.0 5.5 %collective-permute-start.23 = (f32[4,1,1,1,8,128]{5,4,0,3,2,1:T(8,128)S(1)}, f32[4,1,1,1,8,128]{5,4,0,3,2,1:T(8,128)S(1)}, u32[]{:S(2)}, u32[]{:S(2)}) collective-permute-start(f32[4,1,1,1,8,128]{5,4,0,3,2,1:T(8,128)S(1)} %get-tuple-element.76), channel_id=1, source_target_pairs={{0,6},{1,7},{2,4},{3,5},{4,2},{5,3},{6,0},{7,1},{8,14},{9,15},{10,... | collective-permute-start | bytes 49160 | tf_op jit(solution)/shard_map/ppermute | solution.py:558
  190.7 4.6 %collective-permute-start.22 = (f32[4,1,1,1,8,128]{5,4,0,3,2,1:T(8,128)S(1)}, f32[4,1,1,1,8,128]{5,4,0,3,2,1:T(8,128)S(1)}, u32[]{:S(2)}, u32[]{:S(2)}) collective-permute-start(f32[4,1,1,1,8,128]{5,4,0,3,2,1:T(8,128)S(1)} %get-tuple-element.77), channel_id=1, source_target_pairs={{0,4},{1,5},{2,6},{3,7},{4,0},{5,1},{6,2},{7,3},{8,12},{9,13},{10,... | collective-permute-start | bytes 49160 | tf_op jit(solution)/shard_map/ppermute | solution.py:558

commit v8 on v7

--- a/solution.py
+++ b/solution.py
@@ -467,8 +467,8 @@
                 sine, cosine = sincos(phase)
                 for p, (real, imag) in enumerate(parts):
                     at = (c * 2 + p) * 2 * near
-                    o_ref[n, pl.ds(at, near, stride=2), :] = real * cosine - imag * sine
-                    o_ref[n, pl.ds(at + 1, near, stride=2), :] = real * sine + imag * cosine
+                    turned = jnp.stack([real * cosine - imag * sine, real * sine + imag * cosine])
+                    o_ref[n, at : at + 2 * near, :] = jnp.swapaxes(turned, 0, 1).reshape(2 * near, FB)
             return carry
 
         lax.fori_loop(0, group_blocks, body, 0, unroll=4)

time: 215 us -> 216 us (level)
  no operation moved by 1% of the time
where the time goes in v8:
time: 216 us
  waiting for transfers between devices  119 us (55%)
  Pallas kernels  44.8 us (21%)
  starting transfers between devices  43.6 us (20%)
  local copies, waits for them, and re-layouts  5.48 us (3%)
    all_to_all x1, waiting for transfers between devices, local(): lax.all_to_all(packed, 'tm', split_axis=0, concat_axis=0, tiled=True)  44.2 us
    ppermute x6, waiting for transfers between devices, to_groups(): lax.ppermute(outgoing[s], 'wave', [(i, i ^ s) for i in range(groups)])  36.3 us
    pallas_call x5, Pallas kernels, dispersed(): pl.pallas_call(functools.partial(step_kernel, rotate=rotate, hold=hold, f...  31.2 us
    ppermute x20, waiting for transfers between devices, summed(): lax.ppermute(values, ('wave', 'tm'), [(i, i ^ mask) for i in range(size)])  25.3 us
    ppermute x20, starting transfers between devices, summed(): lax.ppermute(values, ('wave', 'tm'), [(i, i ^ mask) for i in range(size)])  16.9 us
    ppermute x4, starting transfers between devices, time_parts(): part = lax.ppermute(part, 'tm', [(i, i ^ mask) for i in range(times)])  7.74 us
    all_to_all x2, starting transfers between devices, to_times(): return lax.all_to_all(values, 'tm', split_axis=0, concat_axis=0, tiled=True)  7.62 us
    all_to_all x1, starting transfers between devices, local(): lax.all_to_all(packed, 'tm', split_axis=0, concat_axis=0, tiled=True)  7.4 us
  transfers between devices with their start and end apart: 33, of which 28 were waited for; matrix products, arithmetic and copies ran while one was open for 3% of the time, Pallas kernels for 2%

profile of v8, /device:TPU:0, one launch (start us, length us, event | category | flops | bytes accessed | tf_op | source)
XLA Modules:
  0.0 215.8 jit_solution(5918586482776363458)
XLA Ops:
  0.7 3.1 %pack.1 = f32[8,512,128]{2,1,0:T(8,128)} custom-call(s32[4]{0:T(128)S(1)} %copy-done.3, f32[4096,128]{1,0:T(8,128)} %bitcast.43), custom_call_target="tpu_custom_call" | custom-call | tf_op jit(solution)/shard_map/pack/pallas_call | solution.py:617
  3.8 7.4 %all-to-all-start = ((f32[8,512,128]{2,1,0:T(8,128)}), f32[8,512,128]{2,1,0:T(8,128)S(1)}, u32[]{:S(2)}, u32[]{:S(2)}) async-start(f32[8,512,128]{2,1,0:T(8,128)} %pack.1), calls=%async_computation | async-start | bytes 4194304 | tf_op jit(solution)/shard_map/all_to_all | solution.py:630
  14.1 1.0 sine_multiply_fusion
  15.2 44.2 %all-to-all-done = f32[8,512,128]{2,1,0:T(8,128)S(1)} async-done(((f32[8,512,128]{2,1,0:T(8,128)}), f32[8,512,128]{2,1,0:T(8,128)S(1)}, u32[]{:S(2)}, u32[]{:S(2)}) %all-to-all-start) | async-done | bytes 2097184 | tf_op jit(solution)/shard_map/all_to_all | solution.py:630
  59.5 6.5 %step.5 = (f32[64,2,32,128]{3,2,1,0:T(8,128)}, f32[1,64,128]{2,1,0:T(8,128)S(1)}) custom-call(f32[64,2,32,128]{3,2,1,0:T(8,128)S(1)} %bitcast.42, f32[4,16,128]{2,1,0:T(8,128)S(1)} %broadcast_in_dim.32.refs_1_.refs_2_.refs_4_, f32[16,16,128]{2,1,0:T(8,128)S(1)} %get-tuple-element.82.refs_2_.refs_5_, f32[16,16,128]{2,1,0:T(8,128)S(1)} %get-tuple-element.83.refs_3_.refs_6_, ...), custom_call_target="tpu_custom_call" | custom-call | flops 1677721600 | bytes 8388608 | tf_op jit(solution)/shard_map/step/pallas_call | solution.py:664
  66.0 1.2 collective-permute-done
  67.2 2.4 %collective-permute-start.3 = (f32[1,64,128]{2,1,0:T(8,128)S(1)}, f32[1,64,128]{2,1,0:T(8,128)S(1)}, u32[]{:S(2)}, u32[]{:S(2)}) collective-permute-start(f32[1,64,128]{2,1,0:T(8,128)S(1)} %add.378), channel_id=1, source_target_pairs={{0,17},{1,16},{2,19},{3,18},{4,21},{5,20},{6,23},{7,22},{8,25},{9,... | collective-permute-start | bytes 98312 | tf_op jit(solution)/shard_map/ppermute | solution.py:507
  72.1 1.5 collective-permute-done.2
  74.2 7.7 %step.6 = (f32[64,2,32,128]{3,2,1,0:T(8,128)S(1)}, f32[1,64,128]{2,1,0:T(8,128)S(1)}) custom-call(f32[64,2,32,128]{3,2,1,0:T(8,128)} %get-tuple-element.36.refs_0_, f32[1,64,128]{2,1,0:T(8,128)S(1)} %add_add_fusion.1.refs_1_, f32[4,16,128]{2,1,0:T(8,128)S(1)} %broadcast_in_dim.32.refs_1_.refs_2_.refs_4_, f32[16,128]{1,0:T(8,128)S(1)} %broadcast_in_dim.33.refs_3_, ...), custom_call_target="tpu_custom_call" | custom-call | flops 1677721600 | bytes 8388608 | tf_op jit(solution)/shard_map/step/pallas_call | solution.py:664
  82.1 1.2 collective-permute-done.4
  83.3 1.4 collective-permute-start.7
  85.2 1.5 collective-permute-start.5
  86.7 1.4 collective-permute-done.7
  89.2 7.0 %step.7 = (f32[64,2,32,128]{3,2,1,0:T(8,128)S(1)}, f32[4,64,128]{2,1,0:T(8,128)S(1)}) custom-call(f32[64,2,32,128]{3,2,1,0:T(8,128)S(1)} %get-tuple-element.38.refs_0_, f32[1,64,128]{2,1,0:T(8,128)S(1)} %add_add_fusion.refs_1_, f32[4,16,128]{2,1,0:T(8,128)S(1)} %broadcast_in_dim.32.refs_1_.refs_2_.refs_4_, f32[16,128]{1,0:T(8,128)S(1)} %broadcast_in_dim.33.refs_3_, ...), custom_call_target="tpu_custom_call" | custom-call | flops 1677721600 | bytes 8388608 | tf_op jit(solution)/shard_map/step/pallas_call | solution.py:664
  97.7 1.5 collective-permute-start.9
  99.3 2.9 %collective-permute-done.9 = f32[2,64,128]{2,1,0:T(8,128)S(1)} collective-permute-done((f32[2,64,128]{2,1,0:T(8,128)S(1)}, f32[2,64,128]{2,1,0:T(8,128)S(1)}, u32[]{:S(2)}, u32[]{:S(2)}) %collective-permute-start.9) | collective-permute-done | bytes 65568 | tf_op jit(solution)/shard_map/ppermute | solution.py:507
  102.3 2.2 %collective-permute-done.14 = f32[2,64,128]{2,1,0:T(8,128)S(1)} collective-permute-done((f32[2,64,128]{2,1,0:T(8,128)S(1)}, f32[2,64,128]{2,1,0:T(8,128)S(1)}, u32[]{:S(2)}, u32[]{:S(2)}) %collective-permute-start.14) | collective-permute-done | bytes 65568 | tf_op jit(solution)/shard_map/ppermute | solution.py:507
  104.6 1.9 collective-permute-done.10
  106.5 1.1 collective-permute-start.11
  107.6 1.7 collective-permute-done.15
  109.3 1.7 collective-permute-start.16
  111.0 1.0 collective-permute-done.11
  112.0 1.6 collective-permute-start.12
  113.6 1.6 collective-permute-start.17
  116.3 1.6 collective-permute-done.17
  118.1 6.2 %step.8 = (f32[64,2,16,128]{3,2,1,0:T(8,128)}, f32[4,64,128]{2,1,0:T(8,128)S(1)}, f32[64,2,16,128]{3,2,1,0:T(8,128)}) custom-call(f32[64,2,32,128]{3,2,1,0:T(8,128)S(1)} %get-tuple-element.40.refs_0_, f32[4,64,128]{2,1,0:T(8,128)S(1)} %pad_maximum_fusion.refs_1_, f32[4,16,128]{2,1,0:T(8,128)S(1)} %broadcast_in_dim.34.refs_4_.refs_2_.refs_1_, ...), custom_call_target="tpu_custom_call" | custom-call | flops 838860800 | bytes 8388608 | tf_op jit(solution)/shard_map/step/pallas_call | solution.py:664
  124.2 4.1 %all-to-all-start.1 = ((f32[8,256,128]{2,1,0:T(8,128)}), f32[8,256,128]{2,1,0:T(8,128)S(1)}, u32[]{:S(2)}, u32[]{:S(2)}) async-start(f32[8,256,128]{2,1,0:T(8,128)} %bitcast.44), calls=%async_computation.1 | async-start | bytes 2097152 | tf_op jit(solution)/shard_map/all_to_all | solution.py:698
  128.5 3.9 %step.9 = (f32[64,2,16,128]{3,2,1,0:T(8,128)}, f32[4,64,128]{2,1,0:T(8,128)S(1)}) custom-call(f32[64,2,16,128]{3,2,1,0:T(8,128)S(1)} %copy-done.4, f32[4,16,128]{2,1,0:T(8,128)S(1)} %broadcast_in_dim.34.refs_4_.refs_2_.refs_1_, f32[16,16,128]{2,1,0:T(8,128)S(1)} %get-tuple-element.79.refs_5_.refs_2_, f32[16,16,128]{2,1,0:T(8,128)S(1)} %get-tuple-element.78.refs_6_.refs_3_, ...), custom_call_target="tpu_custom_call" | custom-call | flops 838860800 | bytes 4194304 | tf_op jit(solution)/shard_map/step/pallas_call | solution.py:664
  132.7 1.1 collective-permute-done.18
  133.8 1.6 collective-permute-start.19
  135.5 3.9 %collective-permute-done.19 = f32[4,64,128]{2,1,0:T(8,128)S(1)} collective-permute-done((f32[4,64,128]{2,1,0:T(8,128)S(1)}, f32[4,64,128]{2,1,0:T(8,128)S(1)}, u32[]{:S(2)}, u32[]{:S(2)}) %collective-permute-start.19) | collective-permute-done | bytes 131104 | tf_op jit(solution)/shard_map/ppermute | solution.py:507
  139.5 2.1 collective-permute-start.20
  141.7 2.1 collective-permute-done.20
  143.8 6.7 %all-to-all-done.1.x_ref = f32[8,256,128]{2,1,0:T(8,128)S(1)} async-done(((f32[8,256,128]{2,1,0:T(8,128)}), f32[8,256,128]{2,1,0:T(8,128)S(1)}, u32[]{:S(2)}, u32[]{:S(2)}) %all-to-all-start.1) | async-done | bytes 1048608 | tf_op jit(solution)/shard_map/all_to_all | solution.py:698
  150.6 2.8 %send.2 = (f32[32,32,128]{2,1,0:T(8,128)}, f32[32,32,128]{2,1,0:T(8,128)}, f32[32,32,128]{2,1,0:T(8,128)}, f32[32,32,128]{2,1,0:T(8,128)}) custom-call(s32[128]{0:T(128)S(1)} %select_reduce_fusion.1.item_ref, s32[4]{0:T(128)S(1)} %convert_reduce_fusion.1.count_ref, f32[8,256,128]{2,1,0:T(8,128)S(1)} %all-to-all-done.1.x_ref), custom_call_target="tpu_custom_call" | custom-call | bytes 4194304 | tf_op jit(solution)/shard_map/send/pallas_call | solution.py:702
  153.4 3.6 %all-to-all-start.2 = ((f32[8,256,128]{2,1,0:T(8,128)}), f32[8,256,128]{2,1,0:T(8,128)S(1)}, u32[]{:S(2)}, u32[]{:S(2)}) async-start(f32[8,256,128]{2,1,0:T(8,128)} %bitcast.19), calls=%async_computation.2 | async-start | bytes 2097152 | tf_op jit(solution)/shard_map/all_to_all | solution.py:698
  157.1 1.6 collective-permute-start.25
  159.2 1.9 collective-permute-start.21
  161.1 11.0 %collective-permute-done.25.refs_2_ = f32[32,32,128]{2,1,0:T(8,128)S(1)} collective-permute-done((f32[32,32,128]{2,1,0:T(8,128)}, f32[32,32,128]{2,1,0:T(8,128)S(1)}, u32[]{:S(2)}, u32[]{:S(2)}) %collective-permute-start.25) | collective-permute-done | bytes 524320 | tf_op jit(solution)/shard_map/ppermute | solution.py:720
  172.1 10.3 %collective-permute-done.26.refs_3_ = f32[32,32,128]{2,1,0:T(8,128)S(1)} collective-permute-done((f32[32,32,128]{2,1,0:T(8,128)}, f32[32,32,128]{2,1,0:T(8,128)S(1)}, u32[]{:S(2)}, u32[]{:S(2)}) %collective-permute-start.26) | collective-permute-done | bytes 524320 | tf_op jit(solution)/shard_map/ppermute | solution.py:720
  182.4 2.8 %send.3 = (f32[32,32,128]{2,1,0:T(8,128)}, f32[32,32,128]{2,1,0:T(8,128)}, f32[32,32,128]{2,1,0:T(8,128)}, f32[32,32,128]{2,1,0:T(8,128)}) custom-call(s32[128]{0:T(128)S(1)} %select_reduce_fusion.1.item_ref, s32[4]{0:T(128)S(1)} %convert_reduce_fusion.1.count_ref, f32[8,256,128]{2,1,0:T(8,128)S(1)} %all-to-all-done.2.x_ref), custom_call_target="tpu_custom_call" | custom-call | bytes 4194304 | tf_op jit(solution)/shard_map/send/pallas_call | solution.py:702
  185.4 1.6 collective-permute-start.28
  187.3 3.7 %collective-permute-start.23 = (f32[4,1,1,1,8,128]{5,4,0,3,2,1:T(8,128)S(1)}, f32[4,1,1,1,8,128]{5,4,0,3,2,1:T(8,128)S(1)}, u32[]{:S(2)}, u32[]{:S(2)}) collective-permute-start(f32[4,1,1,1,8,128]{5,4,0,3,2,1:T(8,128)S(1)} %get-tuple-element.76), channel_id=1, source_target_pairs={{0,6},{1,7},{2,4},{3,5},{4,2},{5,3},{6,0},{7,1},{8,14},{9,15},{10,... | collective-permute-start | bytes 49160 | tf_op jit(solution)/shard_map/ppermute | solution.py:558
  191.2 1.6 collective-permute-done.23
  192.8 2.8 %collective-permute-done.22 = f32[4,1,1,1,8,128]{5,4,0,3,2,1:T(8,128)S(1)} collective-permute-done((f32[4,1,1,1,8,128]{5,4,0,3,2,1:T(8,128)S(1)}, f32[4,1,1,1,8,128]{5,4,0,3,2,1:T(8,128)S(1)}, u32[]{:S(2)}, u32[]{:S(2)}) %collective-permute-start.22) | collective-permute-done | bytes 16416 | tf_op jit(solution)/shard_map/ppermute | solution.py:558
  195.7 4.7 %collective-permute-done.28.refs_6_ = f32[32,32,128]{2,1,0:T(8,128)S(1)} collective-permute-done((f32[32,32,128]{2,1,0:T(8,128)}, f32[32,32,128]{2,1,0:T(8,128)S(1)}, u32[]{:S(2)}, u32[]{:S(2)}) %collective-permute-start.28) | collective-permute-done | bytes 524320 | tf_op jit(solution)/shard_map/ppermute | solution.py:720
  200.4 10.3 %collective-permute-done.29.refs_7_ = f32[32,32,128]{2,1,0:T(8,128)S(1)} collective-permute-done((f32[32,32,128]{2,1,0:T(8,128)}, f32[32,32,128]{2,1,0:T(8,128)S(1)}, u32[]{:S(2)}, u32[]{:S(2)}) %collective-permute-start.29) | collective-permute-done | bytes 524320 | tf_op jit(solution)/shard_map/ppermute | solution.py:720
  210.8 4.9 %place.1 = f32[64,64,128]{2,1,0:T(8,128)} custom-call(s32[64]{0:T(128)S(1)} %select_reduce_fusion.from_ref, f32[4,8,128]{2,1,0:T(8,128)S(1)} %broadcast_in_dim.31.strength_ref, f32[4,8,128]{2,1,0:T(8,128)S(1)} %add_bitcast_fusion.q_ref, f32[32,32,128]{2,1,0:T(8,128)} %get-tuple-element.58.refs_0_, f32[32,32,128]{2,1,0:T(8,128)S(1)} %collective-permute-done.24.refs_1_, ...), custom_call_target="tpu_custom_call" | custom-call | bytes 8388608 | tf_op jit(solution)/shard_map/place/pallas_call | solution.py:738
  (110 shorter events, 13.4 us)
Async XLA Ops:
  0.0 0.7 copy-start.3
  3.7 7.5 %copy-start.6 = (s32[4,64]{1,0:T(4,128)S(1)}, s32[4,64]{1,0:T(4,128)}, u32[]{:S(2)}) copy-start(s32[4,64]{1,0:T(4,128)} %param.13) | copy-start | bytes 3076
  3.7 8.2 %copy-start.5 = (s32[4,64]{1,0:T(4,128)S(1)}, s32[4,64]{1,0:T(4,128)}, u32[]{:S(2)}) copy-start(s32[4,64]{1,0:T(4,128)} %param.14) | copy-start | bytes 3076
  3.8 8.9 %copy-start.9 = (f32[2,4]{1,0:T(2,128)S(1)}, f32[2,4]{1,0:T(2,128)}, u32[]{:S(2)}) copy-start(f32[2,4]{1,0:T(2,128)} %param.15) | copy-start | bytes 100
  3.8 55.6 %all-to-all-start = ((f32[8,512,128]{2,1,0:T(8,128)}), f32[8,512,128]{2,1,0:T(8,128)S(1)}, u32[]{:S(2)}, u32[]{:S(2)}) async-start(f32[8,512,128]{2,1,0:T(8,128)} %pack.1), calls=%async_computation | async-start | bytes 4194304 | tf_op jit(solution)/shard_map/all_to_all | solution.py:630
  11.2 3.0 %copy-start.7 = (f32[16,128]{1,0:T(8,128)S(1)}, f32[16,128]{1,0:T(8,128)}, u32[]{:S(2)}) copy-start(f32[16,128]{1,0:T(8,128)} %constant.274) | copy-start | bytes 24580
  11.2 3.0 %copy-start.8 = (f32[16,128]{1,0:T(8,128)S(1)}, f32[16,128]{1,0:T(8,128)}, u32[]{:S(2)}) copy-start(f32[16,128]{1,0:T(8,128)} %constant.273) | copy-start | bytes 24580
  11.2 48.3 %copy-start = (bf16[512,256]{1,0:T(8,128)(2,1)S(1)}, bf16[512,256]{1,0:T(8,128)(2,1)}, u32[]{:S(2)}) copy-start(bf16[512,256]{1,0:T(8,128)(2,1)} %constant.270.clone.refs_6_.refs_9_) | copy-start | bytes 786436
  11.2 48.3 %copy-start.1 = (bf16[512,256]{1,0:T(8,128)(2,1)S(1)}, bf16[512,256]{1,0:T(8,128)(2,1)}, u32[]{:S(2)}) copy-start(bf16[512,256]{1,0:T(8,128)(2,1)} %constant.269.clone.refs_5_.refs_8_) | copy-start | bytes 786436
  11.2 48.3 %copy-start.2 = (f32[2,16,8,128]{3,2,1,0:T(8,128)S(1)}, f32[2,16,8,128]{3,2,1,0:T(8,128)}, u32[]{:S(2)}) copy-start(f32[2,16,8,128]{3,2,1,0:T(8,128)} %constant.268.clone.refs_4_.refs_7_) | copy-start | bytes 393220
  59.5 11.2 %copy-start.10 = (f32[2,4]{1,0:T(2,128)S(1)}, f32[2,4]{1,0:T(2,128)}, u32[]{:S(2)}) copy-start(f32[2,4]{1,0:T(2,128)} %param.16) | copy-start | bytes 100
  66.0 1.3 collective-permute-start
  67.2 4.8 %collective-permute-start.3 = (f32[1,64,128]{2,1,0:T(8,128)S(1)}, f32[1,64,128]{2,1,0:T(8,128)S(1)}, u32[]{:S(2)}, u32[]{:S(2)}) collective-permute-start(f32[1,64,128]{2,1,0:T(8,128)S(1)} %add.378), channel_id=1, source_target_pairs={{0,17},{1,16},{2,19},{3,18},{4,21},{5,20},{6,23},{7,22},{8,25},{9,... | collective-permute-start | bytes 98312 | tf_op jit(solution)/shard_map/ppermute | solution.py:507
  69.7 3.9 %collective-permute-start.2 = (f32[1,64,128]{2,1,0:T(8,128)S(1)}, f32[1,64,128]{2,1,0:T(8,128)S(1)}, u32[]{:S(2)}, u32[]{:S(2)}) collective-permute-start(f32[1,64,128]{2,1,0:T(8,128)S(1)} %add.378), channel_id=1, source_target_pairs={{0,1},{1,0},{2,3},{3,2},{4,5},{5,4},{6,7},{7,6},{8,9},{9,8},{10,11... | collective-permute-start | bytes 98312 | tf_op jit(solution)/shard_map/ppermute | solution.py:507
  70.2 3.9 %collective-permute-start.1 = (f32[1,64,128]{2,1,0:T(8,128)S(1)}, f32[1,64,128]{2,1,0:T(8,128)S(1)}, u32[]{:S(2)}, u32[]{:S(2)}) collective-permute-start(f32[1,64,128]{2,1,0:T(8,128)S(1)} %add.378), channel_id=1, source_target_pairs={{0,16},{1,17},{2,18},{3,19},{4,20},{5,21},{6,22},{7,23},{8,24},{9,... | collective-permute-start | bytes 98312 | tf_op jit(solution)/shard_map/ppermute | solution.py:507
  82.0 1.3 collective-permute-start.4
  83.3 4.9 %collective-permute-start.7 = (f32[1,64,128]{2,1,0:T(8,128)S(1)}, f32[1,64,128]{2,1,0:T(8,128)S(1)}, u32[]{:S(2)}, u32[]{:S(2)}) collective-permute-start(f32[1,64,128]{2,1,0:T(8,128)S(1)} %add.382), channel_id=1, source_target_pairs={{0,17},{1,16},{2,19},{3,18},{4,21},{5,20},{6,23},{7,22},{8,25},{9,... | collective-permute-start | bytes 98312 | tf_op jit(solution)/shard_map/ppermute | solution.py:507
  84.7 3.9 %collective-permute-start.6 = (f32[1,64,128]{2,1,0:T(8,128)S(1)}, f32[1,64,128]{2,1,0:T(8,128)S(1)}, u32[]{:S(2)}, u32[]{:S(2)}) collective-permute-start(f32[1,64,128]{2,1,0:T(8,128)S(1)} %add.382), channel_id=1, source_target_pairs={{0,1},{1,0},{2,3},{3,2},{4,5},{5,4},{6,7},{7,6},{8,9},{9,8},{10,11... | collective-permute-start | bytes 98312 | tf_op jit(solution)/shard_map/ppermute | solution.py:507
  85.2 3.9 %collective-permute-start.5 = (f32[1,64,128]{2,1,0:T(8,128)S(1)}, f32[1,64,128]{2,1,0:T(8,128)S(1)}, u32[]{:S(2)}, u32[]{:S(2)}) collective-permute-start(f32[1,64,128]{2,1,0:T(8,128)S(1)} %add.382), channel_id=1, source_target_pairs={{0,16},{1,17},{2,18},{3,19},{4,20},{5,21},{6,22},{7,23},{8,24},{9,... | collective-permute-start | bytes 98312 | tf_op jit(solution)/shard_map/ppermute | solution.py:507
  96.2 1.3 collective-permute-start.8
  96.3 1.4 collective-permute-start.13
  97.7 4.4 %collective-permute-start.9 = (f32[2,64,128]{2,1,0:T(8,128)S(1)}, f32[2,64,128]{2,1,0:T(8,128)S(1)}, u32[]{:S(2)}, u32[]{:S(2)}) collective-permute-start(f32[2,64,128]{2,1,0:T(8,128)S(1)} %get-tuple-element.71), channel_id=1, source_target_pairs={{0,1},{1,0},{2,3},{3,2},{4,5},{5,4},{6,7},{7,6},{8,9},{9,8},{10,11... | collective-permute-start | bytes 196616 | tf_op jit(solution)/shard_map/ppermute | solution.py:507
  99.3 5.2 %collective-permute-start.14 = (f32[2,64,128]{2,1,0:T(8,128)S(1)}, f32[2,64,128]{2,1,0:T(8,128)S(1)}, u32[]{:S(2)}, u32[]{:S(2)}) collective-permute-start(f32[2,64,128]{2,1,0:T(8,128)S(1)} %get-tuple-element.72), channel_id=1, source_target_pairs={{0,4},{1,5},{2,6},{3,7},{4,0},{5,1},{6,2},{7,3},{8,12},{9,13},{10,... | collective-permute-start | bytes 196616 | tf_op jit(solution)/shard_map/ppermute | solution.py:507
  102.2 4.3 %collective-permute-start.10 = (f32[2,64,128]{2,1,0:T(8,128)S(1)}, f32[2,64,128]{2,1,0:T(8,128)S(1)}, u32[]{:S(2)}, u32[]{:S(2)}) collective-permute-start(f32[2,64,128]{2,1,0:T(8,128)S(1)} %add.396), channel_id=1, source_target_pairs={{0,2},{1,3},{2,0},{3,1},{4,6},{5,7},{6,4},{7,5},{8,10},{9,11},{10,... | collective-permute-start | bytes 196616 | tf_op jit(solution)/shard_map/ppermute | solution.py:507
  104.5 4.8 %collective-permute-start.15 = (f32[2,64,128]{2,1,0:T(8,128)S(1)}, f32[2,64,128]{2,1,0:T(8,128)S(1)}, u32[]{:S(2)}, u32[]{:S(2)}) collective-permute-start(f32[2,64,128]{2,1,0:T(8,128)S(1)} %add.401), channel_id=1, source_target_pairs={{0,2},{1,3},{2,0},{3,1},{4,6},{5,7},{6,4},{7,5},{8,10},{9,11},{10,... | collective-permute-start | bytes 196616 | tf_op jit(solution)/shard_map/ppermute | solution.py:507
  106.5 5.4 %collective-permute-start.11 = (f32[2,64,128]{2,1,0:T(8,128)S(1)}, f32[2,64,128]{2,1,0:T(8,128)S(1)}, u32[]{:S(2)}, u32[]{:S(2)}) collective-permute-start(f32[2,64,128]{2,1,0:T(8,128)S(1)} %add.397), channel_id=1, source_target_pairs={{0,4},{1,5},{2,6},{3,7},{4,0},{5,1},{6,2},{7,3},{8,12},{9,13},{10,... | collective-permute-start | bytes 196616 | tf_op jit(solution)/shard_map/ppermute | solution.py:507
  109.3 4.3 %collective-permute-start.16 = (f32[2,64,128]{2,1,0:T(8,128)S(1)}, f32[2,64,128]{2,1,0:T(8,128)S(1)}, u32[]{:S(2)}, u32[]{:S(2)}) collective-permute-start(f32[2,64,128]{2,1,0:T(8,128)S(1)} %add.402), channel_id=1, source_target_pairs={{0,1},{1,0},{2,3},{3,2},{4,5},{5,4},{6,7},{7,6},{8,9},{9,8},{10,11... | collective-permute-start | bytes 196616 | tf_op jit(solution)/shard_map/ppermute | solution.py:507
  112.0 4.3 %collective-permute-start.12 = (f32[2,64,128]{2,1,0:T(8,128)S(1)}, f32[2,64,128]{2,1,0:T(8,128)S(1)}, u32[]{:S(2)}, u32[]{:S(2)}) collective-permute-start(f32[2,64,128]{2,1,0:T(8,128)S(1)} %add.398), channel_id=1, source_target_pairs={{0,16},{1,17},{2,18},{3,19},{4,20},{5,21},{6,22},{7,23},{8,24},{9,... | collective-permute-start | bytes 196616 | tf_op jit(solution)/shard_map/ppermute | solution.py:507
  113.6 4.3 %collective-permute-start.17 = (f32[2,64,128]{2,1,0:T(8,128)S(1)}, f32[2,64,128]{2,1,0:T(8,128)S(1)}, u32[]{:S(2)}, u32[]{:S(2)}) collective-permute-start(f32[2,64,128]{2,1,0:T(8,128)S(1)} %add.403), channel_id=1, source_target_pairs={{0,16},{1,17},{2,18},{3,19},{4,20},{5,21},{6,22},{7,23},{8,24},{9,... | collective-permute-start | bytes 196616 | tf_op jit(solution)/shard_map/ppermute | solution.py:507
  124.2 4.3 %copy-start.4 = (f32[64,2,16,128]{3,2,1,0:T(8,128)S(1)}, f32[64,2,16,128]{3,2,1,0:T(8,128)}, u32[]{:S(2)}) copy-start(f32[64,2,16,128]{3,2,1,0:T(8,128)} %get-tuple-element.44.refs_0_) | copy-start | bytes 3145732
  124.2 26.4 %all-to-all-start.1 = ((f32[8,256,128]{2,1,0:T(8,128)}), f32[8,256,128]{2,1,0:T(8,128)S(1)}, u32[]{:S(2)}, u32[]{:S(2)}) async-start(f32[8,256,128]{2,1,0:T(8,128)} %bitcast.44), calls=%async_computation.1 | async-start | bytes 2097152 | tf_op jit(solution)/shard_map/all_to_all | solution.py:698
  132.4 1.4 collective-permute-start.18
  133.8 5.6 %collective-permute-start.19 = (f32[4,64,128]{2,1,0:T(8,128)S(1)}, f32[4,64,128]{2,1,0:T(8,128)S(1)}, u32[]{:S(2)}, u32[]{:S(2)}) collective-permute-start(f32[4,64,128]{2,1,0:T(8,128)S(1)} %add.406), channel_id=1, source_target_pairs={{0,16},{1,17},{2,18},{3,19},{4,20},{5,21},{6,22},{7,23},{8,24},{9,... | collective-permute-start | bytes 393224 | tf_op jit(solution)/shard_map/ppermute | solution.py:507
  139.5 4.3 %collective-permute-start.20 = (f32[4,2,2,1,8,128]{5,4,0,3,2,1:T(8,128)S(1)}, f32[4,2,2,1,8,128]{5,4,0,3,2,1:T(8,128)S(1)}, u32[]{:S(2)}, u32[]{:S(2)}) collective-permute-start(f32[4,2,2,1,8,128]{5,4,0,3,2,1:T(8,128)S(1)} %copy.29), channel_id=1, source_target_pairs={{0,1},{1,0},{2,3},{3,2},{4,5},{5,4},{6,7},{7,6},{8,9},{9,8},{10,11... | collective-permute-start | bytes 196616 | tf_op jit(solution)/shard_map/ppermute | solution.py:558
  153.4 29.0 %all-to-all-start.2 = ((f32[8,256,128]{2,1,0:T(8,128)}), f32[8,256,128]{2,1,0:T(8,128)S(1)}, u32[]{:S(2)}, u32[]{:S(2)}) async-start(f32[8,256,128]{2,1,0:T(8,128)} %bitcast.19), calls=%async_computation.2 | async-start | bytes 2097152 | tf_op jit(solution)/shard_map/all_to_all | solution.py:698
  157.0 4.1 %collective-permute-start.24 = (f32[32,32,128]{2,1,0:T(8,128)}, f32[32,32,128]{2,1,0:T(8,128)S(1)}, u32[]{:S(2)}, u32[]{:S(2)}) collective-permute-start(f32[32,32,128]{2,1,0:T(8,128)} %get-tuple-element.55), channel_id=1, source_target_pairs={{0,8},{8,0},{16,24},{24,16},{1,9},{9,1},{17,25},{25,17},{2,10},{10... | collective-permute-start | bytes 1572872 | tf_op jit(solution)/shard_map/ppermute | solution.py:720
  157.1 15.0 %collective-permute-start.25 = (f32[32,32,128]{2,1,0:T(8,128)}, f32[32,32,128]{2,1,0:T(8,128)S(1)}, u32[]{:S(2)}, u32[]{:S(2)}) collective-permute-start(f32[32,32,128]{2,1,0:T(8,128)} %get-tuple-element.56), channel_id=1, source_target_pairs={{0,16},{8,24},{16,0},{24,8},{1,17},{9,25},{17,1},{25,9},{2,18},{10... | collective-permute-start | bytes 1572872 | tf_op jit(solution)/shard_map/ppermute | solution.py:720
  158.7 23.7 %collective-permute-start.26 = (f32[32,32,128]{2,1,0:T(8,128)}, f32[32,32,128]{2,1,0:T(8,128)S(1)}, u32[]{:S(2)}, u32[]{:S(2)}) collective-permute-start(f32[32,32,128]{2,1,0:T(8,128)} %get-tuple-element.57), channel_id=1, source_target_pairs={{0,24},{8,16},{16,8},{24,0},{1,25},{9,17},{17,9},{25,1},{2,26},{10... | collective-permute-start | bytes 1572872 | tf_op jit(solution)/shard_map/ppermute | solution.py:720
  159.2 31.9 %collective-permute-start.21 = (f32[4,1,1,1,8,128]{5,4,0,3,2,1:T(8,128)S(1)}, f32[4,1,1,1,8,128]{5,4,0,3,2,1:T(8,128)S(1)}, u32[]{:S(2)}, u32[]{:S(2)}) collective-permute-start(f32[4,1,1,1,8,128]{5,4,0,3,2,1:T(8,128)S(1)} %get-tuple-element.75), channel_id=1, source_target_pairs={{0,2},{1,3},{2,0},{3,1},{4,6},{5,7},{6,4},{7,5},{8,10},{9,11},{10,... | collective-permute-start | bytes 49160 | tf_op jit(solution)/shard_map/ppermute | solution.py:558
  185.3 10.4 %collective-permute-start.27 = (f32[32,32,128]{2,1,0:T(8,128)}, f32[32,32,128]{2,1,0:T(8,128)S(1)}, u32[]{:S(2)}, u32[]{:S(2)}) collective-permute-start(f32[32,32,128]{2,1,0:T(8,128)} %get-tuple-element.64), channel_id=1, source_target_pairs={{0,8},{8,0},{16,24},{24,16},{1,9},{9,1},{17,25},{25,17},{2,10},{10... | collective-permute-start | bytes 1572872 | tf_op jit(solution)/shard_map/ppermute | solution.py:720
  185.4 15.0 %collective-permute-start.28 = (f32[32,32,128]{2,1,0:T(8,128)}, f32[32,32,128]{2,1,0:T(8,128)S(1)}, u32[]{:S(2)}, u32[]{:S(2)}) collective-permute-start(f32[32,32,128]{2,1,0:T(8,128)} %get-tuple-element.65), channel_id=1, source_target_pairs={{0,16},{8,24},{16,0},{24,8},{1,17},{9,25},{17,1},{25,9},{2,18},{10... | collective-permute-start | bytes 1572872 | tf_op jit(solution)/shard_map/ppermute | solution.py:720
  186.9 23.7 %collective-permute-start.29 = (f32[32,32,128]{2,1,0:T(8,128)}, f32[32,32,128]{2,1,0:T(8,128)S(1)}, u32[]{:S(2)}, u32[]{:S(2)}) collective-permute-start(f32[32,32,128]{2,1,0:T(8,128)} %get-tuple-element.66), channel_id=1, source_target_pairs={{0,24},{8,16},{16,8},{24,0},{1,25},{9,17},{17,9},{25,1},{2,26},{10... | collective-permute-start | bytes 1572872 | tf_op jit(solution)/shard_map/ppermute | solution.py:720
  187.3 5.5 %collective-permute-start.23 = (f32[4,1,1,1,8,128]{5,4,0,3,2,1:T(8,128)S(1)}, f32[4,1,1,1,8,128]{5,4,0,3,2,1:T(8,128)S(1)}, u32[]{:S(2)}, u32[]{:S(2)}) collective-permute-start(f32[4,1,1,1,8,128]{5,4,0,3,2,1:T(8,128)S(1)} %get-tuple-element.76), channel_id=1, source_target_pairs={{0,6},{1,7},{2,4},{3,5},{4,2},{5,3},{6,0},{7,1},{8,14},{9,15},{10,... | collective-permute-start | bytes 49160 | tf_op jit(solution)/shard_map/ppermute | solution.py:558
  191.0 4.6 %collective-permute-start.22 = (f32[4,1,1,1,8,128]{5,4,0,3,2,1:T(8,128)S(1)}, f32[4,1,1,1,8,128]{5,4,0,3,2,1:T(8,128)S(1)}, u32[]{:S(2)}, u32[]{:S(2)}) collective-permute-start(f32[4,1,1,1,8,128]{5,4,0,3,2,1:T(8,128)S(1)} %get-tuple-element.77), channel_id=1, source_target_pairs={{0,4},{1,5},{2,6},{3,7},{4,0},{5,1},{6,2},{7,3},{8,12},{9,13},{10,... | collective-permute-start | bytes 49160 | tf_op jit(solution)/shard_map/ppermute | solution.py:558
